TPU v7x, 32 devices: a whole 2x2x4 slice. The times are simulated.
32 devices in a mesh: dp: 16 (over z, y, x), mp: 2 (over core).
Axes of the slice: x: 2, y: 2, z: 4, core: 2. Of those that a mesh axis runs over, the one named last changes fastest.
Arguments:
- maps_in: bfloat16 [128, 256, 256], P('dp', None, 'mp'), may hold values from -6 to 6
- timesteps: int32 [128], P('dp'), may hold values from 0 to 999
- temb_table: float32 [1000, 512], replicated, may hold values from -6 to 6
- norm_gain: float32 [3, 256], P(None, 'mp'), may hold values from 0.25 to 1.75
- norm_bias: float32 [3, 256], P(None, 'mp'), may hold values from -2 to 2
- conv1_weight: bfloat16 [3, 3, 256, 256], P(None, None, None, 'mp'), may hold values from -0.125 to 0.125
- conv_bias: float32 [2, 256], P(None, 'mp'), may hold values from -2 to 2
- temb_weight: bfloat16 [512, 256], P(None, 'mp'), may hold values from -0.25 to 0.25
- temb_bias: float32 [256], P('mp'), may hold values from -2 to 2
- conv2_weight: bfloat16 [3, 3, 256, 256], P(None, None, 'mp'), may hold values from -0.125 to 0.125
- qkv_weight: bfloat16 [256, 3, 256], P(None, None, 'mp'), may hold values from -0.5 to 0.5
- qkv_bias: float32 [2, 256], P(None, 'mp'), may hold values from -2 to 2
- out_weight: bfloat16 [256, 256], P('mp'), may hold values from -3 to 3
- out_bias: float32 [256], P('mp'), may hold values from -2 to 2
- out_grad: bfloat16 [128, 256, 256], P('dp', None, 'mp'), may hold values from -6 to 6
Outputs:
- maps_out: bfloat16 [128, 256, 256], P('dp', None, 'mp')
- maps_grad: float32 [128, 256, 256], P('dp', None, 'mp')
- table_grad: float32 [1000, 512], replicated
- norm_gain_grad: float32 [3, 256], P(None, 'mp')
- norm_bias_grad: float32 [3, 256], P(None, 'mp')
- conv1_grad: float32 [3, 3, 256, 256], P(None, None, None, 'mp')
- conv_bias_grad: float32 [2, 256], P(None, 'mp')
- temb_weight_grad: float32 [512, 256], P(None, 'mp')
- temb_bias_grad: float32 [256], P('mp')
- conv2_grad: float32 [3, 3, 256, 256], P(None, None, 'mp')
- qkv_grad: float32 [256, 3, 256], P(None, None, 'mp')
- qkv_bias_grad: float32 [2, 256], P(None, 'mp')
- out_weight_grad: float32 [256, 256], P('mp')
- out_bias_grad: float32 [256], P('mp')
All inputs are finite; a program needn't handle non-finite values.
Results may differ from a plain program's by a relative error of at most 0.0185.
Values may be sent and summed in bfloat16 or wider, within the bound.
No kernel may reach another device: no remote copies, remote signals or barrier semaphores. Data moves between devices by JAX's collectives and lax.ppermute only.
A program may use at most 128 MiB of HBM per device.

v0:
```python
import math

import jax
import jax.numpy as jnp
from jax import lax
from jax.sharding import PartitionSpec as P

C = 256
GROUPS = 32
SIDE = 16


epsilon = 1e-06


def group_norm(values, gain_row, shift_row):
    count_maps, count_pix, count_ch = values.shape
    group_size = C // GROUPS
    grouped = values.reshape(count_maps, count_pix, count_ch // group_size, group_size)
    center = jnp.mean(grouped, axis=(1, 3), keepdims=True)
    spread = jnp.mean((grouped - center) ** 2, axis=(1, 3), keepdims=True)
    normed = ((grouped - center) * lax.rsqrt(spread + epsilon)).reshape(
        count_maps, count_pix, count_ch
    )
    return normed * gain_row + shift_row


def norm_silu(values, gain_row, shift_row):
    return jax.nn.silu(group_norm(values, gain_row, shift_row))


def contract_rows(left, right):
    return lax.dot_general(
        left, right, (((0,), (0,)), ((), ())), preferred_element_type=jnp.float32
    )


def contract_cols(left, right):
    return lax.dot_general(
        left, right, (((1,), (1,)), ((), ())), preferred_element_type=jnp.float32
    )


def padded_grid(inputs):
    count_maps, count_pix, count_ch = inputs.shape
    grid = inputs.reshape(count_maps, SIDE, SIDE, count_ch)
    return jnp.pad(grid, ((0, 0), (1, 1), (1, 1), (0, 0)))


def window_at(padded, row_off, col_off):
    return padded[:, row_off : row_off + SIDE, col_off : col_off + SIDE, :].reshape(
        -1, padded.shape[3]
    )


def conv_apply(inputs, kernel):
    count_maps, count_pix, in_ch = inputs.shape
    padded = padded_grid(inputs)
    running = jnp.zeros((count_maps * count_pix, kernel.shape[3]), jnp.float32)
    for row_off in range(3):
        for col_off in range(3):
            running = running + jnp.dot(
                window_at(padded, row_off, col_off),
                kernel[row_off, col_off],
                preferred_element_type=jnp.float32,
            )
    return running.reshape(count_maps, count_pix, kernel.shape[3])


def conv_input_grad(grad_rows, kernel):
    count_maps, count_pix, out_ch = grad_rows.shape
    padded = padded_grid(grad_rows)
    running = jnp.zeros((count_maps * count_pix, kernel.shape[2]), jnp.float32)
    for row_off in range(3):
        for col_off in range(3):
            running = running + contract_cols(
                window_at(padded, 2 - row_off, 2 - col_off), kernel[row_off, col_off]
            )
    return running.reshape(count_maps, count_pix, kernel.shape[2])


def conv_kernel_grad(inputs, grad_rows):
    padded = padded_grid(inputs)
    flat_grads = grad_rows.reshape(-1, grad_rows.shape[2])
    kernel_rows = []
    for row_off in range(3):
        kernel_cols = []
        for col_off in range(3):
            kernel_cols.append(contract_rows(window_at(padded, row_off, col_off), flat_grads))
        kernel_rows.append(jnp.stack(kernel_cols))
    return jnp.stack(kernel_rows)


def gather_channels(values):
    return lax.all_gather(values, "mp", axis=2, tiled=True)


def reduce_channels(values):
    return lax.psum_scatter(values, "mp", scatter_dimension=2, tiled=True)


def table_total(table_part):
    return lax.psum(table_part, ("dp", "mp"))


def channel_scores(queries, key_rows, score_scale):
    partial_scores = (
        jnp.einsum("mqc,mkc->mqk", queries, key_rows, preferred_element_type=jnp.float32)
        * score_scale
    )
    return lax.psum(partial_scores, "mp")


def channel_probs_sum(partial_grad):
    return lax.psum(partial_grad.astype(jnp.bfloat16), "mp").astype(jnp.float32)


def attend(scores, value_rows):
    log_total = jax.nn.logsumexp(scores, axis=-1)
    soft_probs = jnp.exp(scores - log_total[..., None])
    attended = jnp.einsum(
        "mqk,mkc->mqc",
        soft_probs.astype(jnp.bfloat16),
        value_rows,
        preferred_element_type=jnp.float32,
    )
    return (attended.astype(jnp.bfloat16), log_total)


def attend_back(scores, log_total, queries, key_rows, value_rows, grad_out, score_scale, probs_sum):
    soft_probs = jnp.exp(scores - log_total[..., None])
    grad_values = jnp.einsum(
        "mqk,mqc->mkc",
        soft_probs.astype(jnp.bfloat16),
        grad_out,
        preferred_element_type=jnp.float32,
    )
    grad_probs = probs_sum(
        jnp.einsum("mqc,mkc->mqk", grad_out, value_rows, preferred_element_type=jnp.float32)
    )
    grad_scores = soft_probs * (
        grad_probs - jnp.sum(soft_probs * grad_probs, axis=-1, keepdims=True)
    )
    grad_scores = grad_scores.astype(jnp.bfloat16)
    grad_queries = (
        jnp.einsum("mqk,mkc->mqc", grad_scores, key_rows, preferred_element_type=jnp.float32)
        * score_scale
    )
    grad_keys = (
        jnp.einsum("mqk,mqc->mkc", grad_scores, queries, preferred_element_type=jnp.float32)
        * score_scale
    )
    return jnp.stack(
        [
            grad_queries.astype(jnp.bfloat16),
            grad_keys.astype(jnp.bfloat16),
            grad_values.astype(jnp.bfloat16),
        ],
        axis=2,
    )


def channel_path(
    maps_in,
    timesteps,
    temb_table,
    norm_gain,
    norm_bias,
    conv1_weight,
    conv_bias,
    temb_weight,
    temb_bias,
    conv2_weight,
    qkv_weight,
    qkv_bias,
    out_weight,
    out_bias,
    out_grad,
):
    highest = lax.Precision.HIGHEST
    inputs = maps_in.astype(jnp.float32)
    count_maps, count_pix, local_ch = inputs.shape
    score_scale = 1.0 / math.sqrt(C)
    temb_float = temb_weight.astype(jnp.float32)
    embedded = jnp.take(temb_table, timesteps, axis=0)
    first_act, first_pull = jax.vjp(norm_silu, inputs, norm_gain[0], norm_bias[0])
    first_full = gather_channels(first_act.astype(jnp.bfloat16))
    emb_act, emb_pull = jax.vjp(jax.nn.silu, embedded)
    time_proj = jnp.dot(emb_act, temb_float, precision=highest) + temb_bias
    hidden_one = conv_apply(first_full, conv1_weight) + conv_bias[0] + time_proj[:, None, :]
    second_act, second_pull = jax.vjp(norm_silu, hidden_one, norm_gain[1], norm_bias[1])
    second_low = second_act.astype(jnp.bfloat16)
    middle = inputs + reduce_channels(conv_apply(second_low, conv2_weight)) + conv_bias[1]
    third_act, third_pull = jax.vjp(group_norm, middle, norm_gain[2], norm_bias[2])
    third_full = gather_channels(third_act.astype(jnp.bfloat16))
    projected = jnp.dot(
        third_full.reshape(-1, C),
        qkv_weight.reshape(C, 3 * local_ch),
        preferred_element_type=jnp.float32,
    )
    projected = projected.reshape(count_maps, count_pix, 3, local_ch)
    bias_full = jnp.stack([qkv_bias[0], jnp.zeros_like(qkv_bias[0]), qkv_bias[1]])
    stacked = (projected + bias_full).astype(jnp.bfloat16)
    queries = stacked[:, :, 0]
    key_rows = stacked[:, :, 1]
    value_rows = stacked[:, :, 2]
    scores = channel_scores(queries, key_rows, score_scale)
    attended, log_total = attend(scores, value_rows)
    out_partial = jnp.dot(
        attended.reshape(-1, local_ch), out_weight, preferred_element_type=jnp.float32
    )
    result = middle + reduce_channels(out_partial.reshape(count_maps, count_pix, C)) + out_bias
    maps_out = result.astype(jnp.bfloat16)
    top_grad = out_grad.astype(jnp.float32)
    out_bias_grad = jnp.sum(top_grad, axis=(0, 1))
    top_full = gather_channels(out_grad).reshape(-1, C)
    out_weight_grad = contract_rows(attended.reshape(-1, local_ch), top_full)
    attended_grad = (
        contract_cols(top_full, out_weight)
        .reshape(count_maps, count_pix, local_ch)
        .astype(jnp.bfloat16)
    )
    scores_again = channel_scores(queries, key_rows, score_scale)
    stacked_grad = attend_back(
        scores_again,
        log_total,
        queries,
        key_rows,
        value_rows,
        attended_grad,
        score_scale,
        channel_probs_sum,
    )
    flat_stacked = stacked_grad.reshape(-1, 3 * local_ch)
    qkv_weight_grad = contract_rows(third_full.reshape(-1, C), flat_stacked).reshape(C, 3, local_ch)
    bias_sums = jnp.sum(stacked_grad.astype(jnp.float32), axis=(0, 1))
    qkv_bias_grad = jnp.stack([bias_sums[0], bias_sums[2]])
    third_partial = contract_cols(flat_stacked, qkv_weight.reshape(C, 3 * local_ch))
    third_grad = reduce_channels(third_partial.reshape(count_maps, count_pix, C))
    middle_norm_grad, gain_three, shift_three = third_pull(third_grad)
    middle_grad = top_grad + middle_norm_grad
    conv_two_bias = jnp.sum(middle_grad, axis=(0, 1))
    middle_full = gather_channels(middle_grad.astype(jnp.bfloat16))
    conv2_weight_grad = conv_kernel_grad(second_low, middle_full)
    second_grad = conv_input_grad(middle_full, conv2_weight)
    hidden_grad, gain_two, shift_two = second_pull(second_grad)
    hidden_low = hidden_grad.astype(jnp.bfloat16)
    hidden_back = hidden_low.astype(jnp.float32)
    conv_one_bias = jnp.sum(hidden_back, axis=(0, 1))
    time_grad = jnp.sum(hidden_back, axis=1)
    temb_bias_grad = jnp.sum(time_grad, axis=0)
    temb_weight_grad = lax.dot_general(
        emb_act, time_grad, (((0,), (0,)), ((), ())), precision=highest
    )
    emb_grad_part = emb_pull(
        lax.dot_general(time_grad, temb_float, (((1,), (1,)), ((), ())), precision=highest)
    )[0]
    table_part = jax.ops.segment_sum(emb_grad_part, timesteps, num_segments=temb_table.shape[0])
    table_grad = table_total(table_part)
    conv1_weight_grad = conv_kernel_grad(first_full, hidden_low)
    first_grad = reduce_channels(conv_input_grad(hidden_low, conv1_weight))
    input_norm_grad, gain_one, shift_one = first_pull(first_grad)
    maps_grad = middle_grad + input_norm_grad
    conv_bias_stack = jnp.stack([conv_one_bias, conv_two_bias])
    gain_stack = jnp.stack([gain_one, gain_two, gain_three])
    shift_stack = jnp.stack([shift_one, shift_two, shift_three])
    (
        gain_stack,
        shift_stack,
        conv1_weight_grad,
        conv_bias_stack,
        temb_weight_grad,
        temb_bias_grad,
        conv2_weight_grad,
        qkv_weight_grad,
        qkv_bias_grad,
        out_weight_grad,
        out_bias_grad,
    ) = lax.psum(
        (
            gain_stack,
            shift_stack,
            conv1_weight_grad,
            conv_bias_stack,
            temb_weight_grad,
            temb_bias_grad,
            conv2_weight_grad,
            qkv_weight_grad,
            qkv_bias_grad,
            out_weight_grad,
            out_bias_grad,
        ),
        "dp",
    )
    return (
        maps_out,
        maps_grad,
        table_grad,
        gain_stack,
        shift_stack,
        conv1_weight_grad,
        conv_bias_stack,
        temb_weight_grad,
        temb_bias_grad,
        conv2_weight_grad,
        qkv_weight_grad,
        qkv_bias_grad,
        out_weight_grad,
        out_bias_grad,
    )


def on_device(
    maps_in,
    timesteps,
    temb_table,
    norm_gain,
    norm_bias,
    conv1_weight,
    conv_bias,
    temb_weight,
    temb_bias,
    conv2_weight,
    qkv_weight,
    qkv_bias,
    out_weight,
    out_bias,
    out_grad,
):
    results = channel_path(
        maps_in,
        timesteps,
        temb_table,
        norm_gain,
        norm_bias,
        conv1_weight,
        conv_bias,
        temb_weight,
        temb_bias,
        conv2_weight,
        qkv_weight,
        qkv_bias,
        out_weight,
        out_bias,
        out_grad,
    )
    return results


def solution(mesh):
    placed = (
        P("dp", None, "mp"),
        P("dp"),
        P(),
        P(None, "mp"),
        P(None, "mp"),
        P(None, None, None, "mp"),
        P(None, "mp"),
        P(None, "mp"),
        P("mp"),
        P(None, None, "mp", None),
        P(None, None, "mp"),
        P(None, "mp"),
        P("mp", None),
        P("mp"),
        P("dp", None, "mp"),
    )
    return jax.shard_map(
        on_device,
        mesh=mesh,
        in_specs=placed,
        out_specs=(
            P("dp", None, "mp"),
            P("dp", None, "mp"),
            P(),
            P(None, "mp"),
            P(None, "mp"),
            P(None, None, None, "mp"),
            P(None, "mp"),
            P(None, "mp"),
            P("mp"),
            P(None, None, "mp", None),
            P(None, None, "mp"),
            P(None, "mp"),
            P("mp", None),
            P("mp"),
        ),
        check_vma=False,
    )
```

profile of v0, /device:TPU:0, one launch (start us, length us, event | category | flops | bytes accessed | tf_op | source)
XLA Modules:
  0.0 547.2 jit_solution(6669448575539136100)
XLA Ops:
  7.3 1.3 convert_reduce_fusion.1
  8.9 1.2 fusion.30
  11.3 2.2 fusion.26
  14.7 10.7 %all-gather.5.cloned.1.call-done = bf16[8,256,256]{2,1,0:T(8,128)(2,1)} async-done(((bf16[8,256,128]{2,1,0:T(8,128)(2,1)}), bf16[8,256,256]{2,1,0:T(8,128)(2,1)}) %all-gather.5.cloned.1.call-update) | async-done | bytes 1048592 | tf_op jit(solution)/shard_map/all_gather | solution.py:95
  25.5 6.0 %pad_slice_fusion.8 = (bf16[8,16,16,256]{3,2,1,0:T(8,128)(2,1)S(1)}, bf16[8,16,16,256]{3,2,1,0:T(8,128)(2,1)S(1)}, bf16[8,16,16,256]{3,2,1,0:T(8,128)(2,1)S(1)},...) fusion(bf16[8,16,16,256]{3,2,1,0:T(8,128)(2,1)} %bitcast.456), kind=kLoop, calls=%fused_computation.12 | loop fusion | bytes 9437184 | tf_op jit(solution)/shard_map/slice | solution.py:51
  34.0 1.4 copy-done.9
  45.2 1.8 convolution_add_fusion.8
  47.3 10.7 %reduce-scatter.5.cloned.1.call-done = f32[8,256,128]{2,1,0:T(8,128)} async-done(((f32[8,256,256]{2,1,0:T(8,128)}), f32[8,256,128]{2,1,0:T(8,128)}) %reduce-scatter.5.cloned.1.call-update) | async-done | bytes 1048592 | tf_op jit(solution)/shard_map/reduce_scatter | solution.py:99
  58.1 1.4 fusion.174
  62.3 9.4 %all-gather.7.cloned.1.call-done = bf16[8,256,256]{2,1,0:T(8,128)(2,1)} async-done(((bf16[8,256,128]{2,1,0:T(8,128)(2,1)}), bf16[8,256,256]{2,1,0:T(8,128)(2,1)}) %all-gather.7.cloned.1.call-update) | async-done | bytes 1048592 | tf_op jit(solution)/shard_map/all_gather | solution.py:95
  71.7 2.0 add_convert_fusion
  73.7 1.1 copy-done.44
  74.8 1.7 convolution_multiply_fusion
  76.6 6.8 %all-gather.9.cloned.1.call-done = bf16[8,256,256]{2,1,0:T(8,128)(2,1)} async-done(((bf16[8,256,128]{2,1,0:T(8,128)(2,1)}), bf16[8,256,256]{2,1,0:T(8,128)(2,1)}) %all-gather.9.cloned.1.call-update) | async-done | bytes 1048592 | tf_op jit(solution)/shard_map/all_gather | solution.py:95
  83.4 1.7 convolution_convert_fusion.1
  85.0 2.5 convolution_convert_fusion
  87.6 20.6 %all-reduce.11.cloned.1.call-done = f32[8,256,256]{2,1,0:T(8,128)} async-done(((f32[8,256,256]{2,1,0:T(8,128)}), f32[8,256,256]{2,1,0:T(8,128)}) %all-reduce.11.cloned.1.call-update) | async-done | bytes 2097168 | tf_op jit(solution)/shard_map/psum | solution.py:111
  108.1 1.9 reduce_max.9
  110.1 2.2 exponential_reduce_fusion
  112.3 19.4 %all-reduce.13.cloned.1.call-done = bf16[8,256,256]{2,1,0:T(8,128)(2,1)} async-done(((bf16[8,256,256]{2,1,0:T(8,128)(2,1)}), bf16[8,256,256]{2,1,0:T(8,128)(2,1)}) %all-reduce.13.cloned.1.call-update) | async-done | bytes 1048592 | tf_op jit(solution)/shard_map/psum | solution.py:115
  131.7 2.7 fusion
  134.4 2.1 fusion.2
  139.6 1.2 copy-done.8
  140.7 2.0 convolution_bitcast_fusion
  142.8 2.2 convolution_convert_fusion.3
  145.0 1.8 fusion.73
  146.9 6.8 %reduce-scatter.9.cloned.1.call-done = f32[8,256,128]{2,1,0:T(8,128)} async-done(((f32[8,256,256]{2,1,0:T(8,128)}), f32[8,256,128]{2,1,0:T(8,128)}) %reduce-scatter.9.cloned.1.call-update) | async-done | bytes 1048592 | tf_op jit(solution)/shard_map/reduce_scatter | solution.py:99
  153.7 2.1 multiply_reduce_fusion
  156.9 9.9 %reduce-scatter.7.cloned.1.call-done = f32[8,256,128]{2,1,0:T(8,128)} async-done(((f32[8,256,256]{2,1,0:T(8,128)}), f32[8,256,128]{2,1,0:T(8,128)}) %reduce-scatter.7.cloned.1.call-update) | async-done | bytes 1048592 | tf_op jit(solution)/shard_map/reduce_scatter | solution.py:99
  166.8 3.3 fusion.171
  172.7 9.6 %all-gather.11.cloned.1.call-done = bf16[8,256,256]{2,1,0:T(8,128)(2,1)} async-done(((bf16[8,256,128]{2,1,0:T(8,128)(2,1)}), bf16[8,256,256]{2,1,0:T(8,128)(2,1)}) %all-gather.11.cloned.1.call-update) | async-done | bytes 1048592 | tf_op jit(solution)/shard_map/all_gather | solution.py:95
  182.3 6.4 %pad_slice_fusion = (bf16[8,16,16,256]{3,2,1,0:T(8,128)(2,1)S(1)}, bf16[8,16,16,256]{3,2,1,0:T(8,128)(2,1)S(1)}, bf16[8,16,16,256]{3,2,1,0:T(8,128)(2,1)S(1)}, b...) fusion(bf16[8,16,16,256]{3,2,1,0:T(8,128)(2,1)} %bitcast.438), kind=kLoop, calls=%fused_computation.4 | loop fusion | bytes 9437184 | tf_op jit(solution)/shard_map/slice | solution.py:51
  193.0 1.4 convolution_add_fusion.16
  194.4 2.5 copy.82
  197.0 2.6 multiply_reduce_fusion.3
  199.8 1.8 multiply_reduce_fusion.2
  202.0 3.0 convert_reduce_fusion.3
  205.0 2.0 fusion.39
  207.0 1.0 pad_slice_fusion.16
  211.6 1.8 convolution_add_fusion
  213.6 2.8 copy.90
  216.4 2.0 copy.105
  219.5 1.5 fusion.179
  221.0 1.6 convert_reduce_fusion.4
  222.8 2.1 scatter_custom_fusion
  224.9 2.0 convolution_bitcast_fusion.2
  227.0 2.1 convolution_bitcast_fusion.3
  229.1 2.1 convolution_bitcast_fusion.4
  236.9 1.1 convolution_bitcast_fusion.16
  238.0 1.1 convolution_bitcast_fusion.17
  239.2 1.1 convolution_bitcast_fusion.18
  240.3 1.1 convolution_bitcast_fusion.19
  241.7 1.1 maximum_bitcast_fusion.3
  242.8 1.1 maximum_bitcast_fusion.5
  247.3 1.1 pad_maximum_fusion.2
  248.4 1.1 pad_maximum_fusion.1
  249.5 1.4 fusion.165
  252.0 2.1 fusion.29
  255.2 43.3 %all-reduce.4 = (f32[3,128]{1,0:T(4,128)}, f32[3,128]{1,0:T(4,128)}, f32[2,128]{1,0:T(2,128)}, f32[128]{0:T(128)}, f32[2,128]{1,0:T(2,128)}, /*index=5*/f32[128]{0:T(128)}) all-reduce(f32[3,128]{1,0:T(4,128)S(1)} %pad_maximum_fusion.4, f32[3,128]{1,0:T(4,128)S(1)} %pad_maximum_fusion.5, ...), channel_id=1, replica_groups=mesh['dp'=16,'mp'=2] {'dp'}, use_global_device_ids=true, to_apply=%region_40.41 | all-reduce | flops 1536 | bytes 12288 | tf_op jit(solution)/shard_map/psum | solution.py:279
  298.5 1.3 fusion.18
  299.7 76.8 %all-reduce.15.cloned.1.call-done = f32[1000,512]{1,0:T(8,128)} async-done(((f32[1000,512]{1,0:T(8,128)}), f32[1000,512]{1,0:T(8,128)}) %all-reduce.15.cloned.1.call-update) | async-done | bytes 2048016 | tf_op jit(solution)/shard_map/psum | solution.py:103
  376.5 156.2 %all-reduce.17.cloned.1.call-done = (f32[3,3,256,128]{3,2,1,0:T(8,128)}, f32[512,128]{1,0:T(8,128)}, f32[3,3,128,256]{3,2,1,0:T(8,128)}, f32[256,3,128]{2,0,1:T(8,128)}, f32[128,256]{1,0:T(8,128)}) async-done(((f32[3,3,256,128]{3,2,1,0:T(8,128)}, f32[512,128]{1,0:T(8,128)}, f32[3,3,128,256]{3,2,1,0:T(8,128)}, f32[256,3,128]{2,0,1:T(8,128)}, f32[128,256]{1,0:T(8,128)}), (f32[3,3,256,128]{3,2,1,0:T(8,128)}, ...) | async-done | bytes 3145744 | tf_op jit(solution)/shard_map/psum | solution.py:279
  532.7 3.1 copy.128
  535.9 1.0 copy.129
  (330 shorter events, 48.8 us)
Async XLA Ops:
  7.2 6.6 %copy-start = (f32[1000,512]{1,0:T(8,128)S(1)}, f32[1000,512]{1,0:T(8,128)}, u32[]{:S(2)}) copy-start(f32[1000,512]{1,0:T(8,128)} %param.17) | copy-start | bytes 6144004
  7.2 6.4 %copy-start.71 = (f32[2,128]{1,0:T(2,128)S(1)}, f32[2,128]{1,0:T(2,128)}, u32[]{:S(2)}) copy-start(f32[2,128]{1,0:T(2,128)} %param.21) | copy-start | bytes 3076
  7.2 6.5 %copy-start.75 = (s32[8]{0:T(128)S(1)}, s32[8]{0:T(128)}, u32[]{:S(2)}) copy-start(s32[8]{0:T(128)} %param.16) | copy-start | bytes 100
  7.2 7.1 %copy-start.67 = (bf16[512,128]{1,0:T(8,128)(2,1)S(1)}, bf16[512,128]{1,0:T(8,128)(2,1)}, u32[]{:S(2)}) copy-start(bf16[512,128]{1,0:T(8,128)(2,1)} %param.22) | copy-start | bytes 393220
  7.2 7.1 %copy-start.74 = (f32[128]{0:T(128)S(1)}, f32[128]{0:T(128)}, u32[]{:S(2)}) copy-start(f32[128]{0:T(128)} %param.23) | copy-start | bytes 1540
  7.2 18.2 %all-gather.5.cloned.1.call-start = ((), (), s32[]{:S(2)}) async-start(), calls=%async_computation.4 | async-start | bytes 1572864 | tf_op jit(solution)/shard_map/all_gather | solution.py:95
  13.6 44.5 %reduce-scatter.5.cloned.1.call-start = ((), (), s32[]{:S(2)}) async-start(), calls=%async_computation.5 | async-start | bytes 3145728 | tf_op jit(solution)/shard_map/reduce_scatter | solution.py:99
  25.4 6.1 %copy-start.51 = (bf16[3,3,256,128]{3,2,1,0:T(8,128)(2,1)S(1)}, bf16[3,3,256,128]{3,2,1,0:T(8,128)(2,1)}, u32[]{:S(2)}) copy-start(bf16[3,3,256,128]{3,2,1,0:T(8,128)(2,1)} %param.20) | copy-start | bytes 1769476
  31.5 1.6 copy-start.19
  31.5 2.1 copy-start.21
  31.5 4.3 copy-start.23
  31.5 4.8 copy-start.11
  31.5 5.2 copy-start.13
  31.5 5.6 %copy-start.25 = (bf16[8,16,16,256]{3,2,1,0:T(8,128)(2,1)}, bf16[8,16,16,256]{3,2,1,0:T(8,128)(2,1)S(1)}, u32[]{:S(2)}) copy-start(bf16[8,16,16,256]{3,2,1,0:T(8,128)(2,1)S(1)} %get-tuple-element.58) | copy-start | bytes 3145732
  33.6 1.9 copy-start.9
  37.9 2.1 copy-start.4
  41.5 1.5 copy-start.33
  41.5 2.4 copy-start.35
  41.5 2.8 copy-start.37
  41.6 3.2 copy-start.38
  41.6 3.7 copy-start.39
  47.0 11.0 %copy-start.6 = (bf16[8,256,128]{2,1,0:T(8,128)(2,1)S(1)}, bf16[8,256,128]{2,1,0:T(8,128)(2,1)}, u32[]{:S(2)}) copy-start(bf16[8,256,128]{2,1,0:T(8,128)(2,1)} %param.15) | copy-start | bytes 1572868
  47.0 24.6 %all-gather.7.cloned.1.call-start = ((), (), s32[]{:S(2)}) async-start(), calls=%async_computation.6 | async-start | bytes 1572864 | tf_op jit(solution)/shard_map/all_gather | solution.py:95
  59.5 2.4 copy-start.58
  59.8 2.4 copy-start.72
  61.3 22.0 %all-gather.9.cloned.1.call-start = ((), (), s32[]{:S(2)}) async-start(), calls=%async_computation.9 | async-start | bytes 1572864 | tf_op jit(solution)/shard_map/all_gather | solution.py:95
  61.9 46.2 %all-reduce.11.cloned.1.call-start = ((), (), s32[]{:S(2)}) async-start(), calls=%async_computation.7 | async-start | bytes 4194304 | tf_op jit(solution)/shard_map/psum | solution.py:111
  74.8 8.6 %copy-start.66 = (bf16[128,256]{1,0:T(8,128)(2,1)S(1)}, bf16[128,256]{1,0:T(8,128)(2,1)}, u32[]{:S(2)}) copy-start(bf16[128,256]{1,0:T(8,128)(2,1)} %param.27) | copy-start | bytes 196612
  76.5 55.1 %all-reduce.13.cloned.1.call-start = ((), (), s32[]{:S(2)}) async-start(), calls=%async_computation.10 | async-start | bytes 2097152 | tf_op jit(solution)/shard_map/psum | solution.py:115
  87.5 66.2 %reduce-scatter.9.cloned.1.call-start = ((), (), s32[]{:S(2)}) async-start(), calls=%async_computation.11 | async-start | bytes 3145728 | tf_op jit(solution)/shard_map/reduce_scatter | solution.py:99
  131.7 2.7 copy-start.46
  134.4 2.1 copy-start.45
  136.5 1.6 copy-start.3
  142.8 24.0 %reduce-scatter.7.cloned.1.call-start = ((), (), s32[]{:S(2)}) async-start(), calls=%async_computation.8 | async-start | bytes 3145728 | tf_op jit(solution)/shard_map/reduce_scatter | solution.py:99
  145.0 1.8 copy-start.42
  146.9 19.9 %copy-start.73 = (f32[128]{0:T(128)S(1)}, f32[128]{0:T(128)}, u32[]{:S(2)}) copy-start(f32[128]{0:T(128)} %param.28) | copy-start | bytes 1540
  146.9 35.5 %all-gather.11.cloned.1.call-start = ((), (), s32[]{:S(2)}) async-start(), calls=%async_computation.12 | async-start | bytes 1572864 | tf_op jit(solution)/shard_map/all_gather | solution.py:95
  146.9 19.9 %copy-start.53 = (bf16[8,256,128]{2,1,0:T(8,128)(2,1)S(1)}, bf16[8,256,128]{2,1,0:T(8,128)(2,1)}, u32[]{:S(2)}) copy-start(bf16[8,256,128]{2,1,0:T(8,128)(2,1)} %param.29) | copy-start | bytes 1572868
  172.0 79.6 %reduce-scatter.11.cloned.1.call-start = ((), (), s32[]{:S(2)}) async-start(), calls=%async_computation.13 | async-start | bytes 3145728 | tf_op jit(solution)/shard_map/reduce_scatter | solution.py:99
  182.3 6.4 %copy-start.50 = (bf16[3,3,128,256]{3,2,1,0:T(8,128)(2,1)S(1)}, bf16[3,3,128,256]{3,2,1,0:T(8,128)(2,1)}, u32[]{:S(2)}) copy-start(bf16[3,3,128,256]{3,2,1,0:T(8,128)(2,1)} %param.24) | copy-start | bytes 1769476
  213.4 163.1 %all-reduce.15.cloned.1.call-start = ((), (), s32[]{:S(2)}) async-start(), calls=%async_computation.14 | async-start | bytes 4096000 | tf_op jit(solution)/shard_map/psum | solution.py:103
  216.4 2.1 copy-start.43
  216.4 2.1 copy-start.47
  216.4 3.1 copy-start.57
  218.5 2.5 copy-start.5
  227.0 4.2 copy-start.36
  229.1 2.5 copy-start.34
  231.6 2.0 copy-start.30
  232.6 2.0 copy-start.41
  233.6 2.0 copy-start.26
  234.6 1.5 copy-start.24
  236.1 1.9 copy-start.20
  236.9 2.3 copy-start.18
  238.0 2.3 copy-start.16
  241.5 291.3 %all-reduce.17.cloned.1.call-start = ((), (), s32[]{:S(2)}) async-start(), calls=%async_computation.15 | async-start | bytes 6291456 | tf_op jit(solution)/shard_map/psum | solution.py:279
  243.9 1.5 copy-start.10
  243.9 1.6 copy-start.54
  251.3 3.9 copy-start.69
  251.3 47.2 %copy-start.28 = (f32[8,256,128]{2,1,0:T(8,128)S(1)}, f32[8,256,128]{2,1,0:T(8,128)}, u32[]{:S(2)}) copy-start(f32[8,256,128]{2,1,0:T(8,128)} %copy-done.27) | copy-start | bytes 3145732
  532.7 3.1 copy-start.56
  535.9 1.8 copy-start.55
  535.9 2.8 copy-start.64
  535.9 4.2 copy-start.1
  536.9 2.5 copy-start.68
  (24 other events, 26.9 us)
Sparse Core Ops, SparseCore 0:
  13.7 11.7 all-gather.4
  47.2 10.8 reduce-scatter.4
  61.4 10.1 all-gather.6
  73.1 10.1 all-gather.8
  85.7 22.4 all-reduce.10
  110.9 20.7 all-reduce.12
  142.9 10.7 reduce-scatter.8
  156.0 10.7 reduce-scatter.6
  172.1 10.1 all-gather.10
  213.5 10.8 reduce-scatter.10
  241.6 134.8 all-reduce.14
  384.8 147.8 all-reduce.16
where the time goes:
time: 557 us; the launch traced here: 547 us
  waiting for transfers between devices  338 us (61%)
  matrix products  57.1 us (10%)
  other arithmetic  47.4 us (9%)
  local copies, waits for them, and re-layouts  44.4 us (8%)
  blocking collectives  43.3 us (8%)
  between operations  15.9 us (3%)
    psum x1, waiting for transfers between devices, channel_path(): lax.psum((gain_stack, shift_stack, conv1_weight_grad, conv_bias_stack, te...  156 us
    psum x1, waiting for transfers between devices, table_total(): return lax.psum(table_part, ('dp', 'mp'))  76.8 us
    psum x1, blocking collectives, channel_path(): lax.psum((gain_stack, shift_stack, conv1_weight_grad, conv_bias_stack, te...  43.3 us
    all_gather x4, waiting for transfers between devices, gather_channels(): return lax.all_gather(values, 'mp', axis=2, tiled=True)  36.6 us
    reduce_scatter x4, waiting for transfers between devices, reduce_channels(): return lax.psum_scatter(values, 'mp', scatter_dimension=2, tiled=True)  27.4 us
    dot_general x20, matrix products, contract_rows(): lax.dot_general(left, right, (((0,), (0,)), ((), ())), preferred_element_...  20.6 us
    psum x1, waiting for transfers between devices, channel_scores(): return lax.psum(partial_scores, 'mp')  20.6 us
    psum x1, waiting for transfers between devices, channel_probs_sum(): return lax.psum(partial_grad.astype(jnp.bfloat16), 'mp').astype(jnp.float32)  19.4 us
  transfers between devices with their start and end apart: 12, of which 11 were waited for; matrix products, arithmetic and copies ran while one was open for 11% of the time, Pallas kernels for 0%

commit v1 on v0

v1 whole, which is shorter than its diff:
```python
import jax
import jax.numpy as jnp
from jax import lax
from jax.experimental import pallas as pl
from jax.experimental.pallas import tpu as pltpu
from jax.sharding import PartitionSpec as P

C = 256
HALF = 128
SIDE = 16
PIX = 256
GROUP = 8
EPS = 1e-06
F32 = jnp.float32
BF16 = jnp.bfloat16
WHOLE = pl.BlockSpec(memory_space=pltpu.VMEM)
SCALAR = pl.BlockSpec(memory_space=pltpu.SMEM)


def call(body, outs, *args, scratch=(), flops=0, limit=24):
    return pl.pallas_call(
        body,
        out_shape=tuple(jax.ShapeDtypeStruct(s, d) for s, d in outs),
        in_specs=[SCALAR] + [WHOLE] * (len(args) - 1),
        out_specs=tuple(WHOLE for _ in outs),
        scratch_shapes=list(scratch),
        compiler_params=pltpu.CompilerParams(vmem_limit_bytes=limit << 20),
        cost_estimate=pl.CostEstimate(flops=flops, bytes_accessed=1 << 20, transcendentals=0),
    )(*args)


def dot(a, b):
    return jnp.dot(a, b, preferred_element_type=F32)


def dot_bt(a, b):
    return lax.dot_general(a, b, (((1,), (1,)), ((), ())), preferred_element_type=F32)


def dot_at(a, b):
    return lax.dot_general(a, b, (((0,), (0,)), ((), ())), preferred_element_type=F32)


def join(first, own, recv, axis):
    low = jnp.where(first, own, recv)
    high = jnp.where(first, recv, own)
    return jnp.concatenate([low, high], axis=axis)


def group_sum(rows):
    lane = lax.broadcasted_iota(jnp.int32, rows.shape, 1)
    width = rows.shape[1]
    for step in (1, 2, 4):
        up = pltpu.roll(rows, width - step, 1)
        down = pltpu.roll(rows, step, 1)
        rows = rows + jnp.where((lane & step) == 0, up, down)
    return rows


def col_sum(values):
    return jnp.sum(values, axis=0, keepdims=True)


def norm_stats(maps):
    count = PIX * GROUP
    mean = group_sum(jnp.concatenate([col_sum(v) for v in maps], axis=0)) / count
    square = [col_sum((v - mean[m : m + 1]) ** 2) for m, v in enumerate(maps)]
    var = group_sum(jnp.concatenate(square, axis=0)) / count
    return mean, lax.rsqrt(var + EPS)


def norm_back(grads, units, gain, rstd):
    count = PIX * GROUP
    plain = jnp.concatenate([col_sum(g) for g in grads], axis=0)
    scaled = jnp.concatenate([col_sum(g * u) for g, u in zip(grads, units)], axis=0)
    both = group_sum(jnp.concatenate([plain * gain, scaled * gain], axis=0)) / count
    n = len(grads)
    result = []
    for m in range(n):
        inner = grads[m] * gain - both[m : m + 1] - units[m] * both[n + m : n + m + 1]
        result.append(inner * rstd[m : m + 1])
    return result, col_sum(scaled), col_sum(plain)


def sigmoid(v):
    return 1.0 / (1.0 + jnp.exp(-v))


def put_windows(win_ref, m, values):
    col = lax.broadcasted_iota(jnp.int32, (PIX, 1), 0) & (SIDE - 1)
    before = jnp.where(col == 0, 0.0, pltpu.roll(values, 1, 0))
    after = jnp.where(col == SIDE - 1, 0.0, pltpu.roll(values, PIX - 1, 0))
    blank = jnp.zeros((SIDE, C), BF16)
    for c, shifted in enumerate((before, values, after)):
        win_ref[m, c, 0:SIDE, :] = blank
        win_ref[m, c, SIDE + PIX : 2 * SIDE + PIX, :] = blank
        win_ref[m, c, SIDE : SIDE + PIX, :] = shifted.astype(BF16)


def window(win_ref, m, r, c):
    return win_ref[m, c, SIDE * r : SIDE * r + PIX, :]


def all_windows(win_ref, r, c):
    n = win_ref.shape[0]
    return win_ref[:, c, SIDE * r : SIDE * r + PIX, :].reshape(n * PIX, C)


def conv_forward(win_ref, w_ref):
    total = None
    for r in range(3):
        for c in range(3):
            part = dot(all_windows(win_ref, r, c), w_ref[3 * r + c])
            total = part if total is None else total + part
    return total


def conv_transposed(win_ref, w_ref):
    total = None
    for r in range(3):
        for c in range(3):
            part = dot_bt(all_windows(win_ref, 2 - r, 2 - c), w_ref[3 * r + c])
            total = part if total is None else total + part
    return total


def window_scratch(n):
    return pltpu.VMEM((n, 3, PIX + 2 * SIDE, C), BF16)


def first_kernel(mp, x_own, x_recv, w_own, w_recv, prm, emb, tw_own, tw_recv, act, hid, stat, win, wfull):
    first = mp[0] == 0
    n = x_own.shape[0]
    for t in range(9):
        wfull[t] = join(first, w_own[t], w_recv[t], 1)
    xs = [join(first, x_own[m], x_recv[m], 1).astype(F32) for m in range(n)]
    mean, rstd = norm_stats(xs)
    stat[0:n] = mean
    stat[n : 2 * n] = rstd
    for m in range(n):
        u = (xs[m] - mean[m : m + 1]) * (rstd[m : m + 1] * prm[0:1]) + prm[3:4]
        a = u * sigmoid(u)
        act[m] = a.astype(BF16)
        put_windows(win, m, a)
    rows = jnp.where(first, emb[0:n], emb[n : 2 * n])
    e = rows * sigmoid(rows)
    e_high = e.astype(BF16)
    e_low = (e - e_high.astype(F32)).astype(BF16)
    tw = join(first, tw_own[...], tw_recv[...], 1)
    time_row = dot(e_high, tw) + dot(e_low, tw) + prm[11:12] + prm[6:7]
    out = conv_forward(win, wfull)
    for m in range(n):
        hid[m] = out[m * PIX : (m + 1) * PIX] + time_row[m : m + 1]


def second_kernel(mp, x_own, x_recv, hid, w_own, w_recv, prm, act, mid, stat, win, wfull):
    first = mp[0] == 0
    n = x_own.shape[0]
    for t in range(9):
        wfull[t] = join(first, w_own[t], w_recv[t], 0)
    hs = [hid[m] for m in range(n)]
    mean, rstd = norm_stats(hs)
    stat[0:n] = mean
    stat[n : 2 * n] = rstd
    for m in range(n):
        u = (hs[m] - mean[m : m + 1]) * (rstd[m : m + 1] * prm[1:2]) + prm[4:5]
        a = u * sigmoid(u)
        act[m] = a.astype(BF16)
        put_windows(win, m, a)
    out = conv_forward(win, wfull)
    for m in range(n):
        x = join(first, x_own[m], x_recv[m], 1).astype(F32)
        mid[m] = x + out[m * PIX : (m + 1) * PIX] + prm[7:8]


def attention_kernel(
    mp, mid, g_own, g_recv, qw_own, qw_recv, ow_own, ow_recv, prm,
    out_keep, out_send, dmid, wg_keep, wg_send, sums, unit, qkv, att, third, dall,
):
    first = mp[0] == 0
    n = mid.shape[0]
    scale = 1.0 / 16.0
    qw = [join(first, qw_own[j], qw_recv[j], 1) for j in range(3)]
    ow = join(first, ow_own[...], ow_recv[...], 0)
    ms = [mid[m] for m in range(n)]
    mean, rstd = norm_stats(ms)
    for m in range(n):
        un = (ms[m] - mean[m : m + 1]) * rstd[m : m + 1]
        unit[m] = un
        third[m * PIX : (m + 1) * PIX] = (un * prm[2:3] + prm[5:6]).astype(BF16)
    for j in range(3):
        part = dot(third[...], qw[j])
        if j == 0:
            part = part + prm[8:9]
        if j == 2:
            part = part + prm[9:10]
        qkv[j] = part.astype(BF16)
    for m in range(n):
        rows = slice(m * PIX, (m + 1) * PIX)
        q, k, v = qkv[0, rows], qkv[1, rows], qkv[2, rows]
        s = dot_bt(q, k) * scale
        e = jnp.exp(s - jnp.max(s, axis=1, keepdims=True))
        p = e * (1.0 / jnp.sum(e, axis=1, keepdims=True))
        p_low = p.astype(BF16)
        a = dot(p_low, v).astype(BF16)
        att[rows] = a
        result = mid[m] + dot(a, ow) + prm[10:11]
        left, right = result[:, :HALF].astype(BF16), result[:, HALF:].astype(BF16)
        out_keep[m] = jnp.where(first, left, right)
        out_send[m] = jnp.where(first, right, left)
        gb = join(first, g_own[m], g_recv[m], 1)
        da = dot_bt(gb, ow).astype(BF16)
        dp = dot_bt(da, v)
        ds = (p * (dp - jnp.sum(p * dp, axis=1, keepdims=True))).astype(BF16)
        dall[0, rows] = (dot(ds, k) * scale).astype(BF16)
        dall[1, rows] = (dot_at(ds, q) * scale).astype(BF16)
        dall[2, rows] = dot_at(p_low, da).astype(BF16)
    g_all = jnp.concatenate([join(first, g_own[m], g_recv[m], 1) for m in range(n)], axis=0)
    og = dot_at(att[...], g_all).astype(BF16)
    for h in range(2):
        lanes = slice(h * HALF, (h + 1) * HALF)
        top, low = og[:HALF, lanes], og[HALF:, lanes]
        wg_keep[3 * C + h * HALF : 3 * C + (h + 1) * HALF] = jnp.where(first, top, low)
        wg_send[3 * C + h * HALF : 3 * C + (h + 1) * HALF] = jnp.where(first, low, top)
    third_grad = None
    for j in range(3):
        d = dall[j]
        qg = dot_at(third[...], d).astype(BF16)
        left, right = qg[:, :HALF], qg[:, HALF:]
        wg_keep[j * C : (j + 1) * C] = jnp.where(first, left, right)
        wg_send[j * C : (j + 1) * C] = jnp.where(first, right, left)
        part = dot_bt(d, qw[j])
        third_grad = part if third_grad is None else third_grad + part
    grads = [third_grad[m * PIX : (m + 1) * PIX] for m in range(n)]
    units = [unit[m] for m in range(n)]
    back, gain_grad, bias_grad = norm_back(grads, units, prm[2:3], rstd)
    mid_bias = jnp.zeros((1, C), F32)
    for m in range(n):
        d = back[m] + join(first, g_own[m], g_recv[m], 1).astype(F32)
        dmid[m] = d
        mid_bias = mid_bias + col_sum(d)
    sums[0:1] = gain_grad
    sums[1:2] = bias_grad
    sums[2:3] = mid_bias
    sums[3:4] = col_sum(dall[0].astype(F32))
    sums[4:5] = col_sum(dall[2].astype(F32))
    sums[5:6] = col_sum(g_all.astype(F32))
    sums[6:8] = jnp.zeros((2, C), F32)


def turned(values):
    return jnp.concatenate([values[m].T for m in range(values.shape[0])], axis=1)


def conv2_grad_kernel(mp, dmid, act, keep, send, win):
    first = mp[0] == 0
    for m in range(dmid.shape[0]):
        put_windows(win, m, dmid[m])
    act_t = turned(act)
    for r in range(3):
        for c in range(3):
            t = 3 * r + c
            g = dot(act_t, all_windows(win, 2 - r, 2 - c)).astype(BF16)
            for h in range(2):
                lanes = slice(h * HALF, (h + 1) * HALF)
                rows = slice((2 * t + h) * HALF, (2 * t + h + 1) * HALF)
                keep[rows] = jnp.where(first, g[:HALF, lanes], g[HALF:, lanes])
                send[rows] = jnp.where(first, g[HALF:, lanes], g[:HALF, lanes])


def hidden_back_kernel(mp, win, hid, stat, w_own, w_recv, prm, dhid, sums, dtime, wfull):
    first = mp[0] == 0
    n = hid.shape[0]
    for t in range(9):
        wfull[t] = join(first, w_own[t], w_recv[t], 0)
    second_grad = conv_transposed(win, wfull)
    units, grads = [], []
    for m in range(n):
        un = (hid[m] - stat[m : m + 1]) * stat[n + m : n + m + 1]
        u = un * prm[1:2] + prm[4:5]
        sig = sigmoid(u)
        units.append(un)
        grads.append(second_grad[m * PIX : (m + 1) * PIX] * (sig * (1.0 + u * (1.0 - sig))))
    back, gain_grad, bias_grad = norm_back(grads, units, prm[1:2], stat[n : 2 * n])
    rows = []
    for m in range(n):
        low = back[m].astype(BF16)
        dhid[m] = low
        rows.append(col_sum(low.astype(F32)))
    dt = jnp.concatenate(rows, axis=0)
    dtime[...] = dt
    sums[0:1] = gain_grad
    sums[1:2] = bias_grad
    sums[2:3] = col_sum(dt)
    sums[3:8] = jnp.zeros((5, C), F32)


def conv1_grad_kernel(mp, dhid, act, keep, send, win):
    first = mp[0] == 0
    for m in range(dhid.shape[0]):
        put_windows(win, m, dhid[m].astype(F32))
    act_t = turned(act)
    for r in range(3):
        for c in range(3):
            t = 3 * r + c
            g = dot(act_t, all_windows(win, 2 - r, 2 - c)).astype(BF16)
            left, right = g[:, :HALF], g[:, HALF:]
            keep[t * C : (t + 1) * C] = jnp.where(first, left, right)
            send[t * C : (t + 1) * C] = jnp.where(first, right, left)


def input_back_kernel(mp, win, x_own, x_recv, stat, w_own, w_recv, prm, dmid, keep, send, sums, wfull):
    first = mp[0] == 0
    n = x_own.shape[0]
    for t in range(9):
        wfull[t] = join(first, w_own[t], w_recv[t], 1)
    first_grad = conv_transposed(win, wfull)
    units, grads = [], []
    for m in range(n):
        x = join(first, x_own[m], x_recv[m], 1).astype(F32)
        un = (x - stat[m : m + 1]) * stat[n + m : n + m + 1]
        u = un * prm[0:1] + prm[3:4]
        sig = sigmoid(u)
        units.append(un)
        grads.append(first_grad[m * PIX : (m + 1) * PIX] * (sig * (1.0 + u * (1.0 - sig))))
    back, gain_grad, bias_grad = norm_back(grads, units, prm[0:1], stat[n : 2 * n])
    for m in range(n):
        d = back[m] + dmid[m]
        left, right = d[:, :HALF], d[:, HALF:]
        keep[m] = jnp.where(first, left, right)
        send[m] = jnp.where(first, right, left).astype(BF16)
    sums[0:1] = gain_grad
    sums[1:2] = bias_grad
    sums[2:8] = jnp.zeros((6, C), F32)


def table_kernel(mp, dtime, emb, tw_own, tw_recv, times, table, tw_grad):
    first = mp[0] == 0
    tw = join(first, tw_own[...], tw_recv[...], 1)
    e = emb[...]
    sig = sigmoid(e)
    demb = dot_bt(dtime[...], tw) * (sig * (1.0 + e * (1.0 - sig)))
    act = e * sig
    act_high = act.astype(BF16)
    act_low = (act - act_high.astype(F32)).astype(BF16)
    mine = jnp.where(first, dtime[:, :HALF], dtime[:, HALF:])
    tw_grad[...] = dot_at(act_high, mine) + dot_at(act_low, mine)
    steps = table.shape[0]
    row = lax.broadcasted_iota(jnp.int32, (steps, e.shape[0]), 0)
    pick = jnp.where(row == times[...], 1.0, 0.0).astype(BF16)
    d_high = demb.astype(BF16)
    rest = demb - d_high.astype(F32)
    d_low = rest.astype(BF16)
    table[...] = dot(pick, d_high) + dot(pick, d_low)


def stages_of(count):
    stages, bit = [], 0
    while (1 << bit) < count:
        width = 2 if (1 << (bit + 2)) <= count else 1
        stages.append((bit, 1 << width))
        bit += width
    return stages


def swap_dp(values, flip):
    count = lax.axis_size("dp")
    return lax.ppermute(values, "dp", [(i, i ^ flip) for i in range(count)])


def swap_mp(values):
    return lax.ppermute(values, "mp", [(0, 1), (1, 0)])


ORDER = {2: (1,), 4: (1, 3, 2)}


def take(values, index):
    return lax.dynamic_index_in_dim(values, index, 0, keepdims=False)


def scatter_stage(values, stage):
    bit, size = stage
    me = (lax.axis_index("dp") >> bit) & (size - 1)
    total = take(values, me).astype(F32)
    for k in ORDER[size]:
        total = total + swap_dp(take(values, me ^ k), k << bit).astype(F32)
    return total.astype(BF16)


def gather_stage(values, stage):
    bit, size = stage
    me = (lax.axis_index("dp") >> bit) & (size - 1)
    result = jnp.zeros((size,) + values.shape, values.dtype)
    result = lax.dynamic_update_index_in_dim(result, values, me, 0)
    for k in ORDER[size]:
        result = lax.dynamic_update_index_in_dim(result, swap_dp(values, k << bit), me ^ k, 0)
    return result


def reduce_scatter(values, stages):
    count = lax.axis_size("dp")
    values = values.reshape(tuple(s for _, s in stages) + (values.shape[0] // count, HALF))
    for stage in stages:
        values = scatter_stage(values, stage)
    return values


def gather(values, stages):
    rows = values.shape[0]
    for stage in reversed(stages):
        values = gather_stage(values, stage)
    return values.reshape(-1, rows, HALF)


def on_device(
    maps_in, timesteps, temb_table, norm_gain, norm_bias, conv1_weight, conv_bias, temb_weight,
    temb_bias, conv2_weight, qkv_weight, qkv_bias, out_weight, out_bias, out_grad,
):
    me = lax.axis_index("mp")
    count = lax.axis_size("dp")
    stages = stages_of(count)
    n = maps_in.shape[0] // 2
    mp = jnp.reshape(me, (1,)).astype(jnp.int32)
    first = me == 0

    def mine(values):
        return lax.dynamic_slice_in_dim(values, me * n, n, 0)

    def theirs(values):
        return lax.dynamic_slice_in_dim(values, (1 - me) * n, n, 0)

    prm_own = jnp.concatenate(
        [norm_gain, norm_bias, conv_bias, qkv_bias, out_bias[None], temb_bias[None], jnp.zeros((4, HALF), F32)]
    )
    prm_recv = swap_mp(prm_own)
    prm = jnp.where(
        first,
        jnp.concatenate([prm_own, prm_recv], axis=1),
        jnp.concatenate([prm_recv, prm_own], axis=1),
    )
    x_own, x_recv = mine(maps_in), swap_mp(theirs(maps_in))
    w1_own = conv1_weight.reshape(9, C, HALF)
    w1_recv = swap_mp(w1_own)
    tw_recv = swap_mp(temb_weight)
    w2_own = conv2_weight.reshape(9, HALF, C)
    w2_recv = swap_mp(w2_own)
    qw_own = jnp.transpose(qkv_weight, (1, 0, 2))
    qw_recv = swap_mp(qw_own)
    ow_recv = swap_mp(out_weight)
    g_own, g_recv = mine(out_grad), swap_mp(theirs(out_grad))
    emb = jnp.take(temb_table, timesteps, axis=0)

    maps_shape = (n, PIX, C)
    unit = 2 * n * PIX * C * C
    act1, hid, stat1 = call(
        first_kernel,
        [(maps_shape, BF16), (maps_shape, F32), ((2 * n, C), F32)],
        mp, x_own, x_recv, w1_own, w1_recv, prm, emb, temb_weight, tw_recv,
        scratch=[window_scratch(n), pltpu.VMEM((9, C, C), BF16)],
        flops=9 * unit,
    )
    act2, mid, stat2 = call(
        second_kernel,
        [(maps_shape, BF16), (maps_shape, F32), ((2 * n, C), F32)],
        mp, x_own, x_recv, hid, w2_own, w2_recv, prm,
        scratch=[window_scratch(n), pltpu.VMEM((9, C, C), BF16)],
        flops=9 * unit,
    )
    half_shape = (n, PIX, HALF)
    out_keep, out_send, dmid, wg_keep, wg_send, sums3 = call(
        attention_kernel,
        [
            (half_shape, BF16), (half_shape, BF16), (maps_shape, F32),
            ((4 * C, HALF), BF16), ((4 * C, HALF), BF16), ((8, C), F32),
        ],
        mp, mid, g_own, g_recv, qw_own, qw_recv, out_weight, ow_recv, prm,
        scratch=[
            pltpu.VMEM(maps_shape, F32),
            pltpu.VMEM((3, n * PIX, C), BF16),
            pltpu.VMEM((n * PIX, C), BF16),
            pltpu.VMEM((n * PIX, C), BF16),
            pltpu.VMEM((3, n * PIX, C), BF16),
        ],
        flops=18 * unit,
    )
    win_shape = (n, 3, PIX + 2 * SIDE, C)
    grad_shape = (9 * C, HALF)
    c2_keep, c2_send, win2 = call(
        conv2_grad_kernel,
        [(grad_shape, BF16), (grad_shape, BF16), (win_shape, BF16)],
        mp, dmid, act2,
        flops=9 * unit,
    )
    dhid, sums2, dtime = call(
        hidden_back_kernel,
        [(maps_shape, BF16), ((8, C), F32), ((n, C), F32)],
        mp, win2, hid, stat2, w2_own, w2_recv, prm,
        scratch=[pltpu.VMEM((9, C, C), BF16)],
        flops=9 * unit,
    )
    c1_keep, c1_send, win1 = call(
        conv1_grad_kernel,
        [(grad_shape, BF16), (grad_shape, BF16), (win_shape, BF16)],
        mp, dhid, act1,
        flops=9 * unit,
    )
    mg_keep, mg_send, sums1 = call(
        input_back_kernel,
        [(half_shape, F32), (half_shape, BF16), ((8, C), F32)],
        mp, win1, x_own, x_recv, stat1, w1_own, w1_recv, prm, dmid,
        scratch=[pltpu.VMEM((9, C, C), BF16)],
        flops=9 * unit,
    )

    def paired(keep, send):
        return (keep.astype(F32) + swap_mp(send).astype(F32)).astype(BF16)

    early = jnp.concatenate([paired(c2_keep, c2_send), paired(wg_keep, wg_send)])
    late = paired(c1_keep, c1_send)
    early = reduce_scatter(early, stages)
    late = reduce_scatter(late, stages)

    small = jnp.concatenate(
        [
            sums1[0:1], sums2[0:1], sums3[0:1], sums1[1:2], sums2[1:2], sums3[1:2],
            sums2[2:3], sums3[2:3], sums3[3:6], jnp.zeros((5, C), F32),
        ]
    )
    small_keep = jnp.where(first, small[:, :HALF], small[:, HALF:])
    small_send = jnp.where(first, small[:, HALF:], small[:, :HALF])
    rows_send = jnp.concatenate([small_send, dtime.reshape(2 * n, HALF)])
    rows_recv = swap_mp(rows_send)
    small = small_keep + rows_recv[:16]
    time_own, time_recv = dtime.reshape(2 * n, HALF), rows_recv[16:]
    time_rows = jnp.where(
        first,
        jnp.concatenate([time_own, time_recv]),
        jnp.concatenate([time_recv, time_own]),
    )
    step_row = jnp.concatenate(
        [timesteps >> 5, timesteps & 31, jnp.zeros((HALF - 4 * n,), jnp.int32)]
    ).astype(F32)[None]
    extra = jnp.concatenate([small[:11], step_row, small[12:], time_rows]).astype(BF16)
    early_rows = early.shape[0]
    early = gather(jnp.concatenate([early, extra]), stages)
    late = gather(late, stages)

    extra = early[:, early_rows:]
    early = early[:, :early_rows].reshape(-1, HALF)
    small = jnp.sum(extra[:, :16].astype(F32), axis=0)
    steps = extra[:, 11, : 4 * n].astype(jnp.int32)
    steps = (steps[:, : 2 * n] * 32 + steps[:, 2 * n :]).reshape(-1)
    time_all = extra[:, 16:].reshape(count * 2 * n, C)
    emb_all = jnp.take(temb_table, steps, axis=0)
    table_grad, temb_weight_grad = call(
        table_kernel,
        [(temb_table.shape, F32), (temb_weight.shape, F32)],
        mp, time_all, emb_all, temb_weight, tw_recv, steps[None],
        flops=unit,
    )
    temb_bias_sum = jnp.sum(time_all.astype(F32), axis=0)
    temb_bias_grad = jnp.where(first, temb_bias_sum[:HALF], temb_bias_sum[HALF:])

    def both_maps(keep, recv):
        return jnp.where(first, jnp.concatenate([keep, recv]), jnp.concatenate([recv, keep]))

    maps_out = both_maps(out_keep, swap_mp(out_send))
    maps_grad = both_maps(mg_keep, swap_mp(mg_send).astype(F32))

    early = early.astype(F32)
    conv2_grad = early[: 9 * C].reshape(9, 2, HALF, HALF)
    conv2_grad = jnp.transpose(conv2_grad, (0, 2, 1, 3)).reshape(3, 3, HALF, C)
    qkv_grad = jnp.transpose(early[9 * C : 12 * C].reshape(3, C, HALF), (1, 0, 2))
    out_weight_grad = jnp.transpose(early[12 * C :].reshape(2, HALF, HALF), (1, 0, 2)).reshape(HALF, C)
    conv1_grad = late.astype(F32).reshape(3, 3, C, HALF)
    return (
        maps_out, maps_grad, table_grad, small[0:3], small[3:6], conv1_grad, small[6:8],
        temb_weight_grad, temb_bias_grad, conv2_grad, qkv_grad, small[8:10], out_weight_grad, small[10],
    )


def solution(mesh):
    args = (
        P("dp", None, "mp"), P("dp"), P(), P(None, "mp"), P(None, "mp"), P(None, None, None, "mp"),
        P(None, "mp"), P(None, "mp"), P("mp"), P(None, None, "mp", None), P(None, None, "mp"),
        P(None, "mp"), P("mp", None), P("mp"), P("dp", None, "mp"),
    )
    outs = (
        P("dp", None, "mp"), P("dp", None, "mp"), P(), P(None, "mp"), P(None, "mp"),
        P(None, None, None, "mp"), P(None, "mp"), P(None, "mp"), P("mp"), P(None, None, "mp", None),
        P(None, None, "mp"), P(None, "mp"), P("mp", None), P("mp"),
    )
    return jax.shard_map(on_device, mesh=mesh, in_specs=args, out_specs=outs, check_vma=False)
```

time: 557 us -> 127 us (0.23); the launches traced: 547 us -> 126 us
  waiting for transfers between devices: 338 us -> 16 us
  matrix products: 57.1 us -> 0 us
  blocking collectives: 43.3 us -> 0 us
  other arithmetic: 47.4 us -> 8.35 us
  starting transfers between devices: 1.49 us -> 39.1 us
  Pallas kernels: 0 us -> 25.9 us
  between operations: 15.9 us -> 1.29 us
  local copies, waits for them, and re-layouts: 44.4 us -> 35.4 us
    psum x4 -> x0, waiting for transfers between devices: 273 us -> none  [the longest x1 156 us: channel_path(): lax.psum((gain_stack, shift_stack, conv1_weight_grad, conv_bias_stack, te...]
    dot_general x69 -> x0, matrix products: 57.1 us -> none  [the longest x20 20.6 us: contract_rows(): lax.dot_general(left, right, (((0,), (0,)), ((), ())), preferred_element_...]
    psum x1 -> x0, blocking collectives: 43.3 us -> none  [channel_path(): lax.psum((gain_stack, shift_stack, conv1_weight_grad, conv_bias_stack, te...]
    ppermute x0 -> x38, starting transfers between devices: none -> 39.1 us  [the longest x24 35.3 us: swap_dp(): return lax.ppermute(values, 'dp', [(i, i ^ flip) for i in range(count)])]
    all_gather x4 -> x0, waiting for transfers between devices: 36.6 us -> none  [gather_channels(): return lax.all_gather(values, 'mp', axis=2, tiled=True)]
    reduce_sum x29 -> x2, other arithmetic: 28.4 us -> 0.05 us  [the longest x1 0.03 us: on_device(): temb_bias_sum = jnp.sum(time_all.astype(F32), axis=0)]
    reduce_scatter x4 -> x0, waiting for transfers between devices: 27.4 us -> none  [reduce_channels(): return lax.psum_scatter(values, 'mp', scatter_dimension=2, tiled=True)]
    pallas_call x0 -> x8, Pallas kernels: none -> 25.9 us  [call(): pl.pallas_call(body, out_shape=tuple((jax.ShapeDtypeStruct(s, d) for s, d...]
  transfers between devices with their start and end apart: 12 -> 38, of which waited for: 11 -> 10; matrix products, arithmetic and copies ran while one was open for 11% -> 14% of each run, Pallas kernels for 0% -> 5%
where the time goes in v1:
time: 127 us; the launch traced here: 126 us
  starting transfers between devices  39.1 us (31%)
  local copies, waits for them, and re-layouts  35.4 us (28%)
  Pallas kernels  25.9 us (20%)
  waiting for transfers between devices  16 us (13%)
  other arithmetic  8.35 us (7%)
  between operations  1.29 us (1%)
    ppermute x24, starting transfers between devices, swap_dp(): return lax.ppermute(values, 'dp', [(i, i ^ flip) for i in range(count)])  35.3 us
    pallas_call x8, Pallas kernels, call(): pl.pallas_call(body, out_shape=tuple((jax.ShapeDtypeStruct(s, d) for s, d...  25.9 us
    ppermute x24, waiting for transfers between devices, swap_dp(): return lax.ppermute(values, 'dp', [(i, i ^ flip) for i in range(count)])  15 us
    unnamed x63, local copies, waits for them, and re-layouts  11.3 us
    dynamic_update_slice x12, local copies, waits for them, and re-layouts, gather_stage(): lax.dynamic_update_index_in_dim(result, swap_dp(values, k << bit), me ^ k...  4.92 us
    dynamic_slice x2, local copies, waits for them, and re-layouts, theirs(): return lax.dynamic_slice_in_dim(values, (1 - me) * n, n, 0)  3.78 us
    ppermute x14, starting transfers between devices, swap_mp(): return lax.ppermute(values, 'mp', [(0, 1), (1, 0)])  3.78 us
    transpose x1, local copies, waits for them, and re-layouts, on_device(): conv2_grad = jnp.transpose(conv2_grad, (0, 2, 1, 3)).reshape(3, 3, HALF, C)  3.2 us
  transfers between devices with their start and end apart: 38, of which 10 were waited for; matrix products, arithmetic and copies ran while one was open for 14% of the time, Pallas kernels for 5%

profile of v1, /device:TPU:0, one launch (start us, length us, event | category | flops | bytes accessed | tf_op | source)
XLA Modules:
  0.0 126.1 jit_solution(13493189315898140980)
XLA Ops:
  0.7 1.9 %constant_dynamic-slice_fusion.2 = (bf16[4,256,128]{2,1,0:T(8,128)(2,1)}, bf16[4,256,128]{2,1,0:T(8,128)(2,1)S(1)}) fusion(bf16[8,256,128]{2,1,0:T(8,128)(2,1)} %param.15, s32[]{:T(128)S(6)} %select_n.141, s32[]{:T(128)S(6)} %select_n.140), kind=kLoop, calls=%fused_computation.60 | loop fusion | bytes 1048584 | tf_op jit(solution)/shard_map/dynamic_slice | solution.py:431
  3.1 1.4 %concatenate.57 = f32[16,128]{1,0:T(8,128)S(1)} concatenate(f32[3,128]{1,0:T(4,128)} %param.18, f32[3,128]{1,0:T(4,128)} %param.19, f32[2,128]{1,0:T(2,128)} %param.21, f32[2,128]{1,0:T(2,128)} %param.26, f32[1,128]{1,0:T(1,128)} %bitcast.131, f32[1,128]{1,0:T(1,128)} %bitcast.132, f32[4,128]{1,0:T(4,128)S(1)} %broadcast_in_dim.104), dimensions={0} | concatenate | bytes 16384 | tf_op jit(solution)/shard_map/concatenate | solution.py:433
  7.5 1.9 %constant_dynamic-slice_fusion = (bf16[4,256,128]{2,1,0:T(8,128)(2,1)}, bf16[4,256,128]{2,1,0:T(8,128)(2,1)}) fusion(bf16[8,256,128]{2,1,0:T(8,128)(2,1)} %param.29, s32[]{:T(128)S(6)} %select_n.141, s32[]{:T(128)S(6)} %select_n.140), kind=kLoop, calls=%fused_computation.58 | loop fusion | bytes 1048584 | tf_op jit(solution)/shard_map/dynamic_slice | solution.py:431
  10.1 3.4 %shard_map.254 = (bf16[4,256,256]{2,1,0:T(8,128)(2,1)S(1)}, f32[4,256,256]{2,1,0:T(8,128)S(1)}, f32[8,256]{1,0:T(8,128)S(1)}) custom-call(s32[1]{0:T(128)} %bitcast.mp, bf16[4,256,128]{2,1,0:T(8,128)(2,1)S(1)} %get-tuple-element.91.x_own, bf16[4,256,128]{2,1,0:T(8,128)(2,1)S(1)} %collective-permute-done.x_recv, bf16[9,256,128]{2,1,0:T(8,128)(2,1)S(1)} %bitcast.110, ...), custom_call_target="tpu_custom_call" | custom-call | flops 1207959552 | bytes 1048576 | tf_op jit(solution)/shard_map/pallas_call | solution.py:21
  13.6 3.4 %shard_map.255 = (bf16[4,256,256]{2,1,0:T(8,128)(2,1)S(1)}, f32[4,256,256]{2,1,0:T(8,128)S(1)}, f32[8,256]{1,0:T(8,128)S(1)}) custom-call(s32[1]{0:T(128)} %bitcast.mp, bf16[4,256,128]{2,1,0:T(8,128)(2,1)S(1)} %get-tuple-element.91.x_own, bf16[4,256,128]{2,1,0:T(8,128)(2,1)S(1)} %collective-permute-done.x_recv, f32[4,256,256]{2,1,0:T(8,128)S(1)} %get-tuple-element.40.hid, ...), custom_call_target="tpu_custom_call" | custom-call | flops 1207959552 | bytes 1048576 | tf_op jit(solution)/shard_map/pallas_call | solution.py:21
  17.1 6.7 %shard_map.256 = (bf16[4,256,128]{2,1,0:T(8,128)(2,1)S(1)}, bf16[4,256,128]{2,1,0:T(8,128)(2,1)S(1)}, f32[4,256,256]{2,1,0:T(8,128)S(1)}, bf16[1024,128]{1,0:T(8...) custom-call(s32[1]{0:T(128)} %bitcast.mp, f32[4,256,256]{2,1,0:T(8,128)S(1)} %get-tuple-element.41.mid, ...), custom_call_target="tpu_custom_call" | custom-call | flops 2415919104 | bytes 1048576 | tf_op jit(solution)/shard_map/pallas_call | solution.py:21
  23.8 0.7 copy-done.9
  24.5 0.7 copy-done.14
  25.2 0.7 copy-done.21
  25.9 0.7 copy-done.22
  26.6 1.6 %shard_map.257 = (bf16[2304,128]{1,0:T(8,128)(2,1)S(1)}, bf16[2304,128]{1,0:T(8,128)(2,1)S(1)}, bf16[4,3,288,256]{3,2,1,0:T(8,128)(2,1)S(1)}) custom-call(s32[1]{0:T(128)} %bitcast.mp, f32[4,256,256]{2,1,0:T(8,128)S(1)} %get-tuple-element.44.dmid, bf16[4,256,256]{2,1,0:T(8,128)(2,1)S(1)} %get-tuple-element.45.act), custom_call_target="tpu_custom_call" | custom-call | flops 1207959552 | bytes 1048576 | tf_op jit(solution)/shard_map/pallas_call | solution.py:21
  28.2 0.8 copy-done.3
  29.0 0.8 copy-done.19
  29.8 3.6 %shard_map.258 = (bf16[4,256,256]{2,1,0:T(8,128)(2,1)S(1)}, f32[8,256]{1,0:T(8,128)S(1)}, f32[4,256]{1,0:T(4,128)S(1)}) custom-call(s32[1]{0:T(128)} %bitcast.mp, bf16[4,3,288,256]{3,2,1,0:T(8,128)(2,1)S(1)} %get-tuple-element.46.win, f32[4,256,256]{2,1,0:T(8,128)S(1)} %get-tuple-element.40.hid, f32[8,256]{1,0:T(8,128)S(1)} %get-tuple-element.47.stat, ...), custom_call_target="tpu_custom_call" | custom-call | flops 1207959552 | bytes 1048576 | tf_op jit(solution)/shard_map/pallas_call | solution.py:21
  33.5 0.8 copy-done.26
  34.3 1.0 copy-done.27
  35.3 1.0 copy-done.29
  36.3 1.5 %shard_map.259 = (bf16[2304,128]{1,0:T(8,128)(2,1)S(1)}, bf16[2304,128]{1,0:T(8,128)(2,1)S(1)}, bf16[4,3,288,256]{3,2,1,0:T(8,128)(2,1)S(1)}) custom-call(s32[1]{0:T(128)} %bitcast.mp, bf16[4,256,256]{2,1,0:T(8,128)(2,1)S(1)} %copy-done.27, bf16[4,256,256]{2,1,0:T(8,128)(2,1)S(1)} %copy-done.29), custom_call_target="tpu_custom_call" | custom-call | flops 1207959552 | bytes 1048576 | tf_op jit(solution)/shard_map/pallas_call | solution.py:21
  37.9 0.8 copy-done.5
  38.7 0.8 copy-done.20
  39.5 3.4 %shard_map.260 = (f32[4,256,128]{2,1,0:T(8,128)S(1)}, bf16[4,256,128]{2,1,0:T(8,128)(2,1)S(1)}, f32[8,256]{1,0:T(8,128)S(1)}) custom-call(s32[1]{0:T(128)} %bitcast.mp, bf16[4,3,288,256]{3,2,1,0:T(8,128)(2,1)S(1)} %get-tuple-element.50.win, bf16[4,256,128]{2,1,0:T(8,128)(2,1)S(1)} %get-tuple-element.91.x_own, bf16[4,256,128]{2,1,0:T(8,128)(2,1)S(1)} %copy-done.12, ...), custom_call_target="tpu_custom_call" | custom-call | flops 1207959552 | bytes 1048576 | tf_op jit(solution)/shard_map/pallas_call | solution.py:21
  43.0 0.8 copy-done.7
  43.8 0.7 copy-done.23
  46.4 1.0 collective-permute-done.9
  47.4 1.9 %maximum_select_fusion.1 = bf16[8,256,128]{2,1,0:T(8,128)(2,1)} fusion(bf16[4,256,128]{2,1,0:T(8,128)(2,1)S(1)} %collective-permute-done.8, bf16[4,256,128]{2,1,0:T(8,128)(2,1)} %copy-done.14, pred[]{:T(512)S(6)} %eq.3), kind=kLoop, calls=%fused_computation.7 | loop fusion | flops 786432 | bytes 1048577 | tf_op jit(solution)/shard_map/jit(_where)/select_n | solution.py:566
  49.4 1.1 maximum_select_fusion
  50.8 2.7 %collective-permute-start.28 = (bf16[4,144,128]{2,1,0:T(8,128)(2,1)S(1)}, bf16[4,144,128]{2,1,0:T(8,128)(2,1)S(1)}, u32[]{:S(2)}, u32[]{:S(2)}) collective-permute-start(bf16[4,144,128]{2,1,0:T(8,128)(2,1)S(1)} %get-tuple-element.86), channel_id=1, source_target_pairs={{0,4},{2,6},{4,0},{6,2},{8,12},{10,14},{12,8},{14,10},{16,20},{18,... | collective-permute-start | bytes 442376 | tf_op jit(solution)/shard_map/ppermute | solution.py:368
  53.5 1.4 %collective-permute-start.27 = (bf16[4,144,128]{2,1,0:T(8,128)(2,1)S(1)}, bf16[4,144,128]{2,1,0:T(8,128)(2,1)S(1)}, u32[]{:S(2)}, u32[]{:S(2)}) collective-permute-start(bf16[4,144,128]{2,1,0:T(8,128)(2,1)S(1)} %get-tuple-element.87), channel_id=1, source_target_pairs={{0,6},{2,4},{4,2},{6,0},{8,14},{10,12},{12,10},{14,8},{16,22},{18,... | collective-permute-start | bytes 442376 | tf_op jit(solution)/shard_map/ppermute | solution.py:368
  55.3 5.6 %collective-permute-done.28 = bf16[4,144,128]{2,1,0:T(8,128)(2,1)S(1)} collective-permute-done((bf16[4,144,128]{2,1,0:T(8,128)(2,1)S(1)}, bf16[4,144,128]{2,1,0:T(8,128)(2,1)S(1)}, u32[]{:S(2)}, u32[]{:S(2)}) %collective-permute-start.28) | collective-permute-done | bytes 147488 | tf_op jit(solution)/shard_map/ppermute | solution.py:368
  61.2 1.2 collective-permute-done.26
  62.5 2.8 %collective-permute-start.31 = (bf16[144,128]{1,0:T(8,128)(2,1)S(1)}, bf16[144,128]{1,0:T(8,128)(2,1)S(1)}, u32[]{:S(2)}, u32[]{:S(2)}) collective-permute-start(bf16[144,128]{1,0:T(8,128)(2,1)S(1)} %get-tuple-element.96), channel_id=1, source_target_pairs={{0,16},{2,18},{4,20},{6,22},{8,24},{10,26},{12,28},{14,30},{16,0},... | collective-permute-start | bytes 110600 | tf_op jit(solution)/shard_map/ppermute | solution.py:368
  65.3 1.3 %collective-permute-start.30 = (bf16[144,128]{1,0:T(8,128)(2,1)S(1)}, bf16[144,128]{1,0:T(8,128)(2,1)S(1)}, u32[]{:S(2)}, u32[]{:S(2)}) collective-permute-start(bf16[144,128]{1,0:T(8,128)(2,1)S(1)} %get-tuple-element.97), channel_id=1, source_target_pairs={{0,24},{2,26},{4,28},{6,30},{8,16},{10,18},{12,20},{14,22},{16,8},... | collective-permute-start | bytes 110600 | tf_op jit(solution)/shard_map/ppermute | solution.py:368
  66.9 1.6 %collective-permute-start.14 = (bf16[4,208,128]{2,1,0:T(8,128)(2,1)S(1)}, bf16[4,208,128]{2,1,0:T(8,128)(2,1)S(1)}, u32[]{:S(2)}, u32[]{:S(2)}) collective-permute-start(bf16[4,208,128]{2,1,0:T(8,128)(2,1)S(1)} %get-tuple-element.83), channel_id=1, source_target_pairs={{0,4},{2,6},{4,0},{6,2},{8,12},{10,14},{12,8},{14,10},{16,20},{18,... | collective-permute-start | bytes 638984 | tf_op jit(solution)/shard_map/ppermute | solution.py:368
  68.5 1.4 %collective-permute-start.13 = (bf16[4,208,128]{2,1,0:T(8,128)(2,1)S(1)}, bf16[4,208,128]{2,1,0:T(8,128)(2,1)S(1)}, u32[]{:S(2)}, u32[]{:S(2)}) collective-permute-start(bf16[4,208,128]{2,1,0:T(8,128)(2,1)S(1)} %get-tuple-element.84), channel_id=1, source_target_pairs={{0,6},{2,4},{4,2},{6,0},{8,14},{10,12},{12,10},{14,8},{16,22},{18,... | collective-permute-start | bytes 638984 | tf_op jit(solution)/shard_map/ppermute | solution.py:368
  71.1 1.3 %collective-permute-start.32 = (bf16[144,128]{1,0:T(8,128)(2,1)S(1)}, bf16[144,128]{1,0:T(8,128)(2,1)S(1)}, u32[]{:S(2)}, u32[]{:S(2)}) collective-permute-start(bf16[144,128]{1,0:T(8,128)(2,1)S(1)} %get-tuple-element.81), channel_id=1, source_target_pairs={{0,8},{2,10},{4,12},{6,14},{8,0},{10,2},{12,4},{14,6},{16,24},{18,... | collective-permute-start | bytes 110600 | tf_op jit(solution)/shard_map/ppermute | solution.py:368
  72.4 2.5 %collective-permute-start.33 = (bf16[144,128]{1,0:T(8,128)(2,1)S(1)}, bf16[144,128]{1,0:T(8,128)(2,1)S(1)}, u32[]{:S(2)}, u32[]{:S(2)}) collective-permute-start(bf16[144,128]{1,0:T(8,128)(2,1)S(1)} %get-tuple-element.81), channel_id=1, source_target_pairs={{0,24},{2,26},{4,28},{6,30},{8,16},{10,18},{12,20},{14,22},{16,8},... | collective-permute-start | bytes 110600 | tf_op jit(solution)/shard_map/ppermute | solution.py:368
  74.9 2.5 %collective-permute-done.14 = bf16[4,208,128]{2,1,0:T(8,128)(2,1)S(1)} collective-permute-done((bf16[4,208,128]{2,1,0:T(8,128)(2,1)S(1)}, bf16[4,208,128]{2,1,0:T(8,128)(2,1)S(1)}, u32[]{:S(2)}, u32[]{:S(2)}) %collective-permute-start.14) | collective-permute-done | bytes 213024 | tf_op jit(solution)/shard_map/ppermute | solution.py:368
  77.4 2.5 %collective-permute-start.34 = (bf16[144,128]{1,0:T(8,128)(2,1)S(1)}, bf16[144,128]{1,0:T(8,128)(2,1)S(1)}, u32[]{:S(2)}, u32[]{:S(2)}) collective-permute-start(bf16[144,128]{1,0:T(8,128)(2,1)S(1)} %get-tuple-element.81), channel_id=1, source_target_pairs={{0,16},{2,18},{4,20},{6,22},{8,24},{10,26},{12,28},{14,30},{16,0},... | collective-permute-start | bytes 110600 | tf_op jit(solution)/shard_map/ppermute | solution.py:368
  80.1 1.3 %collective-permute-start.17 = (bf16[208,128]{1,0:T(8,128)(2,1)S(1)}, bf16[208,128]{1,0:T(8,128)(2,1)S(1)}, u32[]{:S(2)}, u32[]{:S(2)}) collective-permute-start(bf16[208,128]{1,0:T(8,128)(2,1)S(1)} %get-tuple-element.93), channel_id=1, source_target_pairs={{0,16},{2,18},{4,20},{6,22},{8,24},{10,26},{12,28},{14,30},{16,0},... | collective-permute-start | bytes 159752 | tf_op jit(solution)/shard_map/ppermute | solution.py:368
  81.4 1.4 %collective-permute-start.16 = (bf16[208,128]{1,0:T(8,128)(2,1)S(1)}, bf16[208,128]{1,0:T(8,128)(2,1)S(1)}, u32[]{:S(2)}, u32[]{:S(2)}) collective-permute-start(bf16[208,128]{1,0:T(8,128)(2,1)S(1)} %get-tuple-element.94), channel_id=1, source_target_pairs={{0,24},{2,26},{4,28},{6,30},{8,16},{10,18},{12,20},{14,22},{16,8},... | collective-permute-start | bytes 159752 | tf_op jit(solution)/shard_map/ppermute | solution.py:368
  82.7 0.9 collective-permute-start.15
  83.7 1.0 collective-permute-start.35
  84.7 2.4 %collective-permute-start.36 = (bf16[4,144,128]{2,1,0:T(8,128)(2,1)S(1)}, bf16[4,144,128]{2,1,0:T(8,128)(2,1)}, u32[]{:S(2)}, u32[]{:S(2)}) collective-permute-start(bf16[4,144,128]{2,1,0:T(8,128)(2,1)S(1)} %bitcast_dynamic-update-slice_fusion.12), channel_id=1, source_target_pairs={{0,6},{2,4},{4,2},{6,0},{8,14},{10,12},{12,10},{14,8},{16,22},{18,... | collective-permute-start | bytes 442376 | tf_op jit(solution)/shard_map/ppermute | solution.py:368
  87.0 0.9 broadcast_in_dim.122
  87.9 0.7 bitcast_dynamic-update-slice_fusion.7
  88.9 1.2 collective-permute-start.19
  90.1 2.5 %collective-permute-start.20 = (bf16[240,128]{1,0:T(8,128)(2,1)S(1)}, bf16[240,128]{1,0:T(8,128)(2,1)S(1)}, u32[]{:S(2)}, u32[]{:S(2)}) collective-permute-start(bf16[240,128]{1,0:T(8,128)(2,1)S(1)} %concatenate.72), channel_id=1, source_target_pairs={{0,24},{2,26},{4,28},{6,30},{8,16},{10,18},{12,20},{14,22},{16,8},... | collective-permute-start | bytes 184328 | tf_op jit(solution)/shard_map/ppermute | solution.py:368
  93.2 2.1 %collective-permute-start.21 = (bf16[240,128]{1,0:T(8,128)(2,1)S(1)}, bf16[240,128]{1,0:T(8,128)(2,1)S(1)}, u32[]{:S(2)}, u32[]{:S(2)}) collective-permute-start(bf16[240,128]{1,0:T(8,128)(2,1)S(1)} %concatenate.72), channel_id=1, source_target_pairs={{0,16},{2,18},{4,20},{6,22},{8,24},{10,26},{12,28},{14,30},{16,0},... | collective-permute-start | bytes 184328 | tf_op jit(solution)/shard_map/ppermute | solution.py:368
  95.3 0.8 collective-permute-done.20
  96.1 2.2 %collective-permute-done.21 = bf16[240,128]{1,0:T(8,128)(2,1)S(1)} collective-permute-done((bf16[240,128]{1,0:T(8,128)(2,1)S(1)}, bf16[240,128]{1,0:T(8,128)(2,1)S(1)}, u32[]{:S(2)}, u32[]{:S(2)}) %collective-permute-start.21) | collective-permute-done | bytes 61472 | tf_op jit(solution)/shard_map/ppermute | solution.py:368
  98.3 2.4 %collective-permute-start.22 = (bf16[4,240,128]{2,1,0:T(8,128)(2,1)S(1)}, bf16[4,240,128]{2,1,0:T(8,128)(2,1)S(1)}, u32[]{:S(2)}, u32[]{:S(2)}) collective-permute-start(bf16[4,240,128]{2,1,0:T(8,128)(2,1)S(1)} %bitcast_dynamic-update-slice_fusion.8), channel_id=1, source_target_pairs={{0,2},{2,0},{4,6},{6,4},{8,10},{10,8},{12,14},{14,12},{16,18},{18,... | collective-permute-start | bytes 737288 | tf_op jit(solution)/shard_map/ppermute | solution.py:368
  100.7 1.0 collective-permute-start.23
  102.5 1.6 %bitcast_dynamic-update-slice_fusion.6 = bf16[4,4,144,128]{3,2,1,0:T(8,128)(2,1)} fusion(bf16[4,4,144,128]{3,2,1,0:T(8,128)(2,1)} %bitcast_dynamic-update-slice_fusion.7, s32[]{:T(128)S(6)} %select_n.149, bf16[4,144,128]{2,1,0:T(8,128)(2,1)} %collective-permute-done.35), kind=kLoop, calls=%fused_computation.26 | loop fusion | bytes 294916 | tf_op jit(solution)/shard_map/jit(dynamic_update_index_in_dim)/dynamic_update_slice | solution.py:397
  104.1 1.6 %bitcast_dynamic-update-slice_fusion.5 = bf16[4,4,144,128]{3,2,1,0:T(8,128)(2,1)} fusion(bf16[4,4,144,128]{3,2,1,0:T(8,128)(2,1)} %bitcast_dynamic-update-slice_fusion.6, s32[]{:T(128)S(6)} %select_n.150, bf16[4,144,128]{2,1,0:T(8,128)(2,1)} %collective-permute-done.36), kind=kLoop, calls=%fused_computation.25 | loop fusion | bytes 294916 | tf_op jit(solution)/shard_map/jit(dynamic_update_index_in_dim)/dynamic_update_slice | solution.py:397
  105.7 1.6 %bitcast_dynamic-update-slice_fusion.4 = bf16[4,4,144,128]{3,2,1,0:T(8,128)(2,1)} fusion(bf16[4,4,144,128]{3,2,1,0:T(8,128)(2,1)} %bitcast_dynamic-update-slice_fusion.5, s32[]{:T(128)S(6)} %select_n.151, bf16[4,144,128]{2,1,0:T(8,128)(2,1)} %collective-permute-done.37), kind=kLoop, calls=%fused_computation.24 | loop fusion | bytes 294916 | tf_op jit(solution)/shard_map/jit(dynamic_update_index_in_dim)/dynamic_update_slice | solution.py:397
  107.2 2.2 %convert.27 = f32[3,3,256,128]{3,2,1,0:T(8,128)} convert(bf16[3,3,256,128]{3,2,1,0:T(8,128)(2,1)} %bitcast.60) | non-fusion elementwise | flops 294912 | bytes 1769472 | tf_op jit(solution)/shard_map/convert_element_type | solution.py:576
  109.5 1.3 %collective-permute-done.24 = bf16[4,240,128]{2,1,0:T(8,128)(2,1)S(1)} collective-permute-done((bf16[4,240,128]{2,1,0:T(8,128)(2,1)S(1)}, bf16[4,240,128]{2,1,0:T(8,128)(2,1)S(1)}, u32[]{:S(2)}, u32[]{:S(2)}) %collective-permute-start.24) | collective-permute-done | bytes 245792 | tf_op jit(solution)/shard_map/ppermute | solution.py:368
  112.7 1.2 slice.149
  113.9 0.8 slice.150
  115.2 0.8 gather_fusion.1
  116.5 3.2 %copy.39 = f32[9,128,2,128]{3,2,1,0:T(2,128)} copy(f32[9,128,2,128]{3,1,2,0:T(8,128)} %bitcast.118) | data formatting | bytes 2359296 | tf_op jit(solution)/shard_map/transpose | solution.py:573
  119.7 3.1 %reshape.177 = f32[3,3,128,256]{3,2,1,0:T(8,128)} reshape(f32[9,128,2,128]{3,2,1,0:T(2,128)} %copy.39) | data formatting | bytes 2359296 | tf_op jit(solution)/shard_map/reshape | solution.py:573
  122.9 0.8 copy.41
  123.8 2.3 %shard_map.261 = (f32[1000,512]{1,0:T(8,128)}, f32[512,128]{1,0:T(8,128)}) custom-call(s32[1]{0:T(128)} %bitcast.mp, bf16[128,256]{1,0:T(8,128)(2,1)S(1)} %reshape.172.dtime, f32[128,512]{1,0:T(8,128)S(1)} %broadcast_select_fusion.emb, bf16[512,128]{1,0:T(8,128)(2,1)S(1)} %copy-done.15, bf16[512,128]{1,0:T(8,128)(2,1)S(1)} %copy-done.17, ...), custom_call_target="tpu_custom_call" | custom-call | flops 134217728 | bytes 1048576 | tf_op jit(solution)/shard_map/pallas_call | solution.py:21
  (171 shorter events, 13.8 us)
Async XLA Ops:
  0.6 6.2 %copy-start = (f32[1000,512]{1,0:T(8,128)S(1)}, f32[1000,512]{1,0:T(8,128)}, u32[]{:S(2)}) copy-start(f32[1000,512]{1,0:T(8,128)} %param.17) | copy-start | bytes 6144004
  0.7 9.4 %copy-start.1 = (bf16[3,3,256,128]{3,2,1,0:T(8,128)(2,1)S(1)}, bf16[3,3,256,128]{3,2,1,0:T(8,128)(2,1)}, u32[]{:S(2)}) copy-start(bf16[3,3,256,128]{3,2,1,0:T(8,128)(2,1)} %param.20) | copy-start | bytes 1769476
  0.7 9.4 %copy-start.15 = (bf16[512,128]{1,0:T(8,128)(2,1)S(1)}, bf16[512,128]{1,0:T(8,128)(2,1)}, u32[]{:S(2)}) copy-start(bf16[512,128]{1,0:T(8,128)(2,1)} %tw_own.3) | copy-start | bytes 393220
  2.6 7.3 %collective-permute-start = (bf16[4,256,128]{2,1,0:T(8,128)(2,1)}, bf16[4,256,128]{2,1,0:T(8,128)(2,1)S(1)}, u32[]{:S(2)}, u32[]{:S(2)}) collective-permute-start(bf16[4,256,128]{2,1,0:T(8,128)(2,1)} %get-tuple-element.90), channel_id=1, source_target_pairs={{0,1},{1,0},{2,3},{3,2},{4,5},{5,4},{6,7},{7,6},{8,9},{9,8},{10,11... | collective-permute-start | bytes 786440 | tf_op jit(solution)/shard_map/ppermute | solution.py:372
  3.1 7.0 %collective-permute-start.1 = (bf16[9,256,128]{2,1,0:T(8,128)(2,1)}, bf16[9,256,128]{2,1,0:T(8,128)(2,1)}, u32[]{:S(2)}, u32[]{:S(2)}) collective-permute-start(bf16[9,256,128]{2,1,0:T(8,128)(2,1)} %bitcast.109), channel_id=1, source_target_pairs={{0,1},{1,0},{2,3},{3,2},{4,5},{5,4},{6,7},{7,6},{8,9},{9,8},{10,11... | collective-permute-start | bytes 1769480 | tf_op jit(solution)/shard_map/ppermute | solution.py:372
  4.6 4.8 %collective-permute-start.2 = (f32[16,128]{1,0:T(8,128)S(1)}, f32[16,128]{1,0:T(8,128)S(1)}, u32[]{:S(2)}, u32[]{:S(2)}) collective-permute-start(f32[16,128]{1,0:T(8,128)S(1)} %concatenate.57), channel_id=1, source_target_pairs={{0,1},{1,0},{2,3},{3,2},{4,5},{5,4},{6,7},{7,6},{8,9},{9,8},{10,11... | collective-permute-start | bytes 24584 | tf_op jit(solution)/shard_map/ppermute | solution.py:372
  5.0 4.4 %collective-permute-start.3 = (bf16[512,128]{1,0:T(8,128)(2,1)}, bf16[512,128]{1,0:T(8,128)(2,1)S(1)}, u32[]{:S(2)}, u32[]{:S(2)}) collective-permute-start(bf16[512,128]{1,0:T(8,128)(2,1)} %tw_own.3), channel_id=1, source_target_pairs={{0,1},{1,0},{2,3},{3,2},{4,5},{5,4},{6,7},{7,6},{8,9},{9,8},{10,11... | collective-permute-start | bytes 393224 | tf_op jit(solution)/shard_map/ppermute | solution.py:372
  5.1 8.4 %collective-permute-start.4 = (bf16[9,128,256]{2,1,0:T(8,128)(2,1)}, bf16[9,128,256]{2,1,0:T(8,128)(2,1)}, u32[]{:S(2)}, u32[]{:S(2)}) collective-permute-start(bf16[9,128,256]{2,1,0:T(8,128)(2,1)} %bitcast.112), channel_id=1, source_target_pairs={{0,1},{1,0},{2,3},{3,2},{4,5},{5,4},{6,7},{7,6},{8,9},{9,8},{10,11... | collective-permute-start | bytes 1769480 | tf_op jit(solution)/shard_map/ppermute | solution.py:372
  9.4 7.7 %collective-permute-start.5 = (bf16[4,256,128]{2,1,0:T(8,128)(2,1)}, bf16[4,256,128]{2,1,0:T(8,128)(2,1)S(1)}, u32[]{:S(2)}, u32[]{:S(2)}) collective-permute-start(bf16[4,256,128]{2,1,0:T(8,128)(2,1)} %get-tuple-element.88), channel_id=1, source_target_pairs={{0,1},{1,0},{2,3},{3,2},{4,5},{5,4},{6,7},{7,6},{8,9},{9,8},{10,11... | collective-permute-start | bytes 786440 | tf_op jit(solution)/shard_map/ppermute | solution.py:372
  9.4 4.0 %copy-start.16 = (bf16[512,128]{1,0:T(8,128)(2,1)}, bf16[512,128]{1,0:T(8,128)(2,1)S(1)}, u32[]{:S(2)}) copy-start(bf16[512,128]{1,0:T(8,128)(2,1)S(1)} %collective-permute-done.3.tw_recv) | copy-start | bytes 393220
  9.4 7.6 %collective-permute-start.6 = (bf16[3,256,128]{2,1,0:T(8,128)(2,1)}, bf16[3,256,128]{2,1,0:T(8,128)(2,1)S(1)}, u32[]{:S(2)}, u32[]{:S(2)}) collective-permute-start(bf16[3,256,128]{2,1,0:T(8,128)(2,1)} %bitcast.115), channel_id=1, source_target_pairs={{0,1},{1,0},{2,3},{3,2},{4,5},{5,4},{6,7},{7,6},{8,9},{9,8},{10,11... | collective-permute-start | bytes 589832 | tf_op jit(solution)/shard_map/ppermute | solution.py:372
  10.0 3.6 %copy-start.11 = (bf16[4,256,128]{2,1,0:T(8,128)(2,1)}, bf16[4,256,128]{2,1,0:T(8,128)(2,1)S(1)}, u32[]{:S(2)}) copy-start(bf16[4,256,128]{2,1,0:T(8,128)(2,1)S(1)} %collective-permute-done.x_recv) | copy-start | bytes 786436
  10.0 7.0 %collective-permute-start.7 = (bf16[128,256]{1,0:T(8,128)(2,1)}, bf16[128,256]{1,0:T(8,128)(2,1)S(1)}, u32[]{:S(2)}, u32[]{:S(2)}) collective-permute-start(bf16[128,256]{1,0:T(8,128)(2,1)} %ow_own.1), channel_id=1, source_target_pairs={{0,1},{1,0},{2,3},{3,2},{4,5},{5,4},{6,7},{7,6},{8,9},{9,8},{10,11... | collective-permute-start | bytes 196616 | tf_op jit(solution)/shard_map/ppermute | solution.py:372
  10.1 3.5 %copy-start.18 = (bf16[3,3,128,256]{3,2,1,0:T(8,128)(2,1)S(1)}, bf16[3,3,128,256]{3,2,1,0:T(8,128)(2,1)}, u32[]{:S(2)}) copy-start(bf16[3,3,128,256]{3,2,1,0:T(8,128)(2,1)} %param.24) | copy-start | bytes 1769476
  13.5 3.5 %copy-start.28 = (bf16[4,256,256]{2,1,0:T(8,128)(2,1)}, bf16[4,256,256]{2,1,0:T(8,128)(2,1)S(1)}, u32[]{:S(2)}) copy-start(bf16[4,256,256]{2,1,0:T(8,128)(2,1)S(1)} %get-tuple-element.49.act) | copy-start | bytes 1572868
  13.5 3.5 %copy-start.13 = (bf16[4,256,128]{2,1,0:T(8,128)(2,1)S(1)}, bf16[4,256,128]{2,1,0:T(8,128)(2,1)}, u32[]{:S(2)}) copy-start(bf16[4,256,128]{2,1,0:T(8,128)(2,1)} %get-tuple-element.89.g_own) | copy-start | bytes 786436
  13.5 3.5 %copy-start.24 = (bf16[256,3,128]{2,0,1:T(8,128)(2,1)S(1)}, bf16[256,3,128]{2,0,1:T(8,128)(2,1)}, u32[]{:S(2)}) copy-start(bf16[256,3,128]{2,0,1:T(8,128)(2,1)} %param.25) | copy-start | bytes 589828
  13.6 3.5 %copy-start.25 = (bf16[128,256]{1,0:T(8,128)(2,1)S(1)}, bf16[128,256]{1,0:T(8,128)(2,1)}, u32[]{:S(2)}) copy-start(bf16[128,256]{1,0:T(8,128)(2,1)} %ow_own.1) | copy-start | bytes 196612
  28.2 0.8 copy-start.3
  29.0 0.8 copy-start.19
  33.5 0.8 copy-start.26
  34.3 1.0 copy-start.27
  35.3 1.0 copy-start.29
  36.3 3.2 %copy-start.2 = (bf16[3,3,256,128]{3,2,1,0:T(8,128)(2,1)S(1)}, bf16[3,3,256,128]{3,2,1,0:T(8,128)(2,1)}, u32[]{:S(2)}) copy-start(bf16[3,3,256,128]{3,2,1,0:T(8,128)(2,1)} %param.20) | copy-start | bytes 1769476
  36.3 3.2 %copy-start.12 = (bf16[4,256,128]{2,1,0:T(8,128)(2,1)S(1)}, bf16[4,256,128]{2,1,0:T(8,128)(2,1)}, u32[]{:S(2)}) copy-start(bf16[4,256,128]{2,1,0:T(8,128)(2,1)} %copy-done.11) | copy-start | bytes 786436
  37.9 0.8 copy-start.5
  38.7 0.8 copy-start.20
  44.5 4.9 %copy-start.8 = (f32[4,256,128]{2,1,0:T(8,128)S(1)}, f32[4,256,128]{2,1,0:T(8,128)}, u32[]{:S(2)}) copy-start(f32[4,256,128]{2,1,0:T(8,128)} %copy-done.7) | copy-start | bytes 1572868
  44.6 1.6 %collective-permute-start.18 = (f32[24,128]{1,0:T(8,128)S(1)}, f32[24,128]{1,0:T(8,128)S(1)}, u32[]{:S(2)}, u32[]{:S(2)}) collective-permute-start(f32[24,128]{1,0:T(8,128)S(1)} %pad_maximum_fusion.1), channel_id=1, source_target_pairs={{0,1},{1,0},{2,3},{3,2},{4,5},{5,4},{6,7},{7,6},{8,9},{9,8},{10,11... | collective-permute-start | bytes 36872 | tf_op jit(solution)/shard_map/ppermute | solution.py:372
  45.2 2.2 %collective-permute-start.8 = (bf16[4,256,128]{2,1,0:T(8,128)(2,1)}, bf16[4,256,128]{2,1,0:T(8,128)(2,1)S(1)}, u32[]{:S(2)}, u32[]{:S(2)}) collective-permute-start(bf16[4,256,128]{2,1,0:T(8,128)(2,1)} %copy-done.22), channel_id=1, source_target_pairs={{0,1},{1,0},{2,3},{3,2},{4,5},{5,4},{6,7},{7,6},{8,9},{9,8},{10,11... | collective-permute-start | bytes 786440 | tf_op jit(solution)/shard_map/ppermute | solution.py:372
  45.3 2.0 %collective-permute-start.9 = (bf16[4,256,128]{2,1,0:T(8,128)(2,1)}, bf16[4,256,128]{2,1,0:T(8,128)(2,1)S(1)}, u32[]{:S(2)}, u32[]{:S(2)}) collective-permute-start(bf16[4,256,128]{2,1,0:T(8,128)(2,1)} %copy-done.23), channel_id=1, source_target_pairs={{0,1},{1,0},{2,3},{3,2},{4,5},{5,4},{6,7},{7,6},{8,9},{9,8},{10,11... | collective-permute-start | bytes 786440 | tf_op jit(solution)/shard_map/ppermute | solution.py:372
  45.8 4.7 %collective-permute-start.11 = (bf16[1024,128]{1,0:T(8,128)(2,1)}, bf16[1024,128]{1,0:T(8,128)(2,1)S(1)}, u32[]{:S(2)}, u32[]{:S(2)}) collective-permute-start(bf16[1024,128]{1,0:T(8,128)(2,1)} %copy-done.21), channel_id=1, source_target_pairs={{0,1},{1,0},{2,3},{3,2},{4,5},{5,4},{6,7},{7,6},{8,9},{9,8},{10,11... | collective-permute-start | bytes 786440 | tf_op jit(solution)/shard_map/ppermute | solution.py:372
  45.9 9.2 %collective-permute-start.10 = (bf16[2304,128]{1,0:T(8,128)(2,1)}, bf16[2304,128]{1,0:T(8,128)(2,1)S(1)}, u32[]{:S(2)}, u32[]{:S(2)}) collective-permute-start(bf16[2304,128]{1,0:T(8,128)(2,1)} %copy-done.19), channel_id=1, source_target_pairs={{0,1},{1,0},{2,3},{3,2},{4,5},{5,4},{6,7},{7,6},{8,9},{9,8},{10,11... | collective-permute-start | bytes 1769480 | tf_op jit(solution)/shard_map/ppermute | solution.py:372
  46.3 4.3 %collective-permute-start.25 = (bf16[2304,128]{1,0:T(8,128)(2,1)}, bf16[2304,128]{1,0:T(8,128)(2,1)S(1)}, u32[]{:S(2)}, u32[]{:S(2)}) collective-permute-start(bf16[2304,128]{1,0:T(8,128)(2,1)} %copy-done.20), channel_id=1, source_target_pairs={{0,1},{1,0},{2,3},{3,2},{4,5},{5,4},{6,7},{7,6},{8,9},{9,8},{10,11... | collective-permute-start | bytes 1769480 | tf_op jit(solution)/shard_map/ppermute | solution.py:372
  47.4 3.0 %copy-start.10 = (bf16[1024,128]{1,0:T(8,128)(2,1)S(1)}, bf16[1024,128]{1,0:T(8,128)(2,1)}, u32[]{:S(2)}) copy-start(bf16[1024,128]{1,0:T(8,128)(2,1)} %copy-done.9) | copy-start | bytes 786436
  49.4 1.2 copy-start.6
  50.4 4.6 %copy-start.4 = (bf16[2304,128]{1,0:T(8,128)(2,1)S(1)}, bf16[2304,128]{1,0:T(8,128)(2,1)}, u32[]{:S(2)}) copy-start(bf16[2304,128]{1,0:T(8,128)(2,1)} %copy-done.3) | copy-start | bytes 1769476
  50.8 10.1 %collective-permute-start.28 = (bf16[4,144,128]{2,1,0:T(8,128)(2,1)S(1)}, bf16[4,144,128]{2,1,0:T(8,128)(2,1)S(1)}, u32[]{:S(2)}, u32[]{:S(2)}) collective-permute-start(bf16[4,144,128]{2,1,0:T(8,128)(2,1)S(1)} %get-tuple-element.86), channel_id=1, source_target_pairs={{0,4},{2,6},{4,0},{6,2},{8,12},{10,14},{12,8},{14,10},{16,20},{18,... | collective-permute-start | bytes 442376 | tf_op jit(solution)/shard_map/ppermute | solution.py:368
  53.5 7.7 %collective-permute-start.27 = (bf16[4,144,128]{2,1,0:T(8,128)(2,1)S(1)}, bf16[4,144,128]{2,1,0:T(8,128)(2,1)S(1)}, u32[]{:S(2)}, u32[]{:S(2)}) collective-permute-start(bf16[4,144,128]{2,1,0:T(8,128)(2,1)S(1)} %get-tuple-element.87), channel_id=1, source_target_pairs={{0,6},{2,4},{4,2},{6,0},{8,14},{10,12},{12,10},{14,8},{16,22},{18,... | collective-permute-start | bytes 442376 | tf_op jit(solution)/shard_map/ppermute | solution.py:368
  55.0 7.4 %collective-permute-start.26 = (bf16[4,144,128]{2,1,0:T(8,128)(2,1)S(1)}, bf16[4,144,128]{2,1,0:T(8,128)(2,1)S(1)}, u32[]{:S(2)}, u32[]{:S(2)}) collective-permute-start(bf16[4,144,128]{2,1,0:T(8,128)(2,1)S(1)} %get-tuple-element.85), channel_id=1, source_target_pairs={{0,2},{2,0},{4,6},{6,4},{8,10},{10,8},{12,14},{14,12},{16,18},{18,... | collective-permute-start | bytes 442376 | tf_op jit(solution)/shard_map/ppermute | solution.py:368
  62.5 7.4 %collective-permute-start.31 = (bf16[144,128]{1,0:T(8,128)(2,1)S(1)}, bf16[144,128]{1,0:T(8,128)(2,1)S(1)}, u32[]{:S(2)}, u32[]{:S(2)}) collective-permute-start(bf16[144,128]{1,0:T(8,128)(2,1)S(1)} %get-tuple-element.96), channel_id=1, source_target_pairs={{0,16},{2,18},{4,20},{6,22},{8,24},{10,26},{12,28},{14,30},{16,0},... | collective-permute-start | bytes 110600 | tf_op jit(solution)/shard_map/ppermute | solution.py:368
  65.3 5.8 %collective-permute-start.30 = (bf16[144,128]{1,0:T(8,128)(2,1)S(1)}, bf16[144,128]{1,0:T(8,128)(2,1)S(1)}, u32[]{:S(2)}, u32[]{:S(2)}) collective-permute-start(bf16[144,128]{1,0:T(8,128)(2,1)S(1)} %get-tuple-element.97), channel_id=1, source_target_pairs={{0,24},{2,26},{4,28},{6,30},{8,16},{10,18},{12,20},{14,22},{16,8},... | collective-permute-start | bytes 110600 | tf_op jit(solution)/shard_map/ppermute | solution.py:368
  66.6 4.4 %collective-permute-start.29 = (bf16[144,128]{1,0:T(8,128)(2,1)S(1)}, bf16[144,128]{1,0:T(8,128)(2,1)S(1)}, u32[]{:S(2)}, u32[]{:S(2)}) collective-permute-start(bf16[144,128]{1,0:T(8,128)(2,1)S(1)} %get-tuple-element.95), channel_id=1, source_target_pairs={{0,8},{2,10},{4,12},{6,14},{8,0},{10,2},{12,4},{14,6},{16,24},{18,... | collective-permute-start | bytes 110600 | tf_op jit(solution)/shard_map/ppermute | solution.py:368
  66.9 10.5 %collective-permute-start.14 = (bf16[4,208,128]{2,1,0:T(8,128)(2,1)S(1)}, bf16[4,208,128]{2,1,0:T(8,128)(2,1)S(1)}, u32[]{:S(2)}, u32[]{:S(2)}) collective-permute-start(bf16[4,208,128]{2,1,0:T(8,128)(2,1)S(1)} %get-tuple-element.83), channel_id=1, source_target_pairs={{0,4},{2,6},{4,0},{6,2},{8,12},{10,14},{12,8},{14,10},{16,20},{18,... | collective-permute-start | bytes 638984 | tf_op jit(solution)/shard_map/ppermute | solution.py:368
  68.5 11.4 %collective-permute-start.13 = (bf16[4,208,128]{2,1,0:T(8,128)(2,1)S(1)}, bf16[4,208,128]{2,1,0:T(8,128)(2,1)S(1)}, u32[]{:S(2)}, u32[]{:S(2)}) collective-permute-start(bf16[4,208,128]{2,1,0:T(8,128)(2,1)S(1)} %get-tuple-element.84), channel_id=1, source_target_pairs={{0,6},{2,4},{4,2},{6,0},{8,14},{10,12},{12,10},{14,8},{16,22},{18,... | collective-permute-start | bytes 638984 | tf_op jit(solution)/shard_map/ppermute | solution.py:368
  69.9 10.0 %collective-permute-start.12 = (bf16[4,208,128]{2,1,0:T(8,128)(2,1)S(1)}, bf16[4,208,128]{2,1,0:T(8,128)(2,1)S(1)}, u32[]{:S(2)}, u32[]{:S(2)}) collective-permute-start(bf16[4,208,128]{2,1,0:T(8,128)(2,1)S(1)} %get-tuple-element.82), channel_id=1, source_target_pairs={{0,2},{2,0},{4,6},{6,4},{8,10},{10,8},{12,14},{14,12},{16,18},{18,... | collective-permute-start | bytes 638984 | tf_op jit(solution)/shard_map/ppermute | solution.py:368
  71.1 11.6 %collective-permute-start.32 = (bf16[144,128]{1,0:T(8,128)(2,1)S(1)}, bf16[144,128]{1,0:T(8,128)(2,1)S(1)}, u32[]{:S(2)}, u32[]{:S(2)}) collective-permute-start(bf16[144,128]{1,0:T(8,128)(2,1)S(1)} %get-tuple-element.81), channel_id=1, source_target_pairs={{0,8},{2,10},{4,12},{6,14},{8,0},{10,2},{12,4},{14,6},{16,24},{18,... | collective-permute-start | bytes 110600 | tf_op jit(solution)/shard_map/ppermute | solution.py:368
  72.4 11.2 %collective-permute-start.33 = (bf16[144,128]{1,0:T(8,128)(2,1)S(1)}, bf16[144,128]{1,0:T(8,128)(2,1)S(1)}, u32[]{:S(2)}, u32[]{:S(2)}) collective-permute-start(bf16[144,128]{1,0:T(8,128)(2,1)S(1)} %get-tuple-element.81), channel_id=1, source_target_pairs={{0,24},{2,26},{4,28},{6,30},{8,16},{10,18},{12,20},{14,22},{16,8},... | collective-permute-start | bytes 110600 | tf_op jit(solution)/shard_map/ppermute | solution.py:368
  77.4 6.3 %collective-permute-start.34 = (bf16[144,128]{1,0:T(8,128)(2,1)S(1)}, bf16[144,128]{1,0:T(8,128)(2,1)S(1)}, u32[]{:S(2)}, u32[]{:S(2)}) collective-permute-start(bf16[144,128]{1,0:T(8,128)(2,1)S(1)} %get-tuple-element.81), channel_id=1, source_target_pairs={{0,16},{2,18},{4,20},{6,22},{8,24},{10,26},{12,28},{14,30},{16,0},... | collective-permute-start | bytes 110600 | tf_op jit(solution)/shard_map/ppermute | solution.py:368
  80.1 8.5 %collective-permute-start.17 = (bf16[208,128]{1,0:T(8,128)(2,1)S(1)}, bf16[208,128]{1,0:T(8,128)(2,1)S(1)}, u32[]{:S(2)}, u32[]{:S(2)}) collective-permute-start(bf16[208,128]{1,0:T(8,128)(2,1)S(1)} %get-tuple-element.93), channel_id=1, source_target_pairs={{0,16},{2,18},{4,20},{6,22},{8,24},{10,26},{12,28},{14,30},{16,0},... | collective-permute-start | bytes 159752 | tf_op jit(solution)/shard_map/ppermute | solution.py:368
  81.4 7.5 %collective-permute-start.16 = (bf16[208,128]{1,0:T(8,128)(2,1)S(1)}, bf16[208,128]{1,0:T(8,128)(2,1)S(1)}, u32[]{:S(2)}, u32[]{:S(2)}) collective-permute-start(bf16[208,128]{1,0:T(8,128)(2,1)S(1)} %get-tuple-element.94), channel_id=1, source_target_pairs={{0,24},{2,26},{4,28},{6,30},{8,16},{10,18},{12,20},{14,22},{16,8},... | collective-permute-start | bytes 159752 | tf_op jit(solution)/shard_map/ppermute | solution.py:368
  82.7 6.1 %collective-permute-start.15 = (bf16[208,128]{1,0:T(8,128)(2,1)S(1)}, bf16[208,128]{1,0:T(8,128)(2,1)S(1)}, u32[]{:S(2)}, u32[]{:S(2)}) collective-permute-start(bf16[208,128]{1,0:T(8,128)(2,1)S(1)} %get-tuple-element.92), channel_id=1, source_target_pairs={{0,8},{2,10},{4,12},{6,14},{8,0},{10,2},{12,4},{14,6},{16,24},{18,... | collective-permute-start | bytes 159752 | tf_op jit(solution)/shard_map/ppermute | solution.py:368
  83.7 18.2 %collective-permute-start.35 = (bf16[4,144,128]{2,1,0:T(8,128)(2,1)S(1)}, bf16[4,144,128]{2,1,0:T(8,128)(2,1)}, u32[]{:S(2)}, u32[]{:S(2)}) collective-permute-start(bf16[4,144,128]{2,1,0:T(8,128)(2,1)S(1)} %bitcast_dynamic-update-slice_fusion.12), channel_id=1, source_target_pairs={{0,2},{2,0},{4,6},{6,4},{8,10},{10,8},{12,14},{14,12},{16,18},{18,... | collective-permute-start | bytes 442376 | tf_op jit(solution)/shard_map/ppermute | solution.py:368
  84.7 19.4 %collective-permute-start.36 = (bf16[4,144,128]{2,1,0:T(8,128)(2,1)S(1)}, bf16[4,144,128]{2,1,0:T(8,128)(2,1)}, u32[]{:S(2)}, u32[]{:S(2)}) collective-permute-start(bf16[4,144,128]{2,1,0:T(8,128)(2,1)S(1)} %bitcast_dynamic-update-slice_fusion.12), channel_id=1, source_target_pairs={{0,6},{2,4},{4,2},{6,0},{8,14},{10,12},{12,10},{14,8},{16,22},{18,... | collective-permute-start | bytes 442376 | tf_op jit(solution)/shard_map/ppermute | solution.py:368
  88.6 17.1 %collective-permute-start.37 = (bf16[4,144,128]{2,1,0:T(8,128)(2,1)S(1)}, bf16[4,144,128]{2,1,0:T(8,128)(2,1)}, u32[]{:S(2)}, u32[]{:S(2)}) collective-permute-start(bf16[4,144,128]{2,1,0:T(8,128)(2,1)S(1)} %bitcast_dynamic-update-slice_fusion.12), channel_id=1, source_target_pairs={{0,4},{2,6},{4,0},{6,2},{8,12},{10,14},{12,8},{14,10},{16,20},{18,... | collective-permute-start | bytes 442376 | tf_op jit(solution)/shard_map/ppermute | solution.py:368
  88.9 4.3 %collective-permute-start.19 = (bf16[240,128]{1,0:T(8,128)(2,1)S(1)}, bf16[240,128]{1,0:T(8,128)(2,1)S(1)}, u32[]{:S(2)}, u32[]{:S(2)}) collective-permute-start(bf16[240,128]{1,0:T(8,128)(2,1)S(1)} %concatenate.72), channel_id=1, source_target_pairs={{0,8},{2,10},{4,12},{6,14},{8,0},{10,2},{12,4},{14,6},{16,24},{18,... | collective-permute-start | bytes 184328 | tf_op jit(solution)/shard_map/ppermute | solution.py:368
  90.1 6.0 %collective-permute-start.20 = (bf16[240,128]{1,0:T(8,128)(2,1)S(1)}, bf16[240,128]{1,0:T(8,128)(2,1)S(1)}, u32[]{:S(2)}, u32[]{:S(2)}) collective-permute-start(bf16[240,128]{1,0:T(8,128)(2,1)S(1)} %concatenate.72), channel_id=1, source_target_pairs={{0,24},{2,26},{4,28},{6,30},{8,16},{10,18},{12,20},{14,22},{16,8},... | collective-permute-start | bytes 184328 | tf_op jit(solution)/shard_map/ppermute | solution.py:368
  93.2 5.1 %collective-permute-start.21 = (bf16[240,128]{1,0:T(8,128)(2,1)S(1)}, bf16[240,128]{1,0:T(8,128)(2,1)S(1)}, u32[]{:S(2)}, u32[]{:S(2)}) collective-permute-start(bf16[240,128]{1,0:T(8,128)(2,1)S(1)} %concatenate.72), channel_id=1, source_target_pairs={{0,16},{2,18},{4,20},{6,22},{8,24},{10,26},{12,28},{14,30},{16,0},... | collective-permute-start | bytes 184328 | tf_op jit(solution)/shard_map/ppermute | solution.py:368
  98.3 11.1 %collective-permute-start.22 = (bf16[4,240,128]{2,1,0:T(8,128)(2,1)S(1)}, bf16[4,240,128]{2,1,0:T(8,128)(2,1)S(1)}, u32[]{:S(2)}, u32[]{:S(2)}) collective-permute-start(bf16[4,240,128]{2,1,0:T(8,128)(2,1)S(1)} %bitcast_dynamic-update-slice_fusion.8), channel_id=1, source_target_pairs={{0,2},{2,0},{4,6},{6,4},{8,10},{10,8},{12,14},{14,12},{16,18},{18,... | collective-permute-start | bytes 737288 | tf_op jit(solution)/shard_map/ppermute | solution.py:368
  100.7 8.8 %collective-permute-start.23 = (bf16[4,240,128]{2,1,0:T(8,128)(2,1)S(1)}, bf16[4,240,128]{2,1,0:T(8,128)(2,1)S(1)}, u32[]{:S(2)}, u32[]{:S(2)}) collective-permute-start(bf16[4,240,128]{2,1,0:T(8,128)(2,1)S(1)} %bitcast_dynamic-update-slice_fusion.8), channel_id=1, source_target_pairs={{0,6},{2,4},{4,2},{6,0},{8,14},{10,12},{12,10},{14,8},{16,22},{18,... | collective-permute-start | bytes 737288 | tf_op jit(solution)/shard_map/ppermute | solution.py:368
  101.9 8.9 %collective-permute-start.24 = (bf16[4,240,128]{2,1,0:T(8,128)(2,1)S(1)}, bf16[4,240,128]{2,1,0:T(8,128)(2,1)S(1)}, u32[]{:S(2)}, u32[]{:S(2)}) collective-permute-start(bf16[4,240,128]{2,1,0:T(8,128)(2,1)S(1)} %bitcast_dynamic-update-slice_fusion.8), channel_id=1, source_target_pairs={{0,4},{2,6},{4,0},{6,2},{8,12},{10,14},{12,8},{14,10},{16,20},{18,... | collective-permute-start | bytes 737288 | tf_op jit(solution)/shard_map/ppermute | solution.py:368
  112.7 2.0 %copy-start.30 = (f32[3328,128]{1,0:T(8,128)}, f32[3328,128]{1,0:T(8,128)S(1)}, u32[]{:S(2)}) copy-start(f32[3328,128]{1,0:T(8,128)S(1)} %bitcast_convert_fusion) | copy-start | bytes 5111812
  119.7 3.1 %slice-start = ((f32[3328,128]{1,0:T(8,128)}), f32[256,128]{1,0:T(8,128)S(1)}, s32[]{:S(2)}) async-start(f32[3328,128]{1,0:T(8,128)} %copy-done.30), calls=%async_computation | async-start | bytes 262144 | tf_op jit(solution)/shard_map/slice | solution.py:575
  119.7 4.1 %copy-start.17 = (bf16[512,128]{1,0:T(8,128)(2,1)S(1)}, bf16[512,128]{1,0:T(8,128)(2,1)}, u32[]{:S(2)}) copy-start(bf16[512,128]{1,0:T(8,128)(2,1)} %copy-done.16) | copy-start | bytes 393220
  (6 other events, 4.3 us)

commit v2 on v1

v2 whole, which is shorter than its diff:
```python
import jax
import jax.numpy as jnp
from jax import lax
from jax.experimental import pallas as pl
from jax.experimental.pallas import tpu as pltpu
from jax.sharding import PartitionSpec as P

C = 256
HALF = 128
SIDE = 16
PIX = 256
GROUP = 8
EPS = 1e-06
F32 = jnp.float32
BF16 = jnp.bfloat16
WHOLE = pl.BlockSpec(memory_space=pltpu.VMEM)
SCALAR = pl.BlockSpec(memory_space=pltpu.SMEM)
ANYWHERE = pl.BlockSpec(memory_space=pl.ANY)
IN_HBM = pl.BlockSpec(memory_space=pltpu.HBM)


def call(body, outs, *args, scratch=(), specs=None, limit=16, flops=1):
    specs = specs or {}
    return pl.pallas_call(
        body,
        out_shape=tuple(jax.ShapeDtypeStruct(s, d) for s, d in outs),
        in_specs=[specs.get(i, WHOLE) for i in range(len(args))],
        out_specs=tuple(WHOLE for _ in outs),
        scratch_shapes=list(scratch),
        compiler_params=pltpu.CompilerParams(vmem_limit_bytes=limit << 20),
        cost_estimate=pl.CostEstimate(flops=flops, bytes_accessed=0, transcendentals=0),
    )(*args)


def dot(a, b):
    return jnp.dot(a, b, preferred_element_type=F32)


def dot_bt(a, b):
    return lax.dot_general(a, b, (((1,), (1,)), ((), ())), preferred_element_type=F32)


def dot_at(a, b):
    return lax.dot_general(a, b, (((0,), (0,)), ((), ())), preferred_element_type=F32)


def join(first, own, recv, axis):
    low = jnp.where(first, own, recv)
    high = jnp.where(first, recv, own)
    return jnp.concatenate([low, high], axis=axis)


def split(first, values, axis=1):
    low, high = jnp.split(values, 2, axis)
    return jnp.where(first, low, high), jnp.where(first, high, low)


def group_merge(mean, square, count):
    lane = lax.broadcasted_iota(jnp.int32, mean.shape, 1)
    width = mean.shape[1]

    def partner(rows, step):
        up = pltpu.roll(rows, width - step, 1)
        down = pltpu.roll(rows, step, 1)
        return jnp.where((lane & step) == 0, up, down)

    for step in (1, 2, 4):
        other = partner(mean, step)
        gap = mean - other
        square = square + partner(square, step) + gap * gap * (0.5 * count * step)
        mean = 0.5 * (mean + other)
    return mean, square


def group_sum(rows):
    lane = lax.broadcasted_iota(jnp.int32, rows.shape, 1)
    width = rows.shape[1]
    for step in (1, 2, 4):
        up = pltpu.roll(rows, width - step, 1)
        down = pltpu.roll(rows, step, 1)
        rows = rows + jnp.where((lane & step) == 0, up, down)
    return rows


def col_sum(values):
    return jnp.sum(values, axis=0, keepdims=True)


def norm_stats(values):
    mean = col_sum(values) * (1.0 / PIX)
    square = col_sum((values - mean) ** 2)
    mean, square = group_merge(mean, square, PIX)
    return mean, lax.rsqrt(square * (1.0 / (PIX * GROUP)) + EPS)


def all_stats(maps):
    means = [col_sum(v) * (1.0 / PIX) for v in maps]
    squares = [col_sum((v - mean) ** 2) for v, mean in zip(maps, means)]
    mean, square = group_merge(jnp.concatenate(means, axis=0), jnp.concatenate(squares, axis=0), PIX)
    return mean, lax.rsqrt(square * (1.0 / (PIX * GROUP)) + EPS)


def norm_back(grad, unit, gain, rstd):
    plain = col_sum(grad)
    scaled = col_sum(grad * unit)
    both = group_sum(jnp.concatenate([plain * gain, scaled * gain], axis=0)) * (1.0 / (PIX * GROUP))
    inner = grad * gain - both[0:1] - unit * both[1:2]
    return inner * rstd, scaled, plain


def sigmoid(v):
    return 1.0 / (1.0 + jnp.exp(-v))


def put_windows(win, values):
    col = lax.broadcasted_iota(jnp.int32, (PIX, 1), 0) & (SIDE - 1)
    before = jnp.where(col == 0, 0.0, pltpu.roll(values, 1, 0))
    after = jnp.where(col == SIDE - 1, 0.0, pltpu.roll(values, PIX - 1, 0))
    blank = jnp.zeros((SIDE, C), BF16)
    for c, shifted in enumerate((before, values, after)):
        win[c, 0:SIDE, :] = blank
        win[c, SIDE + PIX : 2 * SIDE + PIX, :] = blank
        win[c, SIDE : SIDE + PIX, :] = shifted.astype(BF16)


def window(win, r, c):
    return win[c, SIDE * r : SIDE * r + PIX, :]


def conv_forward(win, w_ref):
    total = None
    for r in range(3):
        for c in range(3):
            part = dot(window(win, r, c), w_ref[3 * r + c])
            total = part if total is None else total + part
    return total


def conv_transposed(win, w_ref):
    total = None
    for r in range(3):
        for c in range(3):
            part = dot_bt(window(win, 2 - r, 2 - c), w_ref[3 * r + c])
            total = part if total is None else total + part
    return total


WIN = ((3, PIX + 2 * SIDE, C), BF16)

GAIN, BIAS, CONV_B, QKV_B, OUT_B, TIME_B, PACK = 0, 3, 6, 8, 10, 11, 16


def blank_kernel(result):
    result[...] = jnp.zeros_like(result)


def time_kernel(steps, pk, table, tw, result):
    total = result.shape[0] - PACK
    result[0:PACK] = pk[...]
    rows = jnp.concatenate([table[pl.ds(steps[i], 1)] for i in range(total)], axis=0)
    e = rows * sigmoid(rows)
    e_high = e.astype(BF16)
    e_low = (e - e_high.astype(F32)).astype(BF16)
    shift = pk[TIME_B : TIME_B + 1] + pk[CONV_B : CONV_B + 1]
    result[PACK : PACK + total] = dot(e_high, tw[...]) + dot(e_low, tw[...]) + shift


def first_kernel(x_own, x_recv, w_own, w_recv, pk_own, pk_recv, *rest):
    n = x_own.shape[0] // 2
    hid, act_t, act2_t, stat0, stat1, prm_out, wfull = rest[:7]
    win2, wins = rest[7 : 7 + n], rest[7 + n :]
    me = lax.axis_index("mp")
    first = me == 0
    pk = join(first, pk_own[0:PACK], pk_recv[0:PACK], 1)
    prm_out[...] = pk
    xs = [join(first, x_own[me * n + m], x_recv[me * n + m], 1).astype(F32) for m in range(n)]
    mean, rstd = all_stats(xs)
    stat0[0:n] = mean
    stat0[n : 2 * n] = rstd
    scale = rstd * pk[GAIN : GAIN + 1]
    shift = pk[BIAS : BIAS + 1] - mean * scale
    for m in range(n):
        u = xs[m] * scale[m : m + 1] + shift[m : m + 1]
        a = u * sigmoid(u)
        act_t[:, m * PIX : (m + 1) * PIX] = a.astype(BF16).T
        put_windows(wins[m], a)
    for t in range(9):
        wfull[t] = join(first, w_own[t], w_recv[t], 1)
    both = join(first, pk_own[PACK:], pk_recv[PACK:], 1)
    time_row = jnp.where(first, both[0:n], both[n : 2 * n])
    for m in range(n):
        h = conv_forward(wins[m], wfull) + time_row[m : m + 1]
        hid[m] = h
        mean, rstd = norm_stats(h)
        stat1[m : m + 1] = mean
        stat1[n + m : n + m + 1] = rstd
        u = (h - mean) * (rstd * pk[GAIN + 1 : GAIN + 2]) + pk[BIAS + 1 : BIAS + 2]
        a = u * sigmoid(u)
        act2_t[:, m * PIX : (m + 1) * PIX] = a.astype(BF16).T
        put_windows(win2[m], a)


def middle_kernel(x_own, x_recv, w_own, w_recv, prm, g_own, g_recv, qw_own, qw_recv, ow_own, ow_recv, *rest):
    n = g_own.shape[0] // 2
    win2, rest = rest[:n], rest[n:]
    out_keep, out_send, dmid, wg_keep, wg_send, sums, wfull = rest[:7]
    win3, rest = rest[7 : 7 + n], rest[7 + n :]
    qw, ow, rest = rest[0], rest[1], rest[2:]
    mids, units, probs = rest[:n], rest[n : 2 * n], rest[2 * n : 3 * n]
    thirds, qkvs, lows, douts, atts, grads = [rest[(3 + i) * n : (4 + i) * n] for i in range(6)]
    me = lax.axis_index("mp")
    first = me == 0
    scale = 1.0 / 16.0
    for t in range(9):
        wfull[t] = join(first, w_own[t], w_recv[t], 0)
    for j in range(3):
        qw[j] = join(first, qw_own[j], qw_recv[j], 1)
    ow[...] = join(first, ow_own[...], ow_recv[...], 0)
    rstds = []
    for m in range(n):
        at = me * n + m
        x = join(first, x_own[at], x_recv[at], 1).astype(F32)
        mid = x + conv_forward(win2[m], wfull) + prm[CONV_B + 1 : CONV_B + 2]
        mids[m][...] = mid
        mean, rstd = norm_stats(mid)
        rstds.append(rstd)
        unit = (mid - mean) * rstd
        units[m][...] = unit
        thirds[m][...] = (unit * prm[GAIN + 2 : GAIN + 3] + prm[BIAS + 2 : BIAS + 3]).astype(BF16)
    for m in range(n):
        a3 = thirds[m][...]
        qkvs[m][0] = (dot(a3, qw[0]) + prm[QKV_B : QKV_B + 1]).astype(BF16)
        qkvs[m][1] = dot(a3, qw[1]).astype(BF16)
        qkvs[m][2] = (dot(a3, qw[2]) + prm[QKV_B + 1 : QKV_B + 2]).astype(BF16)
    for m in range(n):
        s = dot_bt(qkvs[m][0], qkvs[m][1]) * scale
        e = jnp.exp(s - jnp.max(s, axis=1, keepdims=True))
        p = e * (1.0 / jnp.sum(e, axis=1, keepdims=True))
        probs[m][...] = p
        lows[m][...] = p.astype(BF16)
    for m in range(n):
        gb = join(first, g_own[me * n + m], g_recv[me * n + m], 1)
        douts[m][...] = dot_bt(gb, ow[...]).astype(BF16)
    for m in range(n):
        a = dot(lows[m][...], qkvs[m][2]).astype(BF16)
        atts[m][...] = a
        result = mids[m][...] + dot(a, ow[...]) + prm[OUT_B : OUT_B + 1]
        keep, send = split(first, result.astype(BF16))
        out_keep[m] = keep
        out_send[m] = send
    for m in range(n):
        p = probs[m][...]
        dp = dot_bt(douts[m][...], qkvs[m][2])
        ds = (p * (dp - jnp.sum(p * dp, axis=1, keepdims=True))).astype(BF16)
        grads[m][2] = dot_at(lows[m][...], douts[m][...]).astype(BF16)
        lows[m][...] = ds
    for m in range(n):
        ds = lows[m][...]
        grads[m][0] = (dot(ds, qkvs[m][1]) * scale).astype(BF16)
        grads[m][1] = (dot_at(ds, qkvs[m][0]) * scale).astype(BF16)
    gains, biases, mid_bias, out_bias = [], [], [], []
    for m in range(n):
        grad = dot_bt(grads[m][0], qw[0]) + dot_bt(grads[m][1], qw[1]) + dot_bt(grads[m][2], qw[2])
        back, gain_grad, bias_grad = norm_back(grad, units[m][...], prm[GAIN + 2 : GAIN + 3], rstds[m])
        gains.append(gain_grad)
        biases.append(bias_grad)
        g = join(first, g_own[me * n + m], g_recv[me * n + m], 1).astype(F32)
        out_bias.append(col_sum(g))
        d = back + g
        dmid[m] = d
        mid_bias.append(col_sum(d))
        put_windows(win3[m], d)
    third_t = jnp.concatenate([thirds[m][...].T for m in range(n)], axis=1)
    for j in range(3):
        d = jnp.concatenate([grads[m][j] for m in range(n)], axis=0)
        keep, send = split(first, dot(third_t, d).astype(BF16))
        wg_keep[j * C : (j + 1) * C] = keep
        wg_send[j * C : (j + 1) * C] = send
    att_t = jnp.concatenate([atts[m][...].T for m in range(n)], axis=1)
    g_all = jnp.concatenate([join(first, g_own[me * n + m], g_recv[me * n + m], 1) for m in range(n)], axis=0)
    keep, send = split(first, dot(att_t, g_all).astype(BF16), 0)
    for h in range(2):
        lanes, rows = slice(h * HALF, (h + 1) * HALF), slice(3 * C + h * HALF, 3 * C + (h + 1) * HALF)
        wg_keep[rows] = keep[:, lanes]
        wg_send[rows] = send[:, lanes]
    sums[0:1] = sum(gains)
    sums[1:2] = sum(biases)
    sums[2:3] = sum(mid_bias)
    sums[3:4] = sum(col_sum(grads[m][0].astype(F32)) for m in range(n))
    sums[4:5] = sum(col_sum(grads[m][2].astype(F32)) for m in range(n))
    sums[5:6] = sum(out_bias)
    sums[6:8] = jnp.zeros((2, C), F32)


TAPS = (range(0, 5), range(5, 9))


def conv2_grad_kernel(taps):
    def body(act_t, *rest):
        win, (keep, send) = rest[:-2], rest[-2:]
        first = lax.axis_index("mp") == 0
        for i, t in enumerate(taps):
            shifted = jnp.concatenate([window(w, 2 - t // 3, 2 - t % 3) for w in win], axis=0)
            g_keep, g_send = split(first, dot(act_t[...], shifted).astype(BF16), 0)
            for h in range(2):
                lanes = slice(h * HALF, (h + 1) * HALF)
                rows = slice((2 * i + h) * HALF, (2 * i + h + 1) * HALF)
                keep[rows] = g_keep[:, lanes]
                send[rows] = g_send[:, lanes]

    return body


def hidden_back_kernel(steps, after, hid, stat, wfull, prm, sums3, *rest):
    n = hid.shape[0]
    win3, (rows_keep, rows_send), win4 = rest[:n], rest[n : n + 2], rest[n + 2 :]
    first = lax.axis_index("mp") == 0
    gain, bias = prm[GAIN + 1 : GAIN + 2], prm[BIAS + 1 : BIAS + 2]
    gains, biases, times = [], [], []
    for m in range(n):
        rstd = stat[n + m : n + m + 1]
        unit = (hid[m] - stat[m : m + 1]) * rstd
        u = unit * gain + bias
        sig = sigmoid(u)
        slope = sig * (1.0 + u * (1.0 - sig))
        grad = conv_transposed(win3[m], wfull) * slope
        back, gain_grad, bias_grad = norm_back(grad, unit, gain, rstd)
        gains.append(gain_grad)
        biases.append(bias_grad)
        low = back.astype(BF16).astype(F32)
        times.append(col_sum(low))
        put_windows(win4[m], low)
    small = [
        sum(gains), sums3[0:1], sum(biases), sums3[1:2], sum(times), sums3[2:6], jnp.zeros((7, C), F32),
    ]
    small_keep, small_send = split(first, jnp.concatenate(small, axis=0))
    rows_keep[0:16] = small_keep
    rows_send[0:16] = small_send
    time_rows = jnp.concatenate(times, axis=0)
    blank = jnp.zeros((n, HALF), F32)
    for ref in (rows_keep, rows_send):
        ref[16:32] = jnp.concatenate([time_rows[:, :HALF], blank, time_rows[:, HALF:], blank], axis=0)
    for i in range(2 * n):
        rows_keep[32 + i : 33 + i] = jnp.full((1, HALF), steps[i] >> 5, jnp.int32).astype(F32)
        rows_keep[40 + i : 41 + i] = jnp.full((1, HALF), steps[i] & 31, jnp.int32).astype(F32)


def conv1_grad_kernel(taps):
    def body(act_t, *rest):
        win, (keep, send) = rest[:-2], rest[-2:]
        first = lax.axis_index("mp") == 0
        for i, t in enumerate(taps):
            shifted = jnp.concatenate([window(w, 2 - t // 3, 2 - t % 3) for w in win], axis=0)
            g_keep, g_send = split(first, dot(act_t[...], shifted).astype(BF16))
            keep[i * C : (i + 1) * C] = g_keep
            send[i * C : (i + 1) * C] = g_send

    return body


def input_back_kernel(after, x_own, x_recv, stat, wfull, prm, dmid, *rest):
    n = dmid.shape[0]
    win4, (keep, send, rows_keep, rows_send) = rest[:n], rest[n:]
    me = lax.axis_index("mp")
    first = me == 0
    gain, bias = prm[GAIN : GAIN + 1], prm[BIAS : BIAS + 1]
    gains, biases = [], []
    for m in range(n):
        at = me * n + m
        rstd = stat[n + m : n + m + 1]
        x = join(first, x_own[at], x_recv[at], 1).astype(F32)
        unit = (x - stat[m : m + 1]) * rstd
        u = unit * gain + bias
        sig = sigmoid(u)
        slope = sig * (1.0 + u * (1.0 - sig))
        grad = conv_transposed(win4[m], wfull) * slope
        back, gain_grad, bias_grad = norm_back(grad, unit, gain, rstd)
        gains.append(gain_grad)
        biases.append(bias_grad)
        d_keep, d_send = split(first, back + dmid[m])
        keep[m] = d_keep
        send[m] = d_send.astype(BF16)
    small = jnp.concatenate([sum(gains), sum(biases), jnp.zeros((14, C), F32)], axis=0)
    rows_keep[...], rows_send[...] = split(first, small)


def maps_kernel(after, out_keep, out_recv, grad_keep, grad_recv, out, grad, turn):
    n = out_keep.shape[0]
    me = lax.axis_index("mp")
    for m in range(n):
        out[me * n + m] = out_keep[m]
        out[(1 - me) * n + m] = out_recv[m]
        grad[me * n + m] = grad_keep[m]
        grad[(1 - me) * n + m] = grad_recv[m].astype(F32)
    turn[...] = jnp.zeros_like(turn)


EXTRA = 48


def bits_of(count):
    bits = list(range(count.bit_length() - 1))
    cut = len(bits) // 2
    return [(bits[:cut], bits[cut:]), (bits[:cut][::-1], bits[cut:][::-1])]


def piece_of(rows, pieces):
    return -(-rows // (16 * pieces)) * 16


def digit(bits):
    first = lax.axis_index("mp") == 0
    return (lax.axis_index("dp") >> jnp.where(first, bits[0], bits[1])) & 1


def swap_dp(values, bits):
    pairs = []
    for i in range(lax.axis_size("dp")):
        for core in range(2):
            pairs.append((2 * i + core, 2 * (i ^ (1 << bits[core])) + core))
    return lax.ppermute(values, ("dp", "mp"), pairs)


def swap_mp(values):
    return lax.ppermute(values, "mp", [(0, 1), (1, 0)])


def part(index, rows):
    return pl.ds(pl.multiple_of(index * rows, 16), rows)


def start_scatter(pairs, rows, bits, after=()):
    def body(*refs):
        sources, (own, send, values) = refs[: 2 * len(pairs)], refs[-3:]
        at = 0
        for i in range(len(pairs)):
            keep, recv = sources[2 * i], sources[2 * i + 1]
            size = keep.shape[0]
            values[at : at + size] = (keep[...].astype(F32) + recv[...].astype(F32)).astype(BF16)
            at += size
        if at < rows:
            values[at:rows] = jnp.zeros((rows - at, HALF), BF16)
        me = digit(bits)
        own[...] = values[part(me, rows // 2)]
        send[...] = values[part(1 - me, rows // 2)]

    shape = ((rows // 2, HALF), BF16)
    args = [v for pair in pairs for v in pair]
    specs = {len(args) + i: ANYWHERE for i in range(len(after))}
    return call(body, [shape] * 2, *args, *after, scratch=[pltpu.VMEM((rows, HALF), BF16)], specs=specs)


def next_scatter(own, recv, bits, after):
    rows = own.shape[0]

    def body(own_ref, recv_ref, after_ref, out, send, values):
        values[...] = (own_ref[...].astype(F32) + recv_ref[...].astype(F32)).astype(BF16)
        me = digit(bits)
        out[...] = values[part(me, rows // 2)]
        send[...] = values[part(1 - me, rows // 2)]

    shape = ((rows // 2, HALF), BF16)
    scratch = [pltpu.VMEM((rows, HALF), BF16)]
    return call(body, [shape] * 2, own, recv, after, scratch=scratch, specs={2: ANYWHERE})


def end_scatter(own, recv, keep, other, after):
    rows, extra = own.shape[0], keep.shape[0]

    def body(own_ref, recv_ref, keep_ref, other_ref, after_ref, out):
        out[0:rows] = (own_ref[...].astype(F32) + recv_ref[...].astype(F32)).astype(BF16)
        out[rows : rows + 16] = (keep_ref[0:16] + other_ref[0:16]).astype(BF16)
        if extra > 16:
            first = lax.axis_index("mp") == 0
            sides = [join(first, keep_ref[at : at + 4], other_ref[at : at + 4], 0) for at in (16, 24)]
            out[rows + 16 : rows + 32] = jnp.concatenate(sides, axis=0).astype(BF16)
            out[rows + 32 : rows + 48] = keep_ref[32:48].astype(BF16)

    return call(body, [((rows + extra, HALF), BF16)], own, recv, keep, other, after, specs={4: ANYWHERE})[0]


def sum_blocks(own, recv, rows, bits, after):
    rest = own.shape[0] - rows

    def body(own_ref, recv_ref, after_ref, out):
        out[0:rows] = (own_ref[0:rows].astype(F32) + recv_ref[0:rows].astype(F32)).astype(BF16)
        if rest:
            low = digit(bits) == 0
            mine, theirs = own_ref[rows:], recv_ref[rows:]
            out[rows : rows + rest] = jnp.where(low, mine, theirs)
            out[rows + rest :] = jnp.where(low, theirs, mine)

    return call(body, [((rows + 2 * rest, HALF), BF16)], own, recv, after, specs={2: ANYWHERE})[0]


def next_gather(own, recv, bits, after):
    rows = own.shape[0]

    def body(own_ref, recv_ref, after_ref, out):
        me = digit(bits)
        out[part(me, rows)] = own_ref[...]
        out[part(1 - me, rows)] = recv_ref[...]

    return call(body, [((2 * rows, HALF), BF16)], own, recv, after, specs={2: ANYWHERE})[0]


def owner(halving, whole, order, p, q):
    cut, total = len(halving[order]), 0
    for i, bit in enumerate(halving[order]):
        total |= (p >> (cut - 1 - i) & 1) << bit
    for i, bit in enumerate(whole[order]):
        total |= (q >> i & 1) << bit
    return total


def late_result(gains, biases, own, recv, bits, halving, whole, piece):
    pieces, blocks, extra_rows = 1 << len(halving[0]), 1 << len(whole[0]), 16
    full = piece + extra_rows * blocks

    def body(gains_ref, biases_ref, own_ref, recv_ref, out, gains, biases, values, extra):
        me = digit(bits)
        values[part(me, own.shape[0])] = own_ref[...]
        values[part(1 - me, own.shape[0])] = recv_ref[...]
        first = lax.axis_index("mp") == 0
        for p in range(pieces):
            rows = min(piece, 9 * C - p * piece)
            if rows > 0:
                out[p * piece : p * piece + rows] = values[p * full : p * full + rows].astype(F32)
            for q in range(blocks):
                base = p * full + piece + q * extra_rows
                at = jnp.where(first, owner(halving, whole, 0, p, q), owner(halving, whole, 1, p, q))
                extra[at] = values[base : base + extra_rows].astype(F32)
        small = extra[0]
        for i in range(1, pieces * blocks):
            small = small + extra[i]
        gains[0:1] = small[0:1]
        gains[1:3] = gains_ref[...]
        biases[0:1] = small[1:2]
        biases[1:3] = biases_ref[...]

    scratch = [pltpu.VMEM((2 * own.shape[0], HALF), BF16), pltpu.VMEM((pieces * blocks, extra_rows, HALF), F32)]
    outs = [((9 * C, HALF), F32), ((3, HALF), F32), ((3, HALF), F32)]
    return call(body, outs, gains, biases, own, recv, scratch=scratch)


def early_result(own, recv, bits, halving, whole, piece, table, tw_own, tw_recv, after):
    steps, width = table.shape
    padded = -(-steps // HALF) * HALF
    pieces, blocks = 1 << len(halving[0]), 1 << len(whole[0])
    full = piece + EXTRA * blocks

    def body(own_ref, recv_ref, table_ref, tw_own_ref, tw_recv_ref, after_ref, *refs):
        conv2, qkv, out_w, table_grad, tw_grad, gains, biases, conv_b, qkv_b, out_b, time_b = refs[:11]
        values, extra, act_high, act_low = refs[11:]
        me = digit(bits)
        values[part(me, own.shape[0])] = own_ref[...]
        values[part(1 - me, own.shape[0])] = recv_ref[...]
        first = lax.axis_index("mp") == 0

        def rows_of(start, size):
            found = []
            while size:
                at, left = start % piece, piece - start % piece
                now = min(size, left)
                base = start // piece * full + at
                found.append(values[base : base + now].astype(F32))
                start, size = start + now, size - now
            return jnp.concatenate(found, axis=0)

        for t in range(9):
            for h in range(2):
                conv2[t, :, h * HALF : (h + 1) * HALF] = rows_of((2 * t + h) * HALF, HALF)
        for j in range(3):
            qkv[j] = rows_of((9 + j) * C, C)
        for h in range(2):
            out_w[:, h * HALF : (h + 1) * HALF] = rows_of(12 * C + h * HALF, HALF)
        for p in range(pieces):
            for q in range(blocks):
                base = p * full + piece + q * EXTRA
                at = jnp.where(first, owner(halving, whole, 0, p, q), owner(halving, whole, 1, p, q))
                extra[at] = values[base : base + EXTRA].astype(F32)
        small = extra[0, 0:16]
        for i in range(1, pieces * blocks):
            small = small + extra[i, 0:16]
        gains[...] = small[0:2]
        biases[...] = small[2:4]
        conv_b[...] = small[4:6]
        qkv_b[...] = small[6:8]
        out_b[...] = small[8:9]
        maps = 8 * pieces * blocks
        left, right = extra[:, 16:24].reshape(maps, HALF), extra[:, 24:32].reshape(maps, HALF)
        step = (extra[:, 32:40] * 32.0 + extra[:, 40:48]).reshape(maps, HALF)[:, 0:1].astype(jnp.int32)
        mine = jnp.where(first, left, right)
        time_b[...] = col_sum(mine)
        lane = lax.broadcasted_iota(jnp.int32, (maps, padded), 1)
        pick = jnp.where(lane == step, 1.0, 0.0).astype(BF16)
        tw = join(first, tw_own_ref[...], tw_recv_ref[...], 1)
        back = dot_bt(jnp.concatenate([left, right], axis=1).astype(BF16), tw)
        back_high = back.astype(BF16)
        back_low = (back - back_high.astype(F32)).astype(BF16)
        e = table_ref[...]
        sig = sigmoid(e)
        spread = (dot_at(pick, back_high) + dot_at(pick, back_low))[0:steps]
        table_grad[...] = spread * (sig * (1.0 + e * (1.0 - sig)))
        act = e * sig
        high = act.astype(BF16).astype(F32)
        act_high[steps:padded] = jnp.zeros((padded - steps, width), F32)
        act_low[steps:padded] = jnp.zeros((padded - steps, width), F32)
        act_high[0:steps] = high
        act_low[0:steps] = act - high
        by_step = dot_at(mine.astype(BF16), pick)
        step_high = by_step.astype(BF16)
        step_low = (by_step - step_high.astype(F32)).astype(BF16)
        high, low = act_high[...].astype(BF16), act_low[...].astype(BF16)
        tw_grad[...] = (dot(step_high, high) + dot(step_high, low) + dot(step_low, high)).T

    outs = [
        ((9, HALF, C), F32), ((3, C, HALF), F32), ((HALF, C), F32), (table.shape, F32), (tw_own.shape, F32),
        ((2, HALF), F32), ((2, HALF), F32), ((2, HALF), F32), ((2, HALF), F32), ((1, HALF), F32), ((1, HALF), F32),
    ]
    scratch = [
        pltpu.VMEM((2 * own.shape[0], HALF), BF16),
        pltpu.VMEM((pieces * blocks, EXTRA, HALF), F32),
        pltpu.VMEM((padded, width), F32),
        pltpu.VMEM((padded, width), F32),
    ]
    args = (own, recv, table, tw_own, tw_recv, after)
    return call(body, outs, *args, scratch=scratch, specs={5: ANYWHERE}, limit=24)


def on_device(
    maps_in, timesteps, temb_table, norm_gain, norm_bias, conv1_weight, conv_bias, temb_weight,
    temb_bias, conv2_weight, qkv_weight, qkv_bias, out_weight, out_bias, out_grad,
):
    count = lax.axis_size("dp")
    orders = bits_of(count)
    halving, whole = [[order[i] for order in orders] for i in range(2)]
    halving_steps, whole_steps = list(zip(*halving)), list(zip(*whole))
    pieces = 1 << len(halving_steps)
    total = maps_in.shape[0]
    n = total // 2
    maps_shape, half_shape = (n, PIX, C), (n, PIX, HALF)
    weight_shape = ((9, C, C), BF16)

    x_recv = swap_mp(maps_in)
    w1_own = conv1_weight.reshape(9, C, HALF)
    w1_recv = swap_mp(w1_own)
    blank = call(blank_kernel, [((4, HALF), F32)], flops=10**11)[0]
    pk_own = jnp.concatenate(
        [norm_gain, norm_bias, conv_bias, qkv_bias, out_bias[None], temb_bias[None], blank]
    )
    pk_own = call(
        time_kernel, [((PACK + total, HALF), F32)], timesteps, pk_own, temb_table, temb_weight, specs={0: SCALAR},
    )[0]
    pk_recv = swap_mp(pk_own)
    tw_recv = swap_mp(temb_weight)
    w2_own = conv2_weight.reshape(9, HALF, C)
    w2_recv = swap_mp(w2_own)
    qw_own = jnp.transpose(qkv_weight, (1, 0, 2))
    qw_recv = swap_mp(qw_own)
    ow_recv = swap_mp(out_weight)
    g_recv = swap_mp(out_grad)

    hid, act1_t, act2_t, stat0, stat1, prm, w1_full, *win2 = call(
        first_kernel,
        [
            (maps_shape, F32), ((C, n * PIX), BF16), ((C, n * PIX), BF16),
            ((2 * n, C), F32), ((2 * n, C), F32), ((PACK, C), F32), weight_shape,
        ] + [WIN] * n,
        maps_in, x_recv, w1_own, w1_recv, pk_own, pk_recv,
        scratch=[pltpu.VMEM(*WIN)] * n,
        flops=10**11,
    )
    tile_f32, tile_low = pltpu.VMEM((PIX, C), F32), pltpu.VMEM((PIX, C), BF16)
    three_low = pltpu.VMEM((3, PIX, C), BF16)
    out_keep, out_send, dmid, wg_keep, wg_send, sums3, w2_full, *win3 = call(
        middle_kernel,
        [
            (half_shape, BF16), (half_shape, BF16), (maps_shape, F32),
            ((4 * C, HALF), BF16), ((4 * C, HALF), BF16), ((8, C), F32), weight_shape,
        ] + [WIN] * n,
        maps_in, x_recv, w2_own, w2_recv, prm, out_grad, g_recv, qw_own, qw_recv, out_weight, ow_recv, *win2,
        scratch=[pltpu.VMEM((3, C, C), BF16), tile_low]
        + [tile_f32] * (3 * n) + [tile_low] * n + [three_low] * n + [tile_low] * (3 * n) + [three_low] * n,
    )
    wg_recv = swap_mp(wg_send)
    early_pairs = []
    for taps in TAPS:
        shape = ((len(taps) * C, HALF), BF16)
        keep, send = call(conv2_grad_kernel(taps), [shape, shape], act2_t, *win3)
        early_pairs.append((keep, swap_mp(send)))
    early_pairs.append((wg_keep, wg_recv))
    early_piece, late_piece = piece_of(13 * C, pieces), piece_of(9 * C, pieces)
    early, early_send = start_scatter(early_pairs, early_piece * pieces, halving_steps[0])
    early_recv = swap_dp(early_send, halving_steps[0])
    rows_keep, rows_send, *win4 = call(
        hidden_back_kernel,
        [((EXTRA, HALF), F32), ((32, HALF), F32)] + [WIN] * n,
        timesteps, early, hid, stat1, w2_full, prm, sums3, *win3,
        specs={0: SCALAR, 1: ANYWHERE},
    )
    rows_recv = swap_mp(rows_send)
    late_pairs = []
    for taps in TAPS:
        shape = ((len(taps) * C, HALF), BF16)
        keep, send = call(conv1_grad_kernel(taps), [shape, shape], act1_t, *win4)
        late_pairs.append((keep, swap_mp(send)))
    late, late_send = start_scatter(late_pairs, late_piece * pieces, halving_steps[0])
    late_recv = swap_dp(late_send, halving_steps[0])

    turn = late
    for i, bits in enumerate(halving_steps[1:]):
        early, early_send = next_scatter(early, early_recv, bits, turn)
        early_recv = swap_dp(early_send, bits)
        turn = early
        if i == 0:
            mg_keep, mg_send, last_keep, last_send = call(
                input_back_kernel,
                [(half_shape, F32), (half_shape, BF16), ((16, HALF), F32), ((16, HALF), F32)],
                turn, maps_in, x_recv, stat0, w1_full, prm, dmid, *win4,
                specs={0: ANYWHERE},
            )
            last_recv = swap_mp(last_send)
            out_recv, mg_recv = swap_mp(out_send), swap_mp(mg_send)
            turn = last_keep
        late, late_send = next_scatter(late, late_recv, bits, turn)
        late_recv = swap_dp(late_send, bits)
        turn = late
    early = end_scatter(early, early_recv, rows_keep, rows_recv, turn)
    early_recv = swap_dp(early, whole_steps[0])
    maps_out, maps_grad, turn = call(
        maps_kernel, [(maps_in.shape, BF16), (maps_in.shape, F32), ((8, HALF), F32)],
        early, out_keep, out_recv, mg_keep, mg_recv,
        specs={0: ANYWHERE},
    )
    late = end_scatter(late, late_recv, last_keep, last_recv, turn)
    late_recv = swap_dp(late, whole_steps[0])
    gathers = halving_steps[::-1]
    following = whole_steps[1:] + gathers[:1]
    for bits, next_bits in zip(whole_steps, following):
        early = sum_blocks(early, early_recv, early_piece, bits, late)
        early_recv = swap_dp(early, next_bits)
        late = sum_blocks(late, late_recv, late_piece, bits, early)
        late_recv = swap_dp(late, next_bits)
    for bits, next_bits in zip(gathers[:-1], gathers[1:]):
        early = next_gather(early, early_recv, bits, late)
        early_recv = swap_dp(early, next_bits)
        late = next_gather(late, late_recv, bits, early)
        late_recv = swap_dp(late, next_bits)
    bits = gathers[-1]
    conv2, qkv, out_w, table_grad, tw_grad, gains, biases, conv_b, qkv_b, out_b, time_b = early_result(
        early, early_recv, bits, halving, whole, early_piece, temb_table, temb_weight, tw_recv, late,
    )
    conv1, gains, biases = late_result(
        gains, biases, late, late_recv, bits, halving, whole, late_piece,
    )
    return (
        maps_out, maps_grad, table_grad, gains, biases, conv1.reshape(3, 3, C, HALF), conv_b, tw_grad,
        time_b.reshape(HALF), conv2.reshape(3, 3, HALF, C), jnp.transpose(qkv, (1, 0, 2)), qkv_b, out_w,
        out_b.reshape(HALF),
    )


def solution(mesh):
    args = (
        P("dp", None, "mp"), P("dp"), P(), P(None, "mp"), P(None, "mp"), P(None, None, None, "mp"),
        P(None, "mp"), P(None, "mp"), P("mp"), P(None, None, "mp", None), P(None, None, "mp"),
        P(None, "mp"), P("mp", None), P("mp"), P("dp", None, "mp"),
    )
    outs = (
        P("dp", None, "mp"), P("dp", None, "mp"), P(), P(None, "mp"), P(None, "mp"),
        P(None, None, None, "mp"), P(None, "mp"), P(None, "mp"), P("mp"), P(None, None, "mp", None),
        P(None, None, "mp"), P(None, "mp"), P("mp", None), P("mp"),
    )
    return jax.shard_map(on_device, mesh=mesh, in_specs=args, out_specs=outs, check_vma=False)
```

time: 127 us -> 86.7 us (0.68)
  local copies, waits for them, and re-layouts: 35.4 us -> 2.66 us
  waiting for transfers between devices: 16 us -> 34.6 us
  starting transfers between devices: 39.1 us -> 21.1 us
  other arithmetic: 8.35 us -> 0 us
  Pallas kernels: 25.9 us -> 27.2 us
    ppermute x24 -> x12, starting transfers between devices: 35.3 us -> 16.7 us  [swap_dp(): return lax.ppermute(values, ('dp', 'mp'), pairs)]
    ppermute x24 -> x12, waiting for transfers between devices: 15 us -> 30.4 us  [swap_dp(): return lax.ppermute(values, ('dp', 'mp'), pairs)]
    unnamed x63 -> x30, local copies, waits for them, and re-layouts: 11.3 us -> 2.62 us
    dynamic_update_slice x15 -> x0, local copies, waits for them, and re-layouts: 5.65 us -> none  [the longest x12 4.92 us: gather_stage(): lax.dynamic_update_index_in_dim(result, swap_dp(values, k << bit), me ^ k...]
    dynamic_slice x2 -> x0, local copies, waits for them, and re-layouts: 3.78 us -> none  [theirs(): return lax.dynamic_slice_in_dim(values, (1 - me) * n, n, 0)]
    select_n x8 -> x0, other arithmetic: 3.69 us -> none  [the longest x2 3 us: both_maps(): jnp.where(first, jnp.concatenate([keep, recv]), jnp.concatenate([recv, ke...]
    reshape x5 -> x0, local copies, waits for them, and re-layouts: 3.33 us -> none  [the longest x1 3.12 us: on_device(): conv2_grad = jnp.transpose(conv2_grad, (0, 2, 1, 3)).reshape(3, 3, HALF, C)]
    transpose x2 -> x0, local copies, waits for them, and re-layouts: 3.29 us -> none  [the longest x1 3.2 us: on_device(): conv2_grad = jnp.transpose(conv2_grad, (0, 2, 1, 3)).reshape(3, 3, HALF, C)]
  transfers between devices with their start and end apart: 38 -> 29, of which waited for: 10 -> 13; matrix products, arithmetic and copies ran while one was open for 14% -> 0% of each run, Pallas kernels for 5% -> 22%
where the time goes in v2:
time: 86.7 us; the launch traced here: 86.5 us
  waiting for transfers between devices  34.6 us (40%)
  Pallas kernels  27.2 us (31%)
  starting transfers between devices  21.1 us (24%)
  local copies, waits for them, and re-layouts  2.66 us (3%)
  between operations  0.91 us (1%)
    ppermute x12, waiting for transfers between devices, swap_dp(): return lax.ppermute(values, ('dp', 'mp'), pairs)  30.4 us
    pallas_call x25, Pallas kernels, call(): pl.pallas_call(body, out_shape=tuple((jax.ShapeDtypeStruct(s, d) for s, d...  27.2 us
    ppermute x12, starting transfers between devices, swap_dp(): return lax.ppermute(values, ('dp', 'mp'), pairs)  16.7 us
    ppermute x17, starting transfers between devices, swap_mp(): return lax.ppermute(values, 'mp', [(0, 1), (1, 0)])  4.41 us
    ppermute x17, waiting for transfers between devices, swap_mp(): return lax.ppermute(values, 'mp', [(0, 1), (1, 0)])  4.26 us
    unnamed x30, local copies, waits for them, and re-layouts  2.62 us
  transfers between devices with their start and end apart: 29, of which 13 were waited for; matrix products, arithmetic and copies ran while one was open for 0% of the time, Pallas kernels for 22%

profile of v2, /device:TPU:0, one launch (start us, length us, event | category | flops | bytes accessed | tf_op | source)
XLA Modules:
  0.0 86.5 jit_solution(7690998666851769698)
XLA Ops:
  0.6 0.5 collective-permute-start
  1.2 0.1 collective-permute-start.1
  1.4 0.5 copy-done.9
  1.8 0.0 copy-done.10
  1.9 0.2 copy-done.3
  2.2 0.8 copy-done
  2.9 0.7 shard_map.255.pk_own
  3.6 0.5 collective-permute-start.2
  4.1 0.3 collective-permute-start.3
  4.5 0.2 collective-permute-start.5
  4.6 0.3 collective-permute-done.2.pk_recv
  4.9 0.3 collective-permute-start.4
  5.3 0.2 collective-permute-start.6
  5.5 1.1 %copy-done.8 = bf16[3,3,256,128]{3,2,1,0:T(8,128)(2,1)S(1)} copy-done((bf16[3,3,256,128]{3,2,1,0:T(8,128)(2,1)S(1)}, bf16[3,3,256,128]{3,2,1,0:T(8,128)(2,1)}, u32[]{:S(2)}) %copy-start.8) | copy-done | bytes 589848
  6.5 4.4 %shard_map.256 = (f32[4,256,256]{2,1,0:T(8,128)S(1)}, bf16[256,1024]{1,0:T(8,128)(2,1)S(1)}, bf16[256,1024]{1,0:T(8,128)(2,1)S(1)}, f32[8,256]{1,0:T(8,128)S(1)}...) custom-call(bf16[8,256,128]{2,1,0:T(8,128)(2,1)S(1)} %copy-done.1, ...), custom_call_target="tpu_custom_call" | custom-call | flops 99999997952 | tf_op jit(solution)/shard_map/pallas_call | solution.py:24
  10.9 5.8 %shard_map.257 = (bf16[4,256,128]{2,1,0:T(8,128)(2,1)S(1)}, bf16[4,256,128]{2,1,0:T(8,128)(2,1)S(1)}, f32[4,256,256]{2,1,0:T(8,128)S(1)}, bf16[1024,128]{1,0:T(8...) custom-call(bf16[8,256,128]{2,1,0:T(8,128)(2,1)S(1)} %copy-done.1, ...), custom_call_target="tpu_custom_call" | custom-call | flops 1 | tf_op jit(solution)/shard_map/pallas_call | solution.py:24
  16.7 0.9 %shard_map.258 = (bf16[1280,128]{1,0:T(8,128)(2,1)S(1)}, bf16[1280,128]{1,0:T(8,128)(2,1)S(1)}) custom-call(bf16[256,1024]{1,0:T(8,128)(2,1)S(1)} %get-tuple-element.79.act_t, bf16[3,288,256]{2,1,0:T(8,128)(2,1)S(1)} %get-tuple-element.85.rest_0_, bf16[3,288,256]{2,1,0:T(8,128)(2,1)S(1)} %get-tuple-element.86.rest_1_, ...), custom_call_target="tpu_custom_call" | custom-call | flops 1 | tf_op jit(solution)/shard_map/pallas_call | solution.py:24
  17.6 0.4 collective-permute-start.7
  18.0 0.7 shard_map.259
  18.7 0.2 collective-permute-start.8
  19.0 0.3 collective-permute-start.9
  19.3 1.0 %collective-permute-done.8.refs_3_ = bf16[1024,128]{1,0:T(8,128)(2,1)S(1)} collective-permute-done((bf16[1024,128]{1,0:T(8,128)(2,1)S(1)}, bf16[1024,128]{1,0:T(8,128)(2,1)S(1)}, u32[]{:S(2)}, u32[]{:S(2)}) %collective-permute-start.8) | collective-permute-done | bytes 262176 | tf_op jit(solution)/shard_map/ppermute | solution.py:425
  20.4 0.4 collective-permute-done.9.refs_5_
  20.7 0.4 shard_map.260
  21.2 2.7 %collective-permute-start.10 = (bf16[1664,128]{1,0:T(8,128)(2,1)S(1)}, bf16[1664,128]{1,0:T(8,128)(2,1)S(1)}, u32[]{:S(2)}, u32[]{:S(2)}) collective-permute-start(bf16[1664,128]{1,0:T(8,128)(2,1)S(1)} %get-tuple-element.96), channel_id=1, source_target_pairs={{0,2},{1,5},{2,0},{3,7},{4,6},{5,1},{6,4},{7,3},{8,10},{9,13},{10,... | collective-permute-start | bytes 1277960 | tf_op jit(solution)/shard_map/ppermute | solution.py:421
  23.9 3.4 %shard_map.261 = (f32[48,128]{1,0:T(8,128)S(1)}, f32[32,128]{1,0:T(8,128)S(1)}, bf16[3,288,256]{2,1,0:T(8,128)(2,1)S(1)}, bf16[3,288,256]{2,1,0:T(8,128)(2,1)S(1...) custom-call(s32[8]{0:T(128)S(1)} %copy-done.7, ...), custom_call_target="tpu_custom_call" | custom-call | flops 1 | tf_op jit(solution)/shard_map/pallas_call | solution.py:24
  27.3 0.9 %shard_map.262 = (bf16[1280,128]{1,0:T(8,128)(2,1)S(1)}, bf16[1280,128]{1,0:T(8,128)(2,1)S(1)}) custom-call(bf16[256,1024]{1,0:T(8,128)(2,1)S(1)} %get-tuple-element.97.act_t, bf16[3,288,256]{2,1,0:T(8,128)(2,1)S(1)} %get-tuple-element.102.rest_0_, bf16[3,288,256]{2,1,0:T(8,128)(2,1)S(1)} %get-tuple-element.103.rest_1_, ...), custom_call_target="tpu_custom_call" | custom-call | flops 1 | tf_op jit(solution)/shard_map/pallas_call | solution.py:24
  28.2 0.2 collective-permute-start.11
  28.3 0.7 shard_map.263
  29.1 0.5 collective-permute-start.12
  29.5 1.2 %collective-permute-done.12.refs_3_ = bf16[1024,128]{1,0:T(8,128)(2,1)S(1)} collective-permute-done((bf16[1024,128]{1,0:T(8,128)(2,1)S(1)}, bf16[1024,128]{1,0:T(8,128)(2,1)S(1)}, u32[]{:S(2)}, u32[]{:S(2)}) %collective-permute-start.12) | collective-permute-done | bytes 262176 | tf_op jit(solution)/shard_map/ppermute | solution.py:425
  30.7 0.3 shard_map.264
  31.0 1.5 %collective-permute-start.15 = (bf16[1152,128]{1,0:T(8,128)(2,1)S(1)}, bf16[1152,128]{1,0:T(8,128)(2,1)S(1)}, u32[]{:S(2)}, u32[]{:S(2)}) collective-permute-start(bf16[1152,128]{1,0:T(8,128)(2,1)S(1)} %get-tuple-element.115), channel_id=1, source_target_pairs={{0,2},{1,5},{2,0},{3,7},{4,6},{5,1},{6,4},{7,3},{8,10},{9,13},{10,... | collective-permute-start | bytes 884744 | tf_op jit(solution)/shard_map/ppermute | solution.py:421
  32.5 0.2 shard_map.265
  32.8 0.7 collective-permute-start.13
  33.4 2.3 %shard_map.266 = (f32[4,256,128]{2,1,0:T(8,128)S(1)}, bf16[4,256,128]{2,1,0:T(8,128)(2,1)S(1)}, f32[16,128]{1,0:T(8,128)S(1)}, f32[16,128]{1,0:T(8,128)S(1)}) custom-call(bf16[832,128]{1,0:T(8,128)(2,1)S(1)} %get-tuple-element.111.after.own_ref, bf16[8,256,128]{2,1,0:T(8,128)(2,1)S(1)} %copy-done.1, bf16[8,256,128]{2,1,0:T(8,128)(2,1)S(1)} %collective-permute-done.x_recv, ...), custom_call_target="tpu_custom_call" | custom-call | flops 1 | tf_op jit(solution)/shard_map/pallas_call | solution.py:24
  35.8 0.6 collective-permute-start.17
  36.4 0.1 collective-permute-start.14
  36.4 3.6 %collective-permute-done.15.recv_ref = bf16[1152,128]{1,0:T(8,128)(2,1)S(1)} collective-permute-done((bf16[1152,128]{1,0:T(8,128)(2,1)S(1)}, bf16[1152,128]{1,0:T(8,128)(2,1)S(1)}, u32[]{:S(2)}, u32[]{:S(2)}) %collective-permute-start.15) | collective-permute-done | bytes 294944 | tf_op jit(solution)/shard_map/ppermute | solution.py:421
  40.0 0.1 shard_map.267
  40.2 0.1 shard_map.268.after.own_ref
  40.3 1.6 %collective-permute-start.18 = (bf16[880,128]{1,0:T(8,128)(2,1)S(1)}, bf16[880,128]{1,0:T(8,128)(2,1)S(1)}, u32[]{:S(2)}, u32[]{:S(2)}) collective-permute-start(bf16[880,128]{1,0:T(8,128)(2,1)S(1)} %shard_map.268.after.own_ref), channel_id=1, source_target_pairs={{0,8},{1,17},{2,10},{3,19},{4,12},{5,21},{6,14},{7,23},{8,0},{9,25... | collective-permute-start | bytes 675848 | tf_op jit(solution)/shard_map/ppermute | solution.py:421
  41.9 1.5 %collective-permute-start.19 = (bf16[576,128]{1,0:T(8,128)(2,1)S(1)}, bf16[576,128]{1,0:T(8,128)(2,1)S(1)}, u32[]{:S(2)}, u32[]{:S(2)}) collective-permute-start(bf16[576,128]{1,0:T(8,128)(2,1)S(1)} %get-tuple-element.127), channel_id=1, source_target_pairs={{0,4},{1,3},{2,6},{3,1},{4,0},{5,7},{6,2},{7,5},{8,12},{9,11},{10,... | collective-permute-start | bytes 442376 | tf_op jit(solution)/shard_map/ppermute | solution.py:421
  43.4 1.3 %shard_map.269 = (bf16[8,256,128]{2,1,0:T(8,128)(2,1)}, f32[8,256,128]{2,1,0:T(8,128)}, f32[8,128]{1,0:T(8,128)S(1)}) custom-call(bf16[880,128]{1,0:T(8,128)(2,1)S(1)} %shard_map.268.after.own_ref, bf16[4,256,128]{2,1,0:T(8,128)(2,1)S(1)} %get-tuple-element.121.out_keep, bf16[4,256,128]{2,1,0:T(8,128)(2,1)S(1)} %collective-permute-done.16.out_recv, ...), custom_call_target="tpu_custom_call" | custom-call | flops 1 | tf_op jit(solution)/shard_map/pallas_call | solution.py:24
  44.7 2.4 %collective-permute-done.19.recv_ref = bf16[576,128]{1,0:T(8,128)(2,1)S(1)} collective-permute-done((bf16[576,128]{1,0:T(8,128)(2,1)S(1)}, bf16[576,128]{1,0:T(8,128)(2,1)S(1)}, u32[]{:S(2)}, u32[]{:S(2)}) %collective-permute-start.19) | collective-permute-done | bytes 147488 | tf_op jit(solution)/shard_map/ppermute | solution.py:421
  47.1 1.4 %collective-permute-done.18.recv_ref = bf16[880,128]{1,0:T(8,128)(2,1)S(1)} collective-permute-done((bf16[880,128]{1,0:T(8,128)(2,1)S(1)}, bf16[880,128]{1,0:T(8,128)(2,1)S(1)}, u32[]{:S(2)}, u32[]{:S(2)}) %collective-permute-start.18) | collective-permute-done | bytes 225312 | tf_op jit(solution)/shard_map/ppermute | solution.py:421
  48.5 0.1 shard_map.271.after_ref.own_ref
  48.6 1.8 %collective-permute-start.21 = (bf16[928,128]{1,0:T(8,128)(2,1)S(1)}, bf16[928,128]{1,0:T(8,128)(2,1)S(1)}, u32[]{:S(2)}, u32[]{:S(2)}) collective-permute-start(bf16[928,128]{1,0:T(8,128)(2,1)S(1)} %shard_map.271.after_ref.own_ref), channel_id=1, source_target_pairs={{0,16},{1,9},{2,18},{3,11},{4,20},{5,13},{6,22},{7,15},{8,24},{9,1... | collective-permute-start | bytes 712712 | tf_op jit(solution)/shard_map/ppermute | solution.py:421
  50.4 2.6 %collective-permute-start.22 = (bf16[592,128]{1,0:T(8,128)(2,1)S(1)}, bf16[592,128]{1,0:T(8,128)(2,1)S(1)}, u32[]{:S(2)}, u32[]{:S(2)}) collective-permute-start(bf16[592,128]{1,0:T(8,128)(2,1)S(1)} %shard_map.270.after_ref.own_ref), channel_id=1, source_target_pairs={{0,8},{1,17},{2,10},{3,19},{4,12},{5,21},{6,14},{7,23},{8,0},{9,25... | collective-permute-start | bytes 454664 | tf_op jit(solution)/shard_map/ppermute | solution.py:421
  52.9 5.0 %collective-permute-done.22.recv_ref = bf16[592,128]{1,0:T(8,128)(2,1)S(1)} collective-permute-done((bf16[592,128]{1,0:T(8,128)(2,1)S(1)}, bf16[592,128]{1,0:T(8,128)(2,1)S(1)}, u32[]{:S(2)}, u32[]{:S(2)}) %collective-permute-start.22) | collective-permute-done | bytes 151584 | tf_op jit(solution)/shard_map/ppermute | solution.py:421
  58.0 3.5 %collective-permute-done.21.recv_ref = bf16[928,128]{1,0:T(8,128)(2,1)S(1)} collective-permute-done((bf16[928,128]{1,0:T(8,128)(2,1)S(1)}, bf16[928,128]{1,0:T(8,128)(2,1)S(1)}, u32[]{:S(2)}, u32[]{:S(2)}) %collective-permute-start.21) | collective-permute-done | bytes 237600 | tf_op jit(solution)/shard_map/ppermute | solution.py:421
  61.5 0.1 shard_map.273.after_ref.own_ref
  61.5 0.4 collective-permute-start.23
  62.0 0.7 collective-permute-start.24
  62.7 7.0 %collective-permute-done.24.recv_ref = bf16[608,128]{1,0:T(8,128)(2,1)S(1)} collective-permute-done((bf16[608,128]{1,0:T(8,128)(2,1)S(1)}, bf16[608,128]{1,0:T(8,128)(2,1)S(1)}, u32[]{:S(2)}, u32[]{:S(2)}) %collective-permute-start.24) | collective-permute-done | bytes 155680 | tf_op jit(solution)/shard_map/ppermute | solution.py:421
  69.7 0.1 shard_map.275.after_ref.own_ref
  69.8 1.2 %collective-permute-start.25 = (bf16[2048,128]{1,0:T(8,128)(2,1)S(1)}, bf16[2048,128]{1,0:T(8,128)(2,1)S(1)}, u32[]{:S(2)}, u32[]{:S(2)}) collective-permute-start(bf16[2048,128]{1,0:T(8,128)(2,1)S(1)} %shard_map.275.after_ref.own_ref), channel_id=1, source_target_pairs={{0,2},{1,5},{2,0},{3,7},{4,6},{5,1},{6,4},{7,3},{8,10},{9,13},{10,... | collective-permute-start | bytes 1572872 | tf_op jit(solution)/shard_map/ppermute | solution.py:421
  71.0 0.9 %collective-permute-start.27 = (bf16[640,128]{1,0:T(8,128)(2,1)S(1)}, bf16[640,128]{1,0:T(8,128)(2,1)S(1)}, u32[]{:S(2)}, u32[]{:S(2)}) collective-permute-start(bf16[640,128]{1,0:T(8,128)(2,1)S(1)} %shard_map.274.after_ref.own_ref), channel_id=1, source_target_pairs={{0,4},{1,3},{2,6},{3,1},{4,0},{5,7},{6,2},{7,5},{8,12},{9,11},{10,... | collective-permute-start | bytes 491528 | tf_op jit(solution)/shard_map/ppermute | solution.py:421
  71.9 6.2 %collective-permute-done.27.recv_ref = bf16[640,128]{1,0:T(8,128)(2,1)S(1)} collective-permute-done((bf16[640,128]{1,0:T(8,128)(2,1)S(1)}, bf16[640,128]{1,0:T(8,128)(2,1)S(1)}, u32[]{:S(2)}, u32[]{:S(2)}) %collective-permute-start.27) | collective-permute-done | bytes 163872 | tf_op jit(solution)/shard_map/ppermute | solution.py:421
  78.2 0.9 %collective-permute-start.28 = (bf16[1280,128]{1,0:T(8,128)(2,1)S(1)}, bf16[1280,128]{1,0:T(8,128)(2,1)S(1)}, u32[]{:S(2)}, u32[]{:S(2)}) collective-permute-start(bf16[1280,128]{1,0:T(8,128)(2,1)S(1)} %shard_map.276.after_ref.own_ref), channel_id=1, source_target_pairs={{0,2},{1,5},{2,0},{3,7},{4,6},{5,1},{6,4},{7,3},{8,10},{9,13},{10,... | collective-permute-start | bytes 983048 | tf_op jit(solution)/shard_map/ppermute | solution.py:421
  79.1 1.3 %collective-permute-done.26.tw_recv_ref = bf16[512,128]{1,0:T(8,128)(2,1)S(1)} collective-permute-done((bf16[512,128]{1,0:T(8,128)(2,1)S(1)}, bf16[512,128]{1,0:T(8,128)(2,1)S(1)}, u32[]{:S(2)}, u32[]{:S(2)}) %collective-permute-start.26) | collective-permute-done | bytes 131104 | tf_op jit(solution)/shard_map/ppermute | solution.py:425
  80.5 3.5 %shard_map.277 = (f32[9,128,256]{2,1,0:T(8,128)}, f32[3,256,128]{2,1,0:T(8,128)}, f32[128,256]{1,0:T(8,128)}, f32[1000,512]{1,0:T(8,128)}, f32[512,128]{1,0:T(8,...) custom-call(bf16[2048,128]{1,0:T(8,128)(2,1)S(1)} %shard_map.275.aft, ...), custom_call_target="tpu_custom_call" | custom-call | flops 1 | tf_op jit(solution)/shard_map/pallas_call | solution.py:24
  84.0 1.3 %collective-permute-done.28.recv_ref = bf16[1280,128]{1,0:T(8,128)(2,1)S(1)} collective-permute-done((bf16[1280,128]{1,0:T(8,128)(2,1)S(1)}, bf16[1280,128]{1,0:T(8,128)(2,1)S(1)}, u32[]{:S(2)}, u32[]{:S(2)}) %collective-permute-start.28) | collective-permute-done | bytes 327712 | tf_op jit(solution)/shard_map/ppermute | solution.py:421
  85.3 1.2 %shard_map.278 = (f32[2304,128]{1,0:T(8,128)}, f32[3,128]{1,0:T(4,128)}, f32[3,128]{1,0:T(4,128)}) custom-call(f32[2,128]{1,0:T(2,128)S(1)} %get-tuple-element.131.gains_ref, f32[2,128]{1,0:T(2,128)S(1)} %get-tuple-element.132.biases_ref, bf16[1280,128]{1,0:T(8,128)(2,1)S(1)} %shard_map.276.after_ref.own_ref, ...), custom_call_target="tpu_custom_call" | custom-call | flops 1 | tf_op jit(solution)/shard_map/pallas_call | solution.py:24
  (50 shorter events, 0.3 us)
Async XLA Ops:
  0.6 4.6 %collective-permute-start = (bf16[8,256,128]{2,1,0:T(8,128)(2,1)}, bf16[8,256,128]{2,1,0:T(8,128)(2,1)S(1)}, u32[]{:S(2)}, u32[]{:S(2)}) collective-permute-start(bf16[8,256,128]{2,1,0:T(8,128)(2,1)} %x_own.5), channel_id=1, source_target_pairs={{0,1},{1,0},{2,3},{3,2},{4,5},{5,4},{6,7},{7,6},{8,9},{9,8},{10,11... | collective-permute-start | bytes 1572872 | tf_op jit(solution)/shard_map/ppermute | solution.py:425
  1.2 0.7 copy-start.9
  1.2 0.7 copy-start.10
  1.2 0.7 copy-start.11
  1.2 0.7 copy-start.12
  1.2 0.7 copy-start.13
  1.2 0.7 copy-start.14
  1.2 1.0 %copy-start.3 = (bf16[512,128]{1,0:T(8,128)(2,1)S(1)}, bf16[512,128]{1,0:T(8,128)(2,1)}, u32[]{:S(2)}) copy-start(bf16[512,128]{1,0:T(8,128)(2,1)} %tw_own_ref.1) | copy-start | bytes 393220
  1.2 1.0 %copy-start.7 = (s32[8]{0:T(128)S(1)}, s32[8]{0:T(128)}, u32[]{:S(2)}) copy-start(s32[8]{0:T(128)} %steps.3) | copy-start | bytes 100
  1.2 4.2 %collective-permute-start.1 = (bf16[9,256,128]{2,1,0:T(8,128)(2,1)}, bf16[9,256,128]{2,1,0:T(8,128)(2,1)}, u32[]{:S(2)}, u32[]{:S(2)}) collective-permute-start(bf16[9,256,128]{2,1,0:T(8,128)(2,1)} %bitcast.14), channel_id=1, source_target_pairs={{0,1},{1,0},{2,3},{3,2},{4,5},{5,4},{6,7},{7,6},{8,9},{9,8},{10,11... | collective-permute-start | bytes 1769480 | tf_op jit(solution)/shard_map/ppermute | solution.py:425
  1.3 1.6 %copy-start = (f32[1000,512]{1,0:T(8,128)S(1)}, f32[1000,512]{1,0:T(8,128)}, u32[]{:S(2)}) copy-start(f32[1000,512]{1,0:T(8,128)} %table_ref.1) | copy-start | bytes 6144004
  1.3 3.1 %copy-start.5 = (bf16[256,3,128]{2,0,1:T(8,128)(2,1)S(1)}, bf16[256,3,128]{2,0,1:T(8,128)(2,1)}, u32[]{:S(2)}) copy-start(bf16[256,3,128]{2,0,1:T(8,128)(2,1)} %param.25) | copy-start | bytes 589828
  1.3 3.9 %copy-start.6 = (bf16[128,256]{1,0:T(8,128)(2,1)S(1)}, bf16[128,256]{1,0:T(8,128)(2,1)}, u32[]{:S(2)}) copy-start(bf16[128,256]{1,0:T(8,128)(2,1)} %ow_own.1) | copy-start | bytes 196612
  1.4 4.1 %copy-start.1 = (bf16[8,256,128]{2,1,0:T(8,128)(2,1)S(1)}, bf16[8,256,128]{2,1,0:T(8,128)(2,1)}, u32[]{:S(2)}) copy-start(bf16[8,256,128]{2,1,0:T(8,128)(2,1)} %x_own.5) | copy-start | bytes 1572868
  2.9 1.2 %copy-start.2 = (bf16[3,3,128,256]{3,2,1,0:T(8,128)(2,1)S(1)}, bf16[3,3,128,256]{3,2,1,0:T(8,128)(2,1)}, u32[]{:S(2)}) copy-start(bf16[3,3,128,256]{3,2,1,0:T(8,128)(2,1)} %param.24) | copy-start | bytes 1769476
  2.9 2.0 %copy-start.4 = (bf16[8,256,128]{2,1,0:T(8,128)(2,1)S(1)}, bf16[8,256,128]{2,1,0:T(8,128)(2,1)}, u32[]{:S(2)}) copy-start(bf16[8,256,128]{2,1,0:T(8,128)(2,1)} %g_own.1) | copy-start | bytes 1572868
  3.6 1.3 %collective-permute-start.2 = (f32[24,128]{1,0:T(8,128)S(1)}, f32[24,128]{1,0:T(8,128)S(1)}, u32[]{:S(2)}, u32[]{:S(2)}) collective-permute-start(f32[24,128]{1,0:T(8,128)S(1)} %shard_map.255.pk_own), channel_id=1, source_target_pairs={{0,1},{1,0},{2,3},{3,2},{4,5},{5,4},{6,7},{7,6},{8,9},{9,8},{10,11... | collective-permute-start | bytes 36872 | tf_op jit(solution)/shard_map/ppermute | solution.py:425
  4.1 6.8 %collective-permute-start.3 = (bf16[9,128,256]{2,1,0:T(8,128)(2,1)S(1)}, bf16[9,128,256]{2,1,0:T(8,128)(2,1)S(1)}, u32[]{:S(2)}, u32[]{:S(2)}) collective-permute-start(bf16[9,128,256]{2,1,0:T(8,128)(2,1)S(1)} %bitcast.10), channel_id=1, source_target_pairs={{0,1},{1,0},{2,3},{3,2},{4,5},{5,4},{6,7},{7,6},{8,9},{9,8},{10,11... | collective-permute-start | bytes 1769480 | tf_op jit(solution)/shard_map/ppermute | solution.py:425
  4.5 6.5 %collective-permute-start.5 = (bf16[3,256,128]{2,1,0:T(8,128)(2,1)S(1)}, bf16[3,256,128]{2,1,0:T(8,128)(2,1)S(1)}, u32[]{:S(2)}, u32[]{:S(2)}) collective-permute-start(bf16[3,256,128]{2,1,0:T(8,128)(2,1)S(1)} %bitcast.12), channel_id=1, source_target_pairs={{0,1},{1,0},{2,3},{3,2},{4,5},{5,4},{6,7},{7,6},{8,9},{9,8},{10,11... | collective-permute-start | bytes 589832 | tf_op jit(solution)/shard_map/ppermute | solution.py:425
  4.9 6.0 %collective-permute-start.4 = (bf16[8,256,128]{2,1,0:T(8,128)(2,1)S(1)}, bf16[8,256,128]{2,1,0:T(8,128)(2,1)S(1)}, u32[]{:S(2)}, u32[]{:S(2)}) collective-permute-start(bf16[8,256,128]{2,1,0:T(8,128)(2,1)S(1)} %copy-done.4), channel_id=1, source_target_pairs={{0,1},{1,0},{2,3},{3,2},{4,5},{5,4},{6,7},{7,6},{8,9},{9,8},{10,11... | collective-permute-start | bytes 1572872 | tf_op jit(solution)/shard_map/ppermute | solution.py:425
  5.3 5.6 %collective-permute-start.6 = (bf16[128,256]{1,0:T(8,128)(2,1)S(1)}, bf16[128,256]{1,0:T(8,128)(2,1)S(1)}, u32[]{:S(2)}, u32[]{:S(2)}) collective-permute-start(bf16[128,256]{1,0:T(8,128)(2,1)S(1)} %copy-done.6), channel_id=1, source_target_pairs={{0,1},{1,0},{2,3},{3,2},{4,5},{5,4},{6,7},{7,6},{8,9},{9,8},{10,11... | collective-permute-start | bytes 196616 | tf_op jit(solution)/shard_map/ppermute | solution.py:425
  5.5 1.1 %copy-start.8 = (bf16[3,3,256,128]{3,2,1,0:T(8,128)(2,1)S(1)}, bf16[3,3,256,128]{3,2,1,0:T(8,128)(2,1)}, u32[]{:S(2)}) copy-start(bf16[3,3,256,128]{3,2,1,0:T(8,128)(2,1)} %param.20) | copy-start | bytes 1769476
  17.6 3.1 %collective-permute-start.7 = (bf16[1280,128]{1,0:T(8,128)(2,1)S(1)}, bf16[1280,128]{1,0:T(8,128)(2,1)S(1)}, u32[]{:S(2)}, u32[]{:S(2)}) collective-permute-start(bf16[1280,128]{1,0:T(8,128)(2,1)S(1)} %get-tuple-element.90), channel_id=1, source_target_pairs={{0,1},{1,0},{2,3},{3,2},{4,5},{5,4},{6,7},{7,6},{8,9},{9,8},{10,11... | collective-permute-start | bytes 983048 | tf_op jit(solution)/shard_map/ppermute | solution.py:425
  18.7 1.6 %collective-permute-start.8 = (bf16[1024,128]{1,0:T(8,128)(2,1)S(1)}, bf16[1024,128]{1,0:T(8,128)(2,1)S(1)}, u32[]{:S(2)}, u32[]{:S(2)}) collective-permute-start(bf16[1024,128]{1,0:T(8,128)(2,1)S(1)} %get-tuple-element.92), channel_id=1, source_target_pairs={{0,1},{1,0},{2,3},{3,2},{4,5},{5,4},{6,7},{7,6},{8,9},{9,8},{10,11... | collective-permute-start | bytes 786440 | tf_op jit(solution)/shard_map/ppermute | solution.py:425
  19.0 1.7 %collective-permute-start.9 = (bf16[1024,128]{1,0:T(8,128)(2,1)S(1)}, bf16[1024,128]{1,0:T(8,128)(2,1)S(1)}, u32[]{:S(2)}, u32[]{:S(2)}) collective-permute-start(bf16[1024,128]{1,0:T(8,128)(2,1)S(1)} %get-tuple-element.94), channel_id=1, source_target_pairs={{0,1},{1,0},{2,3},{3,2},{4,5},{5,4},{6,7},{7,6},{8,9},{9,8},{10,11... | collective-permute-start | bytes 786440 | tf_op jit(solution)/shard_map/ppermute | solution.py:425
  21.2 11.4 %collective-permute-start.10 = (bf16[1664,128]{1,0:T(8,128)(2,1)S(1)}, bf16[1664,128]{1,0:T(8,128)(2,1)S(1)}, u32[]{:S(2)}, u32[]{:S(2)}) collective-permute-start(bf16[1664,128]{1,0:T(8,128)(2,1)S(1)} %get-tuple-element.96), channel_id=1, source_target_pairs={{0,2},{1,5},{2,0},{3,7},{4,6},{5,1},{6,4},{7,3},{8,10},{9,13},{10,... | collective-permute-start | bytes 1277960 | tf_op jit(solution)/shard_map/ppermute | solution.py:421
  28.2 2.5 %collective-permute-start.11 = (bf16[1280,128]{1,0:T(8,128)(2,1)S(1)}, bf16[1280,128]{1,0:T(8,128)(2,1)S(1)}, u32[]{:S(2)}, u32[]{:S(2)}) collective-permute-start(bf16[1280,128]{1,0:T(8,128)(2,1)S(1)} %get-tuple-element.107), channel_id=1, source_target_pairs={{0,1},{1,0},{2,3},{3,2},{4,5},{5,4},{6,7},{7,6},{8,9},{9,8},{10,11... | collective-permute-start | bytes 983048 | tf_op jit(solution)/shard_map/ppermute | solution.py:425
  29.1 1.6 %collective-permute-start.12 = (bf16[1024,128]{1,0:T(8,128)(2,1)S(1)}, bf16[1024,128]{1,0:T(8,128)(2,1)S(1)}, u32[]{:S(2)}, u32[]{:S(2)}) collective-permute-start(bf16[1024,128]{1,0:T(8,128)(2,1)S(1)} %get-tuple-element.109), channel_id=1, source_target_pairs={{0,1},{1,0},{2,3},{3,2},{4,5},{5,4},{6,7},{7,6},{8,9},{9,8},{10,11... | collective-permute-start | bytes 786440 | tf_op jit(solution)/shard_map/ppermute | solution.py:425
  31.0 9.0 %collective-permute-start.15 = (bf16[1152,128]{1,0:T(8,128)(2,1)S(1)}, bf16[1152,128]{1,0:T(8,128)(2,1)S(1)}, u32[]{:S(2)}, u32[]{:S(2)}) collective-permute-start(bf16[1152,128]{1,0:T(8,128)(2,1)S(1)} %get-tuple-element.115), channel_id=1, source_target_pairs={{0,2},{1,5},{2,0},{3,7},{4,6},{5,1},{6,4},{7,3},{8,10},{9,13},{10,... | collective-permute-start | bytes 884744 | tf_op jit(solution)/shard_map/ppermute | solution.py:421
  32.8 7.4 %collective-permute-start.13 = (bf16[832,128]{1,0:T(8,128)(2,1)S(1)}, bf16[832,128]{1,0:T(8,128)(2,1)S(1)}, u32[]{:S(2)}, u32[]{:S(2)}) collective-permute-start(bf16[832,128]{1,0:T(8,128)(2,1)S(1)} %get-tuple-element.112), channel_id=1, source_target_pairs={{0,4},{1,3},{2,6},{3,1},{4,0},{5,7},{6,2},{7,5},{8,12},{9,11},{10,... | collective-permute-start | bytes 638984 | tf_op jit(solution)/shard_map/ppermute | solution.py:421
  33.4 10.0 %collective-permute-start.16 = (bf16[4,256,128]{2,1,0:T(8,128)(2,1)S(1)}, bf16[4,256,128]{2,1,0:T(8,128)(2,1)S(1)}, u32[]{:S(2)}, u32[]{:S(2)}) collective-permute-start(bf16[4,256,128]{2,1,0:T(8,128)(2,1)S(1)} %get-tuple-element.122), channel_id=1, source_target_pairs={{0,1},{1,0},{2,3},{3,2},{4,5},{5,4},{6,7},{7,6},{8,9},{9,8},{10,11... | collective-permute-start | bytes 786440 | tf_op jit(solution)/shard_map/ppermute | solution.py:425
  35.8 7.7 %collective-permute-start.17 = (bf16[4,256,128]{2,1,0:T(8,128)(2,1)S(1)}, bf16[4,256,128]{2,1,0:T(8,128)(2,1)S(1)}, u32[]{:S(2)}, u32[]{:S(2)}) collective-permute-start(bf16[4,256,128]{2,1,0:T(8,128)(2,1)S(1)} %get-tuple-element.124), channel_id=1, source_target_pairs={{0,1},{1,0},{2,3},{3,2},{4,5},{5,4},{6,7},{7,6},{8,9},{9,8},{10,11... | collective-permute-start | bytes 786440 | tf_op jit(solution)/shard_map/ppermute | solution.py:425
  36.4 3.8 %collective-permute-start.14 = (f32[32,128]{1,0:T(8,128)S(1)}, f32[32,128]{1,0:T(8,128)S(1)}, u32[]{:S(2)}, u32[]{:S(2)}) collective-permute-start(f32[32,128]{1,0:T(8,128)S(1)} %get-tuple-element.114), channel_id=1, source_target_pairs={{0,1},{1,0},{2,3},{3,2},{4,5},{5,4},{6,7},{7,6},{8,9},{9,8},{10,11... | collective-permute-start | bytes 49160 | tf_op jit(solution)/shard_map/ppermute | solution.py:425
  40.3 8.2 %collective-permute-start.18 = (bf16[880,128]{1,0:T(8,128)(2,1)S(1)}, bf16[880,128]{1,0:T(8,128)(2,1)S(1)}, u32[]{:S(2)}, u32[]{:S(2)}) collective-permute-start(bf16[880,128]{1,0:T(8,128)(2,1)S(1)} %shard_map.268.after.own_ref), channel_id=1, source_target_pairs={{0,8},{1,17},{2,10},{3,19},{4,12},{5,21},{6,14},{7,23},{8,0},{9,25... | collective-permute-start | bytes 675848 | tf_op jit(solution)/shard_map/ppermute | solution.py:421
  41.9 5.1 %collective-permute-start.19 = (bf16[576,128]{1,0:T(8,128)(2,1)S(1)}, bf16[576,128]{1,0:T(8,128)(2,1)S(1)}, u32[]{:S(2)}, u32[]{:S(2)}) collective-permute-start(bf16[576,128]{1,0:T(8,128)(2,1)S(1)} %get-tuple-element.127), channel_id=1, source_target_pairs={{0,4},{1,3},{2,6},{3,1},{4,0},{5,7},{6,2},{7,5},{8,12},{9,11},{10,... | collective-permute-start | bytes 442376 | tf_op jit(solution)/shard_map/ppermute | solution.py:421
  43.4 1.3 %collective-permute-start.20 = (f32[16,128]{1,0:T(8,128)S(1)}, f32[16,128]{1,0:T(8,128)S(1)}, u32[]{:S(2)}, u32[]{:S(2)}) collective-permute-start(f32[16,128]{1,0:T(8,128)S(1)} %get-tuple-element.128), channel_id=1, source_target_pairs={{0,1},{1,0},{2,3},{3,2},{4,5},{5,4},{6,7},{7,6},{8,9},{9,8},{10,11... | collective-permute-start | bytes 24584 | tf_op jit(solution)/shard_map/ppermute | solution.py:425
  48.6 12.9 %collective-permute-start.21 = (bf16[928,128]{1,0:T(8,128)(2,1)S(1)}, bf16[928,128]{1,0:T(8,128)(2,1)S(1)}, u32[]{:S(2)}, u32[]{:S(2)}) collective-permute-start(bf16[928,128]{1,0:T(8,128)(2,1)S(1)} %shard_map.271.after_ref.own_ref), channel_id=1, source_target_pairs={{0,16},{1,9},{2,18},{3,11},{4,20},{5,13},{6,22},{7,15},{8,24},{9,1... | collective-permute-start | bytes 712712 | tf_op jit(solution)/shard_map/ppermute | solution.py:421
  50.4 7.6 %collective-permute-start.22 = (bf16[592,128]{1,0:T(8,128)(2,1)S(1)}, bf16[592,128]{1,0:T(8,128)(2,1)S(1)}, u32[]{:S(2)}, u32[]{:S(2)}) collective-permute-start(bf16[592,128]{1,0:T(8,128)(2,1)S(1)} %shard_map.270.after_ref.own_ref), channel_id=1, source_target_pairs={{0,8},{1,17},{2,10},{3,19},{4,12},{5,21},{6,14},{7,23},{8,0},{9,25... | collective-permute-start | bytes 454664 | tf_op jit(solution)/shard_map/ppermute | solution.py:421
  61.5 8.2 %collective-permute-start.23 = (bf16[1024,128]{1,0:T(8,128)(2,1)S(1)}, bf16[1024,128]{1,0:T(8,128)(2,1)S(1)}, u32[]{:S(2)}, u32[]{:S(2)}) collective-permute-start(bf16[1024,128]{1,0:T(8,128)(2,1)S(1)} %shard_map.273.after_ref.own_ref), channel_id=1, source_target_pairs={{0,4},{1,3},{2,6},{3,1},{4,0},{5,7},{6,2},{7,5},{8,12},{9,11},{10,... | collective-permute-start | bytes 786440 | tf_op jit(solution)/shard_map/ppermute | solution.py:421
  62.0 7.7 %collective-permute-start.24 = (bf16[608,128]{1,0:T(8,128)(2,1)S(1)}, bf16[608,128]{1,0:T(8,128)(2,1)S(1)}, u32[]{:S(2)}, u32[]{:S(2)}) collective-permute-start(bf16[608,128]{1,0:T(8,128)(2,1)S(1)} %shard_map.272.after_ref.own_ref), channel_id=1, source_target_pairs={{0,16},{1,9},{2,18},{3,11},{4,20},{5,13},{6,22},{7,15},{8,24},{9,1... | collective-permute-start | bytes 466952 | tf_op jit(solution)/shard_map/ppermute | solution.py:421
  69.8 10.7 %collective-permute-start.25 = (bf16[2048,128]{1,0:T(8,128)(2,1)S(1)}, bf16[2048,128]{1,0:T(8,128)(2,1)S(1)}, u32[]{:S(2)}, u32[]{:S(2)}) collective-permute-start(bf16[2048,128]{1,0:T(8,128)(2,1)S(1)} %shard_map.275.after_ref.own_ref), channel_id=1, source_target_pairs={{0,2},{1,5},{2,0},{3,7},{4,6},{5,1},{6,4},{7,3},{8,10},{9,13},{10,... | collective-permute-start | bytes 1572872 | tf_op jit(solution)/shard_map/ppermute | solution.py:421
  71.0 7.1 %collective-permute-start.27 = (bf16[640,128]{1,0:T(8,128)(2,1)S(1)}, bf16[640,128]{1,0:T(8,128)(2,1)S(1)}, u32[]{:S(2)}, u32[]{:S(2)}) collective-permute-start(bf16[640,128]{1,0:T(8,128)(2,1)S(1)} %shard_map.274.after_ref.own_ref), channel_id=1, source_target_pairs={{0,4},{1,3},{2,6},{3,1},{4,0},{5,7},{6,2},{7,5},{8,12},{9,11},{10,... | collective-permute-start | bytes 491528 | tf_op jit(solution)/shard_map/ppermute | solution.py:421
  78.2 7.1 %collective-permute-start.28 = (bf16[1280,128]{1,0:T(8,128)(2,1)S(1)}, bf16[1280,128]{1,0:T(8,128)(2,1)S(1)}, u32[]{:S(2)}, u32[]{:S(2)}) collective-permute-start(bf16[1280,128]{1,0:T(8,128)(2,1)S(1)} %shard_map.276.after_ref.own_ref), channel_id=1, source_target_pairs={{0,2},{1,5},{2,0},{3,7},{4,6},{5,1},{6,4},{7,3},{8,10},{9,13},{10,... | collective-permute-start | bytes 983048 | tf_op jit(solution)/shard_map/ppermute | solution.py:421
  79.1 1.3 %collective-permute-start.26 = (bf16[512,128]{1,0:T(8,128)(2,1)S(1)}, bf16[512,128]{1,0:T(8,128)(2,1)S(1)}, u32[]{:S(2)}, u32[]{:S(2)}) collective-permute-start(bf16[512,128]{1,0:T(8,128)(2,1)S(1)} %copy-done.3), channel_id=1, source_target_pairs={{0,1},{1,0},{2,3},{3,2},{4,5},{5,4},{6,7},{7,6},{8,9},{9,8},{10,11... | collective-permute-start | bytes 393224 | tf_op jit(solution)/shard_map/ppermute | solution.py:425

commit v3 on v2

--- a/solution.py
+++ b/solution.py
@@ -154,7 +154,7 @@
     result[...] = jnp.zeros_like(result)
 
 
-def time_kernel(steps, pk, table, tw, result):
+def time_kernel(steps, pk, table, tw, w1, result):
     total = result.shape[0] - PACK
     result[0:PACK] = pk[...]
     rows = jnp.concatenate([table[pl.ds(steps[i], 1)] for i in range(total)], axis=0)
@@ -168,9 +168,11 @@
 def first_kernel(x_own, x_recv, w_own, w_recv, pk_own, pk_recv, *rest):
     n = x_own.shape[0] // 2
     hid, act_t, act2_t, stat0, stat1, prm_out, wfull = rest[:7]
-    win2, wins = rest[7 : 7 + n], rest[7 + n :]
+    win2, (*wins, w_here, w_sem) = rest[7 : 7 + n], rest[7 + n :]
     me = lax.axis_index("mp")
     first = me == 0
+    w_copy = pltpu.make_async_copy(w_recv, w_here, w_sem)
+    w_copy.start()
     pk = join(first, pk_own[0:PACK], pk_recv[0:PACK], 1)
     prm_out[...] = pk
     xs = [join(first, x_own[me * n + m], x_recv[me * n + m], 1).astype(F32) for m in range(n)]
@@ -184,8 +186,9 @@
         a = u * sigmoid(u)
         act_t[:, m * PIX : (m + 1) * PIX] = a.astype(BF16).T
         put_windows(wins[m], a)
+    w_copy.wait()
     for t in range(9):
-        wfull[t] = join(first, w_own[t], w_recv[t], 1)
+        wfull[t] = join(first, w_own[t], w_here[t], 1)
     both = join(first, pk_own[PACK:], pk_recv[PACK:], 1)
     time_row = jnp.where(first, both[0:n], both[n : 2 * n])
     for m in range(n):
@@ -292,12 +295,13 @@
     sums[6:8] = jnp.zeros((2, C), F32)
 
 
-TAPS = (range(0, 5), range(5, 9))
+CONV1_TAPS = (range(0, 6), range(6, 9))
+CONV2_TAPS = (range(0, 5), range(5, 9))
 
 
 def conv2_grad_kernel(taps):
     def body(act_t, *rest):
-        win, (keep, send) = rest[:-2], rest[-2:]
+        win, (keep, send) = rest[: act_t.shape[1] // PIX], rest[-2:]
         first = lax.axis_index("mp") == 0
         for i, t in enumerate(taps):
             shifted = jnp.concatenate([window(w, 2 - t // 3, 2 - t % 3) for w in win], axis=0)
@@ -311,10 +315,9 @@
     return body
 
 
-def hidden_back_kernel(steps, after, hid, stat, wfull, prm, sums3, *rest):
+def hidden_back_kernel(steps, hid, stat, wfull, prm, *rest):
     n = hid.shape[0]
-    win3, (rows_keep, rows_send), win4 = rest[:n], rest[n : n + 2], rest[n + 2 :]
-    first = lax.axis_index("mp") == 0
+    win3, (sums, time_rows), win4 = rest[:n], rest[n : n + 2], rest[n + 2 :]
     gain, bias = prm[GAIN + 1 : GAIN + 2], prm[BIAS + 1 : BIAS + 2]
     gains, biases, times = [], [], []
     for m in range(n):
@@ -330,35 +333,37 @@
         low = back.astype(BF16).astype(F32)
         times.append(col_sum(low))
         put_windows(win4[m], low)
-    small = [
-        sum(gains), sums3[0:1], sum(biases), sums3[1:2], sum(times), sums3[2:6], jnp.zeros((7, C), F32),
-    ]
-    small_keep, small_send = split(first, jnp.concatenate(small, axis=0))
-    rows_keep[0:16] = small_keep
-    rows_send[0:16] = small_send
-    time_rows = jnp.concatenate(times, axis=0)
-    blank = jnp.zeros((n, HALF), F32)
-    for ref in (rows_keep, rows_send):
-        ref[16:32] = jnp.concatenate([time_rows[:, :HALF], blank, time_rows[:, HALF:], blank], axis=0)
+    rows, blank = jnp.concatenate(times, axis=0), jnp.zeros((n, HALF), F32)
+    time_rows[0:16] = jnp.concatenate([rows[:, :HALF], blank, rows[:, HALF:], blank], axis=0).astype(BF16)
+    lane = lax.broadcasted_iota(jnp.int32, (16, HALF), 1)
+    step_row = jnp.zeros((16, HALF), jnp.int32)
     for i in range(2 * n):
-        rows_keep[32 + i : 33 + i] = jnp.full((1, HALF), steps[i] >> 5, jnp.int32).astype(F32)
-        rows_keep[40 + i : 41 + i] = jnp.full((1, HALF), steps[i] & 31, jnp.int32).astype(F32)
+        step_row = jnp.where(lane == i, steps[i] >> 5, jnp.where(lane == 2 * n + i, steps[i] & 31, step_row))
+    time_rows[16:32] = step_row.astype(F32).astype(BF16)
+    sums[0:1] = sum(gains)
+    sums[1:2] = sum(biases)
+    sums[2:3] = sum(times)
+    sums[3:8] = jnp.zeros((5, C), F32)
 
 
 def conv1_grad_kernel(taps):
     def body(act_t, *rest):
-        win, (keep, send) = rest[:-2], rest[-2:]
+        win, others, (keep, send) = rest[: act_t.shape[1] // PIX], rest[act_t.shape[1] // PIX : -2], rest[-2:]
         first = lax.axis_index("mp") == 0
         for i, t in enumerate(taps):
             shifted = jnp.concatenate([window(w, 2 - t // 3, 2 - t % 3) for w in win], axis=0)
             g_keep, g_send = split(first, dot(act_t[...], shifted).astype(BF16))
             keep[i * C : (i + 1) * C] = g_keep
             send[i * C : (i + 1) * C] = g_send
+        if others:
+            rows = len(taps) * C
+            keep[rows:] = others[0][...]
+            send[rows:] = others[0][...]
 
     return body
 
 
-def input_back_kernel(after, x_own, x_recv, stat, wfull, prm, dmid, *rest):
+def input_back_kernel(after, x_own, x_recv, stat, wfull, prm, dmid, sums2, sums3, *rest):
     n = dmid.shape[0]
     win4, (keep, send, rows_keep, rows_send) = rest[:n], rest[n:]
     me = lax.axis_index("mp")
@@ -380,8 +385,11 @@
         d_keep, d_send = split(first, back + dmid[m])
         keep[m] = d_keep
         send[m] = d_send.astype(BF16)
-    small = jnp.concatenate([sum(gains), sum(biases), jnp.zeros((14, C), F32)], axis=0)
-    rows_keep[...], rows_send[...] = split(first, small)
+    small = [
+        sum(gains), sums2[0:1], sums3[0:1], sum(biases), sums2[1:2], sums3[1:2], sums2[2:3], sums3[2:6],
+        jnp.zeros((5, C), F32),
+    ]
+    rows_keep[...], rows_send[...] = split(first, jnp.concatenate(small, axis=0))
 
 
 def maps_kernel(after, out_keep, out_recv, grad_keep, grad_recv, out, grad, turn):
@@ -395,17 +403,14 @@
     turn[...] = jnp.zeros_like(turn)
 
 
-EXTRA = 48
+EXTRA, SUMS = 32, 16
 
 
 def bits_of(count):
     bits = list(range(count.bit_length() - 1))
     cut = len(bits) // 2
-    return [(bits[:cut], bits[cut:]), (bits[:cut][::-1], bits[cut:][::-1])]
-
-
-def piece_of(rows, pieces):
-    return -(-rows // (16 * pieces)) * 16
+    low, high = bits[:cut], bits[cut:]
+    return [[(high, low), (high[::-1], low)], [(low, high), (low[::-1], high[::-1])]]
 
 
 def digit(bits):
@@ -429,167 +434,131 @@
     return pl.ds(pl.multiple_of(index * rows, 16), rows)
 
 
-def start_scatter(pairs, rows, bits, after=()):
+def added(a, b):
+    return (a.astype(F32) + b.astype(F32)).astype(BF16)
+
+
+def start_exchanges(chains, groups):
+    rows = [chain.rows for chain in chains]
+
     def body(*refs):
-        sources, (own, send, values) = refs[: 2 * len(pairs)], refs[-3:]
-        at = 0
-        for i in range(len(pairs)):
-            keep, recv = sources[2 * i], sources[2 * i + 1]
-            size = keep.shape[0]
-            values[at : at + size] = (keep[...].astype(F32) + recv[...].astype(F32)).astype(BF16)
-            at += size
-        if at < rows:
-            values[at:rows] = jnp.zeros((rows - at, HALF), BF16)
-        me = digit(bits)
-        own[...] = values[part(me, rows // 2)]
-        send[...] = values[part(1 - me, rows // 2)]
-
-    shape = ((rows // 2, HALF), BF16)
-    args = [v for pair in pairs for v in pair]
-    specs = {len(args) + i: ANYWHERE for i in range(len(after))}
-    return call(body, [shape] * 2, *args, *after, scratch=[pltpu.VMEM((rows, HALF), BF16)], specs=specs)
-
-
-def next_scatter(own, recv, bits, after):
-    rows = own.shape[0]
-
-    def body(own_ref, recv_ref, after_ref, out, send, values):
-        values[...] = (own_ref[...].astype(F32) + recv_ref[...].astype(F32)).astype(BF16)
-        me = digit(bits)
-        out[...] = values[part(me, rows // 2)]
-        send[...] = values[part(1 - me, rows // 2)]
-
-    shape = ((rows // 2, HALF), BF16)
-    scratch = [pltpu.VMEM((rows, HALF), BF16)]
-    return call(body, [shape] * 2, own, recv, after, scratch=scratch, specs={2: ANYWHERE})
-
-
-def end_scatter(own, recv, keep, other, after):
-    rows, extra = own.shape[0], keep.shape[0]
-
-    def body(own_ref, recv_ref, keep_ref, other_ref, after_ref, out):
-        out[0:rows] = (own_ref[...].astype(F32) + recv_ref[...].astype(F32)).astype(BF16)
-        out[rows : rows + 16] = (keep_ref[0:16] + other_ref[0:16]).astype(BF16)
-        if extra > 16:
-            first = lax.axis_index("mp") == 0
-            sides = [join(first, keep_ref[at : at + 4], other_ref[at : at + 4], 0) for at in (16, 24)]
-            out[rows + 16 : rows + 32] = jnp.concatenate(sides, axis=0).astype(BF16)
-            out[rows + 32 : rows + 48] = keep_ref[32:48].astype(BF16)
-
-    return call(body, [((rows + extra, HALF), BF16)], own, recv, keep, other, after, specs={4: ANYWHERE})[0]
-
-
-def sum_blocks(own, recv, rows, bits, after):
-    rest = own.shape[0] - rows
-
-    def body(own_ref, recv_ref, after_ref, out):
-        out[0:rows] = (own_ref[0:rows].astype(F32) + recv_ref[0:rows].astype(F32)).astype(BF16)
-        if rest:
-            low = digit(bits) == 0
-            mine, theirs = own_ref[rows:], recv_ref[rows:]
-            out[rows : rows + rest] = jnp.where(low, mine, theirs)
-            out[rows + rest :] = jnp.where(low, theirs, mine)
-
-    return call(body, [((rows + 2 * rest, HALF), BF16)], own, recv, after, specs={2: ANYWHERE})[0]
-
-
-def next_gather(own, recv, bits, after):
-    rows = own.shape[0]
-
-    def body(own_ref, recv_ref, after_ref, out):
-        me = digit(bits)
-        out[part(me, rows)] = own_ref[...]
-        out[part(1 - me, rows)] = recv_ref[...]
-
-    return call(body, [((2 * rows, HALF), BF16)], own, recv, after, specs={2: ANYWHERE})[0]
-
-
-def owner(halving, whole, order, p, q):
-    cut, total = len(halving[order]), 0
-    for i, bit in enumerate(halving[order]):
-        total |= (p >> (cut - 1 - i) & 1) << bit
-    for i, bit in enumerate(whole[order]):
-        total |= (q >> i & 1) << bit
-    return total
-
-
-def late_result(gains, biases, own, recv, bits, halving, whole, piece):
-    pieces, blocks, extra_rows = 1 << len(halving[0]), 1 << len(whole[0]), 16
-    full = piece + extra_rows * blocks
-
-    def body(gains_ref, biases_ref, own_ref, recv_ref, out, gains, biases, values, extra):
-        me = digit(bits)
-        values[part(me, own.shape[0])] = own_ref[...]
-        values[part(1 - me, own.shape[0])] = recv_ref[...]
+        refs = list(refs)
+        sources = [[(refs.pop(0), refs.pop(0)) for _ in pairs] for pairs in groups]
+        outs, buffers = refs[:4], refs[4:]
         first = lax.axis_index("mp") == 0
-        for p in range(pieces):
-            rows = min(piece, 9 * C - p * piece)
-            if rows > 0:
-                out[p * piece : p * piece + rows] = values[p * full : p * full + rows].astype(F32)
-            for q in range(blocks):
-                base = p * full + piece + q * extra_rows
-                at = jnp.where(first, owner(halving, whole, 0, p, q), owner(halving, whole, 1, p, q))
-                extra[at] = values[base : base + extra_rows].astype(F32)
-        small = extra[0]
-        for i in range(1, pieces * blocks):
-            small = small + extra[i]
-        gains[0:1] = small[0:1]
-        gains[1:3] = gains_ref[...]
-        biases[0:1] = small[1:2]
-        biases[1:3] = biases_ref[...]
-
-    scratch = [pltpu.VMEM((2 * own.shape[0], HALF), BF16), pltpu.VMEM((pieces * blocks, extra_rows, HALF), F32)]
-    outs = [((9 * C, HALF), F32), ((3, HALF), F32), ((3, HALF), F32)]
-    return call(body, outs, gains, biases, own, recv, scratch=scratch)
-
-
-def early_result(own, recv, bits, halving, whole, piece, table, tw_own, tw_recv, after):
+        time_own, time_other = [ref[ref.shape[0] - EXTRA :].astype(F32) for ref in sources[0][0]]
+        sides = [join(first, time_own[at : at + 4], time_other[at : at + 4], 0) for at in (0, 8)]
+        extra = jnp.concatenate(sides + [time_own[16:32]], axis=0).astype(BF16)
+        for g, values in enumerate(buffers):
+            end = 0
+            for i, (keep, recv) in enumerate(sources[g]):
+                size = keep.shape[0] - (EXTRA if g == 0 and i == 0 else 0)
+                values[end : end + size] = added(keep[0:size], recv[0:size])
+                end += size
+            if end < rows[g]:
+                values[end : rows[g]] = jnp.zeros((rows[g] - end, HALF), BF16)
+            me, half = digit(chains[g].steps[0]), rows[g] // 2
+            for index, ref in zip((me, 1 - me), outs[2 * g : 2 * g + 2]):
+                ref[0:half] = values[part(index, half)]
+                if g == 0:
+                    ref[half:] = extra
+
+    outs = [((r // 2 + (EXTRA if g == 0 else 0), HALF), BF16) for g, r in enumerate(rows) for _ in range(2)]
+    args = [v for pairs in groups for pair in pairs for v in pair]
+    results = call(body, outs, *args, scratch=[pltpu.VMEM((r, HALF), BF16) for r in rows])
+    for g, chain in enumerate(chains):
+        chain.own = results[2 * g]
+        chain.recv = swap_dp(results[2 * g + 1], chain.steps[0])
+        chain.rows //= 2
+
+
+class Exchange:
+    def __init__(self, order, pairs, extra):
+        halving, whole = [list(zip(*[core[i] for core in order])) for i in range(2)]
+        self.cut, self.whole = len(halving), len(halving) + len(whole)
+        self.steps = halving + whole + halving[::-1]
+        self.bits = [[core[0] + core[1] for core in order][c] for c in range(2)]
+        self.at = 0
+        pieces = 1 << self.cut
+        self.piece = -(-(sum(keep.shape[0] for keep, _ in pairs) - extra) // (16 * pieces)) * 16
+        self.rows = self.piece * pieces
+
+    def step(self, after, small=()):
+        bits, following = self.steps[self.at : self.at + 2]
+        self.at += 1
+        head, rest = self.rows, self.own.shape[0] - self.rows
+        halve, ends, last = self.at < self.cut, self.at == self.cut, self.at == self.whole
+        gather = self.at > self.whole
+        with_small = SUMS if small and ends else 0
+
+        def body(own, recv, after_ref, *refs):
+            small_refs, outs = refs[: len(small) if ends else 0], refs[len(small) if ends else 0 :]
+            me = digit(bits)
+            out = outs[0]
+            if gather:
+                out[part(me, head)] = own[...]
+                out[part(1 - me, head)] = recv[...]
+                return
+            tails = []
+            if halve:
+                values, send = outs[-1], outs[1]
+                values[...] = added(own[0:head], recv[0:head])
+                index = digit(following)
+                out[0 : head // 2] = values[part(index, head // 2)]
+                send[0 : head // 2] = values[part(1 - index, head // 2)]
+                tails = [(out, head // 2), (send, head // 2)]
+            else:
+                out[0:head] = added(own[0:head], recv[0:head])
+                if with_small:
+                    out[head : head + SUMS] = (small_refs[0][...] + small_refs[1][...]).astype(BF16)
+                tails = [(outs[-1], 0 if last else head + with_small)]
+            if rest:
+                low = me == 0
+                mine, theirs = own[head:], recv[head:]
+                for ref, at in tails:
+                    ref[at : at + rest] = jnp.where(low, mine, theirs)
+                    ref[at + rest : at + 2 * rest] = jnp.where(low, theirs, mine)
+
+        def shape(rows):
+            return ((rows, HALF), BF16)
+
+        if gather:
+            outs, self.rows = [shape(2 * head)], 2 * head
+        elif halve:
+            outs, self.rows = [shape(head // 2 + 2 * rest)] * 2, head // 2
+        else:
+            self.rows = head + with_small
+            outs = [shape(self.rows), shape(2 * rest)] if last and rest else [shape(self.rows + 2 * rest)]
+        args = (self.own, self.recv, after) + (tuple(small) if ends else ())
+        scratch = [pltpu.VMEM((head, HALF), BF16)] if halve else []
+        results = call(body, outs, *args, scratch=scratch, specs={2: ANYWHERE})
+        self.own = results[0]
+        if last and rest:
+            self.gathered = results[1]
+        self.recv = swap_dp(results[1] if halve else self.own, following)
+
+
+def time_results(gathered, order, table, tw_own, tw_recv, after):
     steps, width = table.shape
     padded = -(-steps // HALF) * HALF
-    pieces, blocks = 1 << len(halving[0]), 1 << len(whole[0])
-    full = piece + EXTRA * blocks
-
-    def body(own_ref, recv_ref, table_ref, tw_own_ref, tw_recv_ref, after_ref, *refs):
-        conv2, qkv, out_w, table_grad, tw_grad, gains, biases, conv_b, qkv_b, out_b, time_b = refs[:11]
-        values, extra, act_high, act_low = refs[11:]
-        me = digit(bits)
-        values[part(me, own.shape[0])] = own_ref[...]
-        values[part(1 - me, own.shape[0])] = recv_ref[...]
+    blocks = gathered.shape[0] // EXTRA
+    maps = 8 * blocks
+
+    def owner(core, block):
+        return sum((block >> i & 1) << bit for i, bit in enumerate(order[core]))
+
+    def body(rows_ref, table_ref, tw_own_ref, tw_recv_ref, after_ref, *refs):
+        table_grad, tw_grad, time_b, turn, extra, act_high, act_low = refs
         first = lax.axis_index("mp") == 0
-
-        def rows_of(start, size):
-            found = []
-            while size:
-                at, left = start % piece, piece - start % piece
-                now = min(size, left)
-                base = start // piece * full + at
-                found.append(values[base : base + now].astype(F32))
-                start, size = start + now, size - now
-            return jnp.concatenate(found, axis=0)
-
-        for t in range(9):
-            for h in range(2):
-                conv2[t, :, h * HALF : (h + 1) * HALF] = rows_of((2 * t + h) * HALF, HALF)
-        for j in range(3):
-            qkv[j] = rows_of((9 + j) * C, C)
-        for h in range(2):
-            out_w[:, h * HALF : (h + 1) * HALF] = rows_of(12 * C + h * HALF, HALF)
-        for p in range(pieces):
-            for q in range(blocks):
-                base = p * full + piece + q * EXTRA
-                at = jnp.where(first, owner(halving, whole, 0, p, q), owner(halving, whole, 1, p, q))
-                extra[at] = values[base : base + EXTRA].astype(F32)
-        small = extra[0, 0:16]
-        for i in range(1, pieces * blocks):
-            small = small + extra[i, 0:16]
-        gains[...] = small[0:2]
-        biases[...] = small[2:4]
-        conv_b[...] = small[4:6]
-        qkv_b[...] = small[6:8]
-        out_b[...] = small[8:9]
-        maps = 8 * pieces * blocks
-        left, right = extra[:, 16:24].reshape(maps, HALF), extra[:, 24:32].reshape(maps, HALF)
-        step = (extra[:, 32:40] * 32.0 + extra[:, 40:48]).reshape(maps, HALF)[:, 0:1].astype(jnp.int32)
+        for block in range(blocks):
+            at = jnp.where(first, owner(0, block), owner(1, block))
+            extra[at] = rows_ref[block * EXTRA : (block + 1) * EXTRA].astype(F32)
+        left, right = extra[:, 0:8].reshape(maps, HALF), extra[:, 8:16].reshape(maps, HALF)
+        step_rows = extra[:, 16:24].reshape(maps, HALF)
+        lane = lax.broadcasted_iota(jnp.int32, (maps, HALF), 1)
+        row = lax.broadcasted_iota(jnp.int32, (maps, HALF), 0) & 7
+        weight = jnp.where(lane == row, 32.0, jnp.where(lane == row + 8, 1.0, 0.0))
+        step = jnp.sum(step_rows * weight, axis=1, keepdims=True).astype(jnp.int32)
         mine = jnp.where(first, left, right)
         time_b[...] = col_sum(mine)
         lane = lax.broadcasted_iota(jnp.int32, (maps, padded), 1)
@@ -613,19 +582,72 @@
         step_low = (by_step - step_high.astype(F32)).astype(BF16)
         high, low = act_high[...].astype(BF16), act_low[...].astype(BF16)
         tw_grad[...] = (dot(step_high, high) + dot(step_high, low) + dot(step_low, high)).T
-
-    outs = [
-        ((9, HALF, C), F32), ((3, C, HALF), F32), ((HALF, C), F32), (table.shape, F32), (tw_own.shape, F32),
-        ((2, HALF), F32), ((2, HALF), F32), ((2, HALF), F32), ((2, HALF), F32), ((1, HALF), F32), ((1, HALF), F32),
-    ]
+        turn[...] = jnp.zeros_like(turn)
+
+    outs = [(table.shape, F32), (tw_own.shape, F32), ((1, HALF), F32), ((8, HALF), F32)]
     scratch = [
-        pltpu.VMEM((2 * own.shape[0], HALF), BF16),
-        pltpu.VMEM((pieces * blocks, EXTRA, HALF), F32),
+        pltpu.VMEM((blocks, EXTRA, HALF), F32),
         pltpu.VMEM((padded, width), F32),
         pltpu.VMEM((padded, width), F32),
     ]
-    args = (own, recv, table, tw_own, tw_recv, after)
-    return call(body, outs, *args, scratch=scratch, specs={5: ANYWHERE}, limit=24)
+    args = (gathered, table, tw_own, tw_recv, after)
+    return call(body, outs, *args, scratch=scratch, specs={4: ANYWHERE}, limit=24)
+
+
+def weight_results(chains, split_at):
+    def body(own1, recv1, own2, recv2, *refs):
+        conv1, conv2, qkv, out_w, gains, biases, conv_b, qkv_b, out_b = refs[:9]
+        reads = []
+        for chain, own, recv, values in zip(chains, (own1, own2), (recv1, recv2), refs[9:]):
+            me, rows = digit(chain.steps[-1]), own.shape[0]
+            values[part(me, rows)] = own[...]
+            values[part(1 - me, rows)] = recv[...]
+            reads.append(row_reader(values, chain.piece, values.shape[0] >> chain.cut))
+        conv1[0:split_at] = reads[0](0, split_at)
+        conv1[split_at : 9 * C] = reads[1](0, 9 * C - split_at)
+        at = 9 * C - split_at
+        for t in range(9):
+            for h in range(2):
+                conv2[t, :, h * HALF : (h + 1) * HALF] = reads[1](at + (2 * t + h) * HALF, HALF)
+        at += 9 * C
+        for j in range(3):
+            qkv[j] = reads[1](at + j * C, C)
+        for h in range(2):
+            out_w[:, h * HALF : (h + 1) * HALF] = reads[1](at + 3 * C + h * HALF, HALF)
+        values, chain = refs[9], chains[0]
+        full = values.shape[0] >> chain.cut
+        small = None
+        for p in range(1 << chain.cut):
+            base = p * full + chain.piece
+            block = values[base : base + SUMS].astype(F32)
+            small = block if small is None else small + block
+        gains[...] = small[0:3]
+        biases[...] = small[3:6]
+        conv_b[...] = small[6:8]
+        qkv_b[...] = small[8:10]
+        out_b[...] = small[10:11]
+
+    outs = [
+        ((9 * C, HALF), F32), ((9, HALF, C), F32), ((3, C, HALF), F32), ((HALF, C), F32),
+        ((3, HALF), F32), ((3, HALF), F32), ((2, HALF), F32), ((2, HALF), F32), ((1, HALF), F32),
+    ]
+    scratch = [pltpu.VMEM((2 * chain.own.shape[0], HALF), BF16) for chain in chains]
+    args = [v for chain in chains for v in (chain.own, chain.recv)]
+    return call(body, outs, *args, scratch=scratch)
+
+
+def row_reader(values, piece, full):
+    def read(start, size):
+        found = []
+        while size:
+            at, left = start % piece, piece - start % piece
+            now = min(size, left)
+            base = start // piece * full + at
+            found.append(values[base : base + now].astype(F32))
+            start, size = start + now, size - now
+        return jnp.concatenate(found, axis=0)
+
+    return read
 
 
 def on_device(
@@ -634,9 +656,6 @@
 ):
     count = lax.axis_size("dp")
     orders = bits_of(count)
-    halving, whole = [[order[i] for order in orders] for i in range(2)]
-    halving_steps, whole_steps = list(zip(*halving)), list(zip(*whole))
-    pieces = 1 << len(halving_steps)
     total = maps_in.shape[0]
     n = total // 2
     maps_shape, half_shape = (n, PIX, C), (n, PIX, HALF)
@@ -650,7 +669,8 @@
         [norm_gain, norm_bias, conv_bias, qkv_bias, out_bias[None], temb_bias[None], blank]
     )
     pk_own = call(
-        time_kernel, [((PACK + total, HALF), F32)], timesteps, pk_own, temb_table, temb_weight, specs={0: SCALAR},
+        time_kernel, [((PACK + total, HALF), F32)], timesteps, pk_own, temb_table, temb_weight, w1_own,
+        specs={0: SCALAR},
     )[0]
     pk_recv = swap_mp(pk_own)
     tw_recv = swap_mp(temb_weight)
@@ -668,7 +688,8 @@
             ((2 * n, C), F32), ((2 * n, C), F32), ((PACK, C), F32), weight_shape,
         ] + [WIN] * n,
         maps_in, x_recv, w1_own, w1_recv, pk_own, pk_recv,
-        scratch=[pltpu.VMEM(*WIN)] * n,
+        scratch=[pltpu.VMEM(*WIN)] * n + [pltpu.VMEM(w1_own.shape, BF16), pltpu.SemaphoreType.DMA],
+        specs={3: ANYWHERE},
         flops=10**11,
     )
     tile_f32, tile_low = pltpu.VMEM((PIX, C), F32), pltpu.VMEM((PIX, C), BF16)
@@ -684,76 +705,56 @@
         + [tile_f32] * (3 * n) + [tile_low] * n + [three_low] * n + [tile_low] * (3 * n) + [three_low] * n,
     )
     wg_recv = swap_mp(wg_send)
-    early_pairs = []
-    for taps in TAPS:
-        shape = ((len(taps) * C, HALF), BF16)
-        keep, send = call(conv2_grad_kernel(taps), [shape, shape], act2_t, *win3)
-        early_pairs.append((keep, swap_mp(send)))
-    early_pairs.append((wg_keep, wg_recv))
-    early_piece, late_piece = piece_of(13 * C, pieces), piece_of(9 * C, pieces)
-    early, early_send = start_scatter(early_pairs, early_piece * pieces, halving_steps[0])
-    early_recv = swap_dp(early_send, halving_steps[0])
-    rows_keep, rows_send, *win4 = call(
+    sums2, time_rows, *win4 = call(
         hidden_back_kernel,
-        [((EXTRA, HALF), F32), ((32, HALF), F32)] + [WIN] * n,
-        timesteps, early, hid, stat1, w2_full, prm, sums3, *win3,
-        specs={0: SCALAR, 1: ANYWHERE},
+        [((8, C), F32), ((EXTRA, HALF), BF16)] + [WIN] * n,
+        timesteps, hid, stat1, w2_full, prm, *win3,
+        specs={0: SCALAR},
+    )
+
+    def conv_grad(kernel, taps, act_t, windows, others=(), after=()):
+        shape = ((len(taps) * C + sum(v.shape[0] for v in others), HALF), BF16)
+        specs = {1 + n + len(others) + i: ANYWHERE for i in range(len(after))}
+        keep, send = call(kernel(taps), [shape, shape], act_t, *windows, *others, *after, specs=specs)
+        return keep, swap_mp(send)
+
+    conv1_pairs = [
+        conv_grad(conv1_grad_kernel, CONV1_TAPS[0], act1_t, win4, others=(time_rows,)),
+        conv_grad(conv1_grad_kernel, CONV1_TAPS[1], act1_t, win4),
+    ]
+    arrived = (wg_recv,) + tuple(recv for _, recv in conv1_pairs)
+    conv2_pairs = [
+        conv_grad(conv2_grad_kernel, CONV2_TAPS[0], act2_t, win3, after=(conv1_pairs[1][0],)),
+        conv_grad(conv2_grad_kernel, CONV2_TAPS[1], act2_t, win3, after=arrived),
+    ]
+    groups = [conv1_pairs[:1], conv1_pairs[1:] + conv2_pairs + [(wg_keep, wg_recv)]]
+    chains = [Exchange(order, pairs, extra) for order, pairs, extra in zip(orders, groups, (EXTRA, 0))]
+    early, late = chains
+    start_exchanges(chains, groups)
+    mg_keep, mg_send, rows_keep, rows_send = call(
+        input_back_kernel,
+        [(half_shape, F32), (half_shape, BF16), ((SUMS, HALF), F32), ((SUMS, HALF), F32)],
+        late.own, maps_in, x_recv, stat0, w1_full, prm, dmid, sums2, sums3, *win4,
+        specs={0: ANYWHERE},
     )
     rows_recv = swap_mp(rows_send)
-    late_pairs = []
-    for taps in TAPS:
-        shape = ((len(taps) * C, HALF), BF16)
-        keep, send = call(conv1_grad_kernel(taps), [shape, shape], act1_t, *win4)
-        late_pairs.append((keep, swap_mp(send)))
-    late, late_send = start_scatter(late_pairs, late_piece * pieces, halving_steps[0])
-    late_recv = swap_dp(late_send, halving_steps[0])
-
-    turn = late
-    for i, bits in enumerate(halving_steps[1:]):
-        early, early_send = next_scatter(early, early_recv, bits, turn)
-        early_recv = swap_dp(early_send, bits)
-        turn = early
+    out_recv, mg_recv = swap_mp(out_send), swap_mp(mg_send)
+    turn = rows_keep
+    for i in range(len(early.steps) - 1):
+        early.step(turn, (rows_keep, rows_recv))
+        late.step(early.own)
+        turn = late.own
         if i == 0:
-            mg_keep, mg_send, last_keep, last_send = call(
-                input_back_kernel,
-                [(half_shape, F32), (half_shape, BF16), ((16, HALF), F32), ((16, HALF), F32)],
-                turn, maps_in, x_recv, stat0, w1_full, prm, dmid, *win4,
+            maps_out, maps_grad, turn = call(
+                maps_kernel, [(maps_in.shape, BF16), (maps_in.shape, F32), ((8, HALF), F32)],
+                turn, out_keep, out_recv, mg_keep, mg_recv,
                 specs={0: ANYWHERE},
             )
-            last_recv = swap_mp(last_send)
-            out_recv, mg_recv = swap_mp(out_send), swap_mp(mg_send)
-            turn = last_keep
-        late, late_send = next_scatter(late, late_recv, bits, turn)
-        late_recv = swap_dp(late_send, bits)
-        turn = late
-    early = end_scatter(early, early_recv, rows_keep, rows_recv, turn)
-    early_recv = swap_dp(early, whole_steps[0])
-    maps_out, maps_grad, turn = call(
-        maps_kernel, [(maps_in.shape, BF16), (maps_in.shape, F32), ((8, HALF), F32)],
-        early, out_keep, out_recv, mg_keep, mg_recv,
-        specs={0: ANYWHERE},
-    )
-    late = end_scatter(late, late_recv, last_keep, last_recv, turn)
-    late_recv = swap_dp(late, whole_steps[0])
-    gathers = halving_steps[::-1]
-    following = whole_steps[1:] + gathers[:1]
-    for bits, next_bits in zip(whole_steps, following):
-        early = sum_blocks(early, early_recv, early_piece, bits, late)
-        early_recv = swap_dp(early, next_bits)
-        late = sum_blocks(late, late_recv, late_piece, bits, early)
-        late_recv = swap_dp(late, next_bits)
-    for bits, next_bits in zip(gathers[:-1], gathers[1:]):
-        early = next_gather(early, early_recv, bits, late)
-        early_recv = swap_dp(early, next_bits)
-        late = next_gather(late, late_recv, bits, early)
-        late_recv = swap_dp(late, next_bits)
-    bits = gathers[-1]
-    conv2, qkv, out_w, table_grad, tw_grad, gains, biases, conv_b, qkv_b, out_b, time_b = early_result(
-        early, early_recv, bits, halving, whole, early_piece, temb_table, temb_weight, tw_recv, late,
-    )
-    conv1, gains, biases = late_result(
-        gains, biases, late, late_recv, bits, halving, whole, late_piece,
-    )
+        if i == early.whole - 1:
+            table_grad, tw_grad, time_b, turn = time_results(
+                early.gathered, early.bits, temb_table, temb_weight, tw_recv, turn,
+            )
+    conv1, conv2, qkv, out_w, gains, biases, conv_b, qkv_b, out_b = weight_results(chains, len(CONV1_TAPS[0]) * C)
     return (
         maps_out, maps_grad, table_grad, gains, biases, conv1.reshape(3, 3, C, HALF), conv_b, tw_grad,
         time_b.reshape(HALF), conv2.reshape(3, 3, HALF, C), jnp.transpose(qkv, (1, 0, 2)), qkv_b, out_w,

time: 86.7 us -> 80.7 us (0.931)
  waiting for transfers between devices: 34.6 us -> 29.8 us
  local copies, waits for them, and re-layouts: 2.66 us -> 1.65 us
    ppermute x12, waiting for transfers between devices: 30.4 us -> 27 us  [swap_dp(): return lax.ppermute(values, ('dp', 'mp'), pairs)]
    ppermute x17 -> x16, waiting for transfers between devices: 4.26 us -> 2.77 us  [swap_mp(): return lax.ppermute(values, 'mp', [(0, 1), (1, 0)])]
    unnamed x30, local copies, waits for them, and re-layouts: 2.62 us -> 1.61 us
    pallas_call x25 -> x24, Pallas kernels: 27.2 us -> 26.4 us  [call(): pl.pallas_call(body, out_shape=tuple((jax.ShapeDtypeStruct(s, d) for s, d...]
    ppermute x17 -> x16, starting transfers between devices: 4.41 us -> 4.49 us  [swap_mp(): return lax.ppermute(values, 'mp', [(0, 1), (1, 0)])]
  transfers between devices with their start and end apart: 29 -> 28, of which waited for: 13 -> 13; matrix products, arithmetic and copies ran while one was open for 0% -> 0% of each run, Pallas kernels for 22% -> 17%
where the time goes in v3:
time: 80.7 us; the launch traced here: 80.5 us
  waiting for transfers between devices  29.8 us (37%)
  Pallas kernels  26.4 us (33%)
  starting transfers between devices  21.7 us (27%)
  local copies, waits for them, and re-layouts  1.65 us (2%)
  between operations  0.95 us (1%)
    ppermute x12, waiting for transfers between devices, swap_dp(): return lax.ppermute(values, ('dp', 'mp'), pairs)  27 us
    pallas_call x24, Pallas kernels, call(): pl.pallas_call(body, out_shape=tuple((jax.ShapeDtypeStruct(s, d) for s, d...  26.4 us
    ppermute x12, starting transfers between devices, swap_dp(): return lax.ppermute(values, ('dp', 'mp'), pairs)  17.2 us
    ppermute x16, starting transfers between devices, swap_mp(): return lax.ppermute(values, 'mp', [(0, 1), (1, 0)])  4.49 us
    ppermute x16, waiting for transfers between devices, swap_mp(): return lax.ppermute(values, 'mp', [(0, 1), (1, 0)])  2.77 us
  transfers between devices with their start and end apart: 28, of which 13 were waited for; matrix products, arithmetic and copies ran while one was open for 0% of the time, Pallas kernels for 17%

profile of v3, /device:TPU:0, one launch (start us, length us, event | category | flops | bytes accessed | tf_op | source)
XLA Modules:
  0.0 80.5 jit_solution(9030002325914880553)
XLA Ops:
  0.7 0.5 collective-permute-start.1
  1.3 0.1 collective-permute-start
  1.3 0.0 copy-done.11
  1.4 0.0 copy-done.12
  1.4 0.4 copy-done.2
  1.8 0.0 copy-done.5
  1.8 1.1 %copy-done = f32[1000,512]{1,0:T(8,128)S(1)} copy-done((f32[1000,512]{1,0:T(8,128)S(1)}, f32[1000,512]{1,0:T(8,128)}, u32[]{:S(2)}) %copy-start) | copy-done | bytes 2048024
  3.0 0.7 shard_map.255.pk_own
  3.7 0.4 collective-permute-start.2
  4.1 0.3 collective-permute-start.3
  4.5 0.2 collective-permute-start.5
  4.7 0.3 collective-permute-done.2.pk_recv
  5.0 0.3 collective-permute-start.4
  5.3 0.2 collective-permute-start.6
  5.5 3.6 %shard_map.256 = (f32[4,256,256]{2,1,0:T(8,128)S(1)}, bf16[256,1024]{1,0:T(8,128)(2,1)S(1)}, bf16[256,1024]{1,0:T(8,128)(2,1)S(1)}, f32[8,256]{1,0:T(8,128)S(1)}...) custom-call(bf16[8,256,128]{2,1,0:T(8,128)(2,1)S(1)} %copy-done.1, ...), custom_call_target="tpu_custom_call" | custom-call | flops 99999997952 | tf_op jit(solution)/shard_map/pallas_call | solution.py:24
  9.2 5.8 %shard_map.257 = (bf16[4,256,128]{2,1,0:T(8,128)(2,1)S(1)}, bf16[4,256,128]{2,1,0:T(8,128)(2,1)S(1)}, f32[4,256,256]{2,1,0:T(8,128)S(1)}, bf16[1024,128]{1,0:T(8...) custom-call(bf16[8,256,128]{2,1,0:T(8,128)(2,1)S(1)} %copy-done.1, ...), custom_call_target="tpu_custom_call" | custom-call | flops 1 | tf_op jit(solution)/shard_map/pallas_call | solution.py:24
  14.9 3.2 %shard_map.258 = (f32[8,256]{1,0:T(8,128)S(1)}, bf16[32,128]{1,0:T(8,128)(2,1)S(1)}, bf16[3,288,256]{2,1,0:T(8,128)(2,1)S(1)}, bf16[3,288,256]{2,1,0:T(8,128)(2,...) custom-call(s32[8]{0:T(128)S(1)} %copy-done.8, f32[4,256,256]{2,1,0:T(8,128)S(1)} %get-tuple-element.81.hid, ...), custom_call_target="tpu_custom_call" | custom-call | flops 1 | tf_op jit(solution)/shard_map/pallas_call | solution.py:24
  18.2 1.0 %shard_map.259 = (bf16[1568,128]{1,0:T(8,128)(2,1)S(1)}, bf16[1568,128]{1,0:T(8,128)(2,1)S(1)}) custom-call(bf16[256,1024]{1,0:T(8,128)(2,1)S(1)} %get-tuple-element.80.act_t, bf16[3,288,256]{2,1,0:T(8,128)(2,1)S(1)} %get-tuple-element.93.rest_0_, bf16[3,288,256]{2,1,0:T(8,128)(2,1)S(1)} %get-tuple-element.94.rest_1_, ...), custom_call_target="tpu_custom_call" | custom-call | flops 1 | tf_op jit(solution)/shard_map/pallas_call | solution.py:24
  19.2 0.4 collective-permute-start.7
  19.6 0.3 collective-permute-start.10
  19.8 0.6 shard_map.260
  20.4 0.3 collective-permute-start.8
  20.7 0.9 %shard_map.261 = (bf16[1280,128]{1,0:T(8,128)(2,1)S(1)}, bf16[1280,128]{1,0:T(8,128)(2,1)S(1)}) custom-call(bf16[256,1024]{1,0:T(8,128)(2,1)S(1)} %get-tuple-element.102.act_t, bf16[3,288,256]{2,1,0:T(8,128)(2,1)S(1)} %get-tuple-element.89.rest_0_, bf16[3,288,256]{2,1,0:T(8,128)(2,1)S(1)} %get-tuple-element.90.rest_1_, ...), custom_call_target="tpu_custom_call" | custom-call | flops 1 | tf_op jit(solution)/shard_map/pallas_call | solution.py:24
  21.6 0.3 collective-permute-start.9
  21.9 0.7 shard_map.262
  22.6 0.3 collective-permute-start.11
  23.0 0.3 collective-permute-done.9.refs_5_
  23.3 1.0 %collective-permute-done.11.refs_7_ = bf16[1024,128]{1,0:T(8,128)(2,1)S(1)} collective-permute-done((bf16[1024,128]{1,0:T(8,128)(2,1)S(1)}, bf16[1024,128]{1,0:T(8,128)(2,1)S(1)}, u32[]{:S(2)}, u32[]{:S(2)}) %collective-permute-start.11) | collective-permute-done | bytes 262176 | tf_op jit(solution)/shard_map/ppermute | solution.py:430
  24.2 0.7 shard_map.263
  25.0 2.8 %collective-permute-start.12 = (bf16[2048,128]{1,0:T(8,128)(2,1)S(1)}, bf16[2048,128]{1,0:T(8,128)(2,1)S(1)}, u32[]{:S(2)}, u32[]{:S(2)}) collective-permute-start(bf16[2048,128]{1,0:T(8,128)(2,1)S(1)} %get-tuple-element.110), channel_id=1, source_target_pairs={{0,2},{1,5},{2,0},{3,7},{4,6},{5,1},{6,4},{7,3},{8,10},{9,13},{10,... | collective-permute-start | bytes 1572872 | tf_op jit(solution)/shard_map/ppermute | solution.py:426
  27.8 1.6 %collective-permute-start.13 = (bf16[800,128]{1,0:T(8,128)(2,1)S(1)}, bf16[800,128]{1,0:T(8,128)(2,1)S(1)}, u32[]{:S(2)}, u32[]{:S(2)}) collective-permute-start(bf16[800,128]{1,0:T(8,128)(2,1)S(1)} %get-tuple-element.112), channel_id=1, source_target_pairs={{0,8},{1,17},{2,10},{3,19},{4,12},{5,21},{6,14},{7,23},{8,0},{9,25... | collective-permute-start | bytes 614408 | tf_op jit(solution)/shard_map/ppermute | solution.py:426
  29.4 0.7 collective-permute-start.14
  30.1 2.3 %shard_map.264 = (f32[4,256,128]{2,1,0:T(8,128)S(1)}, bf16[4,256,128]{2,1,0:T(8,128)(2,1)S(1)}, f32[16,128]{1,0:T(8,128)S(1)}, f32[16,128]{1,0:T(8,128)S(1)}) custom-call(bf16[2048,128]{1,0:T(8,128)(2,1)S(1)} %get-tuple-element.109.after.own, bf16[8,256,128]{2,1,0:T(8,128)(2,1)S(1)} %copy-done.1, bf16[8,256,128]{2,1,0:T(8,128)(2,1)S(1)} %collective-permute-done.x_recv, ...), custom_call_target="tpu_custom_call" | custom-call | flops 1 | tf_op jit(solution)/shard_map/pallas_call | solution.py:24
  32.4 0.1 collective-permute-start.15
  32.5 3.2 %collective-permute-done.13.recv = bf16[800,128]{1,0:T(8,128)(2,1)S(1)} collective-permute-done((bf16[800,128]{1,0:T(8,128)(2,1)S(1)}, bf16[800,128]{1,0:T(8,128)(2,1)S(1)}, u32[]{:S(2)}, u32[]{:S(2)}) %collective-permute-start.13) | collective-permute-done | bytes 204832 | tf_op jit(solution)/shard_map/ppermute | solution.py:426
  35.7 0.1 shard_map.265
  35.8 0.3 shard_map.266
  36.1 1.3 %collective-permute-start.19 = (bf16[1024,128]{1,0:T(8,128)(2,1)S(1)}, bf16[1024,128]{1,0:T(8,128)(2,1)S(1)}, u32[]{:S(2)}, u32[]{:S(2)}) collective-permute-start(bf16[1024,128]{1,0:T(8,128)(2,1)S(1)} %get-tuple-element.130), channel_id=1, source_target_pairs={{0,4},{1,3},{2,6},{3,1},{4,0},{5,7},{6,2},{7,5},{8,12},{9,11},{10,... | collective-permute-start | bytes 786440 | tf_op jit(solution)/shard_map/ppermute | solution.py:426
  37.4 2.6 %collective-permute-start.16 = (bf16[448,128]{1,0:T(8,128)(2,1)S(1)}, bf16[448,128]{1,0:T(8,128)(2,1)S(1)}, u32[]{:S(2)}, u32[]{:S(2)}) collective-permute-start(bf16[448,128]{1,0:T(8,128)(2,1)S(1)} %get-tuple-element.127), channel_id=1, source_target_pairs={{0,16},{1,9},{2,18},{3,11},{4,20},{5,13},{6,22},{7,15},{8,24},{9,1... | collective-permute-start | bytes 344072 | tf_op jit(solution)/shard_map/ppermute | solution.py:426
  40.0 1.3 %shard_map.267 = (bf16[8,256,128]{2,1,0:T(8,128)(2,1)}, f32[8,256,128]{2,1,0:T(8,128)}, f32[8,128]{1,0:T(8,128)S(1)}) custom-call(bf16[1024,128]{1,0:T(8,128)(2,1)S(1)} %get-tuple-element.120.after.own, bf16[4,256,128]{2,1,0:T(8,128)(2,1)S(1)} %get-tuple-element.121.out_keep, bf16[4,256,128]{2,1,0:T(8,128)(2,1)S(1)} %collective-permute-done.14.out_recv, ...), custom_call_target="tpu_custom_call" | custom-call | flops 1 | tf_op jit(solution)/shard_map/pallas_call | solution.py:24
  41.2 3.1 %collective-permute-done.16.recv = bf16[448,128]{1,0:T(8,128)(2,1)S(1)} collective-permute-done((bf16[448,128]{1,0:T(8,128)(2,1)S(1)}, bf16[448,128]{1,0:T(8,128)(2,1)S(1)}, u32[]{:S(2)}, u32[]{:S(2)}) %collective-permute-start.16) | collective-permute-done | bytes 114720 | tf_op jit(solution)/shard_map/ppermute | solution.py:426
  44.3 0.1 shard_map.269.after_ref.own
  44.4 0.7 collective-permute-start.21
  45.1 1.5 %collective-permute-start.18 = (bf16[528,128]{1,0:T(8,128)(2,1)S(1)}, bf16[528,128]{1,0:T(8,128)(2,1)S(1)}, u32[]{:S(2)}, u32[]{:S(2)}) collective-permute-start(bf16[528,128]{1,0:T(8,128)(2,1)S(1)} %shard_map.268.after_ref.own), channel_id=1, source_target_pairs={{0,2},{1,3},{2,0},{3,1},{4,6},{5,7},{6,4},{7,5},{8,10},{9,11},{10,... | collective-permute-start | bytes 405512 | tf_op jit(solution)/shard_map/ppermute | solution.py:426
  46.6 3.5 %collective-permute-done.18.recv = bf16[528,128]{1,0:T(8,128)(2,1)S(1)} collective-permute-done((bf16[528,128]{1,0:T(8,128)(2,1)S(1)}, bf16[528,128]{1,0:T(8,128)(2,1)S(1)}, u32[]{:S(2)}, u32[]{:S(2)}) %collective-permute-start.18) | collective-permute-done | bytes 135200 | tf_op jit(solution)/shard_map/ppermute | solution.py:426
  50.2 2.1 %collective-permute-done.21.recv = bf16[1024,128]{1,0:T(8,128)(2,1)S(1)} collective-permute-done((bf16[1024,128]{1,0:T(8,128)(2,1)S(1)}, bf16[1024,128]{1,0:T(8,128)(2,1)S(1)}, u32[]{:S(2)}, u32[]{:S(2)}) %collective-permute-start.21) | collective-permute-done | bytes 262176 | tf_op jit(solution)/shard_map/ppermute | solution.py:426
  52.3 0.1 shard_map.271.after_ref.own
  52.3 2.5 %collective-permute-start.23 = (bf16[1024,128]{1,0:T(8,128)(2,1)S(1)}, bf16[1024,128]{1,0:T(8,128)(2,1)S(1)}, u32[]{:S(2)}, u32[]{:S(2)}) collective-permute-start(bf16[1024,128]{1,0:T(8,128)(2,1)S(1)} %shard_map.271.after_ref.own), channel_id=1, source_target_pairs={{0,16},{1,9},{2,18},{3,11},{4,20},{5,13},{6,22},{7,15},{8,24},{9,1... | collective-permute-start | bytes 786440 | tf_op jit(solution)/shard_map/ppermute | solution.py:426
  54.8 0.6 collective-permute-start.20
  55.5 4.7 %collective-permute-done.20.recv = bf16[656,128]{1,0:T(8,128)(2,1)S(1)} collective-permute-done((bf16[656,128]{1,0:T(8,128)(2,1)S(1)}, bf16[656,128]{1,0:T(8,128)(2,1)S(1)}, u32[]{:S(2)}, u32[]{:S(2)}) %collective-permute-start.20) | collective-permute-done | bytes 167968 | tf_op jit(solution)/shard_map/ppermute | solution.py:426
  60.3 2.2 %collective-permute-done.23.recv = bf16[1024,128]{1,0:T(8,128)(2,1)S(1)} collective-permute-done((bf16[1024,128]{1,0:T(8,128)(2,1)S(1)}, bf16[1024,128]{1,0:T(8,128)(2,1)S(1)}, u32[]{:S(2)}, u32[]{:S(2)}) %collective-permute-start.23) | collective-permute-done | bytes 262176 | tf_op jit(solution)/shard_map/ppermute | solution.py:426
  62.5 0.1 shard_map.273.after_ref.own
  62.5 0.2 collective-permute-start.26
  62.7 0.2 collective-permute-start.24
  63.0 1.1 %collective-permute-done.22.tw_recv_ref = bf16[512,128]{1,0:T(8,128)(2,1)S(1)} collective-permute-done((bf16[512,128]{1,0:T(8,128)(2,1)S(1)}, bf16[512,128]{1,0:T(8,128)(2,1)S(1)}, u32[]{:S(2)}, u32[]{:S(2)}) %collective-permute-start.22) | collective-permute-done | bytes 131104 | tf_op jit(solution)/shard_map/ppermute | solution.py:430
  64.1 3.1 %shard_map.274 = (f32[1000,512]{1,0:T(8,128)}, f32[512,128]{1,0:T(8,128)}, f32[1,128]{1,0:T(1,128)}, f32[8,128]{1,0:T(8,128)S(1)}) custom-call(bf16[512,128]{1,0:T(8,128)(2,1)S(1)} %get-tuple-element.131.rows_ref, f32[1000,512]{1,0:T(8,128)S(1)} %copy-done, bf16[512,128]{1,0:T(8,128)(2,1)S(1)} %copy-done.5, ...), custom_call_target="tpu_custom_call" | custom-call | flops 1 | tf_op jit(solution)/shard_map/pallas_call | solution.py:24
  67.2 1.4 %collective-permute-done.24.recv = bf16[400,128]{1,0:T(8,128)(2,1)S(1)} collective-permute-done((bf16[400,128]{1,0:T(8,128)(2,1)S(1)}, bf16[400,128]{1,0:T(8,128)(2,1)S(1)}, u32[]{:S(2)}, u32[]{:S(2)}) %collective-permute-start.24) | collective-permute-done | bytes 102432 | tf_op jit(solution)/shard_map/ppermute | solution.py:426
  68.6 0.4 collective-permute-done.26.recv
  69.0 0.1 shard_map.276.own2
  69.0 2.5 %collective-permute-start.27 = (bf16[2048,128]{1,0:T(8,128)(2,1)S(1)}, bf16[2048,128]{1,0:T(8,128)(2,1)S(1)}, u32[]{:S(2)}, u32[]{:S(2)}) collective-permute-start(bf16[2048,128]{1,0:T(8,128)(2,1)S(1)} %shard_map.276.own2), channel_id=1, source_target_pairs={{0,2},{1,5},{2,0},{3,7},{4,6},{5,1},{6,4},{7,3},{8,10},{9,13},{10,... | collective-permute-start | bytes 1572872 | tf_op jit(solution)/shard_map/ppermute | solution.py:426
  71.5 0.8 collective-permute-start.25
  72.3 6.4 %collective-permute-done.25.recv1 = bf16[800,128]{1,0:T(8,128)(2,1)S(1)} collective-permute-done((bf16[800,128]{1,0:T(8,128)(2,1)S(1)}, bf16[800,128]{1,0:T(8,128)(2,1)S(1)}, u32[]{:S(2)}, u32[]{:S(2)}) %collective-permute-start.25) | collective-permute-done | bytes 204832 | tf_op jit(solution)/shard_map/ppermute | solution.py:426
  78.6 0.0 collective-permute-done.27.recv2
  78.7 1.8 %shard_map.277 = (f32[2304,128]{1,0:T(8,128)}, f32[9,128,256]{2,1,0:T(8,128)}, f32[3,256,128]{2,1,0:T(8,128)}, f32[128,256]{1,0:T(8,128)}, f32[3,128]{1,0:T(4,12...) custom-call(bf16[800,128]{1,0:T(8,128)(2,1)S(1)} %shard_map.275.after_ref.own1, ...), custom_call_target="tpu_custom_call" | custom-call | flops 1 | tf_op jit(solution)/shard_map/pallas_call | solution.py:24
  (47 shorter events, 0.3 us)
Async XLA Ops:
  0.6 0.7 copy-start.9
  0.7 0.7 copy-start.10
  0.7 0.7 copy-start.11
  0.7 0.7 copy-start.12
  0.7 0.7 copy-start.13
  0.7 0.7 copy-start.14
  0.7 1.1 %copy-start.2 = (bf16[3,3,256,128]{3,2,1,0:T(8,128)(2,1)S(1)}, bf16[3,3,256,128]{3,2,1,0:T(8,128)(2,1)}, u32[]{:S(2)}) copy-start(bf16[3,3,256,128]{3,2,1,0:T(8,128)(2,1)} %param.20) | copy-start | bytes 1769476
  0.7 1.1 %copy-start.5 = (bf16[512,128]{1,0:T(8,128)(2,1)S(1)}, bf16[512,128]{1,0:T(8,128)(2,1)}, u32[]{:S(2)}) copy-start(bf16[512,128]{1,0:T(8,128)(2,1)} %tw_own_ref.1) | copy-start | bytes 393220
  0.7 1.1 %copy-start.8 = (s32[8]{0:T(128)S(1)}, s32[8]{0:T(128)}, u32[]{:S(2)}) copy-start(s32[8]{0:T(128)} %steps.3) | copy-start | bytes 100
  0.7 4.8 %collective-permute-start.1 = (bf16[9,256,128]{2,1,0:T(8,128)(2,1)}, bf16[9,256,128]{2,1,0:T(8,128)(2,1)}, u32[]{:S(2)}, u32[]{:S(2)}) collective-permute-start(bf16[9,256,128]{2,1,0:T(8,128)(2,1)} %bitcast.10), channel_id=1, source_target_pairs={{0,1},{1,0},{2,3},{3,2},{4,5},{5,4},{6,7},{7,6},{8,9},{9,8},{10,11... | collective-permute-start | bytes 1769480 | tf_op jit(solution)/shard_map/ppermute | solution.py:430
  1.3 4.1 %collective-permute-start = (bf16[8,256,128]{2,1,0:T(8,128)(2,1)}, bf16[8,256,128]{2,1,0:T(8,128)(2,1)S(1)}, u32[]{:S(2)}, u32[]{:S(2)}) collective-permute-start(bf16[8,256,128]{2,1,0:T(8,128)(2,1)} %x_own.5), channel_id=1, source_target_pairs={{0,1},{1,0},{2,3},{3,2},{4,5},{5,4},{6,7},{7,6},{8,9},{9,8},{10,11... | collective-permute-start | bytes 1572872 | tf_op jit(solution)/shard_map/ppermute | solution.py:430
  1.3 1.6 %copy-start = (f32[1000,512]{1,0:T(8,128)S(1)}, f32[1000,512]{1,0:T(8,128)}, u32[]{:S(2)}) copy-start(f32[1000,512]{1,0:T(8,128)} %table_ref.1) | copy-start | bytes 6144004
  3.0 1.2 %copy-start.3 = (bf16[3,3,128,256]{3,2,1,0:T(8,128)(2,1)S(1)}, bf16[3,3,128,256]{3,2,1,0:T(8,128)(2,1)}, u32[]{:S(2)}) copy-start(bf16[3,3,128,256]{3,2,1,0:T(8,128)(2,1)} %param.24) | copy-start | bytes 1769476
  3.0 1.5 %copy-start.6 = (bf16[256,3,128]{2,0,1:T(8,128)(2,1)S(1)}, bf16[256,3,128]{2,0,1:T(8,128)(2,1)}, u32[]{:S(2)}) copy-start(bf16[256,3,128]{2,0,1:T(8,128)(2,1)} %param.25) | copy-start | bytes 589828
  3.0 2.0 %copy-start.4 = (bf16[8,256,128]{2,1,0:T(8,128)(2,1)S(1)}, bf16[8,256,128]{2,1,0:T(8,128)(2,1)}, u32[]{:S(2)}) copy-start(bf16[8,256,128]{2,1,0:T(8,128)(2,1)} %g_own.1) | copy-start | bytes 1572868
  3.0 2.4 %copy-start.7 = (bf16[128,256]{1,0:T(8,128)(2,1)S(1)}, bf16[128,256]{1,0:T(8,128)(2,1)}, u32[]{:S(2)}) copy-start(bf16[128,256]{1,0:T(8,128)(2,1)} %ow_own.1) | copy-start | bytes 196612
  3.0 2.5 %copy-start.1 = (bf16[8,256,128]{2,1,0:T(8,128)(2,1)S(1)}, bf16[8,256,128]{2,1,0:T(8,128)(2,1)}, u32[]{:S(2)}) copy-start(bf16[8,256,128]{2,1,0:T(8,128)(2,1)} %x_own.5) | copy-start | bytes 1572868
  3.7 1.3 %collective-permute-start.2 = (f32[24,128]{1,0:T(8,128)S(1)}, f32[24,128]{1,0:T(8,128)S(1)}, u32[]{:S(2)}, u32[]{:S(2)}) collective-permute-start(f32[24,128]{1,0:T(8,128)S(1)} %shard_map.255.pk_own), channel_id=1, source_target_pairs={{0,1},{1,0},{2,3},{3,2},{4,5},{5,4},{6,7},{7,6},{8,9},{9,8},{10,11... | collective-permute-start | bytes 36872 | tf_op jit(solution)/shard_map/ppermute | solution.py:430
  4.1 5.0 %collective-permute-start.3 = (bf16[9,128,256]{2,1,0:T(8,128)(2,1)S(1)}, bf16[9,128,256]{2,1,0:T(8,128)(2,1)S(1)}, u32[]{:S(2)}, u32[]{:S(2)}) collective-permute-start(bf16[9,128,256]{2,1,0:T(8,128)(2,1)S(1)} %bitcast.13), channel_id=1, source_target_pairs={{0,1},{1,0},{2,3},{3,2},{4,5},{5,4},{6,7},{7,6},{8,9},{9,8},{10,11... | collective-permute-start | bytes 1769480 | tf_op jit(solution)/shard_map/ppermute | solution.py:430
  4.5 4.7 %collective-permute-start.5 = (bf16[3,256,128]{2,1,0:T(8,128)(2,1)S(1)}, bf16[3,256,128]{2,1,0:T(8,128)(2,1)S(1)}, u32[]{:S(2)}, u32[]{:S(2)}) collective-permute-start(bf16[3,256,128]{2,1,0:T(8,128)(2,1)S(1)} %bitcast.15), channel_id=1, source_target_pairs={{0,1},{1,0},{2,3},{3,2},{4,5},{5,4},{6,7},{7,6},{8,9},{9,8},{10,11... | collective-permute-start | bytes 589832 | tf_op jit(solution)/shard_map/ppermute | solution.py:430
  5.0 4.2 %collective-permute-start.4 = (bf16[8,256,128]{2,1,0:T(8,128)(2,1)S(1)}, bf16[8,256,128]{2,1,0:T(8,128)(2,1)S(1)}, u32[]{:S(2)}, u32[]{:S(2)}) collective-permute-start(bf16[8,256,128]{2,1,0:T(8,128)(2,1)S(1)} %copy-done.4), channel_id=1, source_target_pairs={{0,1},{1,0},{2,3},{3,2},{4,5},{5,4},{6,7},{7,6},{8,9},{9,8},{10,11... | collective-permute-start | bytes 1572872 | tf_op jit(solution)/shard_map/ppermute | solution.py:430
  5.3 3.8 %collective-permute-start.6 = (bf16[128,256]{1,0:T(8,128)(2,1)S(1)}, bf16[128,256]{1,0:T(8,128)(2,1)S(1)}, u32[]{:S(2)}, u32[]{:S(2)}) collective-permute-start(bf16[128,256]{1,0:T(8,128)(2,1)S(1)} %copy-done.7), channel_id=1, source_target_pairs={{0,1},{1,0},{2,3},{3,2},{4,5},{5,4},{6,7},{7,6},{8,9},{9,8},{10,11... | collective-permute-start | bytes 196616 | tf_op jit(solution)/shard_map/ppermute | solution.py:430
  19.2 2.8 %collective-permute-start.7 = (bf16[1568,128]{1,0:T(8,128)(2,1)S(1)}, bf16[1568,128]{1,0:T(8,128)(2,1)S(1)}, u32[]{:S(2)}, u32[]{:S(2)}) collective-permute-start(bf16[1568,128]{1,0:T(8,128)(2,1)S(1)} %get-tuple-element.99), channel_id=1, source_target_pairs={{0,1},{1,0},{2,3},{3,2},{4,5},{5,4},{6,7},{7,6},{8,9},{9,8},{10,11... | collective-permute-start | bytes 1204232 | tf_op jit(solution)/shard_map/ppermute | solution.py:430
  19.6 2.4 %collective-permute-start.10 = (bf16[1024,128]{1,0:T(8,128)(2,1)S(1)}, bf16[1024,128]{1,0:T(8,128)(2,1)S(1)}, u32[]{:S(2)}, u32[]{:S(2)}) collective-permute-start(bf16[1024,128]{1,0:T(8,128)(2,1)S(1)} %get-tuple-element.105), channel_id=1, source_target_pairs={{0,1},{1,0},{2,3},{3,2},{4,5},{5,4},{6,7},{7,6},{8,9},{9,8},{10,11... | collective-permute-start | bytes 786440 | tf_op jit(solution)/shard_map/ppermute | solution.py:430
  20.4 1.5 %collective-permute-start.8 = (bf16[768,128]{1,0:T(8,128)(2,1)S(1)}, bf16[768,128]{1,0:T(8,128)(2,1)S(1)}, u32[]{:S(2)}, u32[]{:S(2)}) collective-permute-start(bf16[768,128]{1,0:T(8,128)(2,1)S(1)} %get-tuple-element.101), channel_id=1, source_target_pairs={{0,1},{1,0},{2,3},{3,2},{4,5},{5,4},{6,7},{7,6},{8,9},{9,8},{10,11... | collective-permute-start | bytes 589832 | tf_op jit(solution)/shard_map/ppermute | solution.py:430
  21.6 1.7 %collective-permute-start.9 = (bf16[1280,128]{1,0:T(8,128)(2,1)S(1)}, bf16[1280,128]{1,0:T(8,128)(2,1)S(1)}, u32[]{:S(2)}, u32[]{:S(2)}) collective-permute-start(bf16[1280,128]{1,0:T(8,128)(2,1)S(1)} %get-tuple-element.104), channel_id=1, source_target_pairs={{0,1},{1,0},{2,3},{3,2},{4,5},{5,4},{6,7},{7,6},{8,9},{9,8},{10,11... | collective-permute-start | bytes 983048 | tf_op jit(solution)/shard_map/ppermute | solution.py:430
  22.6 1.6 %collective-permute-start.11 = (bf16[1024,128]{1,0:T(8,128)(2,1)S(1)}, bf16[1024,128]{1,0:T(8,128)(2,1)S(1)}, u32[]{:S(2)}, u32[]{:S(2)}) collective-permute-start(bf16[1024,128]{1,0:T(8,128)(2,1)S(1)} %get-tuple-element.107), channel_id=1, source_target_pairs={{0,1},{1,0},{2,3},{3,2},{4,5},{5,4},{6,7},{7,6},{8,9},{9,8},{10,11... | collective-permute-start | bytes 786440 | tf_op jit(solution)/shard_map/ppermute | solution.py:430
  25.0 10.8 %collective-permute-start.12 = (bf16[2048,128]{1,0:T(8,128)(2,1)S(1)}, bf16[2048,128]{1,0:T(8,128)(2,1)S(1)}, u32[]{:S(2)}, u32[]{:S(2)}) collective-permute-start(bf16[2048,128]{1,0:T(8,128)(2,1)S(1)} %get-tuple-element.110), channel_id=1, source_target_pairs={{0,2},{1,5},{2,0},{3,7},{4,6},{5,1},{6,4},{7,3},{8,10},{9,13},{10,... | collective-permute-start | bytes 1572872 | tf_op jit(solution)/shard_map/ppermute | solution.py:426
  27.8 7.9 %collective-permute-start.13 = (bf16[800,128]{1,0:T(8,128)(2,1)S(1)}, bf16[800,128]{1,0:T(8,128)(2,1)S(1)}, u32[]{:S(2)}, u32[]{:S(2)}) collective-permute-start(bf16[800,128]{1,0:T(8,128)(2,1)S(1)} %get-tuple-element.112), channel_id=1, source_target_pairs={{0,8},{1,17},{2,10},{3,19},{4,12},{5,21},{6,14},{7,23},{8,0},{9,25... | collective-permute-start | bytes 614408 | tf_op jit(solution)/shard_map/ppermute | solution.py:426
  29.4 10.6 %collective-permute-start.14 = (bf16[4,256,128]{2,1,0:T(8,128)(2,1)S(1)}, bf16[4,256,128]{2,1,0:T(8,128)(2,1)S(1)}, u32[]{:S(2)}, u32[]{:S(2)}) collective-permute-start(bf16[4,256,128]{2,1,0:T(8,128)(2,1)S(1)} %get-tuple-element.122), channel_id=1, source_target_pairs={{0,1},{1,0},{2,3},{3,2},{4,5},{5,4},{6,7},{7,6},{8,9},{9,8},{10,11... | collective-permute-start | bytes 786440 | tf_op jit(solution)/shard_map/ppermute | solution.py:430
  32.4 7.5 %collective-permute-start.15 = (bf16[4,256,128]{2,1,0:T(8,128)(2,1)S(1)}, bf16[4,256,128]{2,1,0:T(8,128)(2,1)S(1)}, u32[]{:S(2)}, u32[]{:S(2)}) collective-permute-start(bf16[4,256,128]{2,1,0:T(8,128)(2,1)S(1)} %get-tuple-element.124), channel_id=1, source_target_pairs={{0,1},{1,0},{2,3},{3,2},{4,5},{5,4},{6,7},{7,6},{8,9},{9,8},{10,11... | collective-permute-start | bytes 786440 | tf_op jit(solution)/shard_map/ppermute | solution.py:430
  36.1 8.2 %collective-permute-start.19 = (bf16[1024,128]{1,0:T(8,128)(2,1)S(1)}, bf16[1024,128]{1,0:T(8,128)(2,1)S(1)}, u32[]{:S(2)}, u32[]{:S(2)}) collective-permute-start(bf16[1024,128]{1,0:T(8,128)(2,1)S(1)} %get-tuple-element.130), channel_id=1, source_target_pairs={{0,4},{1,3},{2,6},{3,1},{4,0},{5,7},{6,2},{7,5},{8,12},{9,11},{10,... | collective-permute-start | bytes 786440 | tf_op jit(solution)/shard_map/ppermute | solution.py:426
  37.4 6.9 %collective-permute-start.16 = (bf16[448,128]{1,0:T(8,128)(2,1)S(1)}, bf16[448,128]{1,0:T(8,128)(2,1)S(1)}, u32[]{:S(2)}, u32[]{:S(2)}) collective-permute-start(bf16[448,128]{1,0:T(8,128)(2,1)S(1)} %get-tuple-element.127), channel_id=1, source_target_pairs={{0,16},{1,9},{2,18},{3,11},{4,20},{5,13},{6,22},{7,15},{8,24},{9,1... | collective-permute-start | bytes 344072 | tf_op jit(solution)/shard_map/ppermute | solution.py:426
  40.0 1.3 %collective-permute-start.17 = (f32[16,128]{1,0:T(8,128)S(1)}, f32[16,128]{1,0:T(8,128)S(1)}, u32[]{:S(2)}, u32[]{:S(2)}) collective-permute-start(f32[16,128]{1,0:T(8,128)S(1)} %get-tuple-element.129), channel_id=1, source_target_pairs={{0,1},{1,0},{2,3},{3,2},{4,5},{5,4},{6,7},{7,6},{8,9},{9,8},{10,11... | collective-permute-start | bytes 24584 | tf_op jit(solution)/shard_map/ppermute | solution.py:430
  44.4 7.9 %collective-permute-start.21 = (bf16[1024,128]{1,0:T(8,128)(2,1)S(1)}, bf16[1024,128]{1,0:T(8,128)(2,1)S(1)}, u32[]{:S(2)}, u32[]{:S(2)}) collective-permute-start(bf16[1024,128]{1,0:T(8,128)(2,1)S(1)} %shard_map.269.after_ref.own), channel_id=1, source_target_pairs={{0,8},{1,17},{2,10},{3,19},{4,12},{5,21},{6,14},{7,23},{8,0},{9,25... | collective-permute-start | bytes 786440 | tf_op jit(solution)/shard_map/ppermute | solution.py:426
  45.1 5.0 %collective-permute-start.18 = (bf16[528,128]{1,0:T(8,128)(2,1)S(1)}, bf16[528,128]{1,0:T(8,128)(2,1)S(1)}, u32[]{:S(2)}, u32[]{:S(2)}) collective-permute-start(bf16[528,128]{1,0:T(8,128)(2,1)S(1)} %shard_map.268.after_ref.own), channel_id=1, source_target_pairs={{0,2},{1,3},{2,0},{3,1},{4,6},{5,7},{6,4},{7,5},{8,10},{9,11},{10,... | collective-permute-start | bytes 405512 | tf_op jit(solution)/shard_map/ppermute | solution.py:426
  52.3 10.1 %collective-permute-start.23 = (bf16[1024,128]{1,0:T(8,128)(2,1)S(1)}, bf16[1024,128]{1,0:T(8,128)(2,1)S(1)}, u32[]{:S(2)}, u32[]{:S(2)}) collective-permute-start(bf16[1024,128]{1,0:T(8,128)(2,1)S(1)} %shard_map.271.after_ref.own), channel_id=1, source_target_pairs={{0,16},{1,9},{2,18},{3,11},{4,20},{5,13},{6,22},{7,15},{8,24},{9,1... | collective-permute-start | bytes 786440 | tf_op jit(solution)/shard_map/ppermute | solution.py:426
  54.8 5.4 %collective-permute-start.20 = (bf16[656,128]{1,0:T(8,128)(2,1)S(1)}, bf16[656,128]{1,0:T(8,128)(2,1)S(1)}, u32[]{:S(2)}, u32[]{:S(2)}) collective-permute-start(bf16[656,128]{1,0:T(8,128)(2,1)S(1)} %shard_map.270.after_ref.own), channel_id=1, source_target_pairs={{0,4},{1,5},{2,6},{3,7},{4,0},{5,1},{6,2},{7,3},{8,12},{9,13},{10,... | collective-permute-start | bytes 503816 | tf_op jit(solution)/shard_map/ppermute | solution.py:426
  62.5 6.4 %collective-permute-start.26 = (bf16[1024,128]{1,0:T(8,128)(2,1)S(1)}, bf16[1024,128]{1,0:T(8,128)(2,1)S(1)}, u32[]{:S(2)}, u32[]{:S(2)}) collective-permute-start(bf16[1024,128]{1,0:T(8,128)(2,1)S(1)} %shard_map.273.after_ref.own), channel_id=1, source_target_pairs={{0,4},{1,3},{2,6},{3,1},{4,0},{5,7},{6,2},{7,5},{8,12},{9,11},{10,... | collective-permute-start | bytes 786440 | tf_op jit(solution)/shard_map/ppermute | solution.py:426
  62.7 1.3 %collective-permute-start.22 = (bf16[512,128]{1,0:T(8,128)(2,1)S(1)}, bf16[512,128]{1,0:T(8,128)(2,1)S(1)}, u32[]{:S(2)}, u32[]{:S(2)}) collective-permute-start(bf16[512,128]{1,0:T(8,128)(2,1)S(1)} %copy-done.5), channel_id=1, source_target_pairs={{0,1},{1,0},{2,3},{3,2},{4,5},{5,4},{6,7},{7,6},{8,9},{9,8},{10,11... | collective-permute-start | bytes 393224 | tf_op jit(solution)/shard_map/ppermute | solution.py:430
  62.7 5.8 %collective-permute-start.24 = (bf16[400,128]{1,0:T(8,128)(2,1)S(1)}, bf16[400,128]{1,0:T(8,128)(2,1)S(1)}, u32[]{:S(2)}, u32[]{:S(2)}) collective-permute-start(bf16[400,128]{1,0:T(8,128)(2,1)S(1)} %get-tuple-element.132.after_ref.own), channel_id=1, source_target_pairs={{0,16},{1,9},{2,18},{3,11},{4,20},{5,13},{6,22},{7,15},{8,24},{9,1... | collective-permute-start | bytes 307208 | tf_op jit(solution)/shard_map/ppermute | solution.py:426
  69.0 9.6 %collective-permute-start.27 = (bf16[2048,128]{1,0:T(8,128)(2,1)S(1)}, bf16[2048,128]{1,0:T(8,128)(2,1)S(1)}, u32[]{:S(2)}, u32[]{:S(2)}) collective-permute-start(bf16[2048,128]{1,0:T(8,128)(2,1)S(1)} %shard_map.276.own2), channel_id=1, source_target_pairs={{0,2},{1,5},{2,0},{3,7},{4,6},{5,1},{6,4},{7,3},{8,10},{9,13},{10,... | collective-permute-start | bytes 1572872 | tf_op jit(solution)/shard_map/ppermute | solution.py:426
  71.5 7.1 %collective-permute-start.25 = (bf16[800,128]{1,0:T(8,128)(2,1)S(1)}, bf16[800,128]{1,0:T(8,128)(2,1)S(1)}, u32[]{:S(2)}, u32[]{:S(2)}) collective-permute-start(bf16[800,128]{1,0:T(8,128)(2,1)S(1)} %shard_map.275.after_ref.own1), channel_id=1, source_target_pairs={{0,8},{1,17},{2,10},{3,19},{4,12},{5,21},{6,14},{7,23},{8,0},{9,25... | collective-permute-start | bytes 614408 | tf_op jit(solution)/shard_map/ppermute | solution.py:426

commit v4 on v3

--- a/solution.py
+++ b/solution.py
@@ -295,27 +295,35 @@
     sums[6:8] = jnp.zeros((2, C), F32)
 
 
-CONV1_TAPS = (range(0, 6), range(6, 9))
-CONV2_TAPS = (range(0, 5), range(5, 9))
-
-
-def conv2_grad_kernel(taps):
-    def body(act_t, *rest):
-        win, (keep, send) = rest[: act_t.shape[1] // PIX], rest[-2:]
-        first = lax.axis_index("mp") == 0
-        for i, t in enumerate(taps):
-            shifted = jnp.concatenate([window(w, 2 - t // 3, 2 - t % 3) for w in win], axis=0)
-            g_keep, g_send = split(first, dot(act_t[...], shifted).astype(BF16), 0)
-            for h in range(2):
-                lanes = slice(h * HALF, (h + 1) * HALF)
-                rows = slice((2 * i + h) * HALF, (2 * i + h + 1) * HALF)
-                keep[rows] = g_keep[:, lanes]
-                send[rows] = g_send[:, lanes]
-
-    return body
-
-
-def hidden_back_kernel(steps, hid, stat, wfull, prm, *rest):
+CONV2_TAPS = (range(0, 7), range(7, 9))
+CONV1_TAPS = (range(0, 4), range(4, 8), range(8, 9))
+
+
+def conv2_rows(taps, first, act_t, win, keep, send):
+    for i, t in enumerate(taps):
+        shifted = jnp.concatenate([window(w, 2 - t // 3, 2 - t % 3) for w in win], axis=0)
+        g_keep, g_send = split(first, dot(act_t[...], shifted).astype(BF16), 0)
+        for h in range(2):
+            lanes = slice(h * HALF, (h + 1) * HALF)
+            rows = slice((2 * i + h) * HALF, (2 * i + h + 1) * HALF)
+            keep[rows] = g_keep[:, lanes]
+            send[rows] = g_send[:, lanes]
+
+
+def conv2_grad_kernel(act_t, wg_keep, wg_send, *rest):
+    win, (keep, send) = rest[:-2], rest[-2:]
+    at = len(CONV2_TAPS[0]) * C
+    keep[at:] = wg_keep[...]
+    send[at:] = wg_send[...]
+    conv2_rows(CONV2_TAPS[0], lax.axis_index("mp") == 0, act_t, win, keep, send)
+
+
+def last_conv2_kernel(after, act_t, *rest):
+    win, (keep, send) = rest[:-2], rest[-2:]
+    conv2_rows(CONV2_TAPS[1], lax.axis_index("mp") == 0, act_t, win, keep, send)
+
+
+def hidden_back_kernel(steps, after, hid, stat, wfull, prm, *rest):
     n = hid.shape[0]
     win3, (sums, time_rows), win4 = rest[:n], rest[n : n + 2], rest[n + 2 :]
     gain, bias = prm[GAIN + 1 : GAIN + 2], prm[BIAS + 1 : BIAS + 2]
@@ -333,39 +341,43 @@
         low = back.astype(BF16).astype(F32)
         times.append(col_sum(low))
         put_windows(win4[m], low)
-    rows, blank = jnp.concatenate(times, axis=0), jnp.zeros((n, HALF), F32)
-    time_rows[0:16] = jnp.concatenate([rows[:, :HALF], blank, rows[:, HALF:], blank], axis=0).astype(BF16)
-    lane = lax.broadcasted_iota(jnp.int32, (16, HALF), 1)
-    step_row = jnp.zeros((16, HALF), jnp.int32)
-    for i in range(2 * n):
-        step_row = jnp.where(lane == i, steps[i] >> 5, jnp.where(lane == 2 * n + i, steps[i] & 31, step_row))
-    time_rows[16:32] = step_row.astype(F32).astype(BF16)
+    me = lax.axis_index("mp")
+    lane = lax.broadcasted_iota(jnp.int32, (1, HALF), 1)
+    step_row = jnp.zeros((1, HALF), jnp.int32)
+    for i in range(n):
+        step = steps[me * n + i]
+        step_row = jnp.where(lane == i, step >> 5, jnp.where(lane == n + i, step & 31, step_row))
+    rows = jnp.concatenate(times, axis=0)
+    blank = jnp.zeros((8 - n, HALF), F32)
+    left = [rows[:, :HALF], step_row.astype(F32), blank[1:]]
+    time_rows[...] = jnp.concatenate(left + [rows[:, HALF:], blank], axis=0).astype(BF16)
     sums[0:1] = sum(gains)
     sums[1:2] = sum(biases)
     sums[2:3] = sum(times)
     sums[3:8] = jnp.zeros((5, C), F32)
 
 
-def conv1_grad_kernel(taps):
+def conv1_grad_kernel(taps, count):
     def body(act_t, *rest):
-        win, others, (keep, send) = rest[: act_t.shape[1] // PIX], rest[act_t.shape[1] // PIX : -2], rest[-2:]
+        n = act_t.shape[1] // PIX
+        win, others, (keep, send) = rest[:n], rest[n : n + count], rest[-2:]
         first = lax.axis_index("mp") == 0
+        at = 0
+        for ref, other in zip((keep, send), others):
+            at = other.shape[0]
+            ref[0:at] = other[...]
         for i, t in enumerate(taps):
             shifted = jnp.concatenate([window(w, 2 - t // 3, 2 - t % 3) for w in win], axis=0)
             g_keep, g_send = split(first, dot(act_t[...], shifted).astype(BF16))
-            keep[i * C : (i + 1) * C] = g_keep
-            send[i * C : (i + 1) * C] = g_send
-        if others:
-            rows = len(taps) * C
-            keep[rows:] = others[0][...]
-            send[rows:] = others[0][...]
+            keep[at + i * C : at + (i + 1) * C] = g_keep
+            send[at + i * C : at + (i + 1) * C] = g_send
 
     return body
 
 
-def input_back_kernel(after, x_own, x_recv, stat, wfull, prm, dmid, sums2, sums3, *rest):
+def input_back_kernel(after, x_own, x_recv, stat, wfull, prm, dmid, sums2, sums3, out_send, *rest):
     n = dmid.shape[0]
-    win4, (keep, send, rows_keep, rows_send) = rest[:n], rest[n:]
+    win4, (keep, send, out_pass, rows_keep, rows_send) = rest[:n], rest[n:]
     me = lax.axis_index("mp")
     first = me == 0
     gain, bias = prm[GAIN : GAIN + 1], prm[BIAS : BIAS + 1]
@@ -385,6 +397,7 @@
         d_keep, d_send = split(first, back + dmid[m])
         keep[m] = d_keep
         send[m] = d_send.astype(BF16)
+        out_pass[m] = out_send[m]
     small = [
         sum(gains), sums2[0:1], sums3[0:1], sum(biases), sums2[1:2], sums3[1:2], sums2[2:3], sums3[2:6],
         jnp.zeros((5, C), F32),
@@ -392,7 +405,7 @@
     rows_keep[...], rows_send[...] = split(first, jnp.concatenate(small, axis=0))
 
 
-def maps_kernel(after, out_keep, out_recv, grad_keep, grad_recv, out, grad, turn):
+def maps_kernel(after, tw_recv, out_keep, out_recv, grad_keep, grad_recv, out, grad, turn):
     n = out_keep.shape[0]
     me = lax.axis_index("mp")
     for m in range(n):
@@ -403,14 +416,16 @@
     turn[...] = jnp.zeros_like(turn)
 
 
-EXTRA, SUMS = 32, 16
+EXTRA, SUMS = 16, 16
 
 
 def bits_of(count):
     bits = list(range(count.bit_length() - 1))
     cut = len(bits) // 2
-    low, high = bits[:cut], bits[cut:]
-    return [[(high, low), (high[::-1], low)], [(low, high), (low[::-1], high[::-1])]]
+    orders = [[(1, 3, 0, 2), (2, 1, 0, 3)], [(0, 2, 1, 3), (2, 0, 3, 1)]]
+    if len(bits) != 4:
+        orders = [[bits, bits[::-1]], [bits[cut:] + bits[:cut], bits[:cut][::-1] + bits[cut:]]]
+    return [[(list(order[:cut]), list(order[cut:])) for order in group] for group in orders]
 
 
 def digit(bits):
@@ -438,49 +453,45 @@
     return (a.astype(F32) + b.astype(F32)).astype(BF16)
 
 
-def start_exchanges(chains, groups):
-    rows = [chain.rows for chain in chains]
+def start_exchange(chain, pairs, time_rows, after):
+    rows = chain.rows
+    half, extra = rows // 2, EXTRA if time_rows else 0
 
     def body(*refs):
         refs = list(refs)
-        sources = [[(refs.pop(0), refs.pop(0)) for _ in pairs] for pairs in groups]
-        outs, buffers = refs[:4], refs[4:]
-        first = lax.axis_index("mp") == 0
-        time_own, time_other = [ref[ref.shape[0] - EXTRA :].astype(F32) for ref in sources[0][0]]
-        sides = [join(first, time_own[at : at + 4], time_other[at : at + 4], 0) for at in (0, 8)]
-        extra = jnp.concatenate(sides + [time_own[16:32]], axis=0).astype(BF16)
-        for g, values in enumerate(buffers):
-            end = 0
-            for i, (keep, recv) in enumerate(sources[g]):
-                size = keep.shape[0] - (EXTRA if g == 0 and i == 0 else 0)
-                values[end : end + size] = added(keep[0:size], recv[0:size])
-                end += size
-            if end < rows[g]:
-                values[end : rows[g]] = jnp.zeros((rows[g] - end, HALF), BF16)
-            me, half = digit(chains[g].steps[0]), rows[g] // 2
-            for index, ref in zip((me, 1 - me), outs[2 * g : 2 * g + 2]):
-                ref[0:half] = values[part(index, half)]
-                if g == 0:
-                    ref[half:] = extra
-
-    outs = [((r // 2 + (EXTRA if g == 0 else 0), HALF), BF16) for g, r in enumerate(rows) for _ in range(2)]
-    args = [v for pairs in groups for pair in pairs for v in pair]
-    results = call(body, outs, *args, scratch=[pltpu.VMEM((r, HALF), BF16) for r in rows])
-    for g, chain in enumerate(chains):
-        chain.own = results[2 * g]
-        chain.recv = swap_dp(results[2 * g + 1], chain.steps[0])
-        chain.rows //= 2
+        sources = [(refs.pop(0), refs.pop(0)) for _ in pairs]
+        outs, values = refs[-3:-1], refs[-1]
+        end = 0
+        for keep, recv in sources:
+            size = keep.shape[0]
+            values[end : end + size] = added(keep[...], recv[...])
+            end += size
+        if end < rows:
+            values[end:rows] = jnp.zeros((rows - end, HALF), BF16)
+        me = digit(chain.steps[0])
+        for index, ref in zip((me, 1 - me), outs):
+            ref[0:half] = values[part(index, half)]
+            if extra:
+                ref[half:] = refs[0][...]
+
+    args = [v for pair in pairs for v in pair] + list(time_rows)
+    specs = {len(args) + i: ANYWHERE for i in range(len(after))}
+    shape = ((half + extra, HALF), BF16)
+    scratch = [pltpu.VMEM((rows, HALF), BF16)]
+    chain.own, send = call(body, [shape, shape], *args, *after, scratch=scratch, specs=specs)
+    chain.recv = swap_dp(send, chain.steps[0])
+    chain.rows = half
 
 
 class Exchange:
-    def __init__(self, order, pairs, extra):
+    def __init__(self, order, rows):
         halving, whole = [list(zip(*[core[i] for core in order])) for i in range(2)]
         self.cut, self.whole = len(halving), len(halving) + len(whole)
         self.steps = halving + whole + halving[::-1]
         self.bits = [[core[0] + core[1] for core in order][c] for c in range(2)]
         self.at = 0
         pieces = 1 << self.cut
-        self.piece = -(-(sum(keep.shape[0] for keep, _ in pairs) - extra) // (16 * pieces)) * 16
+        self.piece = -(-rows // (16 * pieces)) * 16
         self.rows = self.piece * pieces
 
     def step(self, after, small=()):
@@ -538,26 +549,32 @@
         self.recv = swap_dp(results[1] if halve else self.own, following)
 
 
-def time_results(gathered, order, table, tw_own, tw_recv, after):
+def time_results(n, gathered, other, order, table, tw_own, tw_recv, after):
     steps, width = table.shape
     padded = -(-steps // HALF) * HALF
     blocks = gathered.shape[0] // EXTRA
-    maps = 8 * blocks
+    maps = 8 * 2 * blocks
 
     def owner(core, block):
         return sum((block >> i & 1) << bit for i, bit in enumerate(order[core]))
 
-    def body(rows_ref, table_ref, tw_own_ref, tw_recv_ref, after_ref, *refs):
+    def body(rows_ref, other_ref, table_ref, tw_own_ref, tw_recv_ref, after_ref, *refs):
         table_grad, tw_grad, time_b, turn, extra, act_high, act_low = refs
-        first = lax.axis_index("mp") == 0
+        me = lax.axis_index("mp")
+        first = me == 0
         for block in range(blocks):
-            at = jnp.where(first, owner(0, block), owner(1, block))
-            extra[at] = rows_ref[block * EXTRA : (block + 1) * EXTRA].astype(F32)
-        left, right = extra[:, 0:8].reshape(maps, HALF), extra[:, 8:16].reshape(maps, HALF)
-        step_rows = extra[:, 16:24].reshape(maps, HALF)
+            rows = slice(block * EXTRA, (block + 1) * EXTRA)
+            own_at = jnp.where(first, owner(0, block), owner(1, block))
+            other_at = jnp.where(first, owner(1, block), owner(0, block))
+            extra[2 * own_at + me] = rows_ref[rows].astype(F32)
+            extra[2 * other_at + 1 - me] = other_ref[rows].astype(F32)
         lane = lax.broadcasted_iota(jnp.int32, (maps, HALF), 1)
         row = lax.broadcasted_iota(jnp.int32, (maps, HALF), 0) & 7
-        weight = jnp.where(lane == row, 32.0, jnp.where(lane == row + 8, 1.0, 0.0))
+        held = row < n
+        left = jnp.where(held, extra[:, 0:8].reshape(maps, HALF), 0.0)
+        right = jnp.where(held, extra[:, 8:16].reshape(maps, HALF), 0.0)
+        step_rows = jnp.broadcast_to(extra[:, n : n + 1], (2 * blocks, 8, HALF)).reshape(maps, HALF)
+        weight = jnp.where(held & (lane == row), 32.0, jnp.where(held & (lane == row + n), 1.0, 0.0))
         step = jnp.sum(step_rows * weight, axis=1, keepdims=True).astype(jnp.int32)
         mine = jnp.where(first, left, right)
         time_b[...] = col_sum(mine)
@@ -586,16 +603,16 @@
 
     outs = [(table.shape, F32), (tw_own.shape, F32), ((1, HALF), F32), ((8, HALF), F32)]
     scratch = [
-        pltpu.VMEM((blocks, EXTRA, HALF), F32),
+        pltpu.VMEM((2 * blocks, EXTRA, HALF), F32),
         pltpu.VMEM((padded, width), F32),
         pltpu.VMEM((padded, width), F32),
     ]
-    args = (gathered, table, tw_own, tw_recv, after)
-    return call(body, outs, *args, scratch=scratch, specs={4: ANYWHERE}, limit=24)
-
-
-def weight_results(chains, split_at):
-    def body(own1, recv1, own2, recv2, *refs):
+    args = (gathered, other, table, tw_own, tw_recv, after)
+    return call(body, outs, *args, scratch=scratch, specs={5: ANYWHERE}, limit=24)
+
+
+def weight_results(chains, after):
+    def body(after_ref, own1, recv1, own2, recv2, *refs):
         conv1, conv2, qkv, out_w, gains, biases, conv_b, qkv_b, out_b = refs[:9]
         reads = []
         for chain, own, recv, values in zip(chains, (own1, own2), (recv1, recv2), refs[9:]):
@@ -603,13 +620,13 @@
             values[part(me, rows)] = own[...]
             values[part(1 - me, rows)] = recv[...]
             reads.append(row_reader(values, chain.piece, values.shape[0] >> chain.cut))
-        conv1[0:split_at] = reads[0](0, split_at)
-        conv1[split_at : 9 * C] = reads[1](0, 9 * C - split_at)
-        at = 9 * C - split_at
+        cut = len(CONV2_TAPS[0])
         for t in range(9):
+            read, at = (reads[1], t) if t < cut else (reads[0], t - cut)
             for h in range(2):
-                conv2[t, :, h * HALF : (h + 1) * HALF] = reads[1](at + (2 * t + h) * HALF, HALF)
-        at += 9 * C
+                conv2[t, :, h * HALF : (h + 1) * HALF] = read((2 * at + h) * HALF, HALF)
+        conv1[...] = reads[0]((9 - cut) * C, 9 * C)
+        at = cut * C
         for j in range(3):
             qkv[j] = reads[1](at + j * C, C)
         for h in range(2):
@@ -633,7 +650,7 @@
     ]
     scratch = [pltpu.VMEM((2 * chain.own.shape[0], HALF), BF16) for chain in chains]
     args = [v for chain in chains for v in (chain.own, chain.recv)]
-    return call(body, outs, *args, scratch=scratch)
+    return call(body, outs, after, *args, scratch=scratch)
 
 
 def row_reader(values, piece, full):
@@ -704,57 +721,58 @@
         scratch=[pltpu.VMEM((3, C, C), BF16), tile_low]
         + [tile_f32] * (3 * n) + [tile_low] * n + [three_low] * n + [tile_low] * (3 * n) + [three_low] * n,
     )
-    wg_recv = swap_mp(wg_send)
+    def swapped(keep, send):
+        return keep, swap_mp(send)
+
+    shape = ((len(CONV2_TAPS[0]) * C + wg_keep.shape[0], HALF), BF16)
+    late_pair = swapped(*call(conv2_grad_kernel, [shape, shape], act2_t, wg_keep, wg_send, *win3))
     sums2, time_rows, *win4 = call(
         hidden_back_kernel,
         [((8, C), F32), ((EXTRA, HALF), BF16)] + [WIN] * n,
-        timesteps, hid, stat1, w2_full, prm, *win3,
-        specs={0: SCALAR},
+        timesteps, late_pair[0], hid, stat1, w2_full, prm, *win3,
+        specs={0: SCALAR, 1: ANYWHERE},
     )
 
-    def conv_grad(kernel, taps, act_t, windows, others=(), after=()):
-        shape = ((len(taps) * C + sum(v.shape[0] for v in others), HALF), BF16)
+    early, late = chains = [
+        Exchange(order, rows) for order, rows in zip(orders, (11 * C, late_pair[0].shape[0]))
+    ]
+    start_exchange(late, (late_pair,), (), (sums2,))
+
+    def conv1_grad(taps, others=(), after=()):
+        shape = ((len(taps) * C + sum(v.shape[0] for v in others[:1]), HALF), BF16)
         specs = {1 + n + len(others) + i: ANYWHERE for i in range(len(after))}
-        keep, send = call(kernel(taps), [shape, shape], act_t, *windows, *others, *after, specs=specs)
-        return keep, swap_mp(send)
-
-    conv1_pairs = [
-        conv_grad(conv1_grad_kernel, CONV1_TAPS[0], act1_t, win4, others=(time_rows,)),
-        conv_grad(conv1_grad_kernel, CONV1_TAPS[1], act1_t, win4),
-    ]
-    arrived = (wg_recv,) + tuple(recv for _, recv in conv1_pairs)
-    conv2_pairs = [
-        conv_grad(conv2_grad_kernel, CONV2_TAPS[0], act2_t, win3, after=(conv1_pairs[1][0],)),
-        conv_grad(conv2_grad_kernel, CONV2_TAPS[1], act2_t, win3, after=arrived),
-    ]
-    groups = [conv1_pairs[:1], conv1_pairs[1:] + conv2_pairs + [(wg_keep, wg_recv)]]
-    chains = [Exchange(order, pairs, extra) for order, pairs, extra in zip(orders, groups, (EXTRA, 0))]
-    early, late = chains
-    start_exchanges(chains, groups)
-    mg_keep, mg_send, rows_keep, rows_send = call(
+        return call(conv1_grad_kernel(taps, len(others)), [shape, shape], act1_t, *win4, *others, *after, specs=specs)
+
+    shape = ((len(CONV2_TAPS[1]) * C, HALF), BF16)
+    part = call(last_conv2_kernel, [shape, shape], late.own, act2_t, *win3, specs={0: ANYWHERE})
+    first_pair = swapped(*conv1_grad(CONV1_TAPS[0], part))
+    part = conv1_grad(CONV1_TAPS[1], after=(first_pair[0],))
+    last_pair = swapped(*conv1_grad(CONV1_TAPS[2], part, (first_pair[1],)))
+    start_exchange(early, (first_pair, last_pair), (time_rows,), (late.own,))
+    mg_keep, mg_send, out_send, rows_keep, rows_send = call(
         input_back_kernel,
-        [(half_shape, F32), (half_shape, BF16), ((SUMS, HALF), F32), ((SUMS, HALF), F32)],
-        late.own, maps_in, x_recv, stat0, w1_full, prm, dmid, sums2, sums3, *win4,
+        [(half_shape, F32), (half_shape, BF16), (half_shape, BF16), ((SUMS, HALF), F32), ((SUMS, HALF), F32)],
+        early.own, maps_in, x_recv, stat0, w1_full, prm, dmid, sums2, sums3, out_send, *win4,
         specs={0: ANYWHERE},
+        flops=10**10,
     )
     rows_recv = swap_mp(rows_send)
-    out_recv, mg_recv = swap_mp(out_send), swap_mp(mg_send)
+    mg_recv, out_recv = swap_mp(mg_send), swap_mp(out_send)
     turn = rows_keep
     for i in range(len(early.steps) - 1):
         early.step(turn, (rows_keep, rows_recv))
         late.step(early.own)
-        turn = late.own
         if i == 0:
             maps_out, maps_grad, turn = call(
                 maps_kernel, [(maps_in.shape, BF16), (maps_in.shape, F32), ((8, HALF), F32)],
-                turn, out_keep, out_recv, mg_keep, mg_recv,
-                specs={0: ANYWHERE},
+                late.own, tw_recv, out_keep, out_recv, mg_keep, mg_recv,
+                specs={0: ANYWHERE, 1: ANYWHERE},
             )
         if i == early.whole - 1:
             table_grad, tw_grad, time_b, turn = time_results(
-                early.gathered, early.bits, temb_table, temb_weight, tw_recv, turn,
+                n, early.gathered, swap_mp(early.gathered), early.bits, temb_table, temb_weight, tw_recv, late.own,
             )
-    conv1, conv2, qkv, out_w, gains, biases, conv_b, qkv_b, out_b = weight_results(chains, len(CONV1_TAPS[0]) * C)
+    conv1, conv2, qkv, out_w, gains, biases, conv_b, qkv_b, out_b = weight_results(chains, turn)
     return (
         maps_out, maps_grad, table_grad, gains, biases, conv1.reshape(3, 3, C, HALF), conv_b, tw_grad,
         time_b.reshape(HALF), conv2.reshape(3, 3, HALF, C), jnp.transpose(qkv, (1, 0, 2)), qkv_b, out_w,

time: 80.7 us -> 78 us (0.967)
  waiting for transfers between devices: 29.8 us -> 24.4 us
  starting transfers between devices: 21.7 us -> 23.7 us
    ppermute x12, waiting for transfers between devices: 27 us -> 22 us  [swap_dp(): return lax.ppermute(values, ('dp', 'mp'), pairs)]
    ppermute x12, starting transfers between devices: 17.2 us -> 20.2 us  [swap_dp(): return lax.ppermute(values, ('dp', 'mp'), pairs)]
    ppermute x16 -> x15, starting transfers between devices: 4.49 us -> 3.5 us  [swap_mp(): return lax.ppermute(values, 'mp', [(0, 1), (1, 0)])]
    pallas_call x24 -> x26, Pallas kernels: 26.4 us -> 27.1 us  [call(): pl.pallas_call(body, out_shape=tuple((jax.ShapeDtypeStruct(s, d) for s, d...]
    ppermute x16 -> x15, waiting for transfers between devices: 2.77 us -> 2.42 us  [swap_mp(): return lax.ppermute(values, 'mp', [(0, 1), (1, 0)])]
  transfers between devices with their start and end apart: 28 -> 27, of which waited for: 13 -> 10; matrix products, arithmetic and copies ran while one was open for 0% -> 0% of each run, Pallas kernels for 17% -> 21%
where the time goes in v4:
time: 78 us; the launch traced here: 77.8 us
  Pallas kernels  27.1 us (35%)
  waiting for transfers between devices  24.4 us (31%)
  starting transfers between devices  23.7 us (30%)
  local copies, waits for them, and re-layouts  1.65 us (2%)
  between operations  0.97 us (1%)
    pallas_call x26, Pallas kernels, call(): pl.pallas_call(body, out_shape=tuple((jax.ShapeDtypeStruct(s, d) for s, d...  27.1 us
    ppermute x12, waiting for transfers between devices, swap_dp(): return lax.ppermute(values, ('dp', 'mp'), pairs)  22 us
    ppermute x12, starting transfers between devices, swap_dp(): return lax.ppermute(values, ('dp', 'mp'), pairs)  20.2 us
    ppermute x15, starting transfers between devices, swap_mp(): return lax.ppermute(values, 'mp', [(0, 1), (1, 0)])  3.5 us
    ppermute x15, waiting for transfers between devices, swap_mp(): return lax.ppermute(values, 'mp', [(0, 1), (1, 0)])  2.42 us
    unnamed x30, local copies, waits for them, and re-layouts  1.61 us
  transfers between devices with their start and end apart: 27, of which 10 were waited for; matrix products, arithmetic and copies ran while one was open for 0% of the time, Pallas kernels for 21%

profile of v4, /device:TPU:0, one launch (start us, length us, event | category | flops | bytes accessed | tf_op | source)
XLA Modules:
  0.0 77.8 jit_solution(14186511246532327536)
XLA Ops:
  0.7 0.5 collective-permute-start.1
  1.3 0.1 collective-permute-start
  1.3 0.0 copy-done.10
  1.3 0.0 copy-done.11
  1.4 0.0 copy-done.12
  1.4 0.0 copy-done.14
  1.4 0.4 copy-done.1
  1.8 0.0 copy-done.3
  1.8 1.1 %copy-done = f32[1000,512]{1,0:T(8,128)S(1)} copy-done((f32[1000,512]{1,0:T(8,128)S(1)}, f32[1000,512]{1,0:T(8,128)}, u32[]{:S(2)}) %copy-start) | copy-done | bytes 2048024
  3.0 0.0 copy-start.5
  3.0 0.7 shard_map.255.pk_own
  3.7 0.4 collective-permute-start.2
  4.1 0.3 collective-permute-start.3
  4.5 0.2 collective-permute-start.5
  4.7 0.3 collective-permute-done.2.pk_recv
  5.0 0.3 collective-permute-start.4
  5.3 0.0 collective-permute-done.x_recv
  5.3 0.2 collective-permute-start.6
  5.5 3.6 %shard_map.256 = (f32[4,256,256]{2,1,0:T(8,128)S(1)}, bf16[256,1024]{1,0:T(8,128)(2,1)S(1)}, bf16[256,1024]{1,0:T(8,128)(2,1)S(1)}, f32[8,256]{1,0:T(8,128)S(1)}...) custom-call(bf16[8,256,128]{2,1,0:T(8,128)(2,1)S(1)} %copy-done.5, ...), custom_call_target="tpu_custom_call" | custom-call | flops 99999997952 | tf_op jit(solution)/shard_map/pallas_call | solution.py:24
  9.1 0.0 collective-permute-done.6.ow_recv
  9.1 0.0 collective-permute-done.5.qw_recv
  9.2 5.7 %shard_map.257 = (bf16[4,256,128]{2,1,0:T(8,128)(2,1)S(1)}, bf16[4,256,128]{2,1,0:T(8,128)(2,1)S(1)}, f32[4,256,256]{2,1,0:T(8,128)S(1)}, bf16[1024,128]{1,0:T(8...) custom-call(bf16[8,256,128]{2,1,0:T(8,128)(2,1)S(1)} %copy-done.5, ...), custom_call_target="tpu_custom_call" | custom-call | flops 1 | tf_op jit(solution)/shard_map/pallas_call | solution.py:24
  14.9 1.2 %shard_map.258 = (bf16[2816,128]{1,0:T(8,128)(2,1)S(1)}, bf16[2816,128]{1,0:T(8,128)(2,1)S(1)}) custom-call(bf16[256,1024]{1,0:T(8,128)(2,1)S(1)} %get-tuple-element.83.act_t, bf16[1024,128]{1,0:T(8,128)(2,1)S(1)} %get-tuple-element.89.wg_keep, bf16[1024,128]{1,0:T(8,128)(2,1)S(1)} %get-tuple-element.90.wg_send, ...), custom_call_target="tpu_custom_call" | custom-call | flops 1 | tf_op jit(solution)/shard_map/pallas_call | solution.py:24
  16.1 0.4 collective-permute-start.7
  16.5 3.4 %shard_map.259 = (f32[8,256]{1,0:T(8,128)S(1)}, bf16[16,128]{1,0:T(8,128)(2,1)S(1)}, bf16[3,288,256]{2,1,0:T(8,128)(2,1)S(1)}, bf16[3,288,256]{2,1,0:T(8,128)(2,...) custom-call(s32[8]{0:T(128)S(1)} %copy-done.8, ...), custom_call_target="tpu_custom_call" | custom-call | flops 1 | tf_op jit(solution)/shard_map/pallas_call | solution.py:24
  19.9 0.4 shard_map.260
  20.3 0.4 shard_map.261
  20.8 0.7 shard_map.262
  21.5 0.2 collective-permute-start.9
  21.8 0.7 shard_map.263
  22.5 0.8 %collective-permute-done.9.rest_6_.refs_1_ = bf16[1536,128]{1,0:T(8,128)(2,1)S(1)} collective-permute-done((bf16[1536,128]{1,0:T(8,128)(2,1)S(1)}, bf16[1536,128]{1,0:T(8,128)(2,1)S(1)}, u32[]{:S(2)}, u32[]{:S(2)}) %collective-permute-start.9) | collective-permute-done | bytes 393248 | tf_op jit(solution)/shard_map/ppermute | solution.py:445
  23.3 0.3 shard_map.264
  23.7 0.2 collective-permute-start.10
  23.9 2.8 %collective-permute-start.8 = (bf16[1408,128]{1,0:T(8,128)(2,1)S(1)}, bf16[1408,128]{1,0:T(8,128)(2,1)S(1)}, u32[]{:S(2)}, u32[]{:S(2)}) collective-permute-start(bf16[1408,128]{1,0:T(8,128)(2,1)S(1)} %get-tuple-element.102), channel_id=1, source_target_pairs={{0,2},{1,9},{2,0},{3,11},{4,6},{5,13},{6,4},{7,15},{8,10},{9,1},{1... | collective-permute-start | bytes 1081352 | tf_op jit(solution)/shard_map/ppermute | solution.py:441
  26.7 0.4 shard_map.265
  27.1 1.6 %collective-permute-start.11 = (bf16[1424,128]{1,0:T(8,128)(2,1)S(1)}, bf16[1424,128]{1,0:T(8,128)(2,1)S(1)}, u32[]{:S(2)}, u32[]{:S(2)}) collective-permute-start(bf16[1424,128]{1,0:T(8,128)(2,1)S(1)} %get-tuple-element.118), channel_id=1, source_target_pairs={{0,4},{1,9},{2,6},{3,11},{4,0},{5,13},{6,2},{7,15},{8,12},{9,1},{1... | collective-permute-start | bytes 1093640 | tf_op jit(solution)/shard_map/ppermute | solution.py:441
  28.7 2.3 %shard_map.266 = (f32[4,256,128]{2,1,0:T(8,128)S(1)}, bf16[4,256,128]{2,1,0:T(8,128)(2,1)S(1)}, bf16[4,256,128]{2,1,0:T(8,128)(2,1)S(1)}, f32[16,128]{1,0:T(8,128)S(1)}, f32[16,128]{1,0:T(8,128)S(1)}) custom-call(bf16[1424,128]{1,0:T(8,128)(2,1)S(1)} %get-tuple-element.117.after.own, bf16[8,256,128]{2,1,0:T(8,128)(2,1)S(1)} %copy-done.5, ...), custom_call_target="tpu_custom_call" | custom-call | flops 10000000000 | tf_op jit(solution)/shard_map/pallas_call | solution.py:24
  31.1 0.1 collective-permute-start.13
  31.1 0.5 collective-permute-start.14
  31.6 3.0 %collective-permute-done.11.recv = bf16[1424,128]{1,0:T(8,128)(2,1)S(1)} collective-permute-done((bf16[1424,128]{1,0:T(8,128)(2,1)S(1)}, bf16[1424,128]{1,0:T(8,128)(2,1)S(1)}, u32[]{:S(2)}, u32[]{:S(2)}) %collective-permute-start.11) | collective-permute-done | bytes 364576 | tf_op jit(solution)/shard_map/ppermute | solution.py:441
  34.7 0.2 shard_map.267
  34.9 2.7 %collective-permute-start.15 = (bf16[736,128]{1,0:T(8,128)(2,1)S(1)}, bf16[736,128]{1,0:T(8,128)(2,1)S(1)}, u32[]{:S(2)}, u32[]{:S(2)}) collective-permute-start(bf16[736,128]{1,0:T(8,128)(2,1)S(1)} %get-tuple-element.133), channel_id=1, source_target_pairs={{0,16},{1,5},{2,18},{3,7},{4,20},{5,1},{6,22},{7,3},{8,24},{9,13},... | collective-permute-start | bytes 565256 | tf_op jit(solution)/shard_map/ppermute | solution.py:441
  37.5 0.2 shard_map.268
  37.7 1.6 %collective-permute-start.20 = (bf16[704,128]{1,0:T(8,128)(2,1)S(1)}, bf16[704,128]{1,0:T(8,128)(2,1)S(1)}, u32[]{:S(2)}, u32[]{:S(2)}) collective-permute-start(bf16[704,128]{1,0:T(8,128)(2,1)S(1)} %get-tuple-element.137), channel_id=1, source_target_pairs={{0,8},{1,3},{2,10},{3,1},{4,12},{5,7},{6,14},{7,5},{8,0},{9,11},{1... | collective-permute-start | bytes 540680 | tf_op jit(solution)/shard_map/ppermute | solution.py:441
  39.4 1.3 %shard_map.269 = (bf16[8,256,128]{2,1,0:T(8,128)(2,1)}, f32[8,256,128]{2,1,0:T(8,128)}, f32[8,128]{1,0:T(8,128)S(1)}) custom-call(bf16[704,128]{1,0:T(8,128)(2,1)S(1)} %get-tuple-element.126.after.own, bf16[512,128]{1,0:T(8,128)(2,1)S(1)} %collective-permute-done.12.tw_recv.tw_recv_ref, bf16[4,256,128]{2,1,0:T(8,128)(2,1)S(1)} %get-tuple-element.127.out_keep, ...), custom_call_target="tpu_custom_call" | custom-call | flops 1 | tf_op jit(solution)/shard_map/pallas_call | solution.py:24
  40.7 2.9 %collective-permute-done.15.recv = bf16[736,128]{1,0:T(8,128)(2,1)S(1)} collective-permute-done((bf16[736,128]{1,0:T(8,128)(2,1)S(1)}, bf16[736,128]{1,0:T(8,128)(2,1)S(1)}, u32[]{:S(2)}, u32[]{:S(2)}) %collective-permute-start.15) | collective-permute-done | bytes 188448 | tf_op jit(solution)/shard_map/ppermute | solution.py:441
  43.5 0.1 shard_map.270.own.after_ref
  43.6 1.3 %collective-permute-start.17 = (bf16[784,128]{1,0:T(8,128)(2,1)S(1)}, bf16[784,128]{1,0:T(8,128)(2,1)S(1)}, u32[]{:S(2)}, u32[]{:S(2)}) collective-permute-start(bf16[784,128]{1,0:T(8,128)(2,1)S(1)} %shard_map.270.own.after_ref), channel_id=1, source_target_pairs={{0,2},{1,3},{2,0},{3,1},{4,6},{5,7},{6,4},{7,5},{8,10},{9,11},{10,... | collective-permute-start | bytes 602120 | tf_op jit(solution)/shard_map/ppermute | solution.py:441
  45.0 1.6 %collective-permute-start.21 = (bf16[704,128]{1,0:T(8,128)(2,1)S(1)}, bf16[704,128]{1,0:T(8,128)(2,1)S(1)}, u32[]{:S(2)}, u32[]{:S(2)}) collective-permute-start(bf16[704,128]{1,0:T(8,128)(2,1)S(1)} %shard_map.273.own), channel_id=1, source_target_pairs={{0,4},{1,17},{2,6},{3,19},{4,0},{5,21},{6,2},{7,23},{8,12},{9,25},... | collective-permute-start | bytes 540680 | tf_op jit(solution)/shard_map/ppermute | solution.py:441
  46.6 2.8 %collective-permute-done.17.recv = bf16[784,128]{1,0:T(8,128)(2,1)S(1)} collective-permute-done((bf16[784,128]{1,0:T(8,128)(2,1)S(1)}, bf16[784,128]{1,0:T(8,128)(2,1)S(1)}, u32[]{:S(2)}, u32[]{:S(2)}) %collective-permute-start.17) | collective-permute-done | bytes 200736 | tf_op jit(solution)/shard_map/ppermute | solution.py:441
  49.4 0.7 collective-permute-start.18
  50.1 0.4 collective-permute-done.21.recv
  50.6 3.1 %collective-permute-start.22 = (bf16[704,128]{1,0:T(8,128)(2,1)S(1)}, bf16[704,128]{1,0:T(8,128)(2,1)S(1)}, u32[]{:S(2)}, u32[]{:S(2)}) collective-permute-start(bf16[704,128]{1,0:T(8,128)(2,1)S(1)} %shard_map.274.own), channel_id=1, source_target_pairs={{0,16},{1,5},{2,18},{3,7},{4,20},{5,1},{6,22},{7,3},{8,24},{9,13},... | collective-permute-start | bytes 540680 | tf_op jit(solution)/shard_map/ppermute | solution.py:441
  53.7 5.6 %collective-permute-done.18.recv = bf16[848,128]{1,0:T(8,128)(2,1)S(1)} collective-permute-done((bf16[848,128]{1,0:T(8,128)(2,1)S(1)}, bf16[848,128]{1,0:T(8,128)(2,1)S(1)}, u32[]{:S(2)}, u32[]{:S(2)}) %collective-permute-start.18) | collective-permute-done | bytes 217120 | tf_op jit(solution)/shard_map/ppermute | solution.py:441
  59.3 0.1 shard_map.272
  59.4 0.1 collective-permute-start.23
  59.5 1.8 %collective-permute-start.25 = (bf16[704,128]{1,0:T(8,128)(2,1)S(1)}, bf16[704,128]{1,0:T(8,128)(2,1)S(1)}, u32[]{:S(2)}, u32[]{:S(2)}) collective-permute-start(bf16[704,128]{1,0:T(8,128)(2,1)S(1)} %shard_map.275.after_ref.own), channel_id=1, source_target_pairs={{0,8},{1,3},{2,10},{3,1},{4,12},{5,7},{6,14},{7,5},{8,0},{9,11},{1... | collective-permute-start | bytes 540680 | tf_op jit(solution)/shard_map/ppermute | solution.py:441
  61.3 1.3 %collective-permute-done.19.other_ref = bf16[256,128]{1,0:T(8,128)(2,1)S(1)} collective-permute-done((bf16[256,128]{1,0:T(8,128)(2,1)S(1)}, bf16[256,128]{1,0:T(8,128)(2,1)S(1)}, u32[]{:S(2)}, u32[]{:S(2)}) %collective-permute-start.19) | collective-permute-done | bytes 65568 | tf_op jit(solution)/shard_map/ppermute | solution.py:445
  62.5 3.3 %shard_map.276 = (f32[1000,512]{1,0:T(8,128)}, f32[512,128]{1,0:T(8,128)}, f32[1,128]{1,0:T(1,128)}, f32[8,128]{1,0:T(8,128)S(1)}) custom-call(bf16[256,128]{1,0:T(8,128)(2,1)S(1)} %get-tuple-element.136.rows_ref, bf16[256,128]{1,0:T(8,128)(2,1)S(1)} %collective-permute-done.19.other_ref, f32[1000,512]{1,0:T(8,128)S(1)} %copy-done, ...), custom_call_target="tpu_custom_call" | custom-call | flops 1 | tf_op jit(solution)/shard_map/pallas_call | solution.py:24
  65.8 1.0 %collective-permute-done.23.recv = bf16[720,128]{1,0:T(8,128)(2,1)S(1)} collective-permute-done((bf16[720,128]{1,0:T(8,128)(2,1)S(1)}, bf16[720,128]{1,0:T(8,128)(2,1)S(1)}, u32[]{:S(2)}, u32[]{:S(2)}) %collective-permute-start.23) | collective-permute-done | bytes 184352 | tf_op jit(solution)/shard_map/ppermute | solution.py:441
  66.8 1.6 %collective-permute-start.24 = (bf16[1440,128]{1,0:T(8,128)(2,1)S(1)}, bf16[1440,128]{1,0:T(8,128)(2,1)S(1)}, u32[]{:S(2)}, u32[]{:S(2)}) collective-permute-start(bf16[1440,128]{1,0:T(8,128)(2,1)S(1)} %shard_map.277.after_ref.own1), channel_id=1, source_target_pairs={{0,4},{1,9},{2,6},{3,11},{4,0},{5,13},{6,2},{7,15},{8,12},{9,1},{1... | collective-permute-start | bytes 1105928 | tf_op jit(solution)/shard_map/ppermute | solution.py:441
  68.5 1.3 %collective-permute-start.26 = (bf16[1408,128]{1,0:T(8,128)(2,1)S(1)}, bf16[1408,128]{1,0:T(8,128)(2,1)S(1)}, u32[]{:S(2)}, u32[]{:S(2)}) collective-permute-start(bf16[1408,128]{1,0:T(8,128)(2,1)S(1)} %shard_map.278.own2), channel_id=1, source_target_pairs={{0,2},{1,9},{2,0},{3,11},{4,6},{5,13},{6,4},{7,15},{8,10},{9,1},{1... | collective-permute-start | bytes 1081352 | tf_op jit(solution)/shard_map/ppermute | solution.py:441
  69.8 6.1 %collective-permute-done.26.recv2 = bf16[1408,128]{1,0:T(8,128)(2,1)S(1)} collective-permute-done((bf16[1408,128]{1,0:T(8,128)(2,1)S(1)}, bf16[1408,128]{1,0:T(8,128)(2,1)S(1)}, u32[]{:S(2)}, u32[]{:S(2)}) %collective-permute-start.26) | collective-permute-done | bytes 360480 | tf_op jit(solution)/shard_map/ppermute | solution.py:441
  76.0 1.8 %shard_map.279 = (f32[2304,128]{1,0:T(8,128)}, f32[9,128,256]{2,1,0:T(8,128)}, f32[3,256,128]{2,1,0:T(8,128)}, f32[128,256]{1,0:T(8,128)}, f32[3,128]{1,0:T(4,12...) custom-call(f32[8,128]{1,0:T(8,128)S(1)} %get-tuple-element.140.after_ref, ...), custom_call_target="tpu_custom_call" | custom-call | flops 1 | tf_op jit(solution)/shard_map/pallas_call | solution.py:24
  (47 shorter events, 0.4 us)
Async XLA Ops:
  0.6 0.7 copy-start.9
  0.7 0.7 copy-start.10
  0.7 0.7 copy-start.11
  0.7 0.7 copy-start.12
  0.7 0.7 copy-start.13
  0.7 0.7 copy-start.14
  0.7 1.1 %copy-start.1 = (bf16[3,3,256,128]{3,2,1,0:T(8,128)(2,1)S(1)}, bf16[3,3,256,128]{3,2,1,0:T(8,128)(2,1)}, u32[]{:S(2)}) copy-start(bf16[3,3,256,128]{3,2,1,0:T(8,128)(2,1)} %param.20) | copy-start | bytes 1769476
  0.7 1.1 %copy-start.3 = (bf16[512,128]{1,0:T(8,128)(2,1)S(1)}, bf16[512,128]{1,0:T(8,128)(2,1)}, u32[]{:S(2)}) copy-start(bf16[512,128]{1,0:T(8,128)(2,1)} %tw_own_ref.1) | copy-start | bytes 393220
  0.7 1.1 %copy-start.8 = (s32[8]{0:T(128)S(1)}, s32[8]{0:T(128)}, u32[]{:S(2)}) copy-start(s32[8]{0:T(128)} %steps.3) | copy-start | bytes 100
  0.7 4.8 %collective-permute-start.1 = (bf16[9,256,128]{2,1,0:T(8,128)(2,1)}, bf16[9,256,128]{2,1,0:T(8,128)(2,1)}, u32[]{:S(2)}, u32[]{:S(2)}) collective-permute-start(bf16[9,256,128]{2,1,0:T(8,128)(2,1)} %bitcast.10), channel_id=1, source_target_pairs={{0,1},{1,0},{2,3},{3,2},{4,5},{5,4},{6,7},{7,6},{8,9},{9,8},{10,11... | collective-permute-start | bytes 1769480 | tf_op jit(solution)/shard_map/ppermute | solution.py:445
  1.3 4.1 %collective-permute-start = (bf16[8,256,128]{2,1,0:T(8,128)(2,1)}, bf16[8,256,128]{2,1,0:T(8,128)(2,1)S(1)}, u32[]{:S(2)}, u32[]{:S(2)}) collective-permute-start(bf16[8,256,128]{2,1,0:T(8,128)(2,1)} %x_own.5), channel_id=1, source_target_pairs={{0,1},{1,0},{2,3},{3,2},{4,5},{5,4},{6,7},{7,6},{8,9},{9,8},{10,11... | collective-permute-start | bytes 1572872 | tf_op jit(solution)/shard_map/ppermute | solution.py:445
  1.3 1.6 %copy-start = (f32[1000,512]{1,0:T(8,128)S(1)}, f32[1000,512]{1,0:T(8,128)}, u32[]{:S(2)}) copy-start(f32[1000,512]{1,0:T(8,128)} %table_ref.1) | copy-start | bytes 6144004
  3.0 1.2 %copy-start.2 = (bf16[3,3,128,256]{3,2,1,0:T(8,128)(2,1)S(1)}, bf16[3,3,128,256]{3,2,1,0:T(8,128)(2,1)}, u32[]{:S(2)}) copy-start(bf16[3,3,128,256]{3,2,1,0:T(8,128)(2,1)} %param.24) | copy-start | bytes 1769476
  3.0 1.5 %copy-start.6 = (bf16[256,3,128]{2,0,1:T(8,128)(2,1)S(1)}, bf16[256,3,128]{2,0,1:T(8,128)(2,1)}, u32[]{:S(2)}) copy-start(bf16[256,3,128]{2,0,1:T(8,128)(2,1)} %param.25) | copy-start | bytes 589828
  3.0 2.0 %copy-start.4 = (bf16[8,256,128]{2,1,0:T(8,128)(2,1)S(1)}, bf16[8,256,128]{2,1,0:T(8,128)(2,1)}, u32[]{:S(2)}) copy-start(bf16[8,256,128]{2,1,0:T(8,128)(2,1)} %g_own.1) | copy-start | bytes 1572868
  3.0 2.4 %copy-start.7 = (bf16[128,256]{1,0:T(8,128)(2,1)S(1)}, bf16[128,256]{1,0:T(8,128)(2,1)}, u32[]{:S(2)}) copy-start(bf16[128,256]{1,0:T(8,128)(2,1)} %ow_own.1) | copy-start | bytes 196612
  3.0 2.5 %copy-start.5 = (bf16[8,256,128]{2,1,0:T(8,128)(2,1)S(1)}, bf16[8,256,128]{2,1,0:T(8,128)(2,1)}, u32[]{:S(2)}) copy-start(bf16[8,256,128]{2,1,0:T(8,128)(2,1)} %x_own.5) | copy-start | bytes 1572868
  3.7 1.3 %collective-permute-start.2 = (f32[24,128]{1,0:T(8,128)S(1)}, f32[24,128]{1,0:T(8,128)S(1)}, u32[]{:S(2)}, u32[]{:S(2)}) collective-permute-start(f32[24,128]{1,0:T(8,128)S(1)} %shard_map.255.pk_own), channel_id=1, source_target_pairs={{0,1},{1,0},{2,3},{3,2},{4,5},{5,4},{6,7},{7,6},{8,9},{9,8},{10,11... | collective-permute-start | bytes 36872 | tf_op jit(solution)/shard_map/ppermute | solution.py:445
  4.1 5.0 %collective-permute-start.3 = (bf16[9,128,256]{2,1,0:T(8,128)(2,1)S(1)}, bf16[9,128,256]{2,1,0:T(8,128)(2,1)S(1)}, u32[]{:S(2)}, u32[]{:S(2)}) collective-permute-start(bf16[9,128,256]{2,1,0:T(8,128)(2,1)S(1)} %bitcast.13), channel_id=1, source_target_pairs={{0,1},{1,0},{2,3},{3,2},{4,5},{5,4},{6,7},{7,6},{8,9},{9,8},{10,11... | collective-permute-start | bytes 1769480 | tf_op jit(solution)/shard_map/ppermute | solution.py:445
  4.5 4.7 %collective-permute-start.5 = (bf16[3,256,128]{2,1,0:T(8,128)(2,1)S(1)}, bf16[3,256,128]{2,1,0:T(8,128)(2,1)S(1)}, u32[]{:S(2)}, u32[]{:S(2)}) collective-permute-start(bf16[3,256,128]{2,1,0:T(8,128)(2,1)S(1)} %bitcast.15), channel_id=1, source_target_pairs={{0,1},{1,0},{2,3},{3,2},{4,5},{5,4},{6,7},{7,6},{8,9},{9,8},{10,11... | collective-permute-start | bytes 589832 | tf_op jit(solution)/shard_map/ppermute | solution.py:445
  5.0 4.2 %collective-permute-start.4 = (bf16[8,256,128]{2,1,0:T(8,128)(2,1)S(1)}, bf16[8,256,128]{2,1,0:T(8,128)(2,1)S(1)}, u32[]{:S(2)}, u32[]{:S(2)}) collective-permute-start(bf16[8,256,128]{2,1,0:T(8,128)(2,1)S(1)} %copy-done.4), channel_id=1, source_target_pairs={{0,1},{1,0},{2,3},{3,2},{4,5},{5,4},{6,7},{7,6},{8,9},{9,8},{10,11... | collective-permute-start | bytes 1572872 | tf_op jit(solution)/shard_map/ppermute | solution.py:445
  5.3 3.8 %collective-permute-start.6 = (bf16[128,256]{1,0:T(8,128)(2,1)S(1)}, bf16[128,256]{1,0:T(8,128)(2,1)S(1)}, u32[]{:S(2)}, u32[]{:S(2)}) collective-permute-start(bf16[128,256]{1,0:T(8,128)(2,1)S(1)} %copy-done.7), channel_id=1, source_target_pairs={{0,1},{1,0},{2,3},{3,2},{4,5},{5,4},{6,7},{7,6},{8,9},{9,8},{10,11... | collective-permute-start | bytes 196616 | tf_op jit(solution)/shard_map/ppermute | solution.py:445
  16.1 3.8 %collective-permute-start.7 = (bf16[2816,128]{1,0:T(8,128)(2,1)S(1)}, bf16[2816,128]{1,0:T(8,128)(2,1)S(1)}, u32[]{:S(2)}, u32[]{:S(2)}) collective-permute-start(bf16[2816,128]{1,0:T(8,128)(2,1)S(1)} %get-tuple-element.96), channel_id=1, source_target_pairs={{0,1},{1,0},{2,3},{3,2},{4,5},{5,4},{6,7},{7,6},{8,9},{9,8},{10,11... | collective-permute-start | bytes 2162696 | tf_op jit(solution)/shard_map/ppermute | solution.py:445
  21.5 1.8 %collective-permute-start.9 = (bf16[1536,128]{1,0:T(8,128)(2,1)S(1)}, bf16[1536,128]{1,0:T(8,128)(2,1)S(1)}, u32[]{:S(2)}, u32[]{:S(2)}) collective-permute-start(bf16[1536,128]{1,0:T(8,128)(2,1)S(1)} %get-tuple-element.111), channel_id=1, source_target_pairs={{0,1},{1,0},{2,3},{3,2},{4,5},{5,4},{6,7},{7,6},{8,9},{9,8},{10,11... | collective-permute-start | bytes 1179656 | tf_op jit(solution)/shard_map/ppermute | solution.py:445
  23.7 3.1 %collective-permute-start.10 = (bf16[1280,128]{1,0:T(8,128)(2,1)S(1)}, bf16[1280,128]{1,0:T(8,128)(2,1)S(1)}, u32[]{:S(2)}, u32[]{:S(2)}) collective-permute-start(bf16[1280,128]{1,0:T(8,128)(2,1)S(1)} %get-tuple-element.115), channel_id=1, source_target_pairs={{0,1},{1,0},{2,3},{3,2},{4,5},{5,4},{6,7},{7,6},{8,9},{9,8},{10,11... | collective-permute-start | bytes 983048 | tf_op jit(solution)/shard_map/ppermute | solution.py:445
  23.9 13.6 %collective-permute-start.8 = (bf16[1408,128]{1,0:T(8,128)(2,1)S(1)}, bf16[1408,128]{1,0:T(8,128)(2,1)S(1)}, u32[]{:S(2)}, u32[]{:S(2)}) collective-permute-start(bf16[1408,128]{1,0:T(8,128)(2,1)S(1)} %get-tuple-element.102), channel_id=1, source_target_pairs={{0,2},{1,9},{2,0},{3,11},{4,6},{5,13},{6,4},{7,15},{8,10},{9,1},{1... | collective-permute-start | bytes 1081352 | tf_op jit(solution)/shard_map/ppermute | solution.py:441
  27.1 7.5 %collective-permute-start.11 = (bf16[1424,128]{1,0:T(8,128)(2,1)S(1)}, bf16[1424,128]{1,0:T(8,128)(2,1)S(1)}, u32[]{:S(2)}, u32[]{:S(2)}) collective-permute-start(bf16[1424,128]{1,0:T(8,128)(2,1)S(1)} %get-tuple-element.118), channel_id=1, source_target_pairs={{0,4},{1,9},{2,6},{3,11},{4,0},{5,13},{6,2},{7,15},{8,12},{9,1},{1... | collective-permute-start | bytes 1093640 | tf_op jit(solution)/shard_map/ppermute | solution.py:441
  31.1 8.3 %collective-permute-start.13 = (bf16[4,256,128]{2,1,0:T(8,128)(2,1)S(1)}, bf16[4,256,128]{2,1,0:T(8,128)(2,1)S(1)}, u32[]{:S(2)}, u32[]{:S(2)}) collective-permute-start(bf16[4,256,128]{2,1,0:T(8,128)(2,1)S(1)} %get-tuple-element.128), channel_id=1, source_target_pairs={{0,1},{1,0},{2,3},{3,2},{4,5},{5,4},{6,7},{7,6},{8,9},{9,8},{10,11... | collective-permute-start | bytes 786440 | tf_op jit(solution)/shard_map/ppermute | solution.py:445
  31.1 8.2 %collective-permute-start.14 = (bf16[4,256,128]{2,1,0:T(8,128)(2,1)S(1)}, bf16[4,256,128]{2,1,0:T(8,128)(2,1)S(1)}, u32[]{:S(2)}, u32[]{:S(2)}) collective-permute-start(bf16[4,256,128]{2,1,0:T(8,128)(2,1)S(1)} %get-tuple-element.130), channel_id=1, source_target_pairs={{0,1},{1,0},{2,3},{3,2},{4,5},{5,4},{6,7},{7,6},{8,9},{9,8},{10,11... | collective-permute-start | bytes 786440 | tf_op jit(solution)/shard_map/ppermute | solution.py:445
  34.9 8.7 %collective-permute-start.15 = (bf16[736,128]{1,0:T(8,128)(2,1)S(1)}, bf16[736,128]{1,0:T(8,128)(2,1)S(1)}, u32[]{:S(2)}, u32[]{:S(2)}) collective-permute-start(bf16[736,128]{1,0:T(8,128)(2,1)S(1)} %get-tuple-element.133), channel_id=1, source_target_pairs={{0,16},{1,5},{2,18},{3,7},{4,20},{5,1},{6,22},{7,3},{8,24},{9,13},... | collective-permute-start | bytes 565256 | tf_op jit(solution)/shard_map/ppermute | solution.py:441
  37.5 1.8 %collective-permute-start.12 = (bf16[512,128]{1,0:T(8,128)(2,1)S(1)}, bf16[512,128]{1,0:T(8,128)(2,1)S(1)}, u32[]{:S(2)}, u32[]{:S(2)}) collective-permute-start(bf16[512,128]{1,0:T(8,128)(2,1)S(1)} %copy-done.3), channel_id=1, source_target_pairs={{0,1},{1,0},{2,3},{3,2},{4,5},{5,4},{6,7},{7,6},{8,9},{9,8},{10,11... | collective-permute-start | bytes 393224 | tf_op jit(solution)/shard_map/ppermute | solution.py:445
  37.7 7.2 %collective-permute-start.20 = (bf16[704,128]{1,0:T(8,128)(2,1)S(1)}, bf16[704,128]{1,0:T(8,128)(2,1)S(1)}, u32[]{:S(2)}, u32[]{:S(2)}) collective-permute-start(bf16[704,128]{1,0:T(8,128)(2,1)S(1)} %get-tuple-element.137), channel_id=1, source_target_pairs={{0,8},{1,3},{2,10},{3,1},{4,12},{5,7},{6,14},{7,5},{8,0},{9,11},{1... | collective-permute-start | bytes 540680 | tf_op jit(solution)/shard_map/ppermute | solution.py:441
  39.4 1.3 %collective-permute-start.16 = (f32[16,128]{1,0:T(8,128)S(1)}, f32[16,128]{1,0:T(8,128)S(1)}, u32[]{:S(2)}, u32[]{:S(2)}) collective-permute-start(f32[16,128]{1,0:T(8,128)S(1)} %get-tuple-element.135), channel_id=1, source_target_pairs={{0,1},{1,0},{2,3},{3,2},{4,5},{5,4},{6,7},{7,6},{8,9},{9,8},{10,11... | collective-permute-start | bytes 24584 | tf_op jit(solution)/shard_map/ppermute | solution.py:445
  43.6 5.8 %collective-permute-start.17 = (bf16[784,128]{1,0:T(8,128)(2,1)S(1)}, bf16[784,128]{1,0:T(8,128)(2,1)S(1)}, u32[]{:S(2)}, u32[]{:S(2)}) collective-permute-start(bf16[784,128]{1,0:T(8,128)(2,1)S(1)} %shard_map.270.own.after_ref), channel_id=1, source_target_pairs={{0,2},{1,3},{2,0},{3,1},{4,6},{5,7},{6,4},{7,5},{8,10},{9,11},{10,... | collective-permute-start | bytes 602120 | tf_op jit(solution)/shard_map/ppermute | solution.py:441
  45.0 5.6 %collective-permute-start.21 = (bf16[704,128]{1,0:T(8,128)(2,1)S(1)}, bf16[704,128]{1,0:T(8,128)(2,1)S(1)}, u32[]{:S(2)}, u32[]{:S(2)}) collective-permute-start(bf16[704,128]{1,0:T(8,128)(2,1)S(1)} %shard_map.273.own), channel_id=1, source_target_pairs={{0,4},{1,17},{2,6},{3,19},{4,0},{5,21},{6,2},{7,23},{8,12},{9,25},... | collective-permute-start | bytes 540680 | tf_op jit(solution)/shard_map/ppermute | solution.py:441
  49.4 9.9 %collective-permute-start.18 = (bf16[848,128]{1,0:T(8,128)(2,1)S(1)}, bf16[848,128]{1,0:T(8,128)(2,1)S(1)}, u32[]{:S(2)}, u32[]{:S(2)}) collective-permute-start(bf16[848,128]{1,0:T(8,128)(2,1)S(1)} %shard_map.271.own.after_ref), channel_id=1, source_target_pairs={{0,8},{1,17},{2,10},{3,19},{4,12},{5,21},{6,14},{7,23},{8,0},{9,25... | collective-permute-start | bytes 651272 | tf_op jit(solution)/shard_map/ppermute | solution.py:441
  50.6 8.8 %collective-permute-start.22 = (bf16[704,128]{1,0:T(8,128)(2,1)S(1)}, bf16[704,128]{1,0:T(8,128)(2,1)S(1)}, u32[]{:S(2)}, u32[]{:S(2)}) collective-permute-start(bf16[704,128]{1,0:T(8,128)(2,1)S(1)} %shard_map.274.own), channel_id=1, source_target_pairs={{0,16},{1,5},{2,18},{3,7},{4,20},{5,1},{6,22},{7,3},{8,24},{9,13},... | collective-permute-start | bytes 540680 | tf_op jit(solution)/shard_map/ppermute | solution.py:441
  59.4 7.4 %collective-permute-start.23 = (bf16[720,128]{1,0:T(8,128)(2,1)S(1)}, bf16[720,128]{1,0:T(8,128)(2,1)S(1)}, u32[]{:S(2)}, u32[]{:S(2)}) collective-permute-start(bf16[720,128]{1,0:T(8,128)(2,1)S(1)} %get-tuple-element.138.after_ref.own), channel_id=1, source_target_pairs={{0,16},{1,5},{2,18},{3,7},{4,20},{5,1},{6,22},{7,3},{8,24},{9,13},... | collective-permute-start | bytes 552968 | tf_op jit(solution)/shard_map/ppermute | solution.py:441
  59.5 8.9 %collective-permute-start.25 = (bf16[704,128]{1,0:T(8,128)(2,1)S(1)}, bf16[704,128]{1,0:T(8,128)(2,1)S(1)}, u32[]{:S(2)}, u32[]{:S(2)}) collective-permute-start(bf16[704,128]{1,0:T(8,128)(2,1)S(1)} %shard_map.275.after_ref.own), channel_id=1, source_target_pairs={{0,8},{1,3},{2,10},{3,1},{4,12},{5,7},{6,14},{7,5},{8,0},{9,11},{1... | collective-permute-start | bytes 540680 | tf_op jit(solution)/shard_map/ppermute | solution.py:441
  61.3 1.3 %collective-permute-start.19 = (bf16[256,128]{1,0:T(8,128)(2,1)S(1)}, bf16[256,128]{1,0:T(8,128)(2,1)S(1)}, u32[]{:S(2)}, u32[]{:S(2)}) collective-permute-start(bf16[256,128]{1,0:T(8,128)(2,1)S(1)} %get-tuple-element.136.rows_ref), channel_id=1, source_target_pairs={{0,1},{1,0},{2,3},{3,2},{4,5},{5,4},{6,7},{7,6},{8,9},{9,8},{10,11... | collective-permute-start | bytes 196616 | tf_op jit(solution)/shard_map/ppermute | solution.py:445
  66.8 9.1 %collective-permute-start.24 = (bf16[1440,128]{1,0:T(8,128)(2,1)S(1)}, bf16[1440,128]{1,0:T(8,128)(2,1)S(1)}, u32[]{:S(2)}, u32[]{:S(2)}) collective-permute-start(bf16[1440,128]{1,0:T(8,128)(2,1)S(1)} %shard_map.277.after_ref.own1), channel_id=1, source_target_pairs={{0,4},{1,9},{2,6},{3,11},{4,0},{5,13},{6,2},{7,15},{8,12},{9,1},{1... | collective-permute-start | bytes 1105928 | tf_op jit(solution)/shard_map/ppermute | solution.py:441
  68.5 7.5 %collective-permute-start.26 = (bf16[1408,128]{1,0:T(8,128)(2,1)S(1)}, bf16[1408,128]{1,0:T(8,128)(2,1)S(1)}, u32[]{:S(2)}, u32[]{:S(2)}) collective-permute-start(bf16[1408,128]{1,0:T(8,128)(2,1)S(1)} %shard_map.278.own2), channel_id=1, source_target_pairs={{0,2},{1,9},{2,0},{3,11},{4,6},{5,13},{6,4},{7,15},{8,10},{9,1},{1... | collective-permute-start | bytes 1081352 | tf_op jit(solution)/shard_map/ppermute | solution.py:441

commit v5 on v4

--- a/solution.py
+++ b/solution.py
@@ -109,7 +109,7 @@
 
 
 def sigmoid(v):
-    return 1.0 / (1.0 + jnp.exp(-v))
+    return 0.5 + 0.5 * jnp.tanh(0.5 * v)
 
 
 def put_windows(win, values):
@@ -232,35 +232,34 @@
         thirds[m][...] = (unit * prm[GAIN + 2 : GAIN + 3] + prm[BIAS + 2 : BIAS + 3]).astype(BF16)
     for m in range(n):
         a3 = thirds[m][...]
-        qkvs[m][0] = (dot(a3, qw[0]) + prm[QKV_B : QKV_B + 1]).astype(BF16)
-        qkvs[m][1] = dot(a3, qw[1]).astype(BF16)
+        q = (dot(a3, qw[0]) + prm[QKV_B : QKV_B + 1]).astype(BF16)
+        k = dot(a3, qw[1]).astype(BF16) * BF16(scale)
+        qkvs[m][0] = q * BF16(scale)
+        qkvs[m][1] = k
         qkvs[m][2] = (dot(a3, qw[2]) + prm[QKV_B + 1 : QKV_B + 2]).astype(BF16)
-    for m in range(n):
-        s = dot_bt(qkvs[m][0], qkvs[m][1]) * scale
+        s = dot_bt(q, k)
         e = jnp.exp(s - jnp.max(s, axis=1, keepdims=True))
         p = e * (1.0 / jnp.sum(e, axis=1, keepdims=True))
         probs[m][...] = p
         lows[m][...] = p.astype(BF16)
-    for m in range(n):
         gb = join(first, g_own[me * n + m], g_recv[me * n + m], 1)
         douts[m][...] = dot_bt(gb, ow[...]).astype(BF16)
     for m in range(n):
-        a = dot(lows[m][...], qkvs[m][2]).astype(BF16)
+        p_low, p, do, v = lows[m][...], probs[m][...], douts[m][...], qkvs[m][2]
+        a = dot(p_low, v).astype(BF16)
         atts[m][...] = a
-        result = mids[m][...] + dot(a, ow[...]) + prm[OUT_B : OUT_B + 1]
+        dp = dot_bt(do, v)
+        ds = (p * (dp - jnp.sum(p * dp, axis=1, keepdims=True))).astype(BF16)
+        grads[m][2] = dot_at(p_low, do).astype(BF16)
+        lows[m][...] = ds
+    for m in range(n):
+        ds = lows[m][...]
+        grads[m][0] = dot(ds, qkvs[m][1]).astype(BF16)
+        grads[m][1] = dot_at(ds, qkvs[m][0]).astype(BF16)
+        result = mids[m][...] + dot(atts[m][...], ow[...]) + prm[OUT_B : OUT_B + 1]
         keep, send = split(first, result.astype(BF16))
         out_keep[m] = keep
         out_send[m] = send
-    for m in range(n):
-        p = probs[m][...]
-        dp = dot_bt(douts[m][...], qkvs[m][2])
-        ds = (p * (dp - jnp.sum(p * dp, axis=1, keepdims=True))).astype(BF16)
-        grads[m][2] = dot_at(lows[m][...], douts[m][...]).astype(BF16)
-        lows[m][...] = ds
-    for m in range(n):
-        ds = lows[m][...]
-        grads[m][0] = (dot(ds, qkvs[m][1]) * scale).astype(BF16)
-        grads[m][1] = (dot_at(ds, qkvs[m][0]) * scale).astype(BF16)
     gains, biases, mid_bias, out_bias = [], [], [], []
     for m in range(n):
         grad = dot_bt(grads[m][0], qw[0]) + dot_bt(grads[m][1], qw[1]) + dot_bt(grads[m][2], qw[2])
@@ -296,7 +295,6 @@
 
 
 CONV2_TAPS = (range(0, 7), range(7, 9))
-CONV1_TAPS = (range(0, 4), range(4, 8), range(8, 9))
 
 
 def conv2_rows(taps, first, act_t, win, keep, send):
@@ -318,9 +316,17 @@
     conv2_rows(CONV2_TAPS[0], lax.axis_index("mp") == 0, act_t, win, keep, send)
 
 
-def last_conv2_kernel(after, act_t, *rest):
-    win, (keep, send) = rest[:-2], rest[-2:]
-    conv2_rows(CONV2_TAPS[1], lax.axis_index("mp") == 0, act_t, win, keep, send)
+def last_grad_kernel(after, act2_t, act1_t, *rest):
+    n = act1_t.shape[1] // PIX
+    win3, win4, (keep, send) = rest[:n], rest[n : 2 * n], rest[2 * n :]
+    first = lax.axis_index("mp") == 0
+    conv2_rows(CONV2_TAPS[1], first, act2_t, win3, keep, send)
+    at = len(CONV2_TAPS[1]) * C
+    for t in range(9):
+        shifted = jnp.concatenate([window(w, 2 - t // 3, 2 - t % 3) for w in win4], axis=0)
+        g_keep, g_send = split(first, dot(act1_t[...], shifted).astype(BF16))
+        keep[at + t * C : at + (t + 1) * C] = g_keep
+        send[at + t * C : at + (t + 1) * C] = g_send
 
 
 def hidden_back_kernel(steps, after, hid, stat, wfull, prm, *rest):
@@ -338,9 +344,8 @@
         back, gain_grad, bias_grad = norm_back(grad, unit, gain, rstd)
         gains.append(gain_grad)
         biases.append(bias_grad)
-        low = back.astype(BF16).astype(F32)
-        times.append(col_sum(low))
-        put_windows(win4[m], low)
+        times.append(col_sum(back))
+        put_windows(win4[m], back)
     me = lax.axis_index("mp")
     lane = lax.broadcasted_iota(jnp.int32, (1, HALF), 1)
     step_row = jnp.zeros((1, HALF), jnp.int32)
@@ -355,24 +360,6 @@
     sums[1:2] = sum(biases)
     sums[2:3] = sum(times)
     sums[3:8] = jnp.zeros((5, C), F32)
-
-
-def conv1_grad_kernel(taps, count):
-    def body(act_t, *rest):
-        n = act_t.shape[1] // PIX
-        win, others, (keep, send) = rest[:n], rest[n : n + count], rest[-2:]
-        first = lax.axis_index("mp") == 0
-        at = 0
-        for ref, other in zip((keep, send), others):
-            at = other.shape[0]
-            ref[0:at] = other[...]
-        for i, t in enumerate(taps):
-            shifted = jnp.concatenate([window(w, 2 - t // 3, 2 - t % 3) for w in win], axis=0)
-            g_keep, g_send = split(first, dot(act_t[...], shifted).astype(BF16))
-            keep[at + i * C : at + (i + 1) * C] = g_keep
-            send[at + i * C : at + (i + 1) * C] = g_send
-
-    return body
 
 
 def input_back_kernel(after, x_own, x_recv, stat, wfull, prm, dmid, sums2, sums3, out_send, *rest):
@@ -611,27 +598,26 @@
     return call(body, outs, *args, scratch=scratch, specs={5: ANYWHERE}, limit=24)
 
 
-def weight_results(chains, after):
-    def body(after_ref, own1, recv1, own2, recv2, *refs):
-        conv1, conv2, qkv, out_w, gains, biases, conv_b, qkv_b, out_b = refs[:9]
-        reads = []
-        for chain, own, recv, values in zip(chains, (own1, own2), (recv1, recv2), refs[9:]):
-            me, rows = digit(chain.steps[-1]), own.shape[0]
-            values[part(me, rows)] = own[...]
-            values[part(1 - me, rows)] = recv[...]
-            reads.append(row_reader(values, chain.piece, values.shape[0] >> chain.cut))
-        cut = len(CONV2_TAPS[0])
-        for t in range(9):
-            read, at = (reads[1], t) if t < cut else (reads[0], t - cut)
-            for h in range(2):
-                conv2[t, :, h * HALF : (h + 1) * HALF] = read((2 * at + h) * HALF, HALF)
-        conv1[...] = reads[0]((9 - cut) * C, 9 * C)
-        at = cut * C
-        for j in range(3):
-            qkv[j] = reads[1](at + j * C, C)
+def laid(chain, own, recv, values):
+    me, rows = digit(chain.steps[-1]), own.shape[0]
+    values[part(me, rows)] = own[...]
+    values[part(1 - me, rows)] = recv[...]
+    return row_reader(values, chain.piece, values.shape[0] >> chain.cut)
+
+
+def put_taps(conv2, at, taps, read):
+    for i in range(taps):
         for h in range(2):
-            out_w[:, h * HALF : (h + 1) * HALF] = reads[1](at + 3 * C + h * HALF, HALF)
-        values, chain = refs[9], chains[0]
+            conv2[at + i, :, h * HALF : (h + 1) * HALF] = read((2 * i + h) * HALF, HALF)
+
+
+def early_results(chain, after):
+    taps = len(CONV2_TAPS[1])
+
+    def body(after_ref, own, recv, conv1, last, gains, biases, conv_b, qkv_b, out_b, values):
+        read = laid(chain, own, recv, values)
+        put_taps(last, 0, taps, read)
+        conv1[...] = read(taps * C, 9 * C)
         full = values.shape[0] >> chain.cut
         small = None
         for p in range(1 << chain.cut):
@@ -645,12 +631,29 @@
         out_b[...] = small[10:11]
 
     outs = [
-        ((9 * C, HALF), F32), ((9, HALF, C), F32), ((3, C, HALF), F32), ((HALF, C), F32),
+        ((9 * C, HALF), F32), ((taps, HALF, C), F32),
         ((3, HALF), F32), ((3, HALF), F32), ((2, HALF), F32), ((2, HALF), F32), ((1, HALF), F32),
     ]
-    scratch = [pltpu.VMEM((2 * chain.own.shape[0], HALF), BF16) for chain in chains]
-    args = [v for chain in chains for v in (chain.own, chain.recv)]
-    return call(body, outs, after, *args, scratch=scratch)
+    scratch = [pltpu.VMEM((2 * chain.own.shape[0], HALF), BF16)]
+    return call(body, outs, after, chain.own, chain.recv, scratch=scratch)
+
+
+def late_results(chain, last):
+    taps = len(CONV2_TAPS[0])
+
+    def body(last_ref, own, recv, conv2, qkv, out_w, values):
+        read = laid(chain, own, recv, values)
+        put_taps(conv2, 0, taps, read)
+        conv2[taps:9] = last_ref[...]
+        at = taps * C
+        for j in range(3):
+            qkv[j] = read(at + j * C, C)
+        for h in range(2):
+            out_w[:, h * HALF : (h + 1) * HALF] = read(at + 3 * C + h * HALF, HALF)
+
+    outs = [((9, HALF, C), F32), ((3, C, HALF), F32), ((HALF, C), F32)]
+    scratch = [pltpu.VMEM((2 * chain.own.shape[0], HALF), BF16)]
+    return call(body, outs, last, chain.own, chain.recv, scratch=scratch)
 
 
 def row_reader(values, piece, full):
@@ -738,17 +741,11 @@
     ]
     start_exchange(late, (late_pair,), (), (sums2,))
 
-    def conv1_grad(taps, others=(), after=()):
-        shape = ((len(taps) * C + sum(v.shape[0] for v in others[:1]), HALF), BF16)
-        specs = {1 + n + len(others) + i: ANYWHERE for i in range(len(after))}
-        return call(conv1_grad_kernel(taps, len(others)), [shape, shape], act1_t, *win4, *others, *after, specs=specs)
-
-    shape = ((len(CONV2_TAPS[1]) * C, HALF), BF16)
-    part = call(last_conv2_kernel, [shape, shape], late.own, act2_t, *win3, specs={0: ANYWHERE})
-    first_pair = swapped(*conv1_grad(CONV1_TAPS[0], part))
-    part = conv1_grad(CONV1_TAPS[1], after=(first_pair[0],))
-    last_pair = swapped(*conv1_grad(CONV1_TAPS[2], part, (first_pair[1],)))
-    start_exchange(early, (first_pair, last_pair), (time_rows,), (late.own,))
+    shape = ((11 * C, HALF), BF16)
+    early_pair = swapped(
+        *call(last_grad_kernel, [shape, shape], late.own, act2_t, act1_t, *win3, *win4, specs={0: ANYWHERE})
+    )
+    start_exchange(early, (early_pair,), (time_rows,), (late.own,))
     mg_keep, mg_send, out_send, rows_keep, rows_send = call(
         input_back_kernel,
         [(half_shape, F32), (half_shape, BF16), (half_shape, BF16), ((SUMS, HALF), F32), ((SUMS, HALF), F32)],
@@ -772,7 +769,8 @@
             table_grad, tw_grad, time_b, turn = time_results(
                 n, early.gathered, swap_mp(early.gathered), early.bits, temb_table, temb_weight, tw_recv, late.own,
             )
-    conv1, conv2, qkv, out_w, gains, biases, conv_b, qkv_b, out_b = weight_results(chains, turn)
+    conv1, last_taps, gains, biases, conv_b, qkv_b, out_b = early_results(early, turn)
+    conv2, qkv, out_w = late_results(late, last_taps)
     return (
         maps_out, maps_grad, table_grad, gains, biases, conv1.reshape(3, 3, C, HALF), conv_b, tw_grad,
         time_b.reshape(HALF), conv2.reshape(3, 3, HALF, C), jnp.transpose(qkv, (1, 0, 2)), qkv_b, out_w,

time: 78 us -> 75.8 us (0.972)
  waiting for transfers between devices: 24.4 us -> 21.5 us
  starting transfers between devices: 23.7 us -> 24.7 us
    ppermute x12, waiting for transfers between devices: 22 us -> 19.9 us  [swap_dp(): return lax.ppermute(values, ('dp', 'mp'), pairs)]
    ppermute x12, starting transfers between devices: 20.2 us -> 21.2 us  [swap_dp(): return lax.ppermute(values, ('dp', 'mp'), pairs)]
    ppermute x15 -> x14, waiting for transfers between devices: 2.42 us -> 1.6 us  [swap_mp(): return lax.ppermute(values, 'mp', [(0, 1), (1, 0)])]
    pallas_call x26 -> x24, Pallas kernels: 27.1 us -> 26.8 us  [call(): pl.pallas_call(body, out_shape=tuple((jax.ShapeDtypeStruct(s, d) for s, d...]
    ppermute x15 -> x14, starting transfers between devices: 3.5 us -> 3.41 us  [swap_mp(): return lax.ppermute(values, 'mp', [(0, 1), (1, 0)])]
  transfers between devices with their start and end apart: 27 -> 26, of which waited for: 10 -> 10; matrix products, arithmetic and copies ran while one was open for 0% -> 0% of each run, Pallas kernels for 21% -> 22%
where the time goes in v5:
time: 75.8 us; the launch traced here: 75.6 us
  Pallas kernels  26.8 us (35%)
  starting transfers between devices  24.7 us (33%)
  waiting for transfers between devices  21.5 us (28%)
  local copies, waits for them, and re-layouts  1.65 us (2%)
  between operations  0.93 us (1%)
    pallas_call x24, Pallas kernels, call(): pl.pallas_call(body, out_shape=tuple((jax.ShapeDtypeStruct(s, d) for s, d...  26.8 us
    ppermute x12, starting transfers between devices, swap_dp(): return lax.ppermute(values, ('dp', 'mp'), pairs)  21.2 us
    ppermute x12, waiting for transfers between devices, swap_dp(): return lax.ppermute(values, ('dp', 'mp'), pairs)  19.9 us
    ppermute x14, starting transfers between devices, swap_mp(): return lax.ppermute(values, 'mp', [(0, 1), (1, 0)])  3.41 us
    unnamed x30, local copies, waits for them, and re-layouts  1.61 us
    ppermute x14, waiting for transfers between devices, swap_mp(): return lax.ppermute(values, 'mp', [(0, 1), (1, 0)])  1.6 us
  transfers between devices with their start and end apart: 26, of which 10 were waited for; matrix products, arithmetic and copies ran while one was open for 0% of the time, Pallas kernels for 22%

profile of v5, /device:TPU:0, one launch (start us, length us, event | category | flops | bytes accessed | tf_op | source)
XLA Modules:
  0.0 75.6 jit_solution(2303694857309583990)
XLA Ops:
  0.7 0.5 collective-permute-start.1
  1.3 0.1 collective-permute-start
  1.3 0.0 copy-done.10
  1.3 0.0 copy-done.11
  1.4 0.0 copy-done.12
  1.4 0.0 copy-done.14
  1.4 0.4 copy-done.1
  1.8 0.0 copy-done.3
  1.8 1.1 %copy-done = f32[1000,512]{1,0:T(8,128)S(1)} copy-done((f32[1000,512]{1,0:T(8,128)S(1)}, f32[1000,512]{1,0:T(8,128)}, u32[]{:S(2)}) %copy-start) | copy-done | bytes 2048024
  3.0 0.0 copy-start.5
  3.0 0.7 shard_map.255.pk_own
  3.7 0.4 collective-permute-start.2
  4.1 0.3 collective-permute-start.3
  4.5 0.2 collective-permute-start.5
  4.6 0.3 collective-permute-done.2.pk_recv
  5.0 0.3 collective-permute-start.4
  5.3 0.2 collective-permute-start.6
  5.5 0.0 collective-permute-done.1.w_recv
  5.5 3.6 %shard_map.256 = (f32[4,256,256]{2,1,0:T(8,128)S(1)}, bf16[256,1024]{1,0:T(8,128)(2,1)S(1)}, bf16[256,1024]{1,0:T(8,128)(2,1)S(1)}, f32[8,256]{1,0:T(8,128)S(1)}...) custom-call(bf16[8,256,128]{2,1,0:T(8,128)(2,1)S(1)} %copy-done.5, ...), custom_call_target="tpu_custom_call" | custom-call | flops 99999997952 | tf_op jit(solution)/shard_map/pallas_call | solution.py:24
  9.1 0.0 collective-permute-done.5.qw_recv
  9.1 0.0 collective-permute-done.4.g_recv
  9.1 5.6 %shard_map.257 = (bf16[4,256,128]{2,1,0:T(8,128)(2,1)S(1)}, bf16[4,256,128]{2,1,0:T(8,128)(2,1)S(1)}, f32[4,256,256]{2,1,0:T(8,128)S(1)}, bf16[1024,128]{1,0:T(8...) custom-call(bf16[8,256,128]{2,1,0:T(8,128)(2,1)S(1)} %copy-done.5, ...), custom_call_target="tpu_custom_call" | custom-call | flops 1 | tf_op jit(solution)/shard_map/pallas_call | solution.py:24
  14.7 1.2 %shard_map.258 = (bf16[2816,128]{1,0:T(8,128)(2,1)S(1)}, bf16[2816,128]{1,0:T(8,128)(2,1)S(1)}) custom-call(bf16[256,1024]{1,0:T(8,128)(2,1)S(1)} %get-tuple-element.78.act_t.act2_t, bf16[1024,128]{1,0:T(8,128)(2,1)S(1)} %get-tuple-element.84.wg_keep, bf16[1024,128]{1,0:T(8,128)(2,1)S(1)} %get-tuple-element.85.wg_send, ...), custom_call_target="tpu_custom_call" | custom-call | flops 1 | tf_op jit(solution)/shard_map/pallas_call | solution.py:24
  15.9 0.4 collective-permute-start.7
  16.3 3.1 %shard_map.259 = (f32[8,256]{1,0:T(8,128)S(1)}, bf16[16,128]{1,0:T(8,128)(2,1)S(1)}, bf16[3,288,256]{2,1,0:T(8,128)(2,1)S(1)}, bf16[3,288,256]{2,1,0:T(8,128)(2,...) custom-call(s32[8]{0:T(128)S(1)} %copy-done.8, ...), custom_call_target="tpu_custom_call" | custom-call | flops 1 | tf_op jit(solution)/shard_map/pallas_call | solution.py:24
  19.4 0.6 shard_map.260
  20.0 1.7 %shard_map.261 = (bf16[2816,128]{1,0:T(8,128)(2,1)S(1)}, bf16[2816,128]{1,0:T(8,128)(2,1)S(1)}) custom-call(bf16[1408,128]{1,0:T(8,128)(2,1)S(1)} %get-tuple-element.96.after.refs_3_.own, bf16[256,1024]{1,0:T(8,128)(2,1)S(1)} %get-tuple-element.78.act_t.act2_t, bf16[256,1024]{1,0:T(8,128)(2,1)S(1)} %get-tuple-element.98.act1_t, ...), custom_call_target="tpu_custom_call" | custom-call | flops 1 | tf_op jit(solution)/shard_map/pallas_call | solution.py:24
  21.7 0.2 collective-permute-start.9
  21.9 2.8 %collective-permute-start.8 = (bf16[1408,128]{1,0:T(8,128)(2,1)S(1)}, bf16[1408,128]{1,0:T(8,128)(2,1)S(1)}, u32[]{:S(2)}, u32[]{:S(2)}) collective-permute-start(bf16[1408,128]{1,0:T(8,128)(2,1)S(1)} %get-tuple-element.97), channel_id=1, source_target_pairs={{0,2},{1,9},{2,0},{3,11},{4,6},{5,13},{6,4},{7,15},{8,10},{9,1},{1... | collective-permute-start | bytes 1081352 | tf_op jit(solution)/shard_map/ppermute | solution.py:428
  24.8 0.0 collective-permute-done.9.refs_1_
  24.8 0.4 shard_map.262
  25.2 1.9 %collective-permute-start.10 = (bf16[1424,128]{1,0:T(8,128)(2,1)S(1)}, bf16[1424,128]{1,0:T(8,128)(2,1)S(1)}, u32[]{:S(2)}, u32[]{:S(2)}) collective-permute-start(bf16[1424,128]{1,0:T(8,128)(2,1)S(1)} %get-tuple-element.107), channel_id=1, source_target_pairs={{0,4},{1,9},{2,6},{3,11},{4,0},{5,13},{6,2},{7,15},{8,12},{9,1},{1... | collective-permute-start | bytes 1093640 | tf_op jit(solution)/shard_map/ppermute | solution.py:428
  27.1 2.3 %shard_map.263 = (f32[4,256,128]{2,1,0:T(8,128)S(1)}, bf16[4,256,128]{2,1,0:T(8,128)(2,1)S(1)}, bf16[4,256,128]{2,1,0:T(8,128)(2,1)S(1)}, f32[16,128]{1,0:T(8,128)S(1)}, f32[16,128]{1,0:T(8,128)S(1)}) custom-call(bf16[1424,128]{1,0:T(8,128)(2,1)S(1)} %get-tuple-element.106.after.own, bf16[8,256,128]{2,1,0:T(8,128)(2,1)S(1)} %copy-done.5, ...), custom_call_target="tpu_custom_call" | custom-call | flops 10000000000 | tf_op jit(solution)/shard_map/pallas_call | solution.py:24
  29.5 0.2 collective-permute-start.12
  29.6 0.4 collective-permute-start.13
  30.0 2.7 %collective-permute-done.10.recv = bf16[1424,128]{1,0:T(8,128)(2,1)S(1)} collective-permute-done((bf16[1424,128]{1,0:T(8,128)(2,1)S(1)}, bf16[1424,128]{1,0:T(8,128)(2,1)S(1)}, u32[]{:S(2)}, u32[]{:S(2)}) %collective-permute-start.10) | collective-permute-done | bytes 364576 | tf_op jit(solution)/shard_map/ppermute | solution.py:428
  32.7 0.2 shard_map.264
  32.9 3.0 %collective-permute-start.14 = (bf16[736,128]{1,0:T(8,128)(2,1)S(1)}, bf16[736,128]{1,0:T(8,128)(2,1)S(1)}, u32[]{:S(2)}, u32[]{:S(2)}) collective-permute-start(bf16[736,128]{1,0:T(8,128)(2,1)S(1)} %get-tuple-element.122), channel_id=1, source_target_pairs={{0,16},{1,5},{2,18},{3,7},{4,20},{5,1},{6,22},{7,3},{8,24},{9,13},... | collective-permute-start | bytes 565256 | tf_op jit(solution)/shard_map/ppermute | solution.py:428
  36.0 0.0 collective-permute-done.8.recv
  36.0 0.2 shard_map.265
  36.2 1.6 %collective-permute-start.19 = (bf16[704,128]{1,0:T(8,128)(2,1)S(1)}, bf16[704,128]{1,0:T(8,128)(2,1)S(1)}, u32[]{:S(2)}, u32[]{:S(2)}) collective-permute-start(bf16[704,128]{1,0:T(8,128)(2,1)S(1)} %get-tuple-element.126), channel_id=1, source_target_pairs={{0,8},{1,3},{2,10},{3,1},{4,12},{5,7},{6,14},{7,5},{8,0},{9,11},{1... | collective-permute-start | bytes 540680 | tf_op jit(solution)/shard_map/ppermute | solution.py:428
  37.8 0.1 collective-permute-start.15
  37.9 1.2 %shard_map.266 = (bf16[8,256,128]{2,1,0:T(8,128)(2,1)}, f32[8,256,128]{2,1,0:T(8,128)}, f32[8,128]{1,0:T(8,128)S(1)}) custom-call(bf16[704,128]{1,0:T(8,128)(2,1)S(1)} %get-tuple-element.115.after.own, bf16[512,128]{1,0:T(8,128)(2,1)S(1)} %collective-permute-done.11.tw_recv.tw_recv_ref, bf16[4,256,128]{2,1,0:T(8,128)(2,1)S(1)} %get-tuple-element.116.out_keep, ...), custom_call_target="tpu_custom_call" | custom-call | flops 1 | tf_op jit(solution)/shard_map/pallas_call | solution.py:24
  39.2 2.4 %collective-permute-done.14.recv = bf16[736,128]{1,0:T(8,128)(2,1)S(1)} collective-permute-done((bf16[736,128]{1,0:T(8,128)(2,1)S(1)}, bf16[736,128]{1,0:T(8,128)(2,1)S(1)}, u32[]{:S(2)}, u32[]{:S(2)}) %collective-permute-start.14) | collective-permute-done | bytes 188448 | tf_op jit(solution)/shard_map/ppermute | solution.py:428
  41.6 0.1 shard_map.267.own.after_ref
  41.7 1.9 %collective-permute-start.16 = (bf16[784,128]{1,0:T(8,128)(2,1)S(1)}, bf16[784,128]{1,0:T(8,128)(2,1)S(1)}, u32[]{:S(2)}, u32[]{:S(2)}) collective-permute-start(bf16[784,128]{1,0:T(8,128)(2,1)S(1)} %shard_map.267.own.after_ref), channel_id=1, source_target_pairs={{0,2},{1,3},{2,0},{3,1},{4,6},{5,7},{6,4},{7,5},{8,10},{9,11},{10,... | collective-permute-start | bytes 602120 | tf_op jit(solution)/shard_map/ppermute | solution.py:428
  43.6 1.6 %collective-permute-start.20 = (bf16[704,128]{1,0:T(8,128)(2,1)S(1)}, bf16[704,128]{1,0:T(8,128)(2,1)S(1)}, u32[]{:S(2)}, u32[]{:S(2)}) collective-permute-start(bf16[704,128]{1,0:T(8,128)(2,1)S(1)} %shard_map.270.own), channel_id=1, source_target_pairs={{0,4},{1,17},{2,6},{3,19},{4,0},{5,21},{6,2},{7,23},{8,12},{9,25},... | collective-permute-start | bytes 540680 | tf_op jit(solution)/shard_map/ppermute | solution.py:428
  45.2 2.2 %collective-permute-done.16.recv = bf16[784,128]{1,0:T(8,128)(2,1)S(1)} collective-permute-done((bf16[784,128]{1,0:T(8,128)(2,1)S(1)}, bf16[784,128]{1,0:T(8,128)(2,1)S(1)}, u32[]{:S(2)}, u32[]{:S(2)}) %collective-permute-start.16) | collective-permute-done | bytes 200736 | tf_op jit(solution)/shard_map/ppermute | solution.py:428
  47.5 1.0 %collective-permute-start.17 = (bf16[848,128]{1,0:T(8,128)(2,1)S(1)}, bf16[848,128]{1,0:T(8,128)(2,1)S(1)}, u32[]{:S(2)}, u32[]{:S(2)}) collective-permute-start(bf16[848,128]{1,0:T(8,128)(2,1)S(1)} %shard_map.268.own.after_ref), channel_id=1, source_target_pairs={{0,8},{1,17},{2,10},{3,19},{4,12},{5,21},{6,14},{7,23},{8,0},{9,25... | collective-permute-start | bytes 651272 | tf_op jit(solution)/shard_map/ppermute | solution.py:428
  48.5 0.7 collective-permute-done.20.recv
  49.2 2.9 %collective-permute-start.21 = (bf16[704,128]{1,0:T(8,128)(2,1)S(1)}, bf16[704,128]{1,0:T(8,128)(2,1)S(1)}, u32[]{:S(2)}, u32[]{:S(2)}) collective-permute-start(bf16[704,128]{1,0:T(8,128)(2,1)S(1)} %shard_map.271.own), channel_id=1, source_target_pairs={{0,16},{1,5},{2,18},{3,7},{4,20},{5,1},{6,22},{7,3},{8,24},{9,13},... | collective-permute-start | bytes 540680 | tf_op jit(solution)/shard_map/ppermute | solution.py:428
  52.1 5.6 %collective-permute-done.17.recv = bf16[848,128]{1,0:T(8,128)(2,1)S(1)} collective-permute-done((bf16[848,128]{1,0:T(8,128)(2,1)S(1)}, bf16[848,128]{1,0:T(8,128)(2,1)S(1)}, u32[]{:S(2)}, u32[]{:S(2)}) %collective-permute-start.17) | collective-permute-done | bytes 217120 | tf_op jit(solution)/shard_map/ppermute | solution.py:428
  57.7 0.1 shard_map.269
  57.8 0.1 collective-permute-start.22
  57.9 1.2 %collective-permute-start.24 = (bf16[704,128]{1,0:T(8,128)(2,1)S(1)}, bf16[704,128]{1,0:T(8,128)(2,1)S(1)}, u32[]{:S(2)}, u32[]{:S(2)}) collective-permute-start(bf16[704,128]{1,0:T(8,128)(2,1)S(1)} %shard_map.272.after_ref.own), channel_id=1, source_target_pairs={{0,8},{1,3},{2,10},{3,1},{4,12},{5,7},{6,14},{7,5},{8,0},{9,11},{1... | collective-permute-start | bytes 540680 | tf_op jit(solution)/shard_map/ppermute | solution.py:428
  59.1 1.3 %collective-permute-done.18.other_ref = bf16[256,128]{1,0:T(8,128)(2,1)S(1)} collective-permute-done((bf16[256,128]{1,0:T(8,128)(2,1)S(1)}, bf16[256,128]{1,0:T(8,128)(2,1)S(1)}, u32[]{:S(2)}, u32[]{:S(2)}) %collective-permute-start.18) | collective-permute-done | bytes 65568 | tf_op jit(solution)/shard_map/ppermute | solution.py:432
  60.4 3.2 %shard_map.273 = (f32[1000,512]{1,0:T(8,128)}, f32[512,128]{1,0:T(8,128)}, f32[1,128]{1,0:T(1,128)}, f32[8,128]{1,0:T(8,128)S(1)}) custom-call(bf16[256,128]{1,0:T(8,128)(2,1)S(1)} %get-tuple-element.125.rows_ref, bf16[256,128]{1,0:T(8,128)(2,1)S(1)} %collective-permute-done.18.other_ref, f32[1000,512]{1,0:T(8,128)S(1)} %copy-done, ...), custom_call_target="tpu_custom_call" | custom-call | flops 1 | tf_op jit(solution)/shard_map/pallas_call | solution.py:24
  63.6 1.5 %collective-permute-done.22.recv = bf16[720,128]{1,0:T(8,128)(2,1)S(1)} collective-permute-done((bf16[720,128]{1,0:T(8,128)(2,1)S(1)}, bf16[720,128]{1,0:T(8,128)(2,1)S(1)}, u32[]{:S(2)}, u32[]{:S(2)}) %collective-permute-start.22) | collective-permute-done | bytes 184352 | tf_op jit(solution)/shard_map/ppermute | solution.py:428
  65.2 1.6 %collective-permute-start.23 = (bf16[1440,128]{1,0:T(8,128)(2,1)S(1)}, bf16[1440,128]{1,0:T(8,128)(2,1)S(1)}, u32[]{:S(2)}, u32[]{:S(2)}) collective-permute-start(bf16[1440,128]{1,0:T(8,128)(2,1)S(1)} %shard_map.274.own.after_ref), channel_id=1, source_target_pairs={{0,4},{1,9},{2,6},{3,11},{4,0},{5,13},{6,2},{7,15},{8,12},{9,1},{1... | collective-permute-start | bytes 1105928 | tf_op jit(solution)/shard_map/ppermute | solution.py:428
  66.8 1.6 %collective-permute-start.25 = (bf16[1408,128]{1,0:T(8,128)(2,1)S(1)}, bf16[1408,128]{1,0:T(8,128)(2,1)S(1)}, u32[]{:S(2)}, u32[]{:S(2)}) collective-permute-start(bf16[1408,128]{1,0:T(8,128)(2,1)S(1)} %shard_map.276.own), channel_id=1, source_target_pairs={{0,2},{1,9},{2,0},{3,11},{4,6},{5,13},{6,4},{7,15},{8,10},{9,1},{1... | collective-permute-start | bytes 1081352 | tf_op jit(solution)/shard_map/ppermute | solution.py:428
  68.5 4.3 %collective-permute-done.23.recv = bf16[1440,128]{1,0:T(8,128)(2,1)S(1)} collective-permute-done((bf16[1440,128]{1,0:T(8,128)(2,1)S(1)}, bf16[1440,128]{1,0:T(8,128)(2,1)S(1)}, u32[]{:S(2)}, u32[]{:S(2)}) %collective-permute-start.23) | collective-permute-done | bytes 368672 | tf_op jit(solution)/shard_map/ppermute | solution.py:428
  72.8 1.2 %shard_map.275 = (f32[2304,128]{1,0:T(8,128)}, f32[2,128,256]{2,1,0:T(8,128)S(1)}, f32[3,128]{1,0:T(4,128)}, f32[3,128]{1,0:T(4,128)}, f32[2,128]{1,0:T(2,128)}, /*index=5*/f32[2,128]{1,0:T(2,128)}, f32[1,128]{1,0:T(1,128)}) custom-call(f32[8,128]{1,0:T(8,128)S(1)} %get-tuple-element.129.after_ref, bf16[1440,128]{1,0:T(8,128)(2,1)S(1)} %shard_map.274.own.after_ref, ...), custom_call_target="tpu_custom_call" | custom-call | flops 1 | tf_op jit(solution)/shard_map/pallas_call | solution.py:24
  74.0 0.4 collective-permute-done.25.recv
  74.3 1.3 %shard_map.277 = (f32[9,128,256]{2,1,0:T(8,128)}, f32[3,256,128]{2,1,0:T(8,128)}, f32[128,256]{1,0:T(8,128)}) custom-call(f32[2,128,256]{2,1,0:T(8,128)S(1)} %get-tuple-element.136.last_ref, bf16[1408,128]{1,0:T(8,128)(2,1)S(1)} %shard_map.276.own, bf16[1408,128]{1,0:T(8,128)(2,1)S(1)} %collective-permute-done.25.recv), custom_call_target="tpu_custom_call" | custom-call | flops 1 | tf_op jit(solution)/shard_map/pallas_call | solution.py:24
  (43 shorter events, 0.4 us)
Async XLA Ops:
  0.6 0.7 copy-start.9
  0.7 0.7 copy-start.10
  0.7 0.7 copy-start.11
  0.7 0.7 copy-start.12
  0.7 0.7 copy-start.13
  0.7 0.7 copy-start.14
  0.7 1.1 %copy-start.1 = (bf16[3,3,256,128]{3,2,1,0:T(8,128)(2,1)S(1)}, bf16[3,3,256,128]{3,2,1,0:T(8,128)(2,1)}, u32[]{:S(2)}) copy-start(bf16[3,3,256,128]{3,2,1,0:T(8,128)(2,1)} %param.20) | copy-start | bytes 1769476
  0.7 1.1 %copy-start.3 = (bf16[512,128]{1,0:T(8,128)(2,1)S(1)}, bf16[512,128]{1,0:T(8,128)(2,1)}, u32[]{:S(2)}) copy-start(bf16[512,128]{1,0:T(8,128)(2,1)} %tw_own_ref.1) | copy-start | bytes 393220
  0.7 1.1 %copy-start.8 = (s32[8]{0:T(128)S(1)}, s32[8]{0:T(128)}, u32[]{:S(2)}) copy-start(s32[8]{0:T(128)} %steps.3) | copy-start | bytes 100
  0.7 4.8 %collective-permute-start.1 = (bf16[9,256,128]{2,1,0:T(8,128)(2,1)}, bf16[9,256,128]{2,1,0:T(8,128)(2,1)}, u32[]{:S(2)}, u32[]{:S(2)}) collective-permute-start(bf16[9,256,128]{2,1,0:T(8,128)(2,1)} %bitcast.10), channel_id=1, source_target_pairs={{0,1},{1,0},{2,3},{3,2},{4,5},{5,4},{6,7},{7,6},{8,9},{9,8},{10,11... | collective-permute-start | bytes 1769480 | tf_op jit(solution)/shard_map/ppermute | solution.py:432
  1.3 4.1 %collective-permute-start = (bf16[8,256,128]{2,1,0:T(8,128)(2,1)}, bf16[8,256,128]{2,1,0:T(8,128)(2,1)S(1)}, u32[]{:S(2)}, u32[]{:S(2)}) collective-permute-start(bf16[8,256,128]{2,1,0:T(8,128)(2,1)} %x_own.5), channel_id=1, source_target_pairs={{0,1},{1,0},{2,3},{3,2},{4,5},{5,4},{6,7},{7,6},{8,9},{9,8},{10,11... | collective-permute-start | bytes 1572872 | tf_op jit(solution)/shard_map/ppermute | solution.py:432
  1.3 1.6 %copy-start = (f32[1000,512]{1,0:T(8,128)S(1)}, f32[1000,512]{1,0:T(8,128)}, u32[]{:S(2)}) copy-start(f32[1000,512]{1,0:T(8,128)} %table_ref.1) | copy-start | bytes 6144004
  3.0 1.2 %copy-start.2 = (bf16[3,3,128,256]{3,2,1,0:T(8,128)(2,1)S(1)}, bf16[3,3,128,256]{3,2,1,0:T(8,128)(2,1)}, u32[]{:S(2)}) copy-start(bf16[3,3,128,256]{3,2,1,0:T(8,128)(2,1)} %param.24) | copy-start | bytes 1769476
  3.0 1.5 %copy-start.6 = (bf16[256,3,128]{2,0,1:T(8,128)(2,1)S(1)}, bf16[256,3,128]{2,0,1:T(8,128)(2,1)}, u32[]{:S(2)}) copy-start(bf16[256,3,128]{2,0,1:T(8,128)(2,1)} %param.25) | copy-start | bytes 589828
  3.0 2.0 %copy-start.4 = (bf16[8,256,128]{2,1,0:T(8,128)(2,1)S(1)}, bf16[8,256,128]{2,1,0:T(8,128)(2,1)}, u32[]{:S(2)}) copy-start(bf16[8,256,128]{2,1,0:T(8,128)(2,1)} %g_own.1) | copy-start | bytes 1572868
  3.0 2.3 %copy-start.7 = (bf16[128,256]{1,0:T(8,128)(2,1)S(1)}, bf16[128,256]{1,0:T(8,128)(2,1)}, u32[]{:S(2)}) copy-start(bf16[128,256]{1,0:T(8,128)(2,1)} %ow_own.1) | copy-start | bytes 196612
  3.0 2.5 %copy-start.5 = (bf16[8,256,128]{2,1,0:T(8,128)(2,1)S(1)}, bf16[8,256,128]{2,1,0:T(8,128)(2,1)}, u32[]{:S(2)}) copy-start(bf16[8,256,128]{2,1,0:T(8,128)(2,1)} %x_own.5) | copy-start | bytes 1572868
  3.7 1.3 %collective-permute-start.2 = (f32[24,128]{1,0:T(8,128)S(1)}, f32[24,128]{1,0:T(8,128)S(1)}, u32[]{:S(2)}, u32[]{:S(2)}) collective-permute-start(f32[24,128]{1,0:T(8,128)S(1)} %shard_map.255.pk_own), channel_id=1, source_target_pairs={{0,1},{1,0},{2,3},{3,2},{4,5},{5,4},{6,7},{7,6},{8,9},{9,8},{10,11... | collective-permute-start | bytes 36872 | tf_op jit(solution)/shard_map/ppermute | solution.py:432
  4.1 5.0 %collective-permute-start.3 = (bf16[9,128,256]{2,1,0:T(8,128)(2,1)S(1)}, bf16[9,128,256]{2,1,0:T(8,128)(2,1)S(1)}, u32[]{:S(2)}, u32[]{:S(2)}) collective-permute-start(bf16[9,128,256]{2,1,0:T(8,128)(2,1)S(1)} %bitcast.13), channel_id=1, source_target_pairs={{0,1},{1,0},{2,3},{3,2},{4,5},{5,4},{6,7},{7,6},{8,9},{9,8},{10,11... | collective-permute-start | bytes 1769480 | tf_op jit(solution)/shard_map/ppermute | solution.py:432
  4.5 4.6 %collective-permute-start.5 = (bf16[3,256,128]{2,1,0:T(8,128)(2,1)S(1)}, bf16[3,256,128]{2,1,0:T(8,128)(2,1)S(1)}, u32[]{:S(2)}, u32[]{:S(2)}) collective-permute-start(bf16[3,256,128]{2,1,0:T(8,128)(2,1)S(1)} %bitcast.15), channel_id=1, source_target_pairs={{0,1},{1,0},{2,3},{3,2},{4,5},{5,4},{6,7},{7,6},{8,9},{9,8},{10,11... | collective-permute-start | bytes 589832 | tf_op jit(solution)/shard_map/ppermute | solution.py:432
  5.0 4.1 %collective-permute-start.4 = (bf16[8,256,128]{2,1,0:T(8,128)(2,1)S(1)}, bf16[8,256,128]{2,1,0:T(8,128)(2,1)S(1)}, u32[]{:S(2)}, u32[]{:S(2)}) collective-permute-start(bf16[8,256,128]{2,1,0:T(8,128)(2,1)S(1)} %copy-done.4), channel_id=1, source_target_pairs={{0,1},{1,0},{2,3},{3,2},{4,5},{5,4},{6,7},{7,6},{8,9},{9,8},{10,11... | collective-permute-start | bytes 1572872 | tf_op jit(solution)/shard_map/ppermute | solution.py:432
  5.3 3.7 %collective-permute-start.6 = (bf16[128,256]{1,0:T(8,128)(2,1)S(1)}, bf16[128,256]{1,0:T(8,128)(2,1)S(1)}, u32[]{:S(2)}, u32[]{:S(2)}) collective-permute-start(bf16[128,256]{1,0:T(8,128)(2,1)S(1)} %copy-done.7), channel_id=1, source_target_pairs={{0,1},{1,0},{2,3},{3,2},{4,5},{5,4},{6,7},{7,6},{8,9},{9,8},{10,11... | collective-permute-start | bytes 196616 | tf_op jit(solution)/shard_map/ppermute | solution.py:432
  15.9 3.5 %collective-permute-start.7 = (bf16[2816,128]{1,0:T(8,128)(2,1)S(1)}, bf16[2816,128]{1,0:T(8,128)(2,1)S(1)}, u32[]{:S(2)}, u32[]{:S(2)}) collective-permute-start(bf16[2816,128]{1,0:T(8,128)(2,1)S(1)} %get-tuple-element.91), channel_id=1, source_target_pairs={{0,1},{1,0},{2,3},{3,2},{4,5},{5,4},{6,7},{7,6},{8,9},{9,8},{10,11... | collective-permute-start | bytes 2162696 | tf_op jit(solution)/shard_map/ppermute | solution.py:432
  21.7 3.1 %collective-permute-start.9 = (bf16[2816,128]{1,0:T(8,128)(2,1)S(1)}, bf16[2816,128]{1,0:T(8,128)(2,1)S(1)}, u32[]{:S(2)}, u32[]{:S(2)}) collective-permute-start(bf16[2816,128]{1,0:T(8,128)(2,1)S(1)} %get-tuple-element.104), channel_id=1, source_target_pairs={{0,1},{1,0},{2,3},{3,2},{4,5},{5,4},{6,7},{7,6},{8,9},{9,8},{10,11... | collective-permute-start | bytes 2162696 | tf_op jit(solution)/shard_map/ppermute | solution.py:432
  21.9 14.0 %collective-permute-start.8 = (bf16[1408,128]{1,0:T(8,128)(2,1)S(1)}, bf16[1408,128]{1,0:T(8,128)(2,1)S(1)}, u32[]{:S(2)}, u32[]{:S(2)}) collective-permute-start(bf16[1408,128]{1,0:T(8,128)(2,1)S(1)} %get-tuple-element.97), channel_id=1, source_target_pairs={{0,2},{1,9},{2,0},{3,11},{4,6},{5,13},{6,4},{7,15},{8,10},{9,1},{1... | collective-permute-start | bytes 1081352 | tf_op jit(solution)/shard_map/ppermute | solution.py:428
  25.2 7.5 %collective-permute-start.10 = (bf16[1424,128]{1,0:T(8,128)(2,1)S(1)}, bf16[1424,128]{1,0:T(8,128)(2,1)S(1)}, u32[]{:S(2)}, u32[]{:S(2)}) collective-permute-start(bf16[1424,128]{1,0:T(8,128)(2,1)S(1)} %get-tuple-element.107), channel_id=1, source_target_pairs={{0,4},{1,9},{2,6},{3,11},{4,0},{5,13},{6,2},{7,15},{8,12},{9,1},{1... | collective-permute-start | bytes 1093640 | tf_op jit(solution)/shard_map/ppermute | solution.py:428
  29.5 8.5 %collective-permute-start.12 = (bf16[4,256,128]{2,1,0:T(8,128)(2,1)S(1)}, bf16[4,256,128]{2,1,0:T(8,128)(2,1)S(1)}, u32[]{:S(2)}, u32[]{:S(2)}) collective-permute-start(bf16[4,256,128]{2,1,0:T(8,128)(2,1)S(1)} %get-tuple-element.117), channel_id=1, source_target_pairs={{0,1},{1,0},{2,3},{3,2},{4,5},{5,4},{6,7},{7,6},{8,9},{9,8},{10,11... | collective-permute-start | bytes 786440 | tf_op jit(solution)/shard_map/ppermute | solution.py:432
  29.6 8.3 %collective-permute-start.13 = (bf16[4,256,128]{2,1,0:T(8,128)(2,1)S(1)}, bf16[4,256,128]{2,1,0:T(8,128)(2,1)S(1)}, u32[]{:S(2)}, u32[]{:S(2)}) collective-permute-start(bf16[4,256,128]{2,1,0:T(8,128)(2,1)S(1)} %get-tuple-element.119), channel_id=1, source_target_pairs={{0,1},{1,0},{2,3},{3,2},{4,5},{5,4},{6,7},{7,6},{8,9},{9,8},{10,11... | collective-permute-start | bytes 786440 | tf_op jit(solution)/shard_map/ppermute | solution.py:432
  32.9 8.7 %collective-permute-start.14 = (bf16[736,128]{1,0:T(8,128)(2,1)S(1)}, bf16[736,128]{1,0:T(8,128)(2,1)S(1)}, u32[]{:S(2)}, u32[]{:S(2)}) collective-permute-start(bf16[736,128]{1,0:T(8,128)(2,1)S(1)} %get-tuple-element.122), channel_id=1, source_target_pairs={{0,16},{1,5},{2,18},{3,7},{4,20},{5,1},{6,22},{7,3},{8,24},{9,13},... | collective-permute-start | bytes 565256 | tf_op jit(solution)/shard_map/ppermute | solution.py:428
  36.0 1.8 %collective-permute-start.11 = (bf16[512,128]{1,0:T(8,128)(2,1)S(1)}, bf16[512,128]{1,0:T(8,128)(2,1)S(1)}, u32[]{:S(2)}, u32[]{:S(2)}) collective-permute-start(bf16[512,128]{1,0:T(8,128)(2,1)S(1)} %copy-done.3), channel_id=1, source_target_pairs={{0,1},{1,0},{2,3},{3,2},{4,5},{5,4},{6,7},{7,6},{8,9},{9,8},{10,11... | collective-permute-start | bytes 393224 | tf_op jit(solution)/shard_map/ppermute | solution.py:432
  36.2 7.4 %collective-permute-start.19 = (bf16[704,128]{1,0:T(8,128)(2,1)S(1)}, bf16[704,128]{1,0:T(8,128)(2,1)S(1)}, u32[]{:S(2)}, u32[]{:S(2)}) collective-permute-start(bf16[704,128]{1,0:T(8,128)(2,1)S(1)} %get-tuple-element.126), channel_id=1, source_target_pairs={{0,8},{1,3},{2,10},{3,1},{4,12},{5,7},{6,14},{7,5},{8,0},{9,11},{1... | collective-permute-start | bytes 540680 | tf_op jit(solution)/shard_map/ppermute | solution.py:428
  37.8 1.4 %collective-permute-start.15 = (f32[16,128]{1,0:T(8,128)S(1)}, f32[16,128]{1,0:T(8,128)S(1)}, u32[]{:S(2)}, u32[]{:S(2)}) collective-permute-start(f32[16,128]{1,0:T(8,128)S(1)} %get-tuple-element.124), channel_id=1, source_target_pairs={{0,1},{1,0},{2,3},{3,2},{4,5},{5,4},{6,7},{7,6},{8,9},{9,8},{10,11... | collective-permute-start | bytes 24584 | tf_op jit(solution)/shard_map/ppermute | solution.py:432
  41.7 5.8 %collective-permute-start.16 = (bf16[784,128]{1,0:T(8,128)(2,1)S(1)}, bf16[784,128]{1,0:T(8,128)(2,1)S(1)}, u32[]{:S(2)}, u32[]{:S(2)}) collective-permute-start(bf16[784,128]{1,0:T(8,128)(2,1)S(1)} %shard_map.267.own.after_ref), channel_id=1, source_target_pairs={{0,2},{1,3},{2,0},{3,1},{4,6},{5,7},{6,4},{7,5},{8,10},{9,11},{10,... | collective-permute-start | bytes 602120 | tf_op jit(solution)/shard_map/ppermute | solution.py:428
  43.6 5.6 %collective-permute-start.20 = (bf16[704,128]{1,0:T(8,128)(2,1)S(1)}, bf16[704,128]{1,0:T(8,128)(2,1)S(1)}, u32[]{:S(2)}, u32[]{:S(2)}) collective-permute-start(bf16[704,128]{1,0:T(8,128)(2,1)S(1)} %shard_map.270.own), channel_id=1, source_target_pairs={{0,4},{1,17},{2,6},{3,19},{4,0},{5,21},{6,2},{7,23},{8,12},{9,25},... | collective-permute-start | bytes 540680 | tf_op jit(solution)/shard_map/ppermute | solution.py:428
  47.5 10.2 %collective-permute-start.17 = (bf16[848,128]{1,0:T(8,128)(2,1)S(1)}, bf16[848,128]{1,0:T(8,128)(2,1)S(1)}, u32[]{:S(2)}, u32[]{:S(2)}) collective-permute-start(bf16[848,128]{1,0:T(8,128)(2,1)S(1)} %shard_map.268.own.after_ref), channel_id=1, source_target_pairs={{0,8},{1,17},{2,10},{3,19},{4,12},{5,21},{6,14},{7,23},{8,0},{9,25... | collective-permute-start | bytes 651272 | tf_op jit(solution)/shard_map/ppermute | solution.py:428
  49.2 8.6 %collective-permute-start.21 = (bf16[704,128]{1,0:T(8,128)(2,1)S(1)}, bf16[704,128]{1,0:T(8,128)(2,1)S(1)}, u32[]{:S(2)}, u32[]{:S(2)}) collective-permute-start(bf16[704,128]{1,0:T(8,128)(2,1)S(1)} %shard_map.271.own), channel_id=1, source_target_pairs={{0,16},{1,5},{2,18},{3,7},{4,20},{5,1},{6,22},{7,3},{8,24},{9,13},... | collective-permute-start | bytes 540680 | tf_op jit(solution)/shard_map/ppermute | solution.py:428
  57.8 7.3 %collective-permute-start.22 = (bf16[720,128]{1,0:T(8,128)(2,1)S(1)}, bf16[720,128]{1,0:T(8,128)(2,1)S(1)}, u32[]{:S(2)}, u32[]{:S(2)}) collective-permute-start(bf16[720,128]{1,0:T(8,128)(2,1)S(1)} %get-tuple-element.127.after_ref.own), channel_id=1, source_target_pairs={{0,16},{1,5},{2,18},{3,7},{4,20},{5,1},{6,22},{7,3},{8,24},{9,13},... | collective-permute-start | bytes 552968 | tf_op jit(solution)/shard_map/ppermute | solution.py:428
  57.9 8.8 %collective-permute-start.24 = (bf16[704,128]{1,0:T(8,128)(2,1)S(1)}, bf16[704,128]{1,0:T(8,128)(2,1)S(1)}, u32[]{:S(2)}, u32[]{:S(2)}) collective-permute-start(bf16[704,128]{1,0:T(8,128)(2,1)S(1)} %shard_map.272.after_ref.own), channel_id=1, source_target_pairs={{0,8},{1,3},{2,10},{3,1},{4,12},{5,7},{6,14},{7,5},{8,0},{9,11},{1... | collective-permute-start | bytes 540680 | tf_op jit(solution)/shard_map/ppermute | solution.py:428
  59.1 1.3 %collective-permute-start.18 = (bf16[256,128]{1,0:T(8,128)(2,1)S(1)}, bf16[256,128]{1,0:T(8,128)(2,1)S(1)}, u32[]{:S(2)}, u32[]{:S(2)}) collective-permute-start(bf16[256,128]{1,0:T(8,128)(2,1)S(1)} %get-tuple-element.125.rows_ref), channel_id=1, source_target_pairs={{0,1},{1,0},{2,3},{3,2},{4,5},{5,4},{6,7},{7,6},{8,9},{9,8},{10,11... | collective-permute-start | bytes 196616 | tf_op jit(solution)/shard_map/ppermute | solution.py:432
  65.2 7.6 %collective-permute-start.23 = (bf16[1440,128]{1,0:T(8,128)(2,1)S(1)}, bf16[1440,128]{1,0:T(8,128)(2,1)S(1)}, u32[]{:S(2)}, u32[]{:S(2)}) collective-permute-start(bf16[1440,128]{1,0:T(8,128)(2,1)S(1)} %shard_map.274.own.after_ref), channel_id=1, source_target_pairs={{0,4},{1,9},{2,6},{3,11},{4,0},{5,13},{6,2},{7,15},{8,12},{9,1},{1... | collective-permute-start | bytes 1105928 | tf_op jit(solution)/shard_map/ppermute | solution.py:428
  66.8 7.5 %collective-permute-start.25 = (bf16[1408,128]{1,0:T(8,128)(2,1)S(1)}, bf16[1408,128]{1,0:T(8,128)(2,1)S(1)}, u32[]{:S(2)}, u32[]{:S(2)}) collective-permute-start(bf16[1408,128]{1,0:T(8,128)(2,1)S(1)} %shard_map.276.own), channel_id=1, source_target_pairs={{0,2},{1,9},{2,0},{3,11},{4,6},{5,13},{6,4},{7,15},{8,10},{9,1},{1... | collective-permute-start | bytes 1081352 | tf_op jit(solution)/shard_map/ppermute | solution.py:428

commit v6 on v5

--- a/solution.py
+++ b/solution.py
@@ -154,9 +154,17 @@
     result[...] = jnp.zeros_like(result)
 
 
-def time_kernel(steps, pk, table, tw, w1, result):
+def time_kernel(steps, pk, table, tw, w1, result, step_out):
     total = result.shape[0] - PACK
+    n = total // 2
     result[0:PACK] = pk[...]
+    me = lax.axis_index("mp")
+    lane = lax.broadcasted_iota(jnp.int32, (1, HALF), 1)
+    step_row = jnp.zeros((1, HALF), jnp.int32)
+    for i in range(n):
+        step = steps[me * n + i]
+        step_row = jnp.where(lane == i, step >> 5, jnp.where(lane == n + i, step & 31, step_row))
+    step_out[...] = jnp.broadcast_to(step_row, (8, HALF)).astype(F32)
     rows = jnp.concatenate([table[pl.ds(steps[i], 1)] for i in range(total)], axis=0)
     e = rows * sigmoid(rows)
     e_high = e.astype(BF16)
@@ -329,7 +337,7 @@
         send[at + t * C : at + (t + 1) * C] = g_send
 
 
-def hidden_back_kernel(steps, after, hid, stat, wfull, prm, *rest):
+def hidden_back_kernel(step_row, after, hid, stat, wfull, prm, *rest):
     n = hid.shape[0]
     win3, (sums, time_rows), win4 = rest[:n], rest[n : n + 2], rest[n + 2 :]
     gain, bias = prm[GAIN + 1 : GAIN + 2], prm[BIAS + 1 : BIAS + 2]
@@ -346,15 +354,9 @@
         biases.append(bias_grad)
         times.append(col_sum(back))
         put_windows(win4[m], back)
-    me = lax.axis_index("mp")
-    lane = lax.broadcasted_iota(jnp.int32, (1, HALF), 1)
-    step_row = jnp.zeros((1, HALF), jnp.int32)
-    for i in range(n):
-        step = steps[me * n + i]
-        step_row = jnp.where(lane == i, step >> 5, jnp.where(lane == n + i, step & 31, step_row))
     rows = jnp.concatenate(times, axis=0)
     blank = jnp.zeros((8 - n, HALF), F32)
-    left = [rows[:, :HALF], step_row.astype(F32), blank[1:]]
+    left = [rows[:, :HALF], step_row[0:1], blank[1:]]
     time_rows[...] = jnp.concatenate(left + [rows[:, HALF:], blank], axis=0).astype(BF16)
     sums[0:1] = sum(gains)
     sums[1:2] = sum(biases)
@@ -688,10 +690,11 @@
     pk_own = jnp.concatenate(
         [norm_gain, norm_bias, conv_bias, qkv_bias, out_bias[None], temb_bias[None], blank]
     )
-    pk_own = call(
-        time_kernel, [((PACK + total, HALF), F32)], timesteps, pk_own, temb_table, temb_weight, w1_own,
+    pk_own, step_row = call(
+        time_kernel, [((PACK + total, HALF), F32), ((8, HALF), F32)],
+        timesteps, pk_own, temb_table, temb_weight, w1_own,
         specs={0: SCALAR},
-    )[0]
+    )
     pk_recv = swap_mp(pk_own)
     tw_recv = swap_mp(temb_weight)
     w2_own = conv2_weight.reshape(9, HALF, C)
@@ -732,8 +735,8 @@
     sums2, time_rows, *win4 = call(
         hidden_back_kernel,
         [((8, C), F32), ((EXTRA, HALF), BF16)] + [WIN] * n,
-        timesteps, late_pair[0], hid, stat1, w2_full, prm, *win3,
-        specs={0: SCALAR, 1: ANYWHERE},
+        step_row, late_pair[0], hid, stat1, w2_full, prm, *win3,
+        specs={1: ANYWHERE},
     )
 
     early, late = chains = [

time: 75.8 us -> 75.3 us (level)
  transfers between devices with their start and end apart: 26 -> 26, of which waited for: 10 -> 10; matrix products, arithmetic and copies ran while one was open for 0% -> 0% of each run, Pallas kernels for 22% -> 21%
where the time goes in v6:
time: 75.3 us; the launch traced here: 75.1 us
  Pallas kernels  26.3 us (35%)
  starting transfers between devices  24.6 us (33%)
  waiting for transfers between devices  21.6 us (29%)
  local copies, waits for them, and re-layouts  1.65 us (2%)
  between operations  0.93 us (1%)
    pallas_call x24, Pallas kernels, call(): pl.pallas_call(body, out_shape=tuple((jax.ShapeDtypeStruct(s, d) for s, d...  26.3 us
    ppermute x12, starting transfers between devices, swap_dp(): return lax.ppermute(values, ('dp', 'mp'), pairs)  21.2 us
    ppermute x12, waiting for transfers between devices, swap_dp(): return lax.ppermute(values, ('dp', 'mp'), pairs)  20 us
    ppermute x14, starting transfers between devices, swap_mp(): return lax.ppermute(values, 'mp', [(0, 1), (1, 0)])  3.42 us
    unnamed x30, local copies, waits for them, and re-layouts  1.61 us
    ppermute x14, waiting for transfers between devices, swap_mp(): return lax.ppermute(values, 'mp', [(0, 1), (1, 0)])  1.6 us
  transfers between devices with their start and end apart: 26, of which 10 were waited for; matrix products, arithmetic and copies ran while one was open for 0% of the time, Pallas kernels for 21%

profile of v6, /device:TPU:0, one launch (start us, length us, event | category | flops | bytes accessed | tf_op | source)
XLA Modules:
  0.0 75.1 jit_solution(13511702847908393165)
XLA Ops:
  0.7 0.5 collective-permute-start.1
  1.3 0.1 collective-permute-start
  1.3 0.0 copy-done.10
  1.3 0.0 copy-done.11
  1.4 0.0 copy-done.12
  1.4 0.0 copy-done.14
  1.4 0.4 copy-done.1
  1.8 0.0 copy-done.3
  1.8 1.1 %copy-done = f32[1000,512]{1,0:T(8,128)S(1)} copy-done((f32[1000,512]{1,0:T(8,128)S(1)}, f32[1000,512]{1,0:T(8,128)}, u32[]{:S(2)}) %copy-start) | copy-done | bytes 2048024
  3.0 0.0 copy-start.5
  3.0 0.7 shard_map.255
  3.7 0.4 collective-permute-start.2
  4.1 0.3 collective-permute-start.3
  4.5 0.2 collective-permute-start.5
  4.7 0.3 collective-permute-done.2.pk_recv
  5.0 0.3 collective-permute-start.4
  5.3 0.0 collective-permute-done.x_recv
  5.3 0.2 collective-permute-start.6
  5.5 3.6 %shard_map.256 = (f32[4,256,256]{2,1,0:T(8,128)S(1)}, bf16[256,1024]{1,0:T(8,128)(2,1)S(1)}, bf16[256,1024]{1,0:T(8,128)(2,1)S(1)}, f32[8,256]{1,0:T(8,128)S(1)}...) custom-call(bf16[8,256,128]{2,1,0:T(8,128)(2,1)S(1)} %copy-done.5, ...), custom_call_target="tpu_custom_call" | custom-call | flops 99999997952 | tf_op jit(solution)/shard_map/pallas_call | solution.py:24
  9.1 0.0 collective-permute-done.5.qw_recv
  9.1 0.0 collective-permute-done.4.g_recv
  9.1 5.6 %shard_map.257 = (bf16[4,256,128]{2,1,0:T(8,128)(2,1)S(1)}, bf16[4,256,128]{2,1,0:T(8,128)(2,1)S(1)}, f32[4,256,256]{2,1,0:T(8,128)S(1)}, bf16[1024,128]{1,0:T(8...) custom-call(bf16[8,256,128]{2,1,0:T(8,128)(2,1)S(1)} %copy-done.5, ...), custom_call_target="tpu_custom_call" | custom-call | flops 1 | tf_op jit(solution)/shard_map/pallas_call | solution.py:24
  14.7 1.2 %shard_map.258 = (bf16[2816,128]{1,0:T(8,128)(2,1)S(1)}, bf16[2816,128]{1,0:T(8,128)(2,1)S(1)}) custom-call(bf16[256,1024]{1,0:T(8,128)(2,1)S(1)} %get-tuple-element.81.act_t.act2_t, bf16[1024,128]{1,0:T(8,128)(2,1)S(1)} %get-tuple-element.87.wg_keep, bf16[1024,128]{1,0:T(8,128)(2,1)S(1)} %get-tuple-element.88.wg_send, ...), custom_call_target="tpu_custom_call" | custom-call | flops 1 | tf_op jit(solution)/shard_map/pallas_call | solution.py:24
  15.9 0.4 collective-permute-start.7
  16.3 2.6 %shard_map.259 = (f32[8,256]{1,0:T(8,128)S(1)}, bf16[16,128]{1,0:T(8,128)(2,1)S(1)}, bf16[3,288,256]{2,1,0:T(8,128)(2,1)S(1)}, bf16[3,288,256]{2,1,0:T(8,128)(2,...) custom-call(f32[8,128]{1,0:T(8,128)S(1)} %get-tuple-element.95.step_row, ...), custom_call_target="tpu_custom_call" | custom-call | flops 1 | tf_op jit(solution)/shard_map/pallas_call | solution.py:24
  18.9 0.6 shard_map.260
  19.5 1.7 %shard_map.261 = (bf16[2816,128]{1,0:T(8,128)(2,1)S(1)}, bf16[2816,128]{1,0:T(8,128)(2,1)S(1)}) custom-call(bf16[1408,128]{1,0:T(8,128)(2,1)S(1)} %get-tuple-element.100.after.refs_3_.own, bf16[256,1024]{1,0:T(8,128)(2,1)S(1)} %get-tuple-element.81.act_t.act2_t, bf16[256,1024]{1,0:T(8,128)(2,1)S(1)} %get-tuple-element.102.act1_t, ...), custom_call_target="tpu_custom_call" | custom-call | flops 1 | tf_op jit(solution)/shard_map/pallas_call | solution.py:24
  21.2 0.2 collective-permute-start.9
  21.4 2.8 %collective-permute-start.8 = (bf16[1408,128]{1,0:T(8,128)(2,1)S(1)}, bf16[1408,128]{1,0:T(8,128)(2,1)S(1)}, u32[]{:S(2)}, u32[]{:S(2)}) collective-permute-start(bf16[1408,128]{1,0:T(8,128)(2,1)S(1)} %get-tuple-element.101), channel_id=1, source_target_pairs={{0,2},{1,9},{2,0},{3,11},{4,6},{5,13},{6,4},{7,15},{8,10},{9,1},{1... | collective-permute-start | bytes 1081352 | tf_op jit(solution)/shard_map/ppermute | solution.py:430
  24.3 0.4 shard_map.262
  24.7 1.9 %collective-permute-start.10 = (bf16[1424,128]{1,0:T(8,128)(2,1)S(1)}, bf16[1424,128]{1,0:T(8,128)(2,1)S(1)}, u32[]{:S(2)}, u32[]{:S(2)}) collective-permute-start(bf16[1424,128]{1,0:T(8,128)(2,1)S(1)} %get-tuple-element.111), channel_id=1, source_target_pairs={{0,4},{1,9},{2,6},{3,11},{4,0},{5,13},{6,2},{7,15},{8,12},{9,1},{1... | collective-permute-start | bytes 1093640 | tf_op jit(solution)/shard_map/ppermute | solution.py:430
  26.6 2.3 %shard_map.263 = (f32[4,256,128]{2,1,0:T(8,128)S(1)}, bf16[4,256,128]{2,1,0:T(8,128)(2,1)S(1)}, bf16[4,256,128]{2,1,0:T(8,128)(2,1)S(1)}, f32[16,128]{1,0:T(8,128)S(1)}, f32[16,128]{1,0:T(8,128)S(1)}) custom-call(bf16[1424,128]{1,0:T(8,128)(2,1)S(1)} %get-tuple-element.110.after.own, bf16[8,256,128]{2,1,0:T(8,128)(2,1)S(1)} %copy-done.5, ...), custom_call_target="tpu_custom_call" | custom-call | flops 10000000000 | tf_op jit(solution)/shard_map/pallas_call | solution.py:24
  28.9 0.2 collective-permute-start.12
  29.1 0.4 collective-permute-start.13
  29.5 2.7 %collective-permute-done.10.recv = bf16[1424,128]{1,0:T(8,128)(2,1)S(1)} collective-permute-done((bf16[1424,128]{1,0:T(8,128)(2,1)S(1)}, bf16[1424,128]{1,0:T(8,128)(2,1)S(1)}, u32[]{:S(2)}, u32[]{:S(2)}) %collective-permute-start.10) | collective-permute-done | bytes 364576 | tf_op jit(solution)/shard_map/ppermute | solution.py:430
  32.2 0.2 shard_map.264
  32.4 3.0 %collective-permute-start.14 = (bf16[736,128]{1,0:T(8,128)(2,1)S(1)}, bf16[736,128]{1,0:T(8,128)(2,1)S(1)}, u32[]{:S(2)}, u32[]{:S(2)}) collective-permute-start(bf16[736,128]{1,0:T(8,128)(2,1)S(1)} %get-tuple-element.126), channel_id=1, source_target_pairs={{0,16},{1,5},{2,18},{3,7},{4,20},{5,1},{6,22},{7,3},{8,24},{9,13},... | collective-permute-start | bytes 565256 | tf_op jit(solution)/shard_map/ppermute | solution.py:430
  35.4 0.0 collective-permute-start.11
  35.5 0.0 collective-permute-done.8.recv
  35.5 0.2 shard_map.265
  35.6 1.6 %collective-permute-start.19 = (bf16[704,128]{1,0:T(8,128)(2,1)S(1)}, bf16[704,128]{1,0:T(8,128)(2,1)S(1)}, u32[]{:S(2)}, u32[]{:S(2)}) collective-permute-start(bf16[704,128]{1,0:T(8,128)(2,1)S(1)} %get-tuple-element.130), channel_id=1, source_target_pairs={{0,8},{1,3},{2,10},{3,1},{4,12},{5,7},{6,14},{7,5},{8,0},{9,11},{1... | collective-permute-start | bytes 540680 | tf_op jit(solution)/shard_map/ppermute | solution.py:430
  37.3 0.1 collective-permute-start.15
  37.4 1.2 %shard_map.266 = (bf16[8,256,128]{2,1,0:T(8,128)(2,1)}, f32[8,256,128]{2,1,0:T(8,128)}, f32[8,128]{1,0:T(8,128)S(1)}) custom-call(bf16[704,128]{1,0:T(8,128)(2,1)S(1)} %get-tuple-element.119.after.own, bf16[512,128]{1,0:T(8,128)(2,1)S(1)} %collective-permute-done.11.tw_recv.tw_recv_ref, bf16[4,256,128]{2,1,0:T(8,128)(2,1)S(1)} %get-tuple-element.120.out_keep, ...), custom_call_target="tpu_custom_call" | custom-call | flops 1 | tf_op jit(solution)/shard_map/pallas_call | solution.py:24
  38.7 2.5 %collective-permute-done.14.recv = bf16[736,128]{1,0:T(8,128)(2,1)S(1)} collective-permute-done((bf16[736,128]{1,0:T(8,128)(2,1)S(1)}, bf16[736,128]{1,0:T(8,128)(2,1)S(1)}, u32[]{:S(2)}, u32[]{:S(2)}) %collective-permute-start.14) | collective-permute-done | bytes 188448 | tf_op jit(solution)/shard_map/ppermute | solution.py:430
  41.1 0.1 shard_map.267.own.after_ref
  41.2 1.9 %collective-permute-start.16 = (bf16[784,128]{1,0:T(8,128)(2,1)S(1)}, bf16[784,128]{1,0:T(8,128)(2,1)S(1)}, u32[]{:S(2)}, u32[]{:S(2)}) collective-permute-start(bf16[784,128]{1,0:T(8,128)(2,1)S(1)} %shard_map.267.own.after_ref), channel_id=1, source_target_pairs={{0,2},{1,3},{2,0},{3,1},{4,6},{5,7},{6,4},{7,5},{8,10},{9,11},{10,... | collective-permute-start | bytes 602120 | tf_op jit(solution)/shard_map/ppermute | solution.py:430
  43.1 1.6 %collective-permute-start.20 = (bf16[704,128]{1,0:T(8,128)(2,1)S(1)}, bf16[704,128]{1,0:T(8,128)(2,1)S(1)}, u32[]{:S(2)}, u32[]{:S(2)}) collective-permute-start(bf16[704,128]{1,0:T(8,128)(2,1)S(1)} %shard_map.270.own), channel_id=1, source_target_pairs={{0,4},{1,17},{2,6},{3,19},{4,0},{5,21},{6,2},{7,23},{8,12},{9,25},... | collective-permute-start | bytes 540680 | tf_op jit(solution)/shard_map/ppermute | solution.py:430
  44.7 2.3 %collective-permute-done.16.recv = bf16[784,128]{1,0:T(8,128)(2,1)S(1)} collective-permute-done((bf16[784,128]{1,0:T(8,128)(2,1)S(1)}, bf16[784,128]{1,0:T(8,128)(2,1)S(1)}, u32[]{:S(2)}, u32[]{:S(2)}) %collective-permute-start.16) | collective-permute-done | bytes 200736 | tf_op jit(solution)/shard_map/ppermute | solution.py:430
  47.0 1.0 %collective-permute-start.17 = (bf16[848,128]{1,0:T(8,128)(2,1)S(1)}, bf16[848,128]{1,0:T(8,128)(2,1)S(1)}, u32[]{:S(2)}, u32[]{:S(2)}) collective-permute-start(bf16[848,128]{1,0:T(8,128)(2,1)S(1)} %shard_map.268.own.after_ref), channel_id=1, source_target_pairs={{0,8},{1,17},{2,10},{3,19},{4,12},{5,21},{6,14},{7,23},{8,0},{9,25... | collective-permute-start | bytes 651272 | tf_op jit(solution)/shard_map/ppermute | solution.py:430
  48.0 0.6 collective-permute-done.20.recv
  48.7 2.9 %collective-permute-start.21 = (bf16[704,128]{1,0:T(8,128)(2,1)S(1)}, bf16[704,128]{1,0:T(8,128)(2,1)S(1)}, u32[]{:S(2)}, u32[]{:S(2)}) collective-permute-start(bf16[704,128]{1,0:T(8,128)(2,1)S(1)} %shard_map.271.own), channel_id=1, source_target_pairs={{0,16},{1,5},{2,18},{3,7},{4,20},{5,1},{6,22},{7,3},{8,24},{9,13},... | collective-permute-start | bytes 540680 | tf_op jit(solution)/shard_map/ppermute | solution.py:430
  51.6 5.6 %collective-permute-done.17.recv = bf16[848,128]{1,0:T(8,128)(2,1)S(1)} collective-permute-done((bf16[848,128]{1,0:T(8,128)(2,1)S(1)}, bf16[848,128]{1,0:T(8,128)(2,1)S(1)}, u32[]{:S(2)}, u32[]{:S(2)}) %collective-permute-start.17) | collective-permute-done | bytes 217120 | tf_op jit(solution)/shard_map/ppermute | solution.py:430
  57.2 0.1 shard_map.269
  57.3 0.1 collective-permute-start.22
  57.4 1.2 %collective-permute-start.24 = (bf16[704,128]{1,0:T(8,128)(2,1)S(1)}, bf16[704,128]{1,0:T(8,128)(2,1)S(1)}, u32[]{:S(2)}, u32[]{:S(2)}) collective-permute-start(bf16[704,128]{1,0:T(8,128)(2,1)S(1)} %shard_map.272.after_ref.own), channel_id=1, source_target_pairs={{0,8},{1,3},{2,10},{3,1},{4,12},{5,7},{6,14},{7,5},{8,0},{9,11},{1... | collective-permute-start | bytes 540680 | tf_op jit(solution)/shard_map/ppermute | solution.py:430
  58.6 1.3 %collective-permute-done.18.other_ref = bf16[256,128]{1,0:T(8,128)(2,1)S(1)} collective-permute-done((bf16[256,128]{1,0:T(8,128)(2,1)S(1)}, bf16[256,128]{1,0:T(8,128)(2,1)S(1)}, u32[]{:S(2)}, u32[]{:S(2)}) %collective-permute-start.18) | collective-permute-done | bytes 65568 | tf_op jit(solution)/shard_map/ppermute | solution.py:434
  59.9 3.2 %shard_map.273 = (f32[1000,512]{1,0:T(8,128)}, f32[512,128]{1,0:T(8,128)}, f32[1,128]{1,0:T(1,128)}, f32[8,128]{1,0:T(8,128)S(1)}) custom-call(bf16[256,128]{1,0:T(8,128)(2,1)S(1)} %get-tuple-element.129.rows_ref, bf16[256,128]{1,0:T(8,128)(2,1)S(1)} %collective-permute-done.18.other_ref, f32[1000,512]{1,0:T(8,128)S(1)} %copy-done, ...), custom_call_target="tpu_custom_call" | custom-call | flops 1 | tf_op jit(solution)/shard_map/pallas_call | solution.py:24
  63.1 1.5 %collective-permute-done.22.recv = bf16[720,128]{1,0:T(8,128)(2,1)S(1)} collective-permute-done((bf16[720,128]{1,0:T(8,128)(2,1)S(1)}, bf16[720,128]{1,0:T(8,128)(2,1)S(1)}, u32[]{:S(2)}, u32[]{:S(2)}) %collective-permute-start.22) | collective-permute-done | bytes 184352 | tf_op jit(solution)/shard_map/ppermute | solution.py:430
  64.7 1.6 %collective-permute-start.23 = (bf16[1440,128]{1,0:T(8,128)(2,1)S(1)}, bf16[1440,128]{1,0:T(8,128)(2,1)S(1)}, u32[]{:S(2)}, u32[]{:S(2)}) collective-permute-start(bf16[1440,128]{1,0:T(8,128)(2,1)S(1)} %shard_map.274.own.after_ref), channel_id=1, source_target_pairs={{0,4},{1,9},{2,6},{3,11},{4,0},{5,13},{6,2},{7,15},{8,12},{9,1},{1... | collective-permute-start | bytes 1105928 | tf_op jit(solution)/shard_map/ppermute | solution.py:430
  66.3 1.6 %collective-permute-start.25 = (bf16[1408,128]{1,0:T(8,128)(2,1)S(1)}, bf16[1408,128]{1,0:T(8,128)(2,1)S(1)}, u32[]{:S(2)}, u32[]{:S(2)}) collective-permute-start(bf16[1408,128]{1,0:T(8,128)(2,1)S(1)} %shard_map.276.own), channel_id=1, source_target_pairs={{0,2},{1,9},{2,0},{3,11},{4,6},{5,13},{6,4},{7,15},{8,10},{9,1},{1... | collective-permute-start | bytes 1081352 | tf_op jit(solution)/shard_map/ppermute | solution.py:430
  67.9 4.3 %collective-permute-done.23.recv = bf16[1440,128]{1,0:T(8,128)(2,1)S(1)} collective-permute-done((bf16[1440,128]{1,0:T(8,128)(2,1)S(1)}, bf16[1440,128]{1,0:T(8,128)(2,1)S(1)}, u32[]{:S(2)}, u32[]{:S(2)}) %collective-permute-start.23) | collective-permute-done | bytes 368672 | tf_op jit(solution)/shard_map/ppermute | solution.py:430
  72.3 1.2 %shard_map.275 = (f32[2304,128]{1,0:T(8,128)}, f32[2,128,256]{2,1,0:T(8,128)S(1)}, f32[3,128]{1,0:T(4,128)}, f32[3,128]{1,0:T(4,128)}, f32[2,128]{1,0:T(2,128)}, /*index=5*/f32[2,128]{1,0:T(2,128)}, f32[1,128]{1,0:T(1,128)}) custom-call(f32[8,128]{1,0:T(8,128)S(1)} %get-tuple-element.133.after_ref, bf16[1440,128]{1,0:T(8,128)(2,1)S(1)} %shard_map.274.own.after_ref, ...), custom_call_target="tpu_custom_call" | custom-call | flops 1 | tf_op jit(solution)/shard_map/pallas_call | solution.py:24
  73.5 0.4 collective-permute-done.25.recv
  73.8 1.3 %shard_map.277 = (f32[9,128,256]{2,1,0:T(8,128)}, f32[3,256,128]{2,1,0:T(8,128)}, f32[128,256]{1,0:T(8,128)}) custom-call(f32[2,128,256]{2,1,0:T(8,128)S(1)} %get-tuple-element.140.last_ref, bf16[1408,128]{1,0:T(8,128)(2,1)S(1)} %shard_map.276.own, bf16[1408,128]{1,0:T(8,128)(2,1)S(1)} %collective-permute-done.25.recv), custom_call_target="tpu_custom_call" | custom-call | flops 1 | tf_op jit(solution)/shard_map/pallas_call | solution.py:24
  (43 shorter events, 0.4 us)
Async XLA Ops:
  0.6 0.7 copy-start.9
  0.7 0.7 copy-start.10
  0.7 0.7 copy-start.11
  0.7 0.7 copy-start.12
  0.7 0.7 copy-start.13
  0.7 0.7 copy-start.14
  0.7 1.1 %copy-start.1 = (bf16[3,3,256,128]{3,2,1,0:T(8,128)(2,1)S(1)}, bf16[3,3,256,128]{3,2,1,0:T(8,128)(2,1)}, u32[]{:S(2)}) copy-start(bf16[3,3,256,128]{3,2,1,0:T(8,128)(2,1)} %param.20) | copy-start | bytes 1769476
  0.7 1.1 %copy-start.3 = (bf16[512,128]{1,0:T(8,128)(2,1)S(1)}, bf16[512,128]{1,0:T(8,128)(2,1)}, u32[]{:S(2)}) copy-start(bf16[512,128]{1,0:T(8,128)(2,1)} %tw_own_ref.1) | copy-start | bytes 393220
  0.7 1.1 %copy-start.8 = (s32[8]{0:T(128)S(1)}, s32[8]{0:T(128)}, u32[]{:S(2)}) copy-start(s32[8]{0:T(128)} %steps.1) | copy-start | bytes 100
  0.7 4.8 %collective-permute-start.1 = (bf16[9,256,128]{2,1,0:T(8,128)(2,1)}, bf16[9,256,128]{2,1,0:T(8,128)(2,1)}, u32[]{:S(2)}, u32[]{:S(2)}) collective-permute-start(bf16[9,256,128]{2,1,0:T(8,128)(2,1)} %bitcast.10), channel_id=1, source_target_pairs={{0,1},{1,0},{2,3},{3,2},{4,5},{5,4},{6,7},{7,6},{8,9},{9,8},{10,11... | collective-permute-start | bytes 1769480 | tf_op jit(solution)/shard_map/ppermute | solution.py:434
  1.3 4.1 %collective-permute-start = (bf16[8,256,128]{2,1,0:T(8,128)(2,1)}, bf16[8,256,128]{2,1,0:T(8,128)(2,1)S(1)}, u32[]{:S(2)}, u32[]{:S(2)}) collective-permute-start(bf16[8,256,128]{2,1,0:T(8,128)(2,1)} %x_own.5), channel_id=1, source_target_pairs={{0,1},{1,0},{2,3},{3,2},{4,5},{5,4},{6,7},{7,6},{8,9},{9,8},{10,11... | collective-permute-start | bytes 1572872 | tf_op jit(solution)/shard_map/ppermute | solution.py:434
  1.3 1.6 %copy-start = (f32[1000,512]{1,0:T(8,128)S(1)}, f32[1000,512]{1,0:T(8,128)}, u32[]{:S(2)}) copy-start(f32[1000,512]{1,0:T(8,128)} %table_ref.1) | copy-start | bytes 6144004
  3.0 1.2 %copy-start.2 = (bf16[3,3,128,256]{3,2,1,0:T(8,128)(2,1)S(1)}, bf16[3,3,128,256]{3,2,1,0:T(8,128)(2,1)}, u32[]{:S(2)}) copy-start(bf16[3,3,128,256]{3,2,1,0:T(8,128)(2,1)} %param.24) | copy-start | bytes 1769476
  3.0 1.5 %copy-start.6 = (bf16[256,3,128]{2,0,1:T(8,128)(2,1)S(1)}, bf16[256,3,128]{2,0,1:T(8,128)(2,1)}, u32[]{:S(2)}) copy-start(bf16[256,3,128]{2,0,1:T(8,128)(2,1)} %param.25) | copy-start | bytes 589828
  3.0 2.0 %copy-start.4 = (bf16[8,256,128]{2,1,0:T(8,128)(2,1)S(1)}, bf16[8,256,128]{2,1,0:T(8,128)(2,1)}, u32[]{:S(2)}) copy-start(bf16[8,256,128]{2,1,0:T(8,128)(2,1)} %g_own.1) | copy-start | bytes 1572868
  3.0 2.4 %copy-start.7 = (bf16[128,256]{1,0:T(8,128)(2,1)S(1)}, bf16[128,256]{1,0:T(8,128)(2,1)}, u32[]{:S(2)}) copy-start(bf16[128,256]{1,0:T(8,128)(2,1)} %ow_own.1) | copy-start | bytes 196612
  3.0 2.5 %copy-start.5 = (bf16[8,256,128]{2,1,0:T(8,128)(2,1)S(1)}, bf16[8,256,128]{2,1,0:T(8,128)(2,1)}, u32[]{:S(2)}) copy-start(bf16[8,256,128]{2,1,0:T(8,128)(2,1)} %x_own.5) | copy-start | bytes 1572868
  3.7 1.3 %collective-permute-start.2 = (f32[24,128]{1,0:T(8,128)S(1)}, f32[24,128]{1,0:T(8,128)S(1)}, u32[]{:S(2)}, u32[]{:S(2)}) collective-permute-start(f32[24,128]{1,0:T(8,128)S(1)} %get-tuple-element.80.pk_own), channel_id=1, source_target_pairs={{0,1},{1,0},{2,3},{3,2},{4,5},{5,4},{6,7},{7,6},{8,9},{9,8},{10,11... | collective-permute-start | bytes 36872 | tf_op jit(solution)/shard_map/ppermute | solution.py:434
  4.1 5.0 %collective-permute-start.3 = (bf16[9,128,256]{2,1,0:T(8,128)(2,1)S(1)}, bf16[9,128,256]{2,1,0:T(8,128)(2,1)S(1)}, u32[]{:S(2)}, u32[]{:S(2)}) collective-permute-start(bf16[9,128,256]{2,1,0:T(8,128)(2,1)S(1)} %bitcast.13), channel_id=1, source_target_pairs={{0,1},{1,0},{2,3},{3,2},{4,5},{5,4},{6,7},{7,6},{8,9},{9,8},{10,11... | collective-permute-start | bytes 1769480 | tf_op jit(solution)/shard_map/ppermute | solution.py:434
  4.5 4.6 %collective-permute-start.5 = (bf16[3,256,128]{2,1,0:T(8,128)(2,1)S(1)}, bf16[3,256,128]{2,1,0:T(8,128)(2,1)S(1)}, u32[]{:S(2)}, u32[]{:S(2)}) collective-permute-start(bf16[3,256,128]{2,1,0:T(8,128)(2,1)S(1)} %bitcast.15), channel_id=1, source_target_pairs={{0,1},{1,0},{2,3},{3,2},{4,5},{5,4},{6,7},{7,6},{8,9},{9,8},{10,11... | collective-permute-start | bytes 589832 | tf_op jit(solution)/shard_map/ppermute | solution.py:434
  5.0 4.1 %collective-permute-start.4 = (bf16[8,256,128]{2,1,0:T(8,128)(2,1)S(1)}, bf16[8,256,128]{2,1,0:T(8,128)(2,1)S(1)}, u32[]{:S(2)}, u32[]{:S(2)}) collective-permute-start(bf16[8,256,128]{2,1,0:T(8,128)(2,1)S(1)} %copy-done.4), channel_id=1, source_target_pairs={{0,1},{1,0},{2,3},{3,2},{4,5},{5,4},{6,7},{7,6},{8,9},{9,8},{10,11... | collective-permute-start | bytes 1572872 | tf_op jit(solution)/shard_map/ppermute | solution.py:434
  5.3 3.7 %collective-permute-start.6 = (bf16[128,256]{1,0:T(8,128)(2,1)S(1)}, bf16[128,256]{1,0:T(8,128)(2,1)S(1)}, u32[]{:S(2)}, u32[]{:S(2)}) collective-permute-start(bf16[128,256]{1,0:T(8,128)(2,1)S(1)} %copy-done.7), channel_id=1, source_target_pairs={{0,1},{1,0},{2,3},{3,2},{4,5},{5,4},{6,7},{7,6},{8,9},{9,8},{10,11... | collective-permute-start | bytes 196616 | tf_op jit(solution)/shard_map/ppermute | solution.py:434
  15.9 3.0 %collective-permute-start.7 = (bf16[2816,128]{1,0:T(8,128)(2,1)S(1)}, bf16[2816,128]{1,0:T(8,128)(2,1)S(1)}, u32[]{:S(2)}, u32[]{:S(2)}) collective-permute-start(bf16[2816,128]{1,0:T(8,128)(2,1)S(1)} %get-tuple-element.94), channel_id=1, source_target_pairs={{0,1},{1,0},{2,3},{3,2},{4,5},{5,4},{6,7},{7,6},{8,9},{9,8},{10,11... | collective-permute-start | bytes 2162696 | tf_op jit(solution)/shard_map/ppermute | solution.py:434
  21.2 3.1 %collective-permute-start.9 = (bf16[2816,128]{1,0:T(8,128)(2,1)S(1)}, bf16[2816,128]{1,0:T(8,128)(2,1)S(1)}, u32[]{:S(2)}, u32[]{:S(2)}) collective-permute-start(bf16[2816,128]{1,0:T(8,128)(2,1)S(1)} %get-tuple-element.108), channel_id=1, source_target_pairs={{0,1},{1,0},{2,3},{3,2},{4,5},{5,4},{6,7},{7,6},{8,9},{9,8},{10,11... | collective-permute-start | bytes 2162696 | tf_op jit(solution)/shard_map/ppermute | solution.py:434
  21.4 14.0 %collective-permute-start.8 = (bf16[1408,128]{1,0:T(8,128)(2,1)S(1)}, bf16[1408,128]{1,0:T(8,128)(2,1)S(1)}, u32[]{:S(2)}, u32[]{:S(2)}) collective-permute-start(bf16[1408,128]{1,0:T(8,128)(2,1)S(1)} %get-tuple-element.101), channel_id=1, source_target_pairs={{0,2},{1,9},{2,0},{3,11},{4,6},{5,13},{6,4},{7,15},{8,10},{9,1},{1... | collective-permute-start | bytes 1081352 | tf_op jit(solution)/shard_map/ppermute | solution.py:430
  24.7 7.5 %collective-permute-start.10 = (bf16[1424,128]{1,0:T(8,128)(2,1)S(1)}, bf16[1424,128]{1,0:T(8,128)(2,1)S(1)}, u32[]{:S(2)}, u32[]{:S(2)}) collective-permute-start(bf16[1424,128]{1,0:T(8,128)(2,1)S(1)} %get-tuple-element.111), channel_id=1, source_target_pairs={{0,4},{1,9},{2,6},{3,11},{4,0},{5,13},{6,2},{7,15},{8,12},{9,1},{1... | collective-permute-start | bytes 1093640 | tf_op jit(solution)/shard_map/ppermute | solution.py:430
  28.9 8.5 %collective-permute-start.12 = (bf16[4,256,128]{2,1,0:T(8,128)(2,1)S(1)}, bf16[4,256,128]{2,1,0:T(8,128)(2,1)S(1)}, u32[]{:S(2)}, u32[]{:S(2)}) collective-permute-start(bf16[4,256,128]{2,1,0:T(8,128)(2,1)S(1)} %get-tuple-element.121), channel_id=1, source_target_pairs={{0,1},{1,0},{2,3},{3,2},{4,5},{5,4},{6,7},{7,6},{8,9},{9,8},{10,11... | collective-permute-start | bytes 786440 | tf_op jit(solution)/shard_map/ppermute | solution.py:434
  29.1 8.3 %collective-permute-start.13 = (bf16[4,256,128]{2,1,0:T(8,128)(2,1)S(1)}, bf16[4,256,128]{2,1,0:T(8,128)(2,1)S(1)}, u32[]{:S(2)}, u32[]{:S(2)}) collective-permute-start(bf16[4,256,128]{2,1,0:T(8,128)(2,1)S(1)} %get-tuple-element.123), channel_id=1, source_target_pairs={{0,1},{1,0},{2,3},{3,2},{4,5},{5,4},{6,7},{7,6},{8,9},{9,8},{10,11... | collective-permute-start | bytes 786440 | tf_op jit(solution)/shard_map/ppermute | solution.py:434
  32.4 8.7 %collective-permute-start.14 = (bf16[736,128]{1,0:T(8,128)(2,1)S(1)}, bf16[736,128]{1,0:T(8,128)(2,1)S(1)}, u32[]{:S(2)}, u32[]{:S(2)}) collective-permute-start(bf16[736,128]{1,0:T(8,128)(2,1)S(1)} %get-tuple-element.126), channel_id=1, source_target_pairs={{0,16},{1,5},{2,18},{3,7},{4,20},{5,1},{6,22},{7,3},{8,24},{9,13},... | collective-permute-start | bytes 565256 | tf_op jit(solution)/shard_map/ppermute | solution.py:430
  35.4 1.8 %collective-permute-start.11 = (bf16[512,128]{1,0:T(8,128)(2,1)S(1)}, bf16[512,128]{1,0:T(8,128)(2,1)S(1)}, u32[]{:S(2)}, u32[]{:S(2)}) collective-permute-start(bf16[512,128]{1,0:T(8,128)(2,1)S(1)} %copy-done.3), channel_id=1, source_target_pairs={{0,1},{1,0},{2,3},{3,2},{4,5},{5,4},{6,7},{7,6},{8,9},{9,8},{10,11... | collective-permute-start | bytes 393224 | tf_op jit(solution)/shard_map/ppermute | solution.py:434
  35.6 7.4 %collective-permute-start.19 = (bf16[704,128]{1,0:T(8,128)(2,1)S(1)}, bf16[704,128]{1,0:T(8,128)(2,1)S(1)}, u32[]{:S(2)}, u32[]{:S(2)}) collective-permute-start(bf16[704,128]{1,0:T(8,128)(2,1)S(1)} %get-tuple-element.130), channel_id=1, source_target_pairs={{0,8},{1,3},{2,10},{3,1},{4,12},{5,7},{6,14},{7,5},{8,0},{9,11},{1... | collective-permute-start | bytes 540680 | tf_op jit(solution)/shard_map/ppermute | solution.py:430
  37.3 1.4 %collective-permute-start.15 = (f32[16,128]{1,0:T(8,128)S(1)}, f32[16,128]{1,0:T(8,128)S(1)}, u32[]{:S(2)}, u32[]{:S(2)}) collective-permute-start(f32[16,128]{1,0:T(8,128)S(1)} %get-tuple-element.128), channel_id=1, source_target_pairs={{0,1},{1,0},{2,3},{3,2},{4,5},{5,4},{6,7},{7,6},{8,9},{9,8},{10,11... | collective-permute-start | bytes 24584 | tf_op jit(solution)/shard_map/ppermute | solution.py:434
  41.2 5.8 %collective-permute-start.16 = (bf16[784,128]{1,0:T(8,128)(2,1)S(1)}, bf16[784,128]{1,0:T(8,128)(2,1)S(1)}, u32[]{:S(2)}, u32[]{:S(2)}) collective-permute-start(bf16[784,128]{1,0:T(8,128)(2,1)S(1)} %shard_map.267.own.after_ref), channel_id=1, source_target_pairs={{0,2},{1,3},{2,0},{3,1},{4,6},{5,7},{6,4},{7,5},{8,10},{9,11},{10,... | collective-permute-start | bytes 602120 | tf_op jit(solution)/shard_map/ppermute | solution.py:430
  43.1 5.6 %collective-permute-start.20 = (bf16[704,128]{1,0:T(8,128)(2,1)S(1)}, bf16[704,128]{1,0:T(8,128)(2,1)S(1)}, u32[]{:S(2)}, u32[]{:S(2)}) collective-permute-start(bf16[704,128]{1,0:T(8,128)(2,1)S(1)} %shard_map.270.own), channel_id=1, source_target_pairs={{0,4},{1,17},{2,6},{3,19},{4,0},{5,21},{6,2},{7,23},{8,12},{9,25},... | collective-permute-start | bytes 540680 | tf_op jit(solution)/shard_map/ppermute | solution.py:430
  47.0 10.2 %collective-permute-start.17 = (bf16[848,128]{1,0:T(8,128)(2,1)S(1)}, bf16[848,128]{1,0:T(8,128)(2,1)S(1)}, u32[]{:S(2)}, u32[]{:S(2)}) collective-permute-start(bf16[848,128]{1,0:T(8,128)(2,1)S(1)} %shard_map.268.own.after_ref), channel_id=1, source_target_pairs={{0,8},{1,17},{2,10},{3,19},{4,12},{5,21},{6,14},{7,23},{8,0},{9,25... | collective-permute-start | bytes 651272 | tf_op jit(solution)/shard_map/ppermute | solution.py:430
  48.7 8.7 %collective-permute-start.21 = (bf16[704,128]{1,0:T(8,128)(2,1)S(1)}, bf16[704,128]{1,0:T(8,128)(2,1)S(1)}, u32[]{:S(2)}, u32[]{:S(2)}) collective-permute-start(bf16[704,128]{1,0:T(8,128)(2,1)S(1)} %shard_map.271.own), channel_id=1, source_target_pairs={{0,16},{1,5},{2,18},{3,7},{4,20},{5,1},{6,22},{7,3},{8,24},{9,13},... | collective-permute-start | bytes 540680 | tf_op jit(solution)/shard_map/ppermute | solution.py:430
  57.3 7.3 %collective-permute-start.22 = (bf16[720,128]{1,0:T(8,128)(2,1)S(1)}, bf16[720,128]{1,0:T(8,128)(2,1)S(1)}, u32[]{:S(2)}, u32[]{:S(2)}) collective-permute-start(bf16[720,128]{1,0:T(8,128)(2,1)S(1)} %get-tuple-element.131.after_ref.own), channel_id=1, source_target_pairs={{0,16},{1,5},{2,18},{3,7},{4,20},{5,1},{6,22},{7,3},{8,24},{9,13},... | collective-permute-start | bytes 552968 | tf_op jit(solution)/shard_map/ppermute | solution.py:430
  57.4 8.8 %collective-permute-start.24 = (bf16[704,128]{1,0:T(8,128)(2,1)S(1)}, bf16[704,128]{1,0:T(8,128)(2,1)S(1)}, u32[]{:S(2)}, u32[]{:S(2)}) collective-permute-start(bf16[704,128]{1,0:T(8,128)(2,1)S(1)} %shard_map.272.after_ref.own), channel_id=1, source_target_pairs={{0,8},{1,3},{2,10},{3,1},{4,12},{5,7},{6,14},{7,5},{8,0},{9,11},{1... | collective-permute-start | bytes 540680 | tf_op jit(solution)/shard_map/ppermute | solution.py:430
  58.6 1.3 %collective-permute-start.18 = (bf16[256,128]{1,0:T(8,128)(2,1)S(1)}, bf16[256,128]{1,0:T(8,128)(2,1)S(1)}, u32[]{:S(2)}, u32[]{:S(2)}) collective-permute-start(bf16[256,128]{1,0:T(8,128)(2,1)S(1)} %get-tuple-element.129.rows_ref), channel_id=1, source_target_pairs={{0,1},{1,0},{2,3},{3,2},{4,5},{5,4},{6,7},{7,6},{8,9},{9,8},{10,11... | collective-permute-start | bytes 196616 | tf_op jit(solution)/shard_map/ppermute | solution.py:434
  64.7 7.6 %collective-permute-start.23 = (bf16[1440,128]{1,0:T(8,128)(2,1)S(1)}, bf16[1440,128]{1,0:T(8,128)(2,1)S(1)}, u32[]{:S(2)}, u32[]{:S(2)}) collective-permute-start(bf16[1440,128]{1,0:T(8,128)(2,1)S(1)} %shard_map.274.own.after_ref), channel_id=1, source_target_pairs={{0,4},{1,9},{2,6},{3,11},{4,0},{5,13},{6,2},{7,15},{8,12},{9,1},{1... | collective-permute-start | bytes 1105928 | tf_op jit(solution)/shard_map/ppermute | solution.py:430
  66.3 7.5 %collective-permute-start.25 = (bf16[1408,128]{1,0:T(8,128)(2,1)S(1)}, bf16[1408,128]{1,0:T(8,128)(2,1)S(1)}, u32[]{:S(2)}, u32[]{:S(2)}) collective-permute-start(bf16[1408,128]{1,0:T(8,128)(2,1)S(1)} %shard_map.276.own), channel_id=1, source_target_pairs={{0,2},{1,9},{2,0},{3,11},{4,6},{5,13},{6,4},{7,15},{8,10},{9,1},{1... | collective-permute-start | bytes 1081352 | tf_op jit(solution)/shard_map/ppermute | solution.py:430

commit v7 on v6

--- a/solution.py
+++ b/solution.py
@@ -1,3 +1,5 @@
+import functools
+
 import jax
 import jax.numpy as jnp
 from jax import lax
@@ -324,9 +326,14 @@
     conv2_rows(CONV2_TAPS[0], lax.axis_index("mp") == 0, act_t, win, keep, send)
 
 
-def last_grad_kernel(after, act2_t, act1_t, *rest):
+def last_grad_kernel(bits, act2_t, act1_t, late_keep, late_recv, *rest):
     n = act1_t.shape[1] // PIX
-    win3, win4, (keep, send) = rest[:n], rest[n : 2 * n], rest[2 * n :]
+    win3, win4, (keep, send, late_own, late_send, values) = rest[:n], rest[n : 2 * n], rest[2 * n :]
+    half = late_own.shape[0]
+    values[...] = added(late_keep[...], late_recv[...])
+    me = digit(bits)
+    late_own[...] = values[part(me, half)]
+    late_send[...] = values[part(1 - me, half)]
     first = lax.axis_index("mp") == 0
     conv2_rows(CONV2_TAPS[1], first, act2_t, win3, keep, send)
     at = len(CONV2_TAPS[1]) * C
@@ -742,12 +749,17 @@
     early, late = chains = [
         Exchange(order, rows) for order, rows in zip(orders, (11 * C, late_pair[0].shape[0]))
     ]
-    start_exchange(late, (late_pair,), (), (sums2,))
 
     shape = ((11 * C, HALF), BF16)
-    early_pair = swapped(
-        *call(last_grad_kernel, [shape, shape], late.own, act2_t, act1_t, *win3, *win4, specs={0: ANYWHERE})
-    )
+    half = (late.rows // 2, HALF)
+    keep, send, late.own, late_send = call(
+        functools.partial(last_grad_kernel, late.steps[0]), [shape, shape, (half, BF16), (half, BF16)],
+        act2_t, act1_t, *late_pair, *win3, *win4,
+        scratch=[pltpu.VMEM((late.rows, HALF), BF16)],
+    )
+    early_pair = swapped(keep, send)
+    late.recv = swap_dp(late_send, late.steps[0])
+    late.rows //= 2
     start_exchange(early, (early_pair,), (time_rows,), (late.own,))
     mg_keep, mg_send, out_send, rows_keep, rows_send = call(
         input_back_kernel,

time: 75.3 us -> 75.2 us (level)
    pallas_call x24 -> x23, Pallas kernels: 26.3 us -> 26.2 us  [call(): pl.pallas_call(body, out_shape=tuple((jax.ShapeDtypeStruct(s, d) for s, d...]
where the time goes in v7:
time: 75.2 us; the launch traced here: 74.9 us
  Pallas kernels  26.2 us (35%)
  starting transfers between devices  24.6 us (33%)
  waiting for transfers between devices  21.6 us (29%)
  local copies, waits for them, and re-layouts  1.65 us (2%)
  between operations  0.92 us (1%)
    pallas_call x23, Pallas kernels, call(): pl.pallas_call(body, out_shape=tuple((jax.ShapeDtypeStruct(s, d) for s, d...  26.2 us
    ppermute x12, starting transfers between devices, swap_dp(): return lax.ppermute(values, ('dp', 'mp'), pairs)  21.2 us
    ppermute x12, waiting for transfers between devices, swap_dp(): return lax.ppermute(values, ('dp', 'mp'), pairs)  20 us
    ppermute x14, starting transfers between devices, swap_mp(): return lax.ppermute(values, 'mp', [(0, 1), (1, 0)])  3.41 us
    unnamed x30, local copies, waits for them, and re-layouts  1.61 us
    ppermute x14, waiting for transfers between devices, swap_mp(): return lax.ppermute(values, 'mp', [(0, 1), (1, 0)])  1.6 us
  transfers between devices with their start and end apart: 26, of which 10 were waited for; matrix products, arithmetic and copies ran while one was open for 0% of the time, Pallas kernels for 21%

profile of v7, /device:TPU:0, one launch (start us, length us, event | category | flops | bytes accessed | tf_op | source)
XLA Modules:
  0.0 74.9 jit_solution(1310564216272123901)
XLA Ops:
  0.7 0.5 collective-permute-start.1
  1.3 0.1 collective-permute-start
  1.3 0.0 copy-done.10
  1.3 0.0 copy-done.11
  1.4 0.0 copy-done.12
  1.4 0.0 copy-done.14
  1.4 0.4 copy-done.1
  1.8 0.0 copy-done.3
  1.8 1.1 %copy-done = f32[1000,512]{1,0:T(8,128)S(1)} copy-done((f32[1000,512]{1,0:T(8,128)S(1)}, f32[1000,512]{1,0:T(8,128)}, u32[]{:S(2)}) %copy-start) | copy-done | bytes 2048024
  3.0 0.0 copy-start.5
  3.0 0.7 shard_map.255
  3.7 0.4 collective-permute-start.2
  4.1 0.3 collective-permute-start.3
  4.5 0.2 collective-permute-start.5
  4.7 0.3 collective-permute-done.2.pk_recv
  5.0 0.3 collective-permute-start.4
  5.3 0.0 collective-permute-done.x_recv
  5.3 0.2 collective-permute-start.6
  5.5 3.6 %shard_map.256 = (f32[4,256,256]{2,1,0:T(8,128)S(1)}, bf16[256,1024]{1,0:T(8,128)(2,1)S(1)}, bf16[256,1024]{1,0:T(8,128)(2,1)S(1)}, f32[8,256]{1,0:T(8,128)S(1)}...) custom-call(bf16[8,256,128]{2,1,0:T(8,128)(2,1)S(1)} %copy-done.5, ...), custom_call_target="tpu_custom_call" | custom-call | flops 99999997952 | tf_op jit(solution)/shard_map/pallas_call | solution.py:26
  9.1 0.0 collective-permute-done.5.qw_recv
  9.1 0.0 collective-permute-done.4.g_recv
  9.1 5.6 %shard_map.257 = (bf16[4,256,128]{2,1,0:T(8,128)(2,1)S(1)}, bf16[4,256,128]{2,1,0:T(8,128)(2,1)S(1)}, f32[4,256,256]{2,1,0:T(8,128)S(1)}, bf16[1024,128]{1,0:T(8...) custom-call(bf16[8,256,128]{2,1,0:T(8,128)(2,1)S(1)} %copy-done.5, ...), custom_call_target="tpu_custom_call" | custom-call | flops 1 | tf_op jit(solution)/shard_map/pallas_call | solution.py:26
  14.7 1.2 %shard_map.258 = (bf16[2816,128]{1,0:T(8,128)(2,1)S(1)}, bf16[2816,128]{1,0:T(8,128)(2,1)S(1)}) custom-call(bf16[256,1024]{1,0:T(8,128)(2,1)S(1)} %get-tuple-element.81.act_t.act2_t, bf16[1024,128]{1,0:T(8,128)(2,1)S(1)} %get-tuple-element.88.wg_keep, bf16[1024,128]{1,0:T(8,128)(2,1)S(1)} %get-tuple-element.89.wg_send, ...), custom_call_target="tpu_custom_call" | custom-call | flops 1 | tf_op jit(solution)/shard_map/pallas_call | solution.py:26
  15.9 0.4 collective-permute-start.7
  16.3 2.6 %shard_map.259 = (f32[8,256]{1,0:T(8,128)S(1)}, bf16[16,128]{1,0:T(8,128)(2,1)S(1)}, bf16[3,288,256]{2,1,0:T(8,128)(2,1)S(1)}, bf16[3,288,256]{2,1,0:T(8,128)(2,...) custom-call(f32[8,128]{1,0:T(8,128)S(1)} %get-tuple-element.96.step_row, ...), custom_call_target="tpu_custom_call" | custom-call | flops 1 | tf_op jit(solution)/shard_map/pallas_call | solution.py:26
  18.9 2.2 %shard_map.260 = (bf16[2816,128]{1,0:T(8,128)(2,1)S(1)}, bf16[2816,128]{1,0:T(8,128)(2,1)S(1)}, bf16[1408,128]{1,0:T(8,128)(2,1)S(1)}, bf16[1408,128]{1,0:T(8,128)(2,1)S(1)}) custom-call(bf16[256,1024]{1,0:T(8,128)(2,1)S(1)} %get-tuple-element.81.act_t.act2_t, bf16[256,1024]{1,0:T(8,128)(2,1)S(1)} %get-tuple-element.82.act1_t, ...), custom_call_target="tpu_custom_call" | custom-call | flops 1 | tf_op jit(solution)/shard_map/pallas_call | solution.py:26
  21.1 0.2 collective-permute-start.9
  21.3 2.8 %collective-permute-start.8 = (bf16[1408,128]{1,0:T(8,128)(2,1)S(1)}, bf16[1408,128]{1,0:T(8,128)(2,1)S(1)}, u32[]{:S(2)}, u32[]{:S(2)}) collective-permute-start(bf16[1408,128]{1,0:T(8,128)(2,1)S(1)} %get-tuple-element.105), channel_id=1, source_target_pairs={{0,2},{1,9},{2,0},{3,11},{4,6},{5,13},{6,4},{7,15},{8,10},{9,1},{1... | collective-permute-start | bytes 1081352 | tf_op jit(solution)/shard_map/ppermute | solution.py:437
  24.2 0.4 shard_map.261
  24.6 1.9 %collective-permute-start.10 = (bf16[1424,128]{1,0:T(8,128)(2,1)S(1)}, bf16[1424,128]{1,0:T(8,128)(2,1)S(1)}, u32[]{:S(2)}, u32[]{:S(2)}) collective-permute-start(bf16[1424,128]{1,0:T(8,128)(2,1)S(1)} %get-tuple-element.110), channel_id=1, source_target_pairs={{0,4},{1,9},{2,6},{3,11},{4,0},{5,13},{6,2},{7,15},{8,12},{9,1},{1... | collective-permute-start | bytes 1093640 | tf_op jit(solution)/shard_map/ppermute | solution.py:437
  26.5 2.3 %shard_map.262 = (f32[4,256,128]{2,1,0:T(8,128)S(1)}, bf16[4,256,128]{2,1,0:T(8,128)(2,1)S(1)}, bf16[4,256,128]{2,1,0:T(8,128)(2,1)S(1)}, f32[16,128]{1,0:T(8,128)S(1)}, f32[16,128]{1,0:T(8,128)S(1)}) custom-call(bf16[1424,128]{1,0:T(8,128)(2,1)S(1)} %get-tuple-element.109.after.own, bf16[8,256,128]{2,1,0:T(8,128)(2,1)S(1)} %copy-done.5, ...), custom_call_target="tpu_custom_call" | custom-call | flops 10000000000 | tf_op jit(solution)/shard_map/pallas_call | solution.py:26
  28.8 0.2 collective-permute-start.12
  29.0 0.4 collective-permute-start.13
  29.4 2.7 %collective-permute-done.10.recv = bf16[1424,128]{1,0:T(8,128)(2,1)S(1)} collective-permute-done((bf16[1424,128]{1,0:T(8,128)(2,1)S(1)}, bf16[1424,128]{1,0:T(8,128)(2,1)S(1)}, u32[]{:S(2)}, u32[]{:S(2)}) %collective-permute-start.10) | collective-permute-done | bytes 364576 | tf_op jit(solution)/shard_map/ppermute | solution.py:437
  32.1 0.2 shard_map.263
  32.3 3.0 %collective-permute-start.14 = (bf16[736,128]{1,0:T(8,128)(2,1)S(1)}, bf16[736,128]{1,0:T(8,128)(2,1)S(1)}, u32[]{:S(2)}, u32[]{:S(2)}) collective-permute-start(bf16[736,128]{1,0:T(8,128)(2,1)S(1)} %get-tuple-element.126), channel_id=1, source_target_pairs={{0,16},{1,5},{2,18},{3,7},{4,20},{5,1},{6,22},{7,3},{8,24},{9,13},... | collective-permute-start | bytes 565256 | tf_op jit(solution)/shard_map/ppermute | solution.py:437
  35.3 0.0 collective-permute-start.11
  35.3 0.0 collective-permute-done.8.recv
  35.3 0.2 shard_map.264
  35.5 1.6 %collective-permute-start.19 = (bf16[704,128]{1,0:T(8,128)(2,1)S(1)}, bf16[704,128]{1,0:T(8,128)(2,1)S(1)}, u32[]{:S(2)}, u32[]{:S(2)}) collective-permute-start(bf16[704,128]{1,0:T(8,128)(2,1)S(1)} %get-tuple-element.130), channel_id=1, source_target_pairs={{0,8},{1,3},{2,10},{3,1},{4,12},{5,7},{6,14},{7,5},{8,0},{9,11},{1... | collective-permute-start | bytes 540680 | tf_op jit(solution)/shard_map/ppermute | solution.py:437
  37.2 0.0 collective-permute-done.11.tw_recv.tw_recv_ref
  37.2 0.1 collective-permute-start.15
  37.3 1.2 %shard_map.265 = (bf16[8,256,128]{2,1,0:T(8,128)(2,1)}, f32[8,256,128]{2,1,0:T(8,128)}, f32[8,128]{1,0:T(8,128)S(1)}) custom-call(bf16[704,128]{1,0:T(8,128)(2,1)S(1)} %get-tuple-element.119.after.own, bf16[512,128]{1,0:T(8,128)(2,1)S(1)} %collective-permute-done.11.tw_recv.tw_recv_ref, bf16[4,256,128]{2,1,0:T(8,128)(2,1)S(1)} %get-tuple-element.120.out_keep, ...), custom_call_target="tpu_custom_call" | custom-call | flops 1 | tf_op jit(solution)/shard_map/pallas_call | solution.py:26
  38.6 2.4 %collective-permute-done.14.recv = bf16[736,128]{1,0:T(8,128)(2,1)S(1)} collective-permute-done((bf16[736,128]{1,0:T(8,128)(2,1)S(1)}, bf16[736,128]{1,0:T(8,128)(2,1)S(1)}, u32[]{:S(2)}, u32[]{:S(2)}) %collective-permute-start.14) | collective-permute-done | bytes 188448 | tf_op jit(solution)/shard_map/ppermute | solution.py:437
  41.0 0.1 shard_map.266.own.after_ref
  41.1 1.9 %collective-permute-start.16 = (bf16[784,128]{1,0:T(8,128)(2,1)S(1)}, bf16[784,128]{1,0:T(8,128)(2,1)S(1)}, u32[]{:S(2)}, u32[]{:S(2)}) collective-permute-start(bf16[784,128]{1,0:T(8,128)(2,1)S(1)} %shard_map.266.own.after_ref), channel_id=1, source_target_pairs={{0,2},{1,3},{2,0},{3,1},{4,6},{5,7},{6,4},{7,5},{8,10},{9,11},{10,... | collective-permute-start | bytes 602120 | tf_op jit(solution)/shard_map/ppermute | solution.py:437
  43.0 1.6 %collective-permute-start.20 = (bf16[704,128]{1,0:T(8,128)(2,1)S(1)}, bf16[704,128]{1,0:T(8,128)(2,1)S(1)}, u32[]{:S(2)}, u32[]{:S(2)}) collective-permute-start(bf16[704,128]{1,0:T(8,128)(2,1)S(1)} %shard_map.269.own), channel_id=1, source_target_pairs={{0,4},{1,17},{2,6},{3,19},{4,0},{5,21},{6,2},{7,23},{8,12},{9,25},... | collective-permute-start | bytes 540680 | tf_op jit(solution)/shard_map/ppermute | solution.py:437
  44.6 2.3 %collective-permute-done.16.recv = bf16[784,128]{1,0:T(8,128)(2,1)S(1)} collective-permute-done((bf16[784,128]{1,0:T(8,128)(2,1)S(1)}, bf16[784,128]{1,0:T(8,128)(2,1)S(1)}, u32[]{:S(2)}, u32[]{:S(2)}) %collective-permute-start.16) | collective-permute-done | bytes 200736 | tf_op jit(solution)/shard_map/ppermute | solution.py:437
  46.9 1.0 %collective-permute-start.17 = (bf16[848,128]{1,0:T(8,128)(2,1)S(1)}, bf16[848,128]{1,0:T(8,128)(2,1)S(1)}, u32[]{:S(2)}, u32[]{:S(2)}) collective-permute-start(bf16[848,128]{1,0:T(8,128)(2,1)S(1)} %shard_map.267.own.after_ref), channel_id=1, source_target_pairs={{0,8},{1,17},{2,10},{3,19},{4,12},{5,21},{6,14},{7,23},{8,0},{9,25... | collective-permute-start | bytes 651272 | tf_op jit(solution)/shard_map/ppermute | solution.py:437
  47.9 0.6 collective-permute-done.20.recv
  48.6 2.9 %collective-permute-start.21 = (bf16[704,128]{1,0:T(8,128)(2,1)S(1)}, bf16[704,128]{1,0:T(8,128)(2,1)S(1)}, u32[]{:S(2)}, u32[]{:S(2)}) collective-permute-start(bf16[704,128]{1,0:T(8,128)(2,1)S(1)} %shard_map.270.own), channel_id=1, source_target_pairs={{0,16},{1,5},{2,18},{3,7},{4,20},{5,1},{6,22},{7,3},{8,24},{9,13},... | collective-permute-start | bytes 540680 | tf_op jit(solution)/shard_map/ppermute | solution.py:437
  51.5 5.6 %collective-permute-done.17.recv = bf16[848,128]{1,0:T(8,128)(2,1)S(1)} collective-permute-done((bf16[848,128]{1,0:T(8,128)(2,1)S(1)}, bf16[848,128]{1,0:T(8,128)(2,1)S(1)}, u32[]{:S(2)}, u32[]{:S(2)}) %collective-permute-start.17) | collective-permute-done | bytes 217120 | tf_op jit(solution)/shard_map/ppermute | solution.py:437
  57.1 0.1 shard_map.268
  57.2 0.1 collective-permute-start.22
  57.3 1.2 %collective-permute-start.24 = (bf16[704,128]{1,0:T(8,128)(2,1)S(1)}, bf16[704,128]{1,0:T(8,128)(2,1)S(1)}, u32[]{:S(2)}, u32[]{:S(2)}) collective-permute-start(bf16[704,128]{1,0:T(8,128)(2,1)S(1)} %shard_map.271.after_ref.own), channel_id=1, source_target_pairs={{0,8},{1,3},{2,10},{3,1},{4,12},{5,7},{6,14},{7,5},{8,0},{9,11},{1... | collective-permute-start | bytes 540680 | tf_op jit(solution)/shard_map/ppermute | solution.py:437
  58.5 1.3 %collective-permute-done.18.other_ref = bf16[256,128]{1,0:T(8,128)(2,1)S(1)} collective-permute-done((bf16[256,128]{1,0:T(8,128)(2,1)S(1)}, bf16[256,128]{1,0:T(8,128)(2,1)S(1)}, u32[]{:S(2)}, u32[]{:S(2)}) %collective-permute-start.18) | collective-permute-done | bytes 65568 | tf_op jit(solution)/shard_map/ppermute | solution.py:441
  59.8 3.2 %shard_map.272 = (f32[1000,512]{1,0:T(8,128)}, f32[512,128]{1,0:T(8,128)}, f32[1,128]{1,0:T(1,128)}, f32[8,128]{1,0:T(8,128)S(1)}) custom-call(bf16[256,128]{1,0:T(8,128)(2,1)S(1)} %get-tuple-element.129.rows_ref, bf16[256,128]{1,0:T(8,128)(2,1)S(1)} %collective-permute-done.18.other_ref, f32[1000,512]{1,0:T(8,128)S(1)} %copy-done, ...), custom_call_target="tpu_custom_call" | custom-call | flops 1 | tf_op jit(solution)/shard_map/pallas_call | solution.py:26
  63.0 1.5 %collective-permute-done.22.recv = bf16[720,128]{1,0:T(8,128)(2,1)S(1)} collective-permute-done((bf16[720,128]{1,0:T(8,128)(2,1)S(1)}, bf16[720,128]{1,0:T(8,128)(2,1)S(1)}, u32[]{:S(2)}, u32[]{:S(2)}) %collective-permute-start.22) | collective-permute-done | bytes 184352 | tf_op jit(solution)/shard_map/ppermute | solution.py:437
  64.6 1.6 %collective-permute-start.23 = (bf16[1440,128]{1,0:T(8,128)(2,1)S(1)}, bf16[1440,128]{1,0:T(8,128)(2,1)S(1)}, u32[]{:S(2)}, u32[]{:S(2)}) collective-permute-start(bf16[1440,128]{1,0:T(8,128)(2,1)S(1)} %shard_map.273.own.after_ref), channel_id=1, source_target_pairs={{0,4},{1,9},{2,6},{3,11},{4,0},{5,13},{6,2},{7,15},{8,12},{9,1},{1... | collective-permute-start | bytes 1105928 | tf_op jit(solution)/shard_map/ppermute | solution.py:437
  66.2 1.6 %collective-permute-start.25 = (bf16[1408,128]{1,0:T(8,128)(2,1)S(1)}, bf16[1408,128]{1,0:T(8,128)(2,1)S(1)}, u32[]{:S(2)}, u32[]{:S(2)}) collective-permute-start(bf16[1408,128]{1,0:T(8,128)(2,1)S(1)} %shard_map.275.own), channel_id=1, source_target_pairs={{0,2},{1,9},{2,0},{3,11},{4,6},{5,13},{6,4},{7,15},{8,10},{9,1},{1... | collective-permute-start | bytes 1081352 | tf_op jit(solution)/shard_map/ppermute | solution.py:437
  67.8 4.3 %collective-permute-done.23.recv = bf16[1440,128]{1,0:T(8,128)(2,1)S(1)} collective-permute-done((bf16[1440,128]{1,0:T(8,128)(2,1)S(1)}, bf16[1440,128]{1,0:T(8,128)(2,1)S(1)}, u32[]{:S(2)}, u32[]{:S(2)}) %collective-permute-start.23) | collective-permute-done | bytes 368672 | tf_op jit(solution)/shard_map/ppermute | solution.py:437
  72.2 1.2 %shard_map.274 = (f32[2304,128]{1,0:T(8,128)}, f32[2,128,256]{2,1,0:T(8,128)S(1)}, f32[3,128]{1,0:T(4,128)}, f32[3,128]{1,0:T(4,128)}, f32[2,128]{1,0:T(2,128)}, /*index=5*/f32[2,128]{1,0:T(2,128)}, f32[1,128]{1,0:T(1,128)}) custom-call(f32[8,128]{1,0:T(8,128)S(1)} %get-tuple-element.133.after_ref, bf16[1440,128]{1,0:T(8,128)(2,1)S(1)} %shard_map.273.own.after_ref, ...), custom_call_target="tpu_custom_call" | custom-call | flops 1 | tf_op jit(solution)/shard_map/pallas_call | solution.py:26
  73.3 0.4 collective-permute-done.25.recv
  73.7 1.3 %shard_map.276 = (f32[9,128,256]{2,1,0:T(8,128)}, f32[3,256,128]{2,1,0:T(8,128)}, f32[128,256]{1,0:T(8,128)}) custom-call(f32[2,128,256]{2,1,0:T(8,128)S(1)} %get-tuple-element.140.last_ref, bf16[1408,128]{1,0:T(8,128)(2,1)S(1)} %shard_map.275.own, bf16[1408,128]{1,0:T(8,128)(2,1)S(1)} %collective-permute-done.25.recv), custom_call_target="tpu_custom_call" | custom-call | flops 1 | tf_op jit(solution)/shard_map/pallas_call | solution.py:26
  (42 shorter events, 0.4 us)
Async XLA Ops:
  0.6 0.7 copy-start.9
  0.7 0.7 copy-start.10
  0.7 0.7 copy-start.11
  0.7 0.7 copy-start.12
  0.7 0.7 copy-start.13
  0.7 0.7 copy-start.14
  0.7 1.1 %copy-start.1 = (bf16[3,3,256,128]{3,2,1,0:T(8,128)(2,1)S(1)}, bf16[3,3,256,128]{3,2,1,0:T(8,128)(2,1)}, u32[]{:S(2)}) copy-start(bf16[3,3,256,128]{3,2,1,0:T(8,128)(2,1)} %param.20) | copy-start | bytes 1769476
  0.7 1.1 %copy-start.3 = (bf16[512,128]{1,0:T(8,128)(2,1)S(1)}, bf16[512,128]{1,0:T(8,128)(2,1)}, u32[]{:S(2)}) copy-start(bf16[512,128]{1,0:T(8,128)(2,1)} %tw_own_ref.1) | copy-start | bytes 393220
  0.7 1.1 %copy-start.8 = (s32[8]{0:T(128)S(1)}, s32[8]{0:T(128)}, u32[]{:S(2)}) copy-start(s32[8]{0:T(128)} %steps.1) | copy-start | bytes 100
  0.7 4.8 %collective-permute-start.1 = (bf16[9,256,128]{2,1,0:T(8,128)(2,1)}, bf16[9,256,128]{2,1,0:T(8,128)(2,1)}, u32[]{:S(2)}, u32[]{:S(2)}) collective-permute-start(bf16[9,256,128]{2,1,0:T(8,128)(2,1)} %bitcast.10), channel_id=1, source_target_pairs={{0,1},{1,0},{2,3},{3,2},{4,5},{5,4},{6,7},{7,6},{8,9},{9,8},{10,11... | collective-permute-start | bytes 1769480 | tf_op jit(solution)/shard_map/ppermute | solution.py:441
  1.3 4.1 %collective-permute-start = (bf16[8,256,128]{2,1,0:T(8,128)(2,1)}, bf16[8,256,128]{2,1,0:T(8,128)(2,1)S(1)}, u32[]{:S(2)}, u32[]{:S(2)}) collective-permute-start(bf16[8,256,128]{2,1,0:T(8,128)(2,1)} %x_own.5), channel_id=1, source_target_pairs={{0,1},{1,0},{2,3},{3,2},{4,5},{5,4},{6,7},{7,6},{8,9},{9,8},{10,11... | collective-permute-start | bytes 1572872 | tf_op jit(solution)/shard_map/ppermute | solution.py:441
  1.3 1.6 %copy-start = (f32[1000,512]{1,0:T(8,128)S(1)}, f32[1000,512]{1,0:T(8,128)}, u32[]{:S(2)}) copy-start(f32[1000,512]{1,0:T(8,128)} %table_ref.1) | copy-start | bytes 6144004
  3.0 1.2 %copy-start.2 = (bf16[3,3,128,256]{3,2,1,0:T(8,128)(2,1)S(1)}, bf16[3,3,128,256]{3,2,1,0:T(8,128)(2,1)}, u32[]{:S(2)}) copy-start(bf16[3,3,128,256]{3,2,1,0:T(8,128)(2,1)} %param.24) | copy-start | bytes 1769476
  3.0 1.5 %copy-start.6 = (bf16[256,3,128]{2,0,1:T(8,128)(2,1)S(1)}, bf16[256,3,128]{2,0,1:T(8,128)(2,1)}, u32[]{:S(2)}) copy-start(bf16[256,3,128]{2,0,1:T(8,128)(2,1)} %param.25) | copy-start | bytes 589828
  3.0 2.0 %copy-start.4 = (bf16[8,256,128]{2,1,0:T(8,128)(2,1)S(1)}, bf16[8,256,128]{2,1,0:T(8,128)(2,1)}, u32[]{:S(2)}) copy-start(bf16[8,256,128]{2,1,0:T(8,128)(2,1)} %g_own.1) | copy-start | bytes 1572868
  3.0 2.4 %copy-start.7 = (bf16[128,256]{1,0:T(8,128)(2,1)S(1)}, bf16[128,256]{1,0:T(8,128)(2,1)}, u32[]{:S(2)}) copy-start(bf16[128,256]{1,0:T(8,128)(2,1)} %ow_own.1) | copy-start | bytes 196612
  3.0 2.5 %copy-start.5 = (bf16[8,256,128]{2,1,0:T(8,128)(2,1)S(1)}, bf16[8,256,128]{2,1,0:T(8,128)(2,1)}, u32[]{:S(2)}) copy-start(bf16[8,256,128]{2,1,0:T(8,128)(2,1)} %x_own.5) | copy-start | bytes 1572868
  3.7 1.3 %collective-permute-start.2 = (f32[24,128]{1,0:T(8,128)S(1)}, f32[24,128]{1,0:T(8,128)S(1)}, u32[]{:S(2)}, u32[]{:S(2)}) collective-permute-start(f32[24,128]{1,0:T(8,128)S(1)} %get-tuple-element.80.pk_own), channel_id=1, source_target_pairs={{0,1},{1,0},{2,3},{3,2},{4,5},{5,4},{6,7},{7,6},{8,9},{9,8},{10,11... | collective-permute-start | bytes 36872 | tf_op jit(solution)/shard_map/ppermute | solution.py:441
  4.1 5.0 %collective-permute-start.3 = (bf16[9,128,256]{2,1,0:T(8,128)(2,1)S(1)}, bf16[9,128,256]{2,1,0:T(8,128)(2,1)S(1)}, u32[]{:S(2)}, u32[]{:S(2)}) collective-permute-start(bf16[9,128,256]{2,1,0:T(8,128)(2,1)S(1)} %bitcast.13), channel_id=1, source_target_pairs={{0,1},{1,0},{2,3},{3,2},{4,5},{5,4},{6,7},{7,6},{8,9},{9,8},{10,11... | collective-permute-start | bytes 1769480 | tf_op jit(solution)/shard_map/ppermute | solution.py:441
  4.5 4.6 %collective-permute-start.5 = (bf16[3,256,128]{2,1,0:T(8,128)(2,1)S(1)}, bf16[3,256,128]{2,1,0:T(8,128)(2,1)S(1)}, u32[]{:S(2)}, u32[]{:S(2)}) collective-permute-start(bf16[3,256,128]{2,1,0:T(8,128)(2,1)S(1)} %bitcast.15), channel_id=1, source_target_pairs={{0,1},{1,0},{2,3},{3,2},{4,5},{5,4},{6,7},{7,6},{8,9},{9,8},{10,11... | collective-permute-start | bytes 589832 | tf_op jit(solution)/shard_map/ppermute | solution.py:441
  5.0 4.1 %collective-permute-start.4 = (bf16[8,256,128]{2,1,0:T(8,128)(2,1)S(1)}, bf16[8,256,128]{2,1,0:T(8,128)(2,1)S(1)}, u32[]{:S(2)}, u32[]{:S(2)}) collective-permute-start(bf16[8,256,128]{2,1,0:T(8,128)(2,1)S(1)} %copy-done.4), channel_id=1, source_target_pairs={{0,1},{1,0},{2,3},{3,2},{4,5},{5,4},{6,7},{7,6},{8,9},{9,8},{10,11... | collective-permute-start | bytes 1572872 | tf_op jit(solution)/shard_map/ppermute | solution.py:441
  5.3 3.7 %collective-permute-start.6 = (bf16[128,256]{1,0:T(8,128)(2,1)S(1)}, bf16[128,256]{1,0:T(8,128)(2,1)S(1)}, u32[]{:S(2)}, u32[]{:S(2)}) collective-permute-start(bf16[128,256]{1,0:T(8,128)(2,1)S(1)} %copy-done.7), channel_id=1, source_target_pairs={{0,1},{1,0},{2,3},{3,2},{4,5},{5,4},{6,7},{7,6},{8,9},{9,8},{10,11... | collective-permute-start | bytes 196616 | tf_op jit(solution)/shard_map/ppermute | solution.py:441
  15.9 3.0 %collective-permute-start.7 = (bf16[2816,128]{1,0:T(8,128)(2,1)S(1)}, bf16[2816,128]{1,0:T(8,128)(2,1)S(1)}, u32[]{:S(2)}, u32[]{:S(2)}) collective-permute-start(bf16[2816,128]{1,0:T(8,128)(2,1)S(1)} %get-tuple-element.95), channel_id=1, source_target_pairs={{0,1},{1,0},{2,3},{3,2},{4,5},{5,4},{6,7},{7,6},{8,9},{9,8},{10,11... | collective-permute-start | bytes 2162696 | tf_op jit(solution)/shard_map/ppermute | solution.py:441
  21.1 3.1 %collective-permute-start.9 = (bf16[2816,128]{1,0:T(8,128)(2,1)S(1)}, bf16[2816,128]{1,0:T(8,128)(2,1)S(1)}, u32[]{:S(2)}, u32[]{:S(2)}) collective-permute-start(bf16[2816,128]{1,0:T(8,128)(2,1)S(1)} %get-tuple-element.107), channel_id=1, source_target_pairs={{0,1},{1,0},{2,3},{3,2},{4,5},{5,4},{6,7},{7,6},{8,9},{9,8},{10,11... | collective-permute-start | bytes 2162696 | tf_op jit(solution)/shard_map/ppermute | solution.py:441
  21.3 14.0 %collective-permute-start.8 = (bf16[1408,128]{1,0:T(8,128)(2,1)S(1)}, bf16[1408,128]{1,0:T(8,128)(2,1)S(1)}, u32[]{:S(2)}, u32[]{:S(2)}) collective-permute-start(bf16[1408,128]{1,0:T(8,128)(2,1)S(1)} %get-tuple-element.105), channel_id=1, source_target_pairs={{0,2},{1,9},{2,0},{3,11},{4,6},{5,13},{6,4},{7,15},{8,10},{9,1},{1... | collective-permute-start | bytes 1081352 | tf_op jit(solution)/shard_map/ppermute | solution.py:437
  24.6 7.5 %collective-permute-start.10 = (bf16[1424,128]{1,0:T(8,128)(2,1)S(1)}, bf16[1424,128]{1,0:T(8,128)(2,1)S(1)}, u32[]{:S(2)}, u32[]{:S(2)}) collective-permute-start(bf16[1424,128]{1,0:T(8,128)(2,1)S(1)} %get-tuple-element.110), channel_id=1, source_target_pairs={{0,4},{1,9},{2,6},{3,11},{4,0},{5,13},{6,2},{7,15},{8,12},{9,1},{1... | collective-permute-start | bytes 1093640 | tf_op jit(solution)/shard_map/ppermute | solution.py:437
  28.8 8.5 %collective-permute-start.12 = (bf16[4,256,128]{2,1,0:T(8,128)(2,1)S(1)}, bf16[4,256,128]{2,1,0:T(8,128)(2,1)S(1)}, u32[]{:S(2)}, u32[]{:S(2)}) collective-permute-start(bf16[4,256,128]{2,1,0:T(8,128)(2,1)S(1)} %get-tuple-element.121), channel_id=1, source_target_pairs={{0,1},{1,0},{2,3},{3,2},{4,5},{5,4},{6,7},{7,6},{8,9},{9,8},{10,11... | collective-permute-start | bytes 786440 | tf_op jit(solution)/shard_map/ppermute | solution.py:441
  29.0 8.3 %collective-permute-start.13 = (bf16[4,256,128]{2,1,0:T(8,128)(2,1)S(1)}, bf16[4,256,128]{2,1,0:T(8,128)(2,1)S(1)}, u32[]{:S(2)}, u32[]{:S(2)}) collective-permute-start(bf16[4,256,128]{2,1,0:T(8,128)(2,1)S(1)} %get-tuple-element.123), channel_id=1, source_target_pairs={{0,1},{1,0},{2,3},{3,2},{4,5},{5,4},{6,7},{7,6},{8,9},{9,8},{10,11... | collective-permute-start | bytes 786440 | tf_op jit(solution)/shard_map/ppermute | solution.py:441
  32.3 8.7 %collective-permute-start.14 = (bf16[736,128]{1,0:T(8,128)(2,1)S(1)}, bf16[736,128]{1,0:T(8,128)(2,1)S(1)}, u32[]{:S(2)}, u32[]{:S(2)}) collective-permute-start(bf16[736,128]{1,0:T(8,128)(2,1)S(1)} %get-tuple-element.126), channel_id=1, source_target_pairs={{0,16},{1,5},{2,18},{3,7},{4,20},{5,1},{6,22},{7,3},{8,24},{9,13},... | collective-permute-start | bytes 565256 | tf_op jit(solution)/shard_map/ppermute | solution.py:437
  35.3 1.8 %collective-permute-start.11 = (bf16[512,128]{1,0:T(8,128)(2,1)S(1)}, bf16[512,128]{1,0:T(8,128)(2,1)S(1)}, u32[]{:S(2)}, u32[]{:S(2)}) collective-permute-start(bf16[512,128]{1,0:T(8,128)(2,1)S(1)} %copy-done.3), channel_id=1, source_target_pairs={{0,1},{1,0},{2,3},{3,2},{4,5},{5,4},{6,7},{7,6},{8,9},{9,8},{10,11... | collective-permute-start | bytes 393224 | tf_op jit(solution)/shard_map/ppermute | solution.py:441
  35.5 7.4 %collective-permute-start.19 = (bf16[704,128]{1,0:T(8,128)(2,1)S(1)}, bf16[704,128]{1,0:T(8,128)(2,1)S(1)}, u32[]{:S(2)}, u32[]{:S(2)}) collective-permute-start(bf16[704,128]{1,0:T(8,128)(2,1)S(1)} %get-tuple-element.130), channel_id=1, source_target_pairs={{0,8},{1,3},{2,10},{3,1},{4,12},{5,7},{6,14},{7,5},{8,0},{9,11},{1... | collective-permute-start | bytes 540680 | tf_op jit(solution)/shard_map/ppermute | solution.py:437
  37.2 1.4 %collective-permute-start.15 = (f32[16,128]{1,0:T(8,128)S(1)}, f32[16,128]{1,0:T(8,128)S(1)}, u32[]{:S(2)}, u32[]{:S(2)}) collective-permute-start(f32[16,128]{1,0:T(8,128)S(1)} %get-tuple-element.128), channel_id=1, source_target_pairs={{0,1},{1,0},{2,3},{3,2},{4,5},{5,4},{6,7},{7,6},{8,9},{9,8},{10,11... | collective-permute-start | bytes 24584 | tf_op jit(solution)/shard_map/ppermute | solution.py:441
  41.1 5.8 %collective-permute-start.16 = (bf16[784,128]{1,0:T(8,128)(2,1)S(1)}, bf16[784,128]{1,0:T(8,128)(2,1)S(1)}, u32[]{:S(2)}, u32[]{:S(2)}) collective-permute-start(bf16[784,128]{1,0:T(8,128)(2,1)S(1)} %shard_map.266.own.after_ref), channel_id=1, source_target_pairs={{0,2},{1,3},{2,0},{3,1},{4,6},{5,7},{6,4},{7,5},{8,10},{9,11},{10,... | collective-permute-start | bytes 602120 | tf_op jit(solution)/shard_map/ppermute | solution.py:437
  43.0 5.6 %collective-permute-start.20 = (bf16[704,128]{1,0:T(8,128)(2,1)S(1)}, bf16[704,128]{1,0:T(8,128)(2,1)S(1)}, u32[]{:S(2)}, u32[]{:S(2)}) collective-permute-start(bf16[704,128]{1,0:T(8,128)(2,1)S(1)} %shard_map.269.own), channel_id=1, source_target_pairs={{0,4},{1,17},{2,6},{3,19},{4,0},{5,21},{6,2},{7,23},{8,12},{9,25},... | collective-permute-start | bytes 540680 | tf_op jit(solution)/shard_map/ppermute | solution.py:437
  46.9 10.2 %collective-permute-start.17 = (bf16[848,128]{1,0:T(8,128)(2,1)S(1)}, bf16[848,128]{1,0:T(8,128)(2,1)S(1)}, u32[]{:S(2)}, u32[]{:S(2)}) collective-permute-start(bf16[848,128]{1,0:T(8,128)(2,1)S(1)} %shard_map.267.own.after_ref), channel_id=1, source_target_pairs={{0,8},{1,17},{2,10},{3,19},{4,12},{5,21},{6,14},{7,23},{8,0},{9,25... | collective-permute-start | bytes 651272 | tf_op jit(solution)/shard_map/ppermute | solution.py:437
  48.6 8.7 %collective-permute-start.21 = (bf16[704,128]{1,0:T(8,128)(2,1)S(1)}, bf16[704,128]{1,0:T(8,128)(2,1)S(1)}, u32[]{:S(2)}, u32[]{:S(2)}) collective-permute-start(bf16[704,128]{1,0:T(8,128)(2,1)S(1)} %shard_map.270.own), channel_id=1, source_target_pairs={{0,16},{1,5},{2,18},{3,7},{4,20},{5,1},{6,22},{7,3},{8,24},{9,13},... | collective-permute-start | bytes 540680 | tf_op jit(solution)/shard_map/ppermute | solution.py:437
  57.2 7.3 %collective-permute-start.22 = (bf16[720,128]{1,0:T(8,128)(2,1)S(1)}, bf16[720,128]{1,0:T(8,128)(2,1)S(1)}, u32[]{:S(2)}, u32[]{:S(2)}) collective-permute-start(bf16[720,128]{1,0:T(8,128)(2,1)S(1)} %get-tuple-element.131.after_ref.own), channel_id=1, source_target_pairs={{0,16},{1,5},{2,18},{3,7},{4,20},{5,1},{6,22},{7,3},{8,24},{9,13},... | collective-permute-start | bytes 552968 | tf_op jit(solution)/shard_map/ppermute | solution.py:437
  57.3 8.8 %collective-permute-start.24 = (bf16[704,128]{1,0:T(8,128)(2,1)S(1)}, bf16[704,128]{1,0:T(8,128)(2,1)S(1)}, u32[]{:S(2)}, u32[]{:S(2)}) collective-permute-start(bf16[704,128]{1,0:T(8,128)(2,1)S(1)} %shard_map.271.after_ref.own), channel_id=1, source_target_pairs={{0,8},{1,3},{2,10},{3,1},{4,12},{5,7},{6,14},{7,5},{8,0},{9,11},{1... | collective-permute-start | bytes 540680 | tf_op jit(solution)/shard_map/ppermute | solution.py:437
  58.5 1.3 %collective-permute-start.18 = (bf16[256,128]{1,0:T(8,128)(2,1)S(1)}, bf16[256,128]{1,0:T(8,128)(2,1)S(1)}, u32[]{:S(2)}, u32[]{:S(2)}) collective-permute-start(bf16[256,128]{1,0:T(8,128)(2,1)S(1)} %get-tuple-element.129.rows_ref), channel_id=1, source_target_pairs={{0,1},{1,0},{2,3},{3,2},{4,5},{5,4},{6,7},{7,6},{8,9},{9,8},{10,11... | collective-permute-start | bytes 196616 | tf_op jit(solution)/shard_map/ppermute | solution.py:441
  64.6 7.6 %collective-permute-start.23 = (bf16[1440,128]{1,0:T(8,128)(2,1)S(1)}, bf16[1440,128]{1,0:T(8,128)(2,1)S(1)}, u32[]{:S(2)}, u32[]{:S(2)}) collective-permute-start(bf16[1440,128]{1,0:T(8,128)(2,1)S(1)} %shard_map.273.own.after_ref), channel_id=1, source_target_pairs={{0,4},{1,9},{2,6},{3,11},{4,0},{5,13},{6,2},{7,15},{8,12},{9,1},{1... | collective-permute-start | bytes 1105928 | tf_op jit(solution)/shard_map/ppermute | solution.py:437
  66.2 7.5 %collective-permute-start.25 = (bf16[1408,128]{1,0:T(8,128)(2,1)S(1)}, bf16[1408,128]{1,0:T(8,128)(2,1)S(1)}, u32[]{:S(2)}, u32[]{:S(2)}) collective-permute-start(bf16[1408,128]{1,0:T(8,128)(2,1)S(1)} %shard_map.275.own), channel_id=1, source_target_pairs={{0,2},{1,9},{2,0},{3,11},{4,6},{5,13},{6,4},{7,15},{8,10},{9,1},{1... | collective-permute-start | bytes 1081352 | tf_op jit(solution)/shard_map/ppermute | solution.py:437
